TPU v7x, 32 devices: a whole 2x2x4 slice. The times are simulated.
32 devices in a mesh: dp: 4 (over x, core), sp: 8 (over z, y).
Axes of the slice: x: 2, y: 2, z: 4, core: 2. Of those that a mesh axis runs over, the one named last changes fastest.
Arguments:
- tokens: bfloat16 [4, 2048, 1536], P('dp', 'sp'), may hold values from -6 to 6
- cotangent: bfloat16 [4, 2048, 1536], P('dp', 'sp'), may hold values from -6 to 6
- captions: bfloat16 [4, 2, 128, 4096], P('dp', None, 'sp'), may hold values from -6 to 6
- conditioning: float32 [4, 2, 1024], P('dp'), may hold values from -6 to 6
- clip_lens: int32 [4, 2], P('dp'), may hold values from 1024 to 1024, as said below
- w_ada: bfloat16 [1024, 9216], P(None, 'sp'), may hold values from -0.1875 to 0.1875
- b_ada: float32 [9216], P('sp'), may hold values from -3 to 3
- w_query: bfloat16 [1536, 1536], P('sp'), may hold values from -0.15625 to 0.15625
- w_key: bfloat16 [1536, 1536], P('sp'), may hold values from -0.15625 to 0.15625
- w_value: bfloat16 [1536, 1536], P('sp'), may hold values from -0.15625 to 0.15625
- w_out: bfloat16 [1536, 1536], P('sp'), may hold values from -1.25 to 1.25
- gate_cross: float32 [24], replicated, may hold values from -1.5 to 1.5
- w_text_key: bfloat16 [4096, 1536], P('sp'), may hold values from -0.09375 to 0.09375
- w_text_value: bfloat16 [4096, 1536], P('sp'), may hold values from -0.09375 to 0.09375
- w_gate: bfloat16 [1536, 4096], P('sp'), may hold values from -0.15625 to 0.15625
- w_up: bfloat16 [1536, 4096], P('sp'), may hold values from -0.15625 to 0.15625
- w_down: bfloat16 [4096, 1536], P('sp'), may hold values from -0.09375 to 0.09375
Outputs:
- result: bfloat16 [4, 2048, 1536], P('dp', 'sp')
- d_tokens: float32 [4, 2048, 1536], P('dp', 'sp')
- d_captions: float32 [4, 2, 128, 4096], P('dp', None, 'sp')
- d_conditioning: float32 [4, 2, 1024], P('dp')
- d_w_ada: float32 [1024, 9216], P(None, 'sp')
- d_b_ada: float32 [9216], P('sp')
- d_w_query: float32 [1536, 1536], P('sp')
- d_w_key: float32 [1536, 1536], P('sp')
- d_w_value: float32 [1536, 1536], P('sp')
- d_w_out: float32 [1536, 1536], P('sp')
- d_gate_cross: float32 [24], replicated
- d_w_text_key: float32 [4096, 1536], P('sp')
- d_w_text_value: float32 [4096, 1536], P('sp')
- d_w_gate: float32 [1536, 4096], P('sp')
- d_w_up: float32 [1536, 4096], P('sp')
- d_w_down: float32 [4096, 1536], P('sp')
Inputs may be any that keep to these rules, and one draw needn't show every extreme that they name: `clip_lens`: the 2 lengths of a pack sum to 2048; each is 1024 or more, and one of them is half of 2048 or more.
All inputs are finite; a program needn't handle non-finite values.
Results may differ from a plain program's by a relative error of at most 0.04.
Values may be sent and summed in bfloat16 or wider, within the bound.
No kernel may reach another device: no remote copies, remote signals or barrier semaphores. Data moves between devices by JAX's collectives and lax.ppermute only.
A program may use at most 384 MiB of HBM per device.

v0:
```python
import jax
import jax.numpy as jnp
from jax import lax
from jax.sharding import PartitionSpec as P

D = 1536
HEADS = 24
HD = 64
TEXT = 4096
CAP = 128
CLIPS = 2


EPSILON = 1e-06
MASKED = -1e30
HIGHEST = lax.Precision.HIGHEST


def rope_tables(positions):
    half_width = HD // 2
    freq = 10000.0 ** (-(jnp.arange(half_width, dtype=jnp.float32) * 2.0 / HD))
    angle = positions.astype(jnp.float32)[:, None] * freq[None, :]
    return (jnp.cos(angle)[:, None, :], jnp.sin(angle)[:, None, :])


def rotate(values, cos_table, sin_table):
    half_width = values.shape[-1] // 2
    first_half = values[..., :half_width]
    second_half = values[..., half_width:]
    return jnp.concatenate(
        [
            first_half * cos_table - second_half * sin_table,
            first_half * sin_table + second_half * cos_table,
        ],
        axis=-1,
    )


def rotate_back(grads, cos_table, sin_table):
    half_width = grads.shape[-1] // 2
    first_half = grads[..., :half_width]
    second_half = grads[..., half_width:]
    return jnp.concatenate(
        [
            first_half * cos_table + second_half * sin_table,
            second_half * cos_table - first_half * sin_table,
        ],
        axis=-1,
    )


def inverse_rms(values):
    return lax.rsqrt(jnp.mean(values * values, axis=-1, keepdims=True) + EPSILON)


def norm_back(grads, normed, inverse):
    return inverse * (grads - normed * jnp.mean(grads * normed, axis=-1, keepdims=True))


def per_clip(select, values):
    return jnp.einsum("tc,td->cd", select, values, precision=HIGHEST)


def local(
    tokens,
    cotangent,
    captions,
    conditioning,
    clip_lens,
    w_ada,
    b_ada,
    w_query,
    w_key,
    w_value,
    w_out,
    gate_cross,
    w_text_key,
    w_text_value,
    w_gate,
    w_up,
    w_down,
):
    shard = lax.axis_index("sp")
    cycle_size = lax.axis_size("sp")
    tok_rows = tokens.shape[1]
    half_rows = tok_rows // 2
    score_scale = HD ** (-0.5)
    row_index = jnp.arange(tok_rows, dtype=jnp.int32)
    logical_block = jnp.where(row_index < half_rows, shard, 2 * cycle_size - 1 - shard)
    logical = logical_block * half_rows + row_index % half_rows
    lengths = clip_lens[0]
    clip_ends = jnp.cumsum(lengths)
    clip_starts = clip_ends - lengths
    clip_index = 0
    segment = (logical >= clip_ends[clip_index]).astype(jnp.int32)
    offset = jnp.zeros((tok_rows,), jnp.int32)
    for clip_index in range(CLIPS):
        offset = offset + jnp.where(segment == clip_index, clip_starts[clip_index], 0)
    positions = logical - offset
    inputs = tokens[0].astype(jnp.float32)
    cond_row = conditioning[0]
    cond_act = jax.nn.silu(cond_row).astype(jnp.bfloat16)
    mod_part = jnp.dot(cond_act, w_ada, preferred_element_type=jnp.float32) + b_ada[None, :]
    modulation = lax.all_gather(mod_part, "sp", axis=1, tiled=True)
    select = (segment[:, None] == jnp.arange(CLIPS, dtype=jnp.int32)[None, :]).astype(jnp.float32)
    per_token = jnp.dot(select, modulation, precision=HIGHEST)
    shift_one, scale_one, gate_one, shift_two, scale_two, gate_two = jnp.split(per_token, 6, axis=1)
    weights_full = (
        lax.all_gather(w_query, "sp", axis=0, tiled=True),
        lax.all_gather(w_key, "sp", axis=0, tiled=True),
        lax.all_gather(w_value, "sp", axis=0, tiled=True),
        lax.all_gather(w_out, "sp", axis=0, tiled=True),
        lax.all_gather(w_gate, "sp", axis=0, tiled=True),
        lax.all_gather(w_up, "sp", axis=0, tiled=True),
        lax.all_gather(w_down, "sp", axis=0, tiled=True),
        lax.all_gather(w_text_key, "sp", axis=0, tiled=True),
        lax.all_gather(w_text_value, "sp", axis=0, tiled=True),
    )
    (
        query_full,
        key_full,
        value_full,
        out_full,
        gate_full,
        up_full,
        down_full,
        text_key_full,
        text_value_full,
    ) = weights_full
    inverse_one = inverse_rms(inputs)
    normed_one = inputs * inverse_one
    block_in = (normed_one * (1.0 + scale_one) + shift_one).astype(jnp.bfloat16)
    cos_table, sin_table = rope_tables(positions)

    def project(weight):
        return jnp.dot(block_in, weight, preferred_element_type=jnp.float32).reshape(
            tok_rows, HEADS, HD
        )

    query_raw = project(query_full)
    inverse_query = inverse_rms(query_raw)
    query_normed = query_raw * inverse_query
    query_rot = rotate(query_normed, cos_table, sin_table).astype(jnp.bfloat16)
    key_raw = project(key_full)
    inverse_key = inverse_rms(key_raw)
    key_normed = key_raw * inverse_key
    key_rot = rotate(key_normed, cos_table, sin_table).astype(jnp.bfloat16)
    value_rows = project(value_full).astype(jnp.bfloat16)
    caption_feats = captions[0]
    flat_caption = caption_feats.reshape(-1, TEXT)
    cap_key_part = (
        jnp.dot(flat_caption, text_key_full, preferred_element_type=jnp.float32)
        .astype(jnp.bfloat16)
        .reshape(CLIPS, -1, D)
    )
    cap_value_part = (
        jnp.dot(flat_caption, text_value_full, preferred_element_type=jnp.float32)
        .astype(jnp.bfloat16)
        .reshape(CLIPS, -1, D)
    )
    cap_key_all, cap_value_all = (
        lax.all_gather(cap_key_part, "sp", axis=1, tiled=True),
        lax.all_gather(cap_value_part, "sp", axis=1, tiled=True),
    )
    cap_key_heads = cap_key_all.reshape(CLIPS * CAP, HEADS, HD)
    cap_value_heads = cap_value_all.reshape(CLIPS * CAP, HEADS, HD)
    caption_clip = jnp.arange(CLIPS * CAP, dtype=jnp.int32) // CAP
    run_max = jnp.full((HEADS, tok_rows), MASKED, jnp.float32)
    key_piece = lax.all_gather(key_rot, "sp", axis=0, tiled=True)
    value_piece = lax.all_gather(value_rows, "sp", axis=0, tiled=True)
    segment_piece = lax.all_gather(segment, "sp", axis=0, tiled=True)
    scores = (
        jnp.einsum("qhd,khd->hqk", query_rot, key_piece, preferred_element_type=jnp.float32)
        * score_scale
    )
    allowed = (segment[:, None] == segment_piece[None, :])[None]
    scores = jnp.where(allowed, scores, MASKED)
    new_max = jnp.maximum(run_max, jnp.max(scores, axis=-1))
    weights_exp = jnp.where(allowed, jnp.exp(scores - new_max[:, :, None]), 0.0)
    new_total = jnp.sum(weights_exp, axis=-1)
    new_acc = jnp.einsum(
        "hqk,khd->qhd",
        weights_exp.astype(jnp.bfloat16),
        value_piece,
        preferred_element_type=jnp.float32,
    )
    self_out = new_acc / jnp.transpose(new_total)[:, :, None]
    log_total = jnp.transpose(new_max + jnp.log(new_total))
    cross_scores = (
        jnp.einsum("qhd,khd->hqk", query_rot, cap_key_heads, preferred_element_type=jnp.float32)
        * score_scale
    )
    own_clip = (segment[:, None] == caption_clip[None, :])[None]
    cross_probs = jax.nn.softmax(jnp.where(own_clip, cross_scores, MASKED), axis=-1)
    cross_low = cross_probs.astype(jnp.bfloat16)
    cross_out = jnp.einsum(
        "hqk,khd->qhd", cross_low, cap_value_heads, preferred_element_type=jnp.float32
    )
    tanh_gate = jnp.tanh(gate_cross)
    mixed = (
        (self_out + tanh_gate[None, :, None] * cross_out).astype(jnp.bfloat16).reshape(tok_rows, D)
    )
    attn_out = jnp.dot(mixed, out_full, preferred_element_type=jnp.float32)
    middle = inputs + gate_one * attn_out
    inverse_two = inverse_rms(middle)
    normed_two = middle * inverse_two
    ffn_in = (normed_two * (1.0 + scale_two) + shift_two).astype(jnp.bfloat16)
    gate_proj = jnp.dot(ffn_in, gate_full, preferred_element_type=jnp.float32)
    up_proj = jnp.dot(ffn_in, up_full, preferred_element_type=jnp.float32)
    sigmoid_gate = jax.nn.sigmoid(gate_proj)
    silu_gate = jax.nn.silu(gate_proj)
    hidden = (silu_gate * up_proj).astype(jnp.bfloat16)
    branch = jnp.dot(hidden, down_full, preferred_element_type=jnp.float32)
    result = (middle + gate_two * branch).astype(jnp.bfloat16)
    out_grad = cotangent[0].astype(jnp.float32)
    branch_grad = (gate_two * out_grad).astype(jnp.bfloat16)
    hidden_grad = jnp.einsum(
        "td,fd->tf", branch_grad, down_full, preferred_element_type=jnp.float32
    )
    grad_down = jnp.einsum("tf,td->fd", hidden, branch_grad, preferred_element_type=jnp.float32)
    gate_grad = (
        hidden_grad * up_proj * sigmoid_gate * (1.0 + gate_proj * (1.0 - sigmoid_gate))
    ).astype(jnp.bfloat16)
    up_grad = (hidden_grad * silu_gate).astype(jnp.bfloat16)
    ffn_in_grad = jnp.einsum(
        "tf,df->td", gate_grad, gate_full, preferred_element_type=jnp.float32
    ) + jnp.einsum("tf,df->td", up_grad, up_full, preferred_element_type=jnp.float32)
    grad_gate_w = jnp.einsum("td,tf->df", ffn_in, gate_grad, preferred_element_type=jnp.float32)
    grad_up_w = jnp.einsum("td,tf->df", ffn_in, up_grad, preferred_element_type=jnp.float32)
    gate_two_tok = out_grad * branch
    scale_two_tok = ffn_in_grad * normed_two
    middle_grad = out_grad + norm_back(ffn_in_grad * (1.0 + scale_two), normed_two, inverse_two)
    attn_grad = (gate_one * middle_grad).astype(jnp.bfloat16)
    gate_one_tok = middle_grad * attn_out
    grad_out_w = jnp.einsum("td,te->de", mixed, attn_grad, preferred_element_type=jnp.float32)
    mixed_grad = jnp.einsum(
        "te,de->td", attn_grad, out_full, preferred_element_type=jnp.float32
    ).reshape(tok_rows, HEADS, HD)
    gate_cross_part = jnp.sum(mixed_grad * cross_out, axis=(0, 2)) * (1.0 - tanh_gate * tanh_gate)
    self_grad = mixed_grad.astype(jnp.bfloat16)
    cross_grad = (tanh_gate[None, :, None] * mixed_grad).astype(jnp.bfloat16)
    cross_dp = jnp.einsum(
        "qhd,khd->hqk", cross_grad, cap_value_heads, preferred_element_type=jnp.float32
    )
    cap_value_grad = jnp.einsum(
        "hqk,qhd->khd", cross_low, cross_grad, preferred_element_type=jnp.float32
    )
    cross_ds = (
        cross_probs * (cross_dp - jnp.sum(cross_probs * cross_dp, axis=-1, keepdims=True))
    ).astype(jnp.bfloat16)
    query_grad_cross = jnp.einsum(
        "hqk,khd->qhd", cross_ds, cap_key_heads, preferred_element_type=jnp.float32
    )
    cap_key_grad = (
        jnp.einsum("hqk,qhd->khd", cross_ds, query_rot, preferred_element_type=jnp.float32)
        * score_scale
    )
    row_delta = jnp.sum(self_grad.astype(jnp.float32) * self_out, axis=-1)
    query_piece = lax.all_gather(query_rot, "sp", axis=0, tiled=True)
    grad_piece = lax.all_gather(self_grad, "sp", axis=0, tiled=True)
    log_piece = lax.all_gather(log_total.astype(jnp.bfloat16), "sp", axis=0, tiled=True).astype(
        jnp.float32
    )
    delta_piece = lax.all_gather(row_delta.astype(jnp.bfloat16), "sp", axis=0, tiled=True).astype(
        jnp.float32
    )
    segment_piece = lax.all_gather(segment, "sp", axis=0, tiled=True)
    scores = (
        jnp.einsum("qhd,khd->hqk", query_piece, key_rot, preferred_element_type=jnp.float32)
        * score_scale
    )
    allowed = (segment_piece[:, None] == segment[None, :])[None]
    probs = jnp.where(allowed, jnp.exp(scores - jnp.transpose(log_piece)[:, :, None]), 0.0)
    value_acc = jnp.einsum(
        "hqk,qhd->khd", probs.astype(jnp.bfloat16), grad_piece, preferred_element_type=jnp.float32
    )
    prob_grad = jnp.einsum(
        "qhd,khd->hqk", grad_piece, value_rows, preferred_element_type=jnp.float32
    )
    score_grad = (probs * (prob_grad - jnp.transpose(delta_piece)[:, :, None])).astype(jnp.bfloat16)
    key_acc = jnp.einsum(
        "hqk,qhd->khd", score_grad, query_piece, preferred_element_type=jnp.float32
    )
    key_acc, value_acc = (key_acc, value_acc)
    key_piece = lax.all_gather(key_rot, "sp", axis=0, tiled=True)
    value_piece = lax.all_gather(value_rows, "sp", axis=0, tiled=True)
    segment_piece = lax.all_gather(segment, "sp", axis=0, tiled=True)
    scores = (
        jnp.einsum("qhd,khd->hqk", query_rot, key_piece, preferred_element_type=jnp.float32)
        * score_scale
    )
    allowed = (segment[:, None] == segment_piece[None, :])[None]
    probs = jnp.where(allowed, jnp.exp(scores - jnp.transpose(log_total)[:, :, None]), 0.0)
    prob_grad = jnp.einsum(
        "qhd,khd->hqk", self_grad, value_piece, preferred_element_type=jnp.float32
    )
    score_grad = (probs * (prob_grad - jnp.transpose(row_delta)[:, :, None])).astype(jnp.bfloat16)
    query_acc = jnp.einsum(
        "hqk,khd->qhd", score_grad, key_piece, preferred_element_type=jnp.float32
    )
    query_rot_grad = (query_acc + query_grad_cross) * score_scale
    key_rot_grad = key_acc * score_scale
    query_raw_grad = (
        norm_back(rotate_back(query_rot_grad, cos_table, sin_table), query_normed, inverse_query)
        .astype(jnp.bfloat16)
        .reshape(tok_rows, D)
    )
    key_raw_grad = (
        norm_back(rotate_back(key_rot_grad, cos_table, sin_table), key_normed, inverse_key)
        .astype(jnp.bfloat16)
        .reshape(tok_rows, D)
    )
    value_raw_grad = value_acc.astype(jnp.bfloat16).reshape(tok_rows, D)
    block_in_grad = (
        jnp.einsum("te,de->td", query_raw_grad, query_full, preferred_element_type=jnp.float32)
        + jnp.einsum("te,de->td", key_raw_grad, key_full, preferred_element_type=jnp.float32)
        + jnp.einsum("te,de->td", value_raw_grad, value_full, preferred_element_type=jnp.float32)
    )
    grad_query_w = jnp.einsum(
        "td,te->de", block_in, query_raw_grad, preferred_element_type=jnp.float32
    )
    grad_key_w = jnp.einsum("td,te->de", block_in, key_raw_grad, preferred_element_type=jnp.float32)
    grad_value_w = jnp.einsum(
        "td,te->de", block_in, value_raw_grad, preferred_element_type=jnp.float32
    )
    scale_one_tok = block_in_grad * normed_one
    inputs_grad = middle_grad + norm_back(
        block_in_grad * (1.0 + scale_one), normed_one, inverse_one
    )
    mod_grad_part = jnp.concatenate(
        [
            per_clip(select, block_in_grad),
            per_clip(select, scale_one_tok),
            per_clip(select, gate_one_tok),
            per_clip(select, ffn_in_grad),
            per_clip(select, scale_two_tok),
            per_clip(select, gate_two_tok),
        ],
        axis=1,
    )
    cap_key_home, cap_value_home, mod_grad = (
        lax.psum_scatter(
            cap_key_grad.reshape(CLIPS, CAP, D).astype(jnp.bfloat16),
            "sp",
            scatter_dimension=1,
            tiled=True,
        ).astype(jnp.float32),
        lax.psum_scatter(
            cap_value_grad.reshape(CLIPS, CAP, D).astype(jnp.bfloat16),
            "sp",
            scatter_dimension=1,
            tiled=True,
        ).astype(jnp.float32),
        lax.psum_scatter(
            mod_grad_part.astype(jnp.bfloat16), "sp", scatter_dimension=1, tiled=True
        ).astype(jnp.float32),
    )
    cap_key_low = cap_key_home.astype(jnp.bfloat16)
    cap_value_low = cap_value_home.astype(jnp.bfloat16)
    mod_low = mod_grad.astype(jnp.bfloat16)
    caption_grad = jnp.einsum(
        "cpd,ed->cpe", cap_key_low, text_key_full, preferred_element_type=jnp.float32
    ) + jnp.einsum(
        "cpd,ed->cpe", cap_value_low, text_value_full, preferred_element_type=jnp.float32
    )
    grad_text_key = jnp.einsum(
        "cpe,cpd->ed", caption_feats, cap_key_low, preferred_element_type=jnp.float32
    )
    grad_text_value = jnp.einsum(
        "cpe,cpd->ed", caption_feats, cap_value_low, preferred_element_type=jnp.float32
    )
    grad_ada = jnp.einsum("cu,cv->uv", cond_act, mod_low, preferred_element_type=jnp.float32)
    grad_bias = jnp.sum(mod_low.astype(jnp.float32), axis=0)
    cond_part = jnp.einsum("cv,uv->cu", mod_low, w_ada, preferred_element_type=jnp.float32)
    cond_sum, gate_sum = lax.psum((cond_part, gate_cross_part), "sp")
    sigmoid_cond = jax.nn.sigmoid(cond_row)
    cond_grad = cond_sum * sigmoid_cond * (1.0 + cond_row * (1.0 - sigmoid_cond))
    home = (
        lax.psum_scatter(
            grad_query_w.astype(jnp.bfloat16), "sp", scatter_dimension=0, tiled=True
        ).astype(jnp.float32),
        lax.psum_scatter(
            grad_key_w.astype(jnp.bfloat16), "sp", scatter_dimension=0, tiled=True
        ).astype(jnp.float32),
        lax.psum_scatter(
            grad_value_w.astype(jnp.bfloat16), "sp", scatter_dimension=0, tiled=True
        ).astype(jnp.float32),
        lax.psum_scatter(
            grad_out_w.astype(jnp.bfloat16), "sp", scatter_dimension=0, tiled=True
        ).astype(jnp.float32),
        lax.psum_scatter(
            grad_gate_w.astype(jnp.bfloat16), "sp", scatter_dimension=0, tiled=True
        ).astype(jnp.float32),
        lax.psum_scatter(
            grad_up_w.astype(jnp.bfloat16), "sp", scatter_dimension=0, tiled=True
        ).astype(jnp.float32),
        lax.psum_scatter(
            grad_down.astype(jnp.bfloat16), "sp", scatter_dimension=0, tiled=True
        ).astype(jnp.float32),
        lax.psum_scatter(
            grad_text_key.astype(jnp.bfloat16), "sp", scatter_dimension=0, tiled=True
        ).astype(jnp.float32),
        lax.psum_scatter(
            grad_text_value.astype(jnp.bfloat16), "sp", scatter_dimension=0, tiled=True
        ).astype(jnp.float32),
    )
    totals = (
        lax.psum(home[0].astype(jnp.bfloat16), "dp").astype(jnp.float32),
        lax.psum(home[1].astype(jnp.bfloat16), "dp").astype(jnp.float32),
        lax.psum(home[2].astype(jnp.bfloat16), "dp").astype(jnp.float32),
        lax.psum(home[3].astype(jnp.bfloat16), "dp").astype(jnp.float32),
        lax.psum(home[4].astype(jnp.bfloat16), "dp").astype(jnp.float32),
        lax.psum(home[5].astype(jnp.bfloat16), "dp").astype(jnp.float32),
        lax.psum(home[6].astype(jnp.bfloat16), "dp").astype(jnp.float32),
        lax.psum(home[7].astype(jnp.bfloat16), "dp").astype(jnp.float32),
        lax.psum(home[8].astype(jnp.bfloat16), "dp").astype(jnp.float32),
        lax.psum(grad_ada.astype(jnp.bfloat16), "dp").astype(jnp.float32),
        lax.psum(grad_bias.astype(jnp.bfloat16), "dp").astype(jnp.float32),
        lax.psum(gate_sum.astype(jnp.bfloat16), "dp").astype(jnp.float32),
    )
    (
        d_query,
        d_key,
        d_value,
        d_out,
        d_gate_w,
        d_up_w,
        d_down_w,
        d_text_key,
        d_text_value,
        d_ada,
        d_bias,
        d_gate_cross,
    ) = totals
    return (
        result[None],
        inputs_grad[None],
        caption_grad[None],
        cond_grad[None],
        d_ada,
        d_bias,
        d_query,
        d_key,
        d_value,
        d_out,
        d_gate_cross,
        d_text_key,
        d_text_value,
        d_gate_w,
        d_up_w,
        d_down_w,
    )


def solution(mesh):
    return jax.shard_map(
        local,
        mesh=mesh,
        in_specs=(
            P("dp", "sp", None),
            P("dp", "sp", None),
            P("dp", None, "sp", None),
            P("dp", None, None),
            P("dp", None),
            P(None, "sp"),
            P("sp"),
            P("sp", None),
            P("sp", None),
            P("sp", None),
            P("sp", None),
            P(),
            P("sp", None),
            P("sp", None),
            P("sp", None),
            P("sp", None),
            P("sp", None),
        ),
        out_specs=(
            P("dp", "sp", None),
            P("dp", "sp", None),
            P("dp", None, "sp", None),
            P("dp", None, None),
            P(None, "sp"),
            P("sp"),
            P("sp", None),
            P("sp", None),
            P("sp", None),
            P("sp", None),
            P(),
            P("sp", None),
            P("sp", None),
            P("sp", None),
            P("sp", None),
            P("sp", None),
        ),
        check_vma=False,
    )
```

profile of v0, /device:TPU:0, one launch (start us, length us, event | category | flops | bytes accessed | tf_op | source)
XLA Modules:
  0.0 3542.9 jit_solution(18147114157476209594)
XLA Ops:
  11.4 32.8 all_gather.61
  56.0 37.3 %all-gather.21.cloned.1.call-done = bf16[1536,1536]{1,0:T(8,128)(2,1)} async-done(((bf16[192,1536]{1,0:T(8,128)(2,1)}), bf16[1536,1536]{1,0:T(8,128)(2,1)}) %all-gather.21.cloned.1.call-update) | async-done | bytes 4718608 | tf_op jit(solution)/shard_map/all_gather | solution.py:110
  93.3 5.1 fusion.136
  101.5 72.1 %all-gather.19.cloned.1.call-done = bf16[1536,1536]{1,0:T(8,128)(2,1)} async-done(((bf16[192,1536]{1,0:T(8,128)(2,1)}), bf16[1536,1536]{1,0:T(8,128)(2,1)}) %all-gather.19.cloned.1.call-update) | async-done | bytes 4718608 | tf_op jit(solution)/shard_map/all_gather | solution.py:109
  173.6 5.1 fusion.135
  190.6 63.2 %all-gather.15.cloned.1.call-done = bf16[1536,1536]{1,0:T(8,128)(2,1)} async-done(((bf16[192,1536]{1,0:T(8,128)(2,1)}), bf16[1536,1536]{1,0:T(8,128)(2,1)}) %all-gather.15.cloned.1.call-update) | async-done | bytes 4718608 | tf_op jit(solution)/shard_map/all_gather | solution.py:111
  263.9 17.9 all-gather
  285.9 68.6 %all-gather.23.cloned.1.call-done = bf16[2048,24,64]{0,2,1:T(8,128)(2,1)} async-done(((bf16[256,24,64]{0,2,1:T(8,128)(2,1)}), bf16[2048,24,64]{0,2,1:T(8,128)(2,1)}) %all-gather.23.cloned.1.call-update) | async-done | bytes 6291472 | tf_op jit(solution)/shard_map/all_gather | solution.py:169
  354.5 22.4 select_reduce_fusion
  378.2 23.4 fusion.2
  401.6 129.6 %all-gather.25.cloned.1.call-done = bf16[4096,1536]{1,0:T(8,128)(2,1)} async-done(((bf16[512,1536]{1,0:T(8,128)(2,1)}), bf16[4096,1536]{1,0:T(8,128)(2,1)}) %all-gather.25.cloned.1.call-update) | async-done | bytes 12582928 | tf_op jit(solution)/shard_map/all_gather | solution.py:117
  531.2 6.7 convolution_convert_fusion.10
  537.9 36.7 %all_gather.69 = bf16[2,128,1536]{2,1,0:T(8,128)(2,1)} all-gather(bf16[2,16,1536]{2,1,0:T(8,128)(2,1)S(1)} %bitcast.261), channel_id=1, replica_groups=mesh['dp'=4,'sp'=8] {'sp'}, dimensions={1}, use_global_device_ids=true | all-gather | bytes 884736 | tf_op jit(solution)/shard_map/all_gather | solution.py:163
  580.8 133.2 %all-gather.27.cloned.1.call-done = bf16[4096,1536]{1,0:T(8,128)(2,1)} async-done(((bf16[512,1536]{1,0:T(8,128)(2,1)}), bf16[4096,1536]{1,0:T(8,128)(2,1)}) %all-gather.27.cloned.1.call-update) | async-done | bytes 12582928 | tf_op jit(solution)/shard_map/all_gather | solution.py:116
  714.0 6.7 convolution_convert_fusion.9
  720.8 36.7 %all_gather.71 = bf16[2,128,1536]{2,1,0:T(8,128)(2,1)} all-gather(bf16[2,16,1536]{2,1,0:T(8,128)(2,1)S(1)} %bitcast.262), channel_id=1, replica_groups=mesh['dp'=4,'sp'=8] {'sp'}, dimensions={1}, use_global_device_ids=true | all-gather | bytes 884736 | tf_op jit(solution)/shard_map/all_gather | solution.py:162
  763.7 6.6 fusion.134
  770.3 5.0 fusion.63
  775.4 50.0 %all-gather.17.cloned.1.call-done = bf16[2048,24,64]{0,2,1:T(8,128)(2,1)} async-done(((bf16[256,24,64]{0,2,1:T(8,128)(2,1)}), bf16[2048,24,64]{0,2,1:T(8,128)(2,1)}) %all-gather.17.cloned.1.call-update) | async-done | bytes 6291472 | tf_op jit(solution)/shard_map/all_gather | solution.py:170
  825.3 23.2 fusion.57
  848.5 57.1 %all-gather.29.cloned.1.call-done = bf16[1536,1536]{1,0:T(8,128)(2,1)} async-done(((bf16[192,1536]{1,0:T(8,128)(2,1)}), bf16[1536,1536]{1,0:T(8,128)(2,1)}) %all-gather.29.cloned.1.call-update) | async-done | bytes 4718608 | tf_op jit(solution)/shard_map/all_gather | solution.py:112
  905.6 5.7 multiply_reduce_fusion.5
  915.2 167.2 %all-gather.31.cloned.1.call-done = bf16[1536,4096]{1,0:T(8,128)(2,1)} async-done(((bf16[192,4096]{1,0:T(8,128)(2,1)}), bf16[1536,4096]{1,0:T(8,128)(2,1)}) %all-gather.31.cloned.1.call-update) | async-done | bytes 12582928 | tf_op jit(solution)/shard_map/all_gather | solution.py:113
  1082.4 9.5 fusion.137
  1091.9 167.2 %all-gather.33.cloned.1.call-done = bf16[1536,4096]{1,0:T(8,128)(2,1)} async-done(((bf16[192,4096]{1,0:T(8,128)(2,1)}), bf16[1536,4096]{1,0:T(8,128)(2,1)}) %all-gather.33.cloned.1.call-update) | async-done | bytes 12582928 | tf_op jit(solution)/shard_map/all_gather | solution.py:114
  1259.1 9.7 fusion.138
  1268.8 167.2 %all-gather.35.cloned.1.call-done = bf16[4096,1536]{1,0:T(8,128)(2,1)} async-done(((bf16[512,1536]{1,0:T(8,128)(2,1)}), bf16[4096,1536]{1,0:T(8,128)(2,1)}) %all-gather.35.cloned.1.call-update) | async-done | bytes 12582928 | tf_op jit(solution)/shard_map/all_gather | solution.py:115
  1436.0 11.5 multiply_convert_fusion.5
  1447.5 8.4 fusion.140
  1455.9 11.2 multiply_reduce_fusion.4
  1467.1 7.6 fusion.139
  1494.0 31.3 all_gather.77
  1527.4 10.4 all-gather.37.cloned.1.call-done
  1537.8 21.3 fusion.131
  1559.2 6.9 multiply_reduce_fusion
  1577.4 5.3 fusion.75
  1586.7 31.3 all_gather.79
  1622.8 29.0 multiply_bitcast_fusion.1
  1651.8 27.6 multiply_bitcast_fusion
  1708.1 22.8 fusion.70
  1745.1 4.9 convolution_convert_fusion.3
  1750.0 5.0 convolution_convert_fusion.6
  1755.1 5.1 convolution_convert_fusion.5
  1760.4 5.0 convolution_convert_fusion.4
  1765.5 9.9 convolution_convert_fusion.2
  1775.4 9.9 convolution_convert_fusion.1
  1785.4 10.3 convolution_convert_fusion
  1796.7 7.3 fusion.16
  1804.1 7.4 fusion.17
  1811.6 28.7 reduce-scatter.37.cloned.1.call-done
  1843.6 94.6 %reduce-scatter.25.cloned.1.call-done = bf16[192,1536]{1,0:T(8,128)(2,1)} async-done(((bf16[1536,1536]{1,0:T(8,128)(2,1)}), bf16[192,1536]{1,0:T(8,128)(2,1)}) %reduce-scatter.25.cloned.1.call-update) | async-done | bytes 589840 | tf_op jit(solution)/shard_map/reduce_scatter | solution.py:388
  1938.2 99.1 %reduce-scatter.19.cloned.1.call-done = bf16[192,1536]{1,0:T(8,128)(2,1)} async-done(((bf16[1536,1536]{1,0:T(8,128)(2,1)}), bf16[192,1536]{1,0:T(8,128)(2,1)}) %reduce-scatter.19.cloned.1.call-update) | async-done | bytes 589840 | tf_op jit(solution)/shard_map/reduce_scatter | solution.py:379
  2037.3 98.8 %reduce-scatter.21.cloned.1.call-done = bf16[192,1536]{1,0:T(8,128)(2,1)} async-done(((bf16[1536,1536]{1,0:T(8,128)(2,1)}), bf16[192,1536]{1,0:T(8,128)(2,1)}) %reduce-scatter.21.cloned.1.call-update) | async-done | bytes 589840 | tf_op jit(solution)/shard_map/reduce_scatter | solution.py:382
  2136.2 98.7 %reduce-scatter.23.cloned.1.call-done = bf16[192,1536]{1,0:T(8,128)(2,1)} async-done(((bf16[1536,1536]{1,0:T(8,128)(2,1)}), bf16[192,1536]{1,0:T(8,128)(2,1)}) %reduce-scatter.23.cloned.1.call-update) | async-done | bytes 589840 | tf_op jit(solution)/shard_map/reduce_scatter | solution.py:385
  2234.8 210.7 %reduce-scatter.31.cloned.1.call-done = bf16[192,4096]{1,0:T(8,128)(2,1)} async-done(((bf16[1536,4096]{1,0:T(8,128)(2,1)}), bf16[192,4096]{1,0:T(8,128)(2,1)}) %reduce-scatter.31.cloned.1.call-update) | async-done | bytes 1572880 | tf_op jit(solution)/shard_map/reduce_scatter | solution.py:391
  2445.6 210.0 %reduce-scatter.33.cloned.1.call-done = bf16[192,4096]{1,0:T(8,128)(2,1)} async-done(((bf16[1536,4096]{1,0:T(8,128)(2,1)}), bf16[192,4096]{1,0:T(8,128)(2,1)}) %reduce-scatter.33.cloned.1.call-update) | async-done | bytes 1572880 | tf_op jit(solution)/shard_map/reduce_scatter | solution.py:394
  2655.5 210.0 %reduce-scatter.35.cloned.1.call-done = bf16[512,1536]{1,0:T(8,128)(2,1)} async-done(((bf16[4096,1536]{1,0:T(8,128)(2,1)}), bf16[512,1536]{1,0:T(8,128)(2,1)}) %reduce-scatter.35.cloned.1.call-update) | async-done | bytes 1572880 | tf_op jit(solution)/shard_map/reduce_scatter | solution.py:397
  2865.6 210.3 %reduce-scatter.27.cloned.1.call-done = bf16[512,1536]{0,1:T(8,128)(2,1)} async-done(((bf16[4096,1536]{0,1:T(8,128)(2,1)}), bf16[512,1536]{0,1:T(8,128)(2,1)}) %reduce-scatter.27.cloned.1.call-update) | async-done | bytes 1572880 | tf_op jit(solution)/shard_map/reduce_scatter | solution.py:400
  3075.8 210.4 %reduce-scatter.29.cloned.1.call-done = bf16[512,1536]{0,1:T(8,128)(2,1)} async-done(((bf16[4096,1536]{0,1:T(8,128)(2,1)}), bf16[512,1536]{0,1:T(8,128)(2,1)}) %reduce-scatter.29.cloned.1.call-update) | async-done | bytes 1572880 | tf_op jit(solution)/shard_map/reduce_scatter | solution.py:403
  3287.2 8.3 fusion.20
  3295.5 9.4 fusion.28
  3308.8 36.2 %all-reduce = (f32[2,1024]{1,0:T(2,128)S(1)}, bf16[24]{0:T(256)(128)(2,1)S(1)}) all-reduce(f32[2,1024]{1,0:T(2,128)S(1)} %fusion.87, f32[24]{0:T(128)S(1)} %subtract_multiply_fusion), channel_id=1, replica_groups=mesh['dp'=4,'sp'=8] {'sp'}, use_global_device_ids=true, to_apply=%region_18.19 | all-reduce | flops 2072 | bytes 16528 | tf_op jit(solution)/shard_map/psum | solution.py:375
  3345.2 6.5 all-reduce.1
  3353.4 160.2 %all-reduce.5.cloned.1.call-done = (bf16[512,1536]{0,1:T(8,128)(2,1)}, bf16[512,1536]{0,1:T(8,128)(2,1)}, bf16[1024,1152]{1,0:T(8,128)(2,1)}, bf16[192,1536]{1,0...) async-done(((bf16[512,1536]{0,1:T(8,128)(2,1)}, ...) | async-done | bytes 12582928 | tf_op jit(solution)/shard_map/psum | solution.py:415
  (362 shorter events, 180.2 us)
Async XLA Ops:
  7.2 37.1 %copy-start.88 = (s32[1,2]{1,0:T(1,128)S(1)}, s32[1,2]{1,0:T(1,128)}, u32[]{:S(2)}) copy-start(s32[1,2]{1,0:T(1,128)} %param.21) | copy-start | bytes 28
  7.2 39.0 %copy-start.3 = (bf16[1,256,1536]{2,1,0:T(8,128)(2,1)S(1)}, bf16[1,256,1536]{2,1,0:T(8,128)(2,1)}, u32[]{:S(2)}) copy-start(bf16[1,256,1536]{2,1,0:T(8,128)(2,1)} %param.17) | copy-start | bytes 2359300
  7.2 86.1 %all-gather.21.cloned.1.call-start = ((), (), s32[]{:S(2)}) async-start(), calls=%async_computation.15 | async-start | bytes 5308416 | tf_op jit(solution)/shard_map/all_gather | solution.py:110
  8.0 165.6 %all-gather.19.cloned.1.call-start = ((), (), s32[]{:S(2)}) async-start(), calls=%async_computation.14 | async-start | bytes 5308416 | tf_op jit(solution)/shard_map/all_gather | solution.py:109
  8.7 245.1 %all-gather.15.cloned.1.call-start = ((), (), s32[]{:S(2)}) async-start(), calls=%async_computation.12 | async-start | bytes 5308416 | tf_op jit(solution)/shard_map/all_gather | solution.py:111
  9.4 345.1 %all-gather.23.cloned.1.call-start = ((), (), s32[]{:S(2)}) async-start(), calls=%async_computation.16 | async-start | bytes 7077888 | tf_op jit(solution)/shard_map/all_gather | solution.py:169
  44.3 238.2 %copy-start.66 = (s32[256]{0:T(256)}, s32[256]{0:T(256)S(1)}, u32[]{:S(2)}) copy-start(s32[256]{0:T(256)S(1)} %compare_convert_fusion) | copy-start | bytes 3076
  187.6 166.9 %copy-start.26 = (bf16[256,24,32]{0,2,1:T(8,128)(2,1)}, bf16[256,24,32]{0,2,1:T(8,128)(2,1)S(1)}, u32[]{:S(2)}) copy-start(bf16[256,24,32]{0,2,1:T(8,128)(2,1)S(1)} %get-tuple-element.92) | copy-start | bytes 1179652
  189.4 341.8 %all-gather.25.cloned.1.call-start = ((), (), s32[]{:S(2)}) async-start(), calls=%async_computation.17 | async-start | bytes 14155776 | tf_op jit(solution)/shard_map/all_gather | solution.py:117
  190.0 524.0 %all-gather.27.cloned.1.call-start = ((), (), s32[]{:S(2)}) async-start(), calls=%async_computation.18 | async-start | bytes 14155776 | tf_op jit(solution)/shard_map/all_gather | solution.py:116
  190.6 634.7 %all-gather.17.cloned.1.call-start = ((), (), s32[]{:S(2)}) async-start(), calls=%async_computation.13 | async-start | bytes 7077888 | tf_op jit(solution)/shard_map/all_gather | solution.py:170
  261.0 644.6 %all-gather.29.cloned.1.call-start = ((), (), s32[]{:S(2)}) async-start(), calls=%async_computation.19 | async-start | bytes 5308416 | tf_op jit(solution)/shard_map/all_gather | solution.py:112
  261.8 820.6 %all-gather.31.cloned.1.call-start = ((), (), s32[]{:S(2)}) async-start(), calls=%async_computation.20 | async-start | bytes 14155776 | tf_op jit(solution)/shard_map/all_gather | solution.py:113
  262.5 996.6 %all-gather.33.cloned.1.call-start = ((), (), s32[]{:S(2)}) async-start(), calls=%async_computation.21 | async-start | bytes 14155776 | tf_op jit(solution)/shard_map/all_gather | solution.py:114
  263.1 1172.9 %all-gather.35.cloned.1.call-start = ((), (), s32[]{:S(2)}) async-start(), calls=%async_computation.22 | async-start | bytes 14155776 | tf_op jit(solution)/shard_map/all_gather | solution.py:115
  263.8 1273.9 %all-gather.37.cloned.1.call-start = ((), (), s32[]{:S(2)}) async-start(), calls=%async_computation.23 | async-start | bytes 7077888 | tf_op jit(solution)/shard_map/all_gather | solution.py:259
  285.7 1366.2 %all-gather.39.cloned.1.call-start = ((), (), s32[]{:S(2)}) async-start(), calls=%async_computation.24 | async-start | bytes 7077888 | tf_op jit(solution)/shard_map/all_gather | solution.py:260
  354.5 23.7 copy-start.19
  378.2 153.0 %copy-start.22 = (bf16[1,2,16,4096]{3,2,1,0:T(8,128)(2,1)S(1)}, bf16[1,2,16,4096]{3,2,1,0:T(8,128)(2,1)}, u32[]{:S(2)}) copy-start(bf16[1,2,16,4096]{3,2,1,0:T(8,128)(2,1)} %param.19) | copy-start | bytes 786436
  720.8 42.9 %copy-start.27 = (bf16[256,24,32]{0,2,1:T(8,128)(2,1)S(1)}, bf16[256,24,32]{0,2,1:T(8,128)(2,1)}, u32[]{:S(2)}) copy-start(bf16[256,24,32]{0,2,1:T(8,128)(2,1)} %copy-done.26) | copy-start | bytes 1179652
  911.4 563.4 %copy-start.85 = (f32[256]{0:T(256)}, f32[256]{0:T(256)S(1)}, u32[]{:S(2)}) copy-start(f32[256]{0:T(256)S(1)} %add_rsqrt_fusion.2) | copy-start | bytes 3076
  915.2 343.9 %copy-start.21 = (bf16[256,1536]{1,0:T(8,128)(2,1)}, bf16[256,1536]{1,0:T(8,128)(2,1)S(1)}, u32[]{:S(2)}) copy-start(bf16[256,1536]{1,0:T(8,128)(2,1)S(1)} %fusion.55) | copy-start | bytes 2359300
  1447.5 8.4 copy-start.45
  1447.5 8.4 copy-start.8
  1455.9 18.9 slice-start
  1455.9 18.9 slice-start.1
  1467.1 7.7 slice-start.2
  1467.1 7.7 copy-start.15
  1467.1 7.7 copy-start.24
  1483.3 312.7 %reduce-scatter.15.cloned.1.call-start = ((), (), s32[]{:S(2)}) async-start(), calls=%async_computation.25 | async-start | bytes 884736 | tf_op jit(solution)/shard_map/reduce_scatter | solution.py:342
  1490.1 47.6 %copy-start.37 = (bf16[256,24,32]{0,2,1:T(8,128)(2,1)S(1)}, bf16[256,24,32]{0,2,1:T(8,128)(2,1)}, u32[]{:S(2)}) copy-start(bf16[256,24,32]{0,2,1:T(8,128)(2,1)} %copy-done.36) | copy-start | bytes 1179652
  1490.1 47.6 %copy-start.39 = (bf16[256,24,32]{0,2,1:T(8,128)(2,1)S(1)}, bf16[256,24,32]{0,2,1:T(8,128)(2,1)}, u32[]{:S(2)}) copy-start(bf16[256,24,32]{0,2,1:T(8,128)(2,1)} %copy-done.38) | copy-start | bytes 1179652
  1537.7 21.4 copy-start.74
  1537.7 21.4 copy-start.49
  1537.7 21.4 copy-start.52
  1537.8 21.4 copy-start.82
  1559.1 7.0 slice-start.3
  1559.2 6.9 slice-start.4
  1566.1 6.0 copy-start.28
  1577.3 226.7 %reduce-scatter.17.cloned.1.call-start = ((), (), s32[]{:S(2)}) async-start(), calls=%async_computation.26 | async-start | bytes 884736 | tf_op jit(solution)/shard_map/reduce_scatter | solution.py:348
  1622.7 217.6 %reduce-scatter.37.cloned.1.call-start = ((), (), s32[]{:S(2)}) async-start(), calls=%async_computation.36 | async-start | bytes 2654208
  1622.8 29.0 copy-start.59
  1651.8 27.6 copy-start.63
  1651.8 27.6 copy-start.65
  1706.8 24.2 copy-start.42
  1706.8 24.2 slice-start.9
  1706.8 25.7 slice-start.7
  1708.1 24.3 copy-start.41
  1708.1 22.9 slice-start.10
  1708.1 24.3 slice-start.8
  1745.0 193.2 %reduce-scatter.25.cloned.1.call-start = ((), (), s32[]{:S(2)}) async-start(), calls=%async_computation.30 | async-start | bytes 5308416 | tf_op jit(solution)/shard_map/reduce_scatter | solution.py:388
  1750.0 287.3 %reduce-scatter.19.cloned.1.call-start = ((), (), s32[]{:S(2)}) async-start(), calls=%async_computation.27 | async-start | bytes 5308416 | tf_op jit(solution)/shard_map/reduce_scatter | solution.py:379
  1755.1 381.1 %reduce-scatter.21.cloned.1.call-start = ((), (), s32[]{:S(2)}) async-start(), calls=%async_computation.28 | async-start | bytes 5308416 | tf_op jit(solution)/shard_map/reduce_scatter | solution.py:382
  1760.2 474.6 %reduce-scatter.23.cloned.1.call-start = ((), (), s32[]{:S(2)}) async-start(), calls=%async_computation.29 | async-start | bytes 5308416 | tf_op jit(solution)/shard_map/reduce_scatter | solution.py:385
  1765.4 680.2 %reduce-scatter.31.cloned.1.call-start = ((), (), s32[]{:S(2)}) async-start(), calls=%async_computation.33 | async-start | bytes 14155776 | tf_op jit(solution)/shard_map/reduce_scatter | solution.py:391
  1775.4 880.2 %reduce-scatter.33.cloned.1.call-start = ((), (), s32[]{:S(2)}) async-start(), calls=%async_computation.34 | async-start | bytes 14155776 | tf_op jit(solution)/shard_map/reduce_scatter | solution.py:394
  1785.4 1080.2 %reduce-scatter.35.cloned.1.call-start = ((), (), s32[]{:S(2)}) async-start(), calls=%async_computation.35 | async-start | bytes 14155776 | tf_op jit(solution)/shard_map/reduce_scatter | solution.py:397
  1795.7 1280.1 %reduce-scatter.27.cloned.1.call-start = ((), (), s32[]{:S(2)}) async-start(), calls=%async_computation.31 | async-start | bytes 14155776 | tf_op jit(solution)/shard_map/reduce_scatter | solution.py:400
  1804.0 1482.2 %reduce-scatter.29.cloned.1.call-start = ((), (), s32[]{:S(2)}) async-start(), calls=%async_computation.32 | async-start | bytes 14155776 | tf_op jit(solution)/shard_map/reduce_scatter | solution.py:403
  1811.5 28.8 copy-start.77
  1811.6 1702.0 %all-reduce.5.cloned.1.call-start = ((), (), s32[]{:S(2)}) async-start(), calls=%async_computation.37 | async-start | bytes 25165824 | tf_op jit(solution)/shard_map/psum | solution.py:415
  3287.2 8.3 copy-start.53
  3295.5 9.5 copy-start.6
  3295.5 9.5 copy-start.18
  (64 other events, 155.4 us)
Sparse Core Ops, SparseCore 0:
  10.2 83.0 all-gather.20
  95.5 78.0 all-gather.18
  175.8 78.0 all-gather.14
  256.3 98.1 all-gather.22
  356.6 174.6 all-gather.24
  533.3 180.7 all-gather.26
  716.6 108.6 all-gather.16
  827.5 78.0 all-gather.28
  907.8 174.5 all-gather.30
  1084.4 174.6 all-gather.32
  1261.3 174.6 all-gather.34
  1437.9 99.7 all-gather.36
  1539.8 99.9 all-gather.38
  1643.0 60.4 reduce-scatter.14
  1707.0 61.4 reduce-scatter.16
  1772.4 67.8 reduce-scatter.36
  1843.9 94.3 reduce-scatter.24
  1942.3 95.0 reduce-scatter.18
  2041.0 95.1 reduce-scatter.20
  2139.7 95.1 reduce-scatter.22
  2238.4 207.1 reduce-scatter.30
  2449.2 206.3 reduce-scatter.32
  2659.1 206.3 reduce-scatter.34
  2869.0 206.7 reduce-scatter.26
  3079.5 206.7 reduce-scatter.28
  3290.2 223.3 all-reduce.4
where the time goes:
time: 3550 us; the launch traced here: 3540 us
  waiting for transfers between devices  2760 us (78%)
  matrix products  374 us (11%)
  blocking collectives  229 us (6%)
  other arithmetic  88.1 us (2%)
  local copies, waits for them, and re-layouts  74.4 us (2%)
    reduce_scatter x1, waiting for transfers between devices, local(): lax.psum_scatter(grad_gate_w.astype(jnp.bfloat16), 'sp', scatter_dimensio...  211 us
    reduce_scatter x1, waiting for transfers between devices, local(): lax.psum_scatter(grad_text_value.astype(jnp.bfloat16), 'sp', scatter_dime...  210 us
    reduce_scatter x1, waiting for transfers between devices, local(): lax.psum_scatter(grad_text_key.astype(jnp.bfloat16), 'sp', scatter_dimens...  210 us
    reduce_scatter x1, waiting for transfers between devices, local(): lax.psum_scatter(grad_down.astype(jnp.bfloat16), 'sp', scatter_dimension=...  210 us
    reduce_scatter x1, waiting for transfers between devices, local(): lax.psum_scatter(grad_up_w.astype(jnp.bfloat16), 'sp', scatter_dimension=...  210 us
    all_gather x1, waiting for transfers between devices, local(): lax.all_gather(w_up, 'sp', axis=0, tiled=True)  167 us
    all_gather x1, waiting for transfers between devices, local(): lax.all_gather(w_down, 'sp', axis=0, tiled=True)  167 us
    all_gather x1, waiting for transfers between devices, local(): lax.all_gather(w_gate, 'sp', axis=0, tiled=True)  167 us
  transfers between devices with their start and end apart: 26, of which 23 were waited for; matrix products, arithmetic and copies ran while one was open for 14% of the time, Pallas kernels for 0%

commit v1 on v0

--- a/solution.py
+++ b/solution.py
@@ -1,6 +1,10 @@
+import functools
+
 import jax
 import jax.numpy as jnp
 from jax import lax
+from jax.experimental import pallas as pl
+from jax.experimental.pallas import tpu as pltpu
 from jax.sharding import PartitionSpec as P
 
 D = 1536
@@ -452,9 +456,697 @@
     )
 
 
+MIN_CLIP = 1024
+N_DP = 4
+VMEM_BYTES = 48 * 1024 * 1024
+NT = (((1,), (1,)), ((), ()))
+TN = (((0,), (0,)), ((), ()))
+F32 = jnp.float32
+BF16 = jnp.bfloat16
+
+
+def dot(left, right, dims=(((1,), (0,)), ((), ()))):
+    return lax.dot_general(left, right, dims, preferred_element_type=F32)
+
+
+class Ring:
+    def __init__(self, size):
+        self.size = size
+        self.order = list(range(0, size, 2)) + list(range(size - 1, 0, -2))
+        self.up = [(self.order[i], self.order[(i + 1) % size]) for i in range(size)]
+        self.down = [(b, a) for a, b in self.up]
+        place = [0] * size
+        for spot, device in enumerate(self.order):
+            place[device] = spot
+        self.spot = jnp.array(place, jnp.int32)[lax.axis_index("sp")]
+
+    def device(self, shift):
+        return jnp.array(self.order, jnp.int32)[(self.spot + shift + self.size) % self.size]
+
+    def send_up(self, value):
+        return lax.ppermute(value, "sp", self.up)
+
+    def send_down(self, value):
+        return lax.ppermute(value, "sp", self.down)
+
+    def gather(self, own):
+        half = own.shape[0] // 2
+        blocks = [(self.device(0), 0, own)]
+        above = below = own
+        for step in range(1, self.size // 2):
+            above, below = self.send_up(above), self.send_down(below)
+            blocks += [(self.device(-step), 0, above), (self.device(step), 0, below)]
+        step = self.size // 2
+        blocks += [
+            (self.device(step), 0, self.send_up(above[:half])),
+            (self.device(step), half, self.send_down(below[half:])),
+        ]
+        return blocks
+
+    def gather_whole(self, own):
+        whole = jnp.zeros((self.size,) + own.shape, own.dtype)
+        for device, start, block in self.gather(own):
+            whole = lax.dynamic_update_slice(
+                whole, block[None], (device, start) + (0,) * (own.ndim - 1)
+            )
+        return whole
+
+    def scatter(self, part):
+        far = self.size // 2
+        first = part(self.device(far))
+        half = first.shape[0] // 2
+        above = self.send_up(first[:half].astype(BF16))
+        below = self.send_down(first[half:].astype(BF16))
+        for step in range(far - 1, 0, -1):
+            upper, lower = part(self.device(step)), part(self.device(-step))
+            if step == far - 1:
+                upper = jnp.concatenate([upper[:half] + above.astype(F32), upper[half:].astype(F32)])
+                lower = jnp.concatenate([lower[:half].astype(F32), lower[half:] + below.astype(F32)])
+            else:
+                upper = upper + above.astype(F32)
+                lower = lower + below.astype(F32)
+            above = self.send_up(upper.astype(BF16))
+            below = self.send_down(lower.astype(BF16))
+        return part(self.device(0)) + above.astype(F32) + below.astype(F32)
+
+
+def across(value, bit):
+    return lax.ppermute(value, "dp", [(i, i ^ bit) for i in range(N_DP)])
+
+
+def gather_packs(value):
+    far = across(value, 2)
+    return [value, far, across(value, 1), across(far, 1)]
+
+
+def sum_packs(parts):
+    own = parts[0].astype(F32) + across(parts[2].astype(BF16), 1).astype(F32)
+    far = parts[1].astype(F32) + across(parts[3].astype(BF16), 1).astype(F32)
+    return own + across(far.astype(BF16), 2).astype(F32)
+
+
+def in_order(blocks):
+    member = lax.axis_index("dp")
+    stacked = jnp.stack(blocks)
+    place = jnp.array([0, 2, 1, 3], jnp.int32)
+    return jnp.stack(
+        [lax.dynamic_index_in_dim(stacked, place[member ^ i], 0, False) for i in range(N_DP)]
+    )
+
+
+def gather_small(value, axis_name):
+    size = lax.axis_size(axis_name)
+    return lax.all_to_all(
+        jnp.broadcast_to(value[None], (size,) + value.shape), axis_name, 0, 0, tiled=True
+    )
+
+
+def exchange(value):
+    return lax.all_to_all(value, "sp", 0, 0, tiled=True)
+
+
+def turn(values, cos, sin):
+    half = HD // 2
+    a, b = values[:half], values[half:]
+    return jnp.concatenate([a * cos - b * sin, a * sin + b * cos], axis=0)
+
+
+def turn_back(grads, cos, sin):
+    half = HD // 2
+    a, b = grads[:half], grads[half:]
+    return jnp.concatenate([a * cos + b * sin, b * cos - a * sin], axis=0)
+
+
+def head_inverse(values):
+    return lax.rsqrt(jnp.mean(values * values, axis=0, keepdims=True) + EPSILON)
+
+
+def project_kernel(x_ref, shift_ref, scale_ref, w_ref, cos_ref, sin_ref, in_ref, out_ref, raw_ref):
+    heads = w_ref.shape[0] // (3 * HD)
+    half = x_ref.shape[1] // 2
+    for clip in range(CLIPS):
+        x = x_ref[0, clip * half : (clip + 1) * half, :].astype(F32)
+        inverse = lax.rsqrt(jnp.mean(x * x, axis=-1, keepdims=True) + EPSILON)
+        block = x * inverse * (1.0 + scale_ref[clip : clip + 1, :]) + shift_ref[clip : clip + 1, :]
+        block = block.astype(BF16)
+        in_ref[clip] = block
+        raw = dot(w_ref[...], block, NT)
+        raw_ref[clip] = raw[: 2 * heads * HD]
+        cos, sin = cos_ref[clip], sin_ref[clip]
+        for head in range(2 * heads):
+            rows = raw[head * HD : (head + 1) * HD]
+            rotated = turn(rows * head_inverse(rows), cos, sin)
+            out_ref[clip, head * HD : (head + 1) * HD, :] = rotated.astype(BF16)
+        out_ref[clip, 2 * heads * HD :, :] = raw[2 * heads * HD :].astype(BF16)
+
+
+def project(tokens, shift, scale, weight, cos, sin):
+    devices, rows, width = tokens.shape
+    half = rows // 2
+    columns = weight.shape[0]
+    length = devices * half
+    return pl.pallas_call(
+        project_kernel,
+        grid=(devices,),
+        in_specs=[
+            pl.BlockSpec((1, rows, width), lambda i: (i, 0, 0)),
+            pl.BlockSpec((CLIPS, width), lambda i: (0, 0)),
+            pl.BlockSpec((CLIPS, width), lambda i: (0, 0)),
+            pl.BlockSpec((columns, width), lambda i: (0, 0)),
+            pl.BlockSpec((CLIPS, HD // 2, half), lambda i: (0, 0, i)),
+            pl.BlockSpec((CLIPS, HD // 2, half), lambda i: (0, 0, i)),
+        ],
+        out_specs=[
+            pl.BlockSpec((CLIPS, half, width), lambda i: (0, i, 0)),
+            pl.BlockSpec((CLIPS, columns, half), lambda i: (0, 0, i)),
+            pl.BlockSpec((CLIPS, 2 * columns // 3, half), lambda i: (0, 0, i)),
+        ],
+        out_shape=[
+            jax.ShapeDtypeStruct((CLIPS, length, width), BF16),
+            jax.ShapeDtypeStruct((CLIPS, columns, length), BF16),
+            jax.ShapeDtypeStruct((CLIPS, 2 * columns // 3, length), F32),
+        ],
+        compiler_params=pltpu.CompilerParams(vmem_limit_bytes=VMEM_BYTES),
+        cost_estimate=pl.CostEstimate(
+            flops=2 * CLIPS * length * width * columns,
+            bytes_accessed=4 * CLIPS * length * width + 8 * CLIPS * length * columns,
+            transcendentals=0,
+        ),
+    )(tokens, shift, scale, weight, cos, sin)
+
+
+def cross_probabilities(cap_key, query):
+    scores = dot(cap_key, query, TN) * HD**-0.5
+    grown = jnp.exp(scores - jnp.max(scores, axis=0, keepdims=True))
+    return grown / jnp.sum(grown, axis=0, keepdims=True)
+
+
+def attend_kernel(
+    gate_ref, q_ref, k_ref, v_ref, ck_ref, cv_ref, mixed_ref, self_ref, cross_ref, log_ref, *, block
+):
+    length = q_ref.shape[2]
+    half = mixed_ref.shape[2]
+    gate = gate_ref[pl.program_id(1)]
+    keys = k_ref[0]
+    for start in range(0, length, block):
+        query = q_ref[0, :, start : start + block]
+        grown = jnp.exp(dot(keys, query, TN) * HD**-0.5)
+        total = jnp.sum(grown, axis=0, keepdims=True)
+        self_out = dot(v_ref[0], grown.astype(BF16)) / total
+        probs = cross_probabilities(ck_ref[...], query)
+        cross_out = dot(cv_ref[...], probs.astype(BF16))
+        self_ref[0, :, start : start + block] = self_out
+        cross_ref[0, :, start : start + block] = cross_out
+        log_ref[0, 0, :, start : start + block] = jnp.log(total)
+        mixed = (self_out + gate * cross_out).astype(BF16)
+        for piece in range(block // half):
+            mixed_ref[start // half + piece] = mixed[:, piece * half : (piece + 1) * half]
+
+
+def attend(gate, qkv, cap_key, cap_value, half):
+    clips, columns, length = qkv.shape
+    heads = columns // (3 * HD)
+    head_spec = lambda first: pl.BlockSpec((1, HD, length), lambda c, h: (c, first * heads + h, 0))
+    cap_spec = pl.BlockSpec((HD, CAP), lambda c, h: (h, c))
+    own_spec = pl.BlockSpec((1, HD, length), lambda c, h: (c, h, 0))
+    return pl.pallas_call(
+        functools.partial(attend_kernel, block=2 * half),
+        grid=(clips, heads),
+        in_specs=[
+            pl.BlockSpec(memory_space=pltpu.SMEM),
+            head_spec(0),
+            head_spec(1),
+            head_spec(2),
+            cap_spec,
+            cap_spec,
+        ],
+        out_specs=[
+            pl.BlockSpec((length // half, HD, half), lambda c, h: (0, h, c)),
+            own_spec,
+            own_spec,
+            pl.BlockSpec((1, 1, 1, length), lambda c, h: (c, h, 0, 0)),
+        ],
+        out_shape=[
+            jax.ShapeDtypeStruct((length // half, heads * HD, clips * half), BF16),
+            jax.ShapeDtypeStruct((clips, heads * HD, length), F32),
+            jax.ShapeDtypeStruct((clips, heads * HD, length), F32),
+            jax.ShapeDtypeStruct((clips, heads, 1, length), F32),
+        ],
+        compiler_params=pltpu.CompilerParams(vmem_limit_bytes=VMEM_BYTES),
+        cost_estimate=pl.CostEstimate(
+            flops=4 * clips * heads * length * length * HD * 4,
+            bytes_accessed=clips * heads * length * HD * 20,
+            transcendentals=clips * heads * length * length,
+        ),
+    )(gate, qkv, qkv, qkv, cap_key, cap_value)
+
+
+def attend_back_kernel(
+    gate_ref,
+    q_ref,
+    k_ref,
+    v_ref,
+    ck_ref,
+    cv_ref,
+    grad_ref,
+    self_ref,
+    cross_ref,
+    log_ref,
+    raw_q_ref,
+    raw_k_ref,
+    cos_ref,
+    sin_ref,
+    grads_ref,
+    cap_ref,
+    gate_grad_ref,
+    key_acc,
+    value_acc,
+    *,
+    block,
+):
+    length = q_ref.shape[2]
+    half = grad_ref.shape[2]
+    score_scale = HD**-0.5
+    gate = gate_ref[pl.program_id(1)]
+    keys, values = k_ref[0], v_ref[0]
+    cap_key, cap_value = ck_ref[...], cv_ref[...]
+    cap_key_grad = jnp.zeros((HD, CAP), F32)
+    cap_value_grad = jnp.zeros((HD, CAP), F32)
+    for start in range(0, length, block):
+        span = slice(start, start + block)
+        query = q_ref[0, :, span]
+        grad = jnp.concatenate(
+            [grad_ref[start // half + piece] for piece in range(block // half)], axis=1
+        )
+        wide = grad.astype(F32)
+        delta = jnp.sum(wide * self_ref[0, :, span], axis=0, keepdims=True)
+        gate_grad_ref[0, 0, :, span] = jnp.sum(
+            wide * cross_ref[0, :, span], axis=0, keepdims=True
+        )
+        probs = jnp.exp(dot(keys, query, TN) * score_scale - log_ref[0, 0, :, span])
+        score_grad = (probs * (dot(values, grad, TN) - delta)).astype(BF16)
+        value_part = dot(grad, probs.astype(BF16), NT)
+        key_part = dot(query, score_grad, NT)
+        if start == 0:
+            value_acc[...] = value_part
+            key_acc[...] = key_part
+        else:
+            value_acc[...] += value_part
+            key_acc[...] += key_part
+        query_grad = dot(keys, score_grad)
+        cross_grad = (gate * wide).astype(BF16)
+        cross_probs = cross_probabilities(cap_key, query)
+        cross_dp = dot(cap_value, cross_grad, TN)
+        cross_score = cross_probs * (
+            cross_dp - jnp.sum(cross_probs * cross_dp, axis=0, keepdims=True)
+        )
+        cross_score = cross_score.astype(BF16)
+        cap_value_grad += dot(cross_grad, cross_probs.astype(BF16), NT)
+        cap_key_grad += dot(query, cross_score, NT)
+        query_grad = (query_grad + dot(cap_key, cross_score)) * score_scale
+        raw = raw_q_ref[0, :, span]
+        inverse = head_inverse(raw)
+        normed = raw * inverse
+        turned = turn_back(query_grad, cos_ref[0, :, span], sin_ref[0, :, span])
+        mean = jnp.mean(turned * normed, axis=0, keepdims=True)
+        grads_ref[0, 0, :, span] = (inverse * (turned - normed * mean)).astype(BF16)
+    for start in range(0, length, block):
+        span = slice(start, start + block)
+        raw = raw_k_ref[0, :, span]
+        inverse = head_inverse(raw)
+        normed = raw * inverse
+        turned = turn_back(
+            key_acc[:, span] * score_scale, cos_ref[0, :, span], sin_ref[0, :, span]
+        )
+        mean = jnp.mean(turned * normed, axis=0, keepdims=True)
+        grads_ref[0, 1, :, span] = (inverse * (turned - normed * mean)).astype(BF16)
+        grads_ref[0, 2, :, span] = value_acc[:, span].astype(BF16)
+    cap_ref[0] = (cap_key_grad * score_scale).astype(BF16)
+    cap_ref[1] = cap_value_grad.astype(BF16)
+
+
+def attend_back(gate, qkv, cap_key, cap_value, grad, self_out, cross_out, log_total, raw, cos, sin):
+    clips, columns, length = qkv.shape
+    heads = columns // (3 * HD)
+    half = length // grad.shape[0]
+    head_spec = lambda first: pl.BlockSpec((1, HD, length), lambda c, h: (c, first * heads + h, 0))
+    cap_spec = pl.BlockSpec((HD, CAP), lambda c, h: (h, c))
+    table_spec = pl.BlockSpec((1, HD // 2, length), lambda c, h: (c, 0, 0))
+    row_spec = pl.BlockSpec((1, 1, 1, length), lambda c, h: (c, h, 0, 0))
+    return pl.pallas_call(
+        functools.partial(attend_back_kernel, block=2 * half),
+        grid=(clips, heads),
+        in_specs=[
+            pl.BlockSpec(memory_space=pltpu.SMEM),
+            head_spec(0),
+            head_spec(1),
+            head_spec(2),
+            cap_spec,
+            cap_spec,
+            pl.BlockSpec((length // half, HD, half), lambda c, h: (0, h, c)),
+            head_spec(0),
+            head_spec(0),
+            row_spec,
+            head_spec(0),
+            head_spec(1),
+            table_spec,
+            table_spec,
+        ],
+        out_specs=[
+            pl.BlockSpec((1, 3, HD, length), lambda c, h: (c, 0, h, 0)),
+            pl.BlockSpec((2, HD, CAP), lambda c, h: (0, h, c)),
+            row_spec,
+        ],
+        out_shape=[
+            jax.ShapeDtypeStruct((clips, 3, heads * HD, length), BF16),
+            jax.ShapeDtypeStruct((2, heads * HD, clips * CAP), BF16),
+            jax.ShapeDtypeStruct((clips, heads, 1, length), F32),
+        ],
+        scratch_shapes=[pltpu.VMEM((HD, length), F32), pltpu.VMEM((HD, length), F32)],
+        compiler_params=pltpu.CompilerParams(vmem_limit_bytes=VMEM_BYTES),
+        cost_estimate=pl.CostEstimate(
+            flops=10 * clips * heads * length * length * HD * 4,
+            bytes_accessed=clips * heads * length * HD * 32,
+            transcendentals=clips * heads * length * length,
+        ),
+    )(
+        gate,
+        qkv,
+        qkv,
+        qkv,
+        cap_key,
+        cap_value,
+        grad,
+        self_out,
+        cross_out,
+        log_total,
+        raw,
+        raw,
+        cos,
+        sin,
+    )
+
+
+def clip_sums(values):
+    return jnp.sum(values.reshape(CLIPS, -1, values.shape[-1]), axis=1)
+
+
+def split_heads(
+    tokens,
+    cotangent,
+    captions,
+    conditioning,
+    clip_lens,
+    w_ada,
+    b_ada,
+    w_query,
+    w_key,
+    w_value,
+    w_out,
+    gate_cross,
+    w_text_key,
+    w_text_value,
+    w_gate,
+    w_up,
+    w_down,
+):
+    shard = lax.axis_index("sp")
+    member = lax.axis_index("dp")
+    size = lax.axis_size("sp")
+    ring = Ring(size)
+    rows = tokens.shape[1]
+    half = rows // 2
+    own_cols = D // size
+    heads = HEADS // size
+    ff = w_gate.shape[1]
+    ff_rows = ff // size
+    ff_part = ff_rows // N_DP
+    k_rows = D // size
+    k_part = k_rows // N_DP
+    text_rows = w_text_key.shape[0]
+
+    inputs = tokens[0].astype(F32)
+    out_grad = cotangent[0].astype(F32)
+
+    cond_row = conditioning[0]
+    cond_act = jax.nn.silu(cond_row).astype(BF16)
+    mod_part = dot(cond_act, w_ada) + b_ada[None, :]
+    modulation = jnp.transpose(gather_small(mod_part, "sp"), (1, 0, 2)).reshape(CLIPS, -1)
+    shift_one, scale_one, gate_one, shift_two, scale_two, gate_two = jnp.split(modulation, 6, axis=1)
+
+    def by_row(values):
+        return jnp.repeat(values, half, axis=0)
+
+    start = member * k_part
+    quarter = jnp.stack(
+        [
+            lax.dynamic_slice(w, (start, 0), (k_part, D)).reshape(k_part, size, own_cols)
+            for w in (w_query, w_key, w_value)
+        ],
+        axis=2,
+    )
+    quarter = jnp.transpose(quarter, (1, 0, 2, 3)).reshape(size, k_part, 3 * own_cols)
+    w_qkv = in_order(gather_packs(exchange(quarter)))
+    w_qkv = jnp.transpose(w_qkv, (3, 1, 0, 2)).reshape(3 * own_cols, D)
+
+    cap_part = captions[0].reshape(-1, size, text_rows)
+    caption_cols = exchange(jnp.transpose(cap_part, (1, 0, 2)))
+    caption_cols = (
+        caption_cols.reshape(size, CLIPS, -1, text_rows).transpose(1, 0, 2, 3).reshape(-1, text_rows)
+    )
+    cap_terms = jnp.stack(
+        [
+            dot(w, caption_cols, (((0,), (1,)), ((), ()))).astype(BF16)
+            for w in (w_text_key, w_text_value)
+        ]
+    )
+
+    token_blocks = ring.gather_whole(tokens[0])
+
+    cap_heads = ring.scatter(
+        lambda device: jnp.transpose(
+            lax.dynamic_slice(
+                cap_terms, (0, device * own_cols, 0), (2, own_cols, CLIPS * CAP)
+            ),
+            (1, 0, 2),
+        )
+    ).astype(BF16)
+    cap_key, cap_value = cap_heads[:, 0], cap_heads[:, 1]
+
+    lane = jnp.arange(size * half, dtype=jnp.int32)
+    mirrored = (size - 1 - lane // half) * half + lane % half
+    freq = 10000.0 ** (-(jnp.arange(HD // 2, dtype=F32) * 2.0 / HD))
+    angle = jnp.stack([lane, mirrored]).astype(F32)[:, None, :] * freq[None, :, None]
+    cos, sin = jnp.cos(angle), jnp.sin(angle)
+
+    block_in, qkv, raw = project(token_blocks, shift_one, scale_one, w_qkv, cos, sin)
+
+    out_piece = lax.dynamic_slice(w_out, (0, member * (D // N_DP)), (k_rows, D // N_DP))
+    gate_piece = jnp.concatenate(
+        [
+            lax.dynamic_slice(w, (0, i * ff_rows + member * ff_part), (k_rows, ff_part))
+            for w in (w_gate, w_up)
+            for i in range(size)
+        ],
+        axis=1,
+    )
+    down_piece = lax.dynamic_slice(w_down, (member * ff_part, 0), (ff_part, D))
+    token_blocks, out_piece, gate_piece, down_piece = lax.optimization_barrier(
+        (token_blocks, out_piece, gate_piece, down_piece)
+    )
+    out_cols = ring.gather_whole(out_piece).reshape(D, D // N_DP)
+    out_full = jnp.transpose(in_order(gather_packs(out_cols)), (1, 0, 2)).reshape(D, D)
+    gate_up = ring.gather_whole(gate_piece).reshape(D, 2 * ff // N_DP)
+    down = ring.gather_whole(down_piece).reshape(ff // N_DP, D)
+
+    tanh_gate = jnp.tanh(gate_cross)
+    own_gate = lax.dynamic_slice(tanh_gate, (shard * heads,), (heads,))
+    mixed_blocks, self_out, cross_out, log_total = attend(own_gate, qkv, cap_key, cap_value, half)
+    mixed = exchange(mixed_blocks).reshape(D, rows)
+    attn_out = dot(mixed, out_full, TN)
+
+    inverse_one = inverse_rms(inputs)
+    normed_one = inputs * inverse_one
+    middle = inputs + by_row(gate_one) * attn_out
+    inverse_two = inverse_rms(middle)
+    normed_two = middle * inverse_two
+    ffn_in = (normed_two * (1.0 + by_row(scale_two)) + by_row(shift_two)).astype(BF16)
+    branch_grad = (by_row(gate_two) * out_grad).astype(BF16)
+    branch_grads = jnp.concatenate(gather_packs(branch_grad))
+    ffn_ins = jnp.concatenate(gather_packs(ffn_in))
+    hidden_units = ff // N_DP
+    gate_proj = dot(ffn_ins, gate_up[:, :hidden_units])
+    up_proj = dot(ffn_ins, gate_up[:, hidden_units:])
+    sigmoid_gate = jax.nn.sigmoid(gate_proj)
+    silu_gate = gate_proj * sigmoid_gate
+    hidden = (silu_gate * up_proj).astype(BF16)
+    hidden_grad = dot(branch_grads, down, NT)
+    gate_grad = (
+        hidden_grad * up_proj * sigmoid_gate * (1.0 + gate_proj * (1.0 - sigmoid_gate))
+    ).astype(BF16)
+    up_grad = (hidden_grad * silu_gate).astype(BF16)
+    ffn_terms = dot(gate_grad, gate_up[:, :hidden_units], NT) + dot(
+        up_grad, gate_up[:, hidden_units:], NT
+    )
+    ffn_in_grad = sum_packs([ffn_terms[i * rows : (i + 1) * rows] for i in range(N_DP)])
+    branch_terms = dot(hidden, down)
+    branch = sum_packs([branch_terms[i * rows : (i + 1) * rows] for i in range(N_DP)])
+    result = (middle + by_row(gate_two) * branch).astype(BF16)
+    grad_down = dot(hidden, branch_grads, TN).astype(BF16)
+    grad_gate = dot(ffn_ins, gate_grad, TN).astype(BF16)
+    grad_up = dot(ffn_ins, up_grad, TN).astype(BF16)
+
+    middle_grad = out_grad + norm_back(
+        ffn_in_grad * (1.0 + by_row(scale_two)), normed_two, inverse_two
+    )
+    attn_grad = (by_row(gate_one) * middle_grad).astype(BF16)
+    mixed_grad = dot(out_full, attn_grad, NT).astype(BF16).reshape(size, own_cols, rows)
+    grad_out = dot(mixed, attn_grad).astype(BF16)
+    head_grad = exchange(mixed_grad)
+
+    grads, cap_grads, gate_rows = attend_back(
+        own_gate, qkv, cap_key, cap_value, head_grad, self_out, cross_out, log_total, raw, cos, sin
+    )
+    grads = grads.reshape(CLIPS, 3 * own_cols, size * half)
+
+    def token_grad(device):
+        columns = lax.dynamic_slice(
+            grads, (0, 0, device * half), (CLIPS, 3 * own_cols, half)
+        )
+        return jnp.concatenate([dot(columns[c], w_qkv, TN) for c in range(CLIPS)])
+
+    block_in_grad = ring.scatter(token_grad)
+    grad_qkv = (
+        dot(block_in[0], grads[0], (((0,), (1,)), ((), ())))
+        + dot(block_in[1], grads[1], (((0,), (1,)), ((), ())))
+    ).astype(BF16)
+
+    inputs_grad = middle_grad + norm_back(
+        block_in_grad * (1.0 + by_row(scale_one)), normed_one, inverse_one
+    )
+
+    mod_terms = jnp.concatenate(
+        [
+            clip_sums(block_in_grad),
+            clip_sums(block_in_grad * normed_one),
+            clip_sums(middle_grad * attn_out),
+            clip_sums(ffn_in_grad),
+            clip_sums(ffn_in_grad * normed_two),
+            clip_sums(out_grad * branch),
+        ],
+        axis=1,
+    )
+    mod_terms = jnp.transpose(mod_terms.reshape(CLIPS, size, -1), (1, 0, 2))
+    mod_low = jnp.sum(exchange(mod_terms), axis=0).astype(BF16)
+    cond_part = dot(mod_low, w_ada, NT)
+    cond_sum = jnp.sum(gather_small(cond_part, "sp"), axis=0)
+    sigmoid_cond = jax.nn.sigmoid(cond_row)
+    cond_grad = cond_sum * sigmoid_cond * (1.0 + cond_row * (1.0 - sigmoid_cond))
+    both = jnp.concatenate([cond_act, mod_low], axis=1)
+    both_all = gather_small(both, "dp").reshape(N_DP * CLIPS, -1)
+    cond_all, mod_all = both_all[:, : cond_act.shape[1]], both_all[:, cond_act.shape[1] :]
+    d_ada = dot(cond_all, mod_all, TN)
+    d_bias = jnp.sum(mod_all.astype(F32), axis=0)
+    gate_own = jnp.sum(gate_rows, axis=(0, 2, 3))
+    gate_all = jnp.sum(
+        gather_small(gather_small(gate_own, "sp").reshape(-1), "dp"), axis=0
+    )
+    d_gate_cross = gate_all * (1.0 - tanh_gate * tanh_gate)
+
+    cap_all = ring.gather_whole(jnp.transpose(cap_grads, (1, 0, 2)))
+    cap_all = cap_all.reshape(D, 2, CLIPS * CAP)
+    caption_grad = dot(w_text_key, cap_all[:, 0]) + dot(w_text_value, cap_all[:, 1])
+    caption_grad = caption_grad.astype(BF16).reshape(text_rows, CLIPS, size, -1)
+    caption_grad = exchange(jnp.transpose(caption_grad, (2, 1, 3, 0)))
+    caption_grad = (
+        jnp.transpose(caption_grad, (1, 2, 0, 3)).reshape(CLIPS, -1, size * text_rows).astype(F32)
+    )
+    text_terms = [
+        dot(caption_cols, cap_all[:, i], (((0,), (1,)), ((), ()))).astype(BF16) for i in range(2)
+    ]
+    text_rows_part = text_rows // N_DP
+    text_terms = jnp.concatenate(text_terms, axis=1)
+
+    def rows_for(offset):
+        return lax.dynamic_slice(
+            text_terms, ((member ^ offset) * text_rows_part, 0), (text_rows_part, 2 * D)
+        )
+
+    text_home = sum_packs([rows_for(offset) for offset in (0, 2, 1, 3)]).astype(BF16)
+    text_home = in_order(gather_packs(text_home)).reshape(text_rows, 2 * D).astype(F32)
+    d_text_key, d_text_value = text_home[:, :D], text_home[:, D:]
+
+    down_home = ring.scatter(
+        lambda device: lax.dynamic_slice(grad_down, (device * ff_part, 0), (ff_part, D))
+    ).astype(BF16)
+    d_down = in_order(gather_packs(down_home)).reshape(ff_rows, D).astype(F32)
+
+    def gate_home(terms):
+        home = ring.scatter(
+            lambda device: lax.dynamic_slice(
+                terms, (device * k_rows, 0), (k_rows, hidden_units)
+            )
+        ).astype(BF16)
+        whole = in_order(gather_packs(home.reshape(k_rows, size, ff_part)))
+        return jnp.transpose(whole, (1, 2, 0, 3)).reshape(k_rows, ff).astype(F32)
+
+    d_gate_w = gate_home(grad_gate)
+    d_up_w = gate_home(grad_up)
+
+    out_cols_part = D // N_DP
+
+    def cols_for(offset):
+        return lax.dynamic_slice(grad_out, (0, (member ^ offset) * out_cols_part), (D, out_cols_part))
+
+    out_sum = sum_packs([cols_for(offset) for offset in (0, 2, 1, 3)])
+    out_home = ring.scatter(
+        lambda device: lax.dynamic_slice(out_sum, (device * k_rows, 0), (k_rows, out_cols_part))
+    ).astype(BF16)
+    d_out = jnp.transpose(in_order(gather_packs(out_home)), (1, 0, 2)).reshape(k_rows, D).astype(F32)
+
+    grad_qkv = grad_qkv.reshape(size, N_DP, k_part, 3 * own_cols)
+
+    def quarter_for(offset):
+        return lax.dynamic_index_in_dim(grad_qkv, member ^ offset, 1, False)
+
+    qkv_sum = sum_packs([quarter_for(offset) for offset in (0, 2, 1, 3)]).astype(BF16)
+    qkv_home = in_order(gather_packs(exchange(qkv_sum)))
+    qkv_home = qkv_home.reshape(N_DP, size, k_part, 3, own_cols)
+    qkv_home = jnp.transpose(qkv_home, (3, 0, 2, 1, 4)).reshape(3, k_rows, D).astype(F32)
+    return (
+        result[None],
+        inputs_grad[None],
+        caption_grad[None],
+        cond_grad[None],
+        d_ada,
+        d_bias,
+        qkv_home[0],
+        qkv_home[1],
+        qkv_home[2],
+        d_out,
+        d_gate_cross,
+        d_text_key,
+        d_text_value,
+        d_gate_w,
+        d_up_w,
+        d_down,
+    )
+
+
+def layer(*arrays):
+    tokens, clip_lens = arrays[0], arrays[4]
+    size = lax.axis_size("sp")
+    pack = tokens.shape[1] * size
+    even = HEADS % size == 0 and size % 2 == 0 and size >= 4
+    fixed = pack == clip_lens.shape[1] * MIN_CLIP and tokens.shape[1] % 256 == 0
+    if even and fixed and lax.axis_size("dp") == N_DP:
+        return split_heads(*arrays)
+    return local(*arrays)
+
+
 def solution(mesh):
     return jax.shard_map(
-        local,
+        layer,
         mesh=mesh,
         in_specs=(
             P("dp", "sp", None),

time: 3550 us -> 996 us (0.28)
  waiting for transfers between devices: 2760 us -> 287 us
  matrix products: 374 us -> 115 us
  blocking collectives: 229 us -> 0 us
  starting transfers between devices: 1.65 us -> 191 us
  local copies, waits for them, and re-layouts: 74.4 us -> 193 us
  Pallas kernels: 0 us -> 59.1 us
    reduce_scatter x11 -> x0, waiting for transfers between devices: 1440 us -> none  [the longest x1 211 us: local(): lax.psum_scatter(grad_gate_w.astype(jnp.bfloat16), 'sp', scatter_dimensio...]
    all_gather x13 -> x0, waiting for transfers between devices: 1120 us -> none  [the longest x1 167 us: local(): lax.all_gather(w_up, 'sp', axis=0, tiled=True)]
    ppermute x0 -> x133, waiting for transfers between devices: none -> 278 us  [the longest x44 154 us: send_up(): return lax.ppermute(value, 'sp', self.up)]
    dot_general x48 -> x39, matrix products: 367 us -> 115 us  [dot(): return lax.dot_general(left, right, dims, preferred_element_type=F32)]
    all_gather x6 -> x0, blocking collectives: 187 us -> none  [the longest x1 36.7 us: local(): lax.all_gather(cap_key_part, 'sp', axis=1, tiled=True)]
    psum x1 -> x0, waiting for transfers between devices: 160 us -> none  [local(): lax.psum(home[7].astype(jnp.bfloat16), 'dp').astype(jnp.float32)]
    ppermute x0 -> x133, starting transfers between devices: none -> 137 us  [the longest x44 59.8 us: send_up(): return lax.ppermute(value, 'sp', self.up)]
    pallas_call x0 -> x3, Pallas kernels: none -> 59.1 us  [the longest x1 26.7 us: attend_back(): pl.pallas_call(functools.partial(attend_back_kernel, block=2 * half), gri...]
  transfers between devices with their start and end apart: 26 -> 145, of which waited for: 23 -> 61; matrix products, arithmetic and copies ran while one was open for 14% -> 35% of each run, Pallas kernels for 0% -> 6%
where the time goes in v1:
time: 996 us; the launch traced here: 982 us
  waiting for transfers between devices  287 us (29%)
  local copies, waits for them, and re-layouts  193 us (19%)
  starting transfers between devices  191 us (19%)
  matrix products  115 us (12%)
  other arithmetic  93.5 us (9%)
  Pallas kernels  59.1 us (6%)
  between operations  42.4 us (4%)
    ppermute x44, waiting for transfers between devices, send_up(): return lax.ppermute(value, 'sp', self.up)  154 us
    dot_general x39, matrix products, dot(): return lax.dot_general(left, right, dims, preferred_element_type=F32)  115 us
    ppermute x44, waiting for transfers between devices, send_down(): return lax.ppermute(value, 'sp', self.down)  82.2 us
    ppermute x44, starting transfers between devices, send_up(): return lax.ppermute(value, 'sp', self.up)  59.8 us
    ppermute x44, starting transfers between devices, send_down(): return lax.ppermute(value, 'sp', self.down)  55.9 us
    ppermute x45, waiting for transfers between devices, across(): return lax.ppermute(value, 'dp', [(i, i ^ bit) for i in range(N_DP)])  42.3 us
    unnamed x225, local copies, waits for them, and re-layouts  34.5 us
    all_to_all x7, starting transfers between devices, exchange(): return lax.all_to_all(value, 'sp', 0, 0, tiled=True)  33.6 us
  transfers between devices with their start and end apart: 145, of which 61 were waited for; matrix products, arithmetic and copies ran while one was open for 35% of the time, Pallas kernels for 6%

profile of v1, /device:TPU:0, one launch (start us, length us, event | category | flops | bytes accessed | tf_op | source)
XLA Modules:
  0.0 981.5 jit_solution(10995687620913055968)
XLA Ops:
  5.6 6.3 all-to-all-start.2
  81.5 6.0 all-to-all-start
  100.6 6.0 all-to-all-start.1
  128.3 12.7 %collective-permute-done.18 = bf16[192,2,256]{2,0,1:T(8,128)(2,1)} collective-permute-done((bf16[192,2,256]{2,0,1:T(8,128)(2,1)}, bf16[192,2,256]{2,0,1:T(8,128)(2,1)}, u32[]{:S(2)}, u32[]{:S(2)}) %collective-permute-start.18) | collective-permute-done | bytes 196640 | tf_op jit(solution)/shard_map/ppermute | solution.py:490
  143.3 7.6 collective-permute-done.8
  150.9 4.6 collective-permute-start.4
  163.8 3.9 copy.297.w_ref
  167.7 5.6 collective-permute-done.4
  191.4 13.5 %shard_map.1197 = (bf16[2,1024,1536]{2,1,0:T(8,128)(2,1)}, bf16[2,576,1024]{2,1,0:T(8,128)(2,1)S(1)}, f32[2,384,1024]{2,1,0:T(8,128)}) custom-call(bf16[8,256,1536]{2,1,0:T(8,128)(2,1)} %bitcast_dynamic-update-slice_fusion.22.x_ref, f32[2,1536]{1,0:T(2,128)S(1)} %get-tuple-element.154.shift_ref, f32[2,1536]{1,0:T(2,128)S(1)} %get-tuple-element.153.scale_ref, ...), custom_call_target="tpu_custom_call" | custom-call | flops 3623878656 | bytes 22020096 | tf_op jit(solution)/shard_map/pallas_call | solution.py:608
  206.3 19.0 %shard_map.1198 = (bf16[8,192,256]{2,1,0:T(8,128)(2,1)}, f32[2,192,1024]{2,1,0:T(8,128)S(1)}, f32[2,192,1024]{2,1,0:T(8,128)S(1)}, f32[2,3,1,1024]{3,2,1,0:T(1,128)S(1)}) custom-call(f32[3]{0:T(128)S(1)} %dynamic_slice.727.gate_ref, bf16[2,576,1024]{2,1,0:T(8,128)(2,1)} %copy-done.8, bf16[2,576,1024]{2,1,0:T(8,128)(2,1)} %copy-done.8, ...), custom_call_target="tpu_custom_call" | custom-call | flops 6442450944 | bytes 7864320 | tf_op jit(solution)/shard_map/pallas_call | solution.py:672
  227.6 4.2 all-to-all-start.3
  240.3 14.4 %collective-permute-done.21 = bf16[192,384]{1,0:T(8,128)(2,1)S(1)} collective-permute-done((bf16[192,384]{1,0:T(8,128)(2,1)}, bf16[192,384]{1,0:T(8,128)(2,1)S(1)}, u32[]{:S(2)}, u32[]{:S(2)}) %collective-permute-start.21) | collective-permute-done | bytes 147488 | tf_op jit(solution)/shard_map/ppermute | solution.py:487
  258.2 5.5 collective-permute-done.22
  268.3 16.7 %collective-permute-done.23 = bf16[192,384]{1,0:T(8,128)(2,1)S(1)} collective-permute-done((bf16[192,384]{1,0:T(8,128)(2,1)S(1)}, bf16[192,384]{1,0:T(8,128)(2,1)S(1)}, u32[]{:S(2)}, u32[]{:S(2)}) %collective-permute-start.23) | collective-permute-done | bytes 147488 | tf_op jit(solution)/shard_map/ppermute | solution.py:487
  303.4 4.4 collective-permute-done.43
  310.9 8.8 collective-permute-done.45
  321.5 8.2 collective-permute-done.46
  331.2 4.9 collective-permute-done.47
  337.9 4.1 collective-permute-done.48
  344.1 7.2 fusion.50
  351.3 8.3 collective-permute-done.35
  361.9 14.4 %collective-permute-done.37 = bf16[192,2048]{1,0:T(8,128)(2,1)S(1)} collective-permute-done((bf16[192,2048]{1,0:T(8,128)(2,1)S(1)}, bf16[192,2048]{1,0:T(8,128)(2,1)S(1)}, u32[]{:S(2)}, u32[]{:S(2)}) %collective-permute-start.37) | collective-permute-done | bytes 786464 | tf_op jit(solution)/shard_map/ppermute | solution.py:487
  384.1 6.8 copy.300
  390.8 4.4 multiply_reduce_fusion.1
  397.1 11.3 %collective-permute-done.30 = bf16[256,1536]{1,0:T(8,128)(2,1)S(1)} collective-permute-done((bf16[256,1536]{1,0:T(8,128)(2,1)S(1)}, bf16[256,1536]{1,0:T(8,128)(2,1)S(1)}, u32[]{:S(2)}, u32[]{:S(2)}) %collective-permute-start.30) | collective-permute-done | bytes 786464 | tf_op jit(solution)/shard_map/ppermute | solution.py:534
  414.7 11.0 %multiply_convert_fusion.1 = (bf16[1024,1024]{1,0:T(8,128)(2,1)}, bf16[1024,1024]{1,0:T(8,128)(2,1)}, bf16[1024,1024]{1,0:T(8,128)(2,1)}) fusion(f32[1024,1024]{1,0:T(8,128)} %fusion.50, f32[1024,1024]{1,0:T(8,128)S(1)} %fusion.8, bf16[1536,2048]{1,0:T(8,128)(2,1)S(1)} %bitcast.547, bf16[256,1536]{1,0:T(8,128)(2,1)S(1)} %collective-permute-done.32, ...), kind=kOutput, calls=%fused_computation.13 | convolution fusion | flops 3249537024 | bytes 20971520 | tf_op jit(solution)/shard_map/dot_general | solution.py:469
  425.8 5.1 fusion.6
  430.9 5.1 fusion.124
  440.2 5.2 fusion.125
  449.5 3.7 convolution_convert_fusion.3
  455.4 5.5 convolution_convert_fusion.2
  461.0 7.0 convolution_convert_fusion.1
  482.2 10.2 %collective-permute-done.101 = bf16[192,1024]{1,0:T(8,128)(2,1)S(1)} collective-permute-done((bf16[192,1024]{1,0:T(8,128)(2,1)S(1)}, bf16[192,1024]{1,0:T(8,128)(2,1)S(1)}, u32[]{:S(2)}, u32[]{:S(2)}) %collective-permute-start.101) | collective-permute-done | bytes 393248 | tf_op jit(solution)/shard_map/ppermute | solution.py:487
  493.6 4.4 collective-permute-done.123
  498.5 8.1 collective-permute-done.112
  512.5 7.7 collective-permute-done.102
  521.9 5.0 collective-permute-done.113
  533.1 8.0 collective-permute-done.106
  543.0 4.9 collective-permute-done.117
  566.5 4.7 convolution_convert_fusion
  595.0 3.8 collective-permute-done.119
  600.9 5.8 collective-permute-done.130
  611.6 3.7 copy.321
  615.3 5.4 reshape.439
  620.7 5.6 copy.322
  626.3 5.0 reshape.440
  644.6 26.7 %shard_map.1199 = (bf16[2,3,192,1024]{3,2,1,0:T(8,128)(2,1)}, bf16[2,192,256]{2,1,0:T(8,128)(2,1)}, f32[2,3,1,1024]{3,2,1,0:T(1,128)S(1)}) custom-call(f32[3]{0:T(128)S(1)} %dynamic_slice.727.gate_ref, bf16[2,576,1024]{2,1,0:T(8,128)(2,1)} %copy-done.8, bf16[2,576,1024]{2,1,0:T(8,128)(2,1)} %copy-done.8, bf16[2,576,1024]{2,1,0:T(8,128)(2,1)} %copy-done.8, ...), custom_call_target="tpu_custom_call" | custom-call | flops 16106127360 | bytes 12582912 | tf_op jit(solution)/shard_map/pallas_call | solution.py:796
  699.8 3.8 all-to-all-start.10
  703.6 4.3 fusion.2
  707.9 5.1 add_convert_fusion
  715.9 3.9 copy.313
  748.8 3.8 collective-permute-done.69
  757.4 4.2 collective-permute-done.70
  763.7 9.9 %collective-permute-done.71 = bf16[192,2,256]{2,0,1:T(8,128)(2,1)S(1)} collective-permute-done((bf16[192,2,256]{2,0,1:T(8,128)(2,1)S(1)}, bf16[192,2,256]{2,0,1:T(8,128)(2,1)S(1)}, u32[]{:S(2)}, u32[]{:S(2)}) %collective-permute-start.71) | collective-permute-done | bytes 196640 | tf_op jit(solution)/shard_map/ppermute | solution.py:490
  789.3 4.5 all-to-all-start.5
  822.4 4.2 all-to-all-start.9
  860.9 4.9 collective-permute-done.60
  870.3 10.5 %collective-permute-done.77 = bf16[8,48,576]{2,1,0:T(8,128)(2,1)S(1)} collective-permute-done((bf16[8,48,576]{2,1,0:T(8,128)(2,1)}, bf16[8,48,576]{2,1,0:T(8,128)(2,1)S(1)}, u32[]{:S(2)}, u32[]{:S(2)}) %collective-permute-start.77) | collective-permute-done | bytes 442400 | tf_op jit(solution)/shard_map/ppermute | solution.py:534
  888.3 8.0 reshape.442
  896.3 11.0 %fusion.116 = (f32[1,4,48,8,192]{4,0,2,3,1:T(1,128)}, f32[1,4,48,8,192]{4,0,2,3,1:T(1,128)}, f32[1,4,48,8,192]{4,0,2,3,1:T(1,128)S(1)}) fusion(f32[3,4,48,8,192]{4,0,2,3,1:T(4,128)} %bitcast.516), kind=kLoop, calls=%fused_computation.430 | loop fusion | bytes 7077888 | tf_op jit(solution)/shard_map/slice | solution.py:1125
  931.7 4.8 all-to-all-start.6
  952.0 4.0 all-to-all-start.7
  968.5 6.5 copy.320
  975.1 6.0 fusion.115
  (727 shorter events, 479.6 us)
Async XLA Ops:
  0.7 114.3 %collective-permute-start = (bf16[256,1536]{1,0:T(8,128)(2,1)}, bf16[256,1536]{1,0:T(8,128)(2,1)}, u32[]{:S(2)}, u32[]{:S(2)}) collective-permute-start(bf16[256,1536]{1,0:T(8,128)(2,1)} %bitcast.514), channel_id=1, source_target_pairs={{0,2},{2,4},{4,6},{6,7},{7,5},{5,3},{3,1},{1,0},{8,10},{10,12},{12... | collective-permute-start | bytes 2359304 | tf_op jit(solution)/shard_map/ppermute | solution.py:487
  3.8 113.2 %collective-permute-start.1 = (bf16[256,1536]{1,0:T(8,128)(2,1)}, bf16[256,1536]{1,0:T(8,128)(2,1)}, u32[]{:S(2)}, u32[]{:S(2)}) collective-permute-start(bf16[256,1536]{1,0:T(8,128)(2,1)} %bitcast.515), channel_id=1, source_target_pairs={{2,0},{4,2},{6,4},{7,6},{5,7},{3,5},{1,3},{0,1},{10,8},{12,10},{14... | collective-permute-start | bytes 2359304 | tf_op jit(solution)/shard_map/ppermute | solution.py:490
  5.6 75.2 %all-to-all-start.2 = ((bf16[8,32,512]{2,1,0:T(8,128)(2,1)}), bf16[8,32,512]{2,1,0:T(8,128)(2,1)}, u32[]{:S(2)}, u32[]{:S(2)}) async-start(bf16[8,32,512]{2,1,0:T(8,128)(2,1)} %copy.298), calls=%async_computation.2 | async-start | bytes 524288 | tf_op jit(solution)/shard_map/all_to_all | solution.py:565
  81.5 19.1 %all-to-all-start = ((f32[8,2,1152]{2,1,0:T(2,128)}), f32[8,2,1152]{2,1,0:T(2,128)}, u32[]{:S(2)}, u32[]{:S(2)}) async-start(f32[8,2,1152]{2,1,0:T(2,128)} %broadcast_in_dim.211), calls=%async_computation | async-start | bytes 147456 | tf_op jit(solution)/shard_map/all_to_all | solution.py:559
  100.6 27.7 %all-to-all-start.1 = ((bf16[8,48,576]{2,1,0:T(8,128)(2,1)}), bf16[8,48,576]{2,1,0:T(8,128)(2,1)}, u32[]{:S(2)}, u32[]{:S(2)}) async-start(bf16[8,48,576]{2,1,0:T(8,128)(2,1)} %reshape.407), calls=%async_computation.1 | async-start | bytes 983040 | tf_op jit(solution)/shard_map/all_to_all | solution.py:565
  110.2 49.5 %collective-permute-start.52 = (bf16[256,1536]{1,0:T(8,128)(2,1)}, bf16[256,1536]{1,0:T(8,128)(2,1)}, u32[]{:S(2)}, u32[]{:S(2)}) collective-permute-start(bf16[256,1536]{1,0:T(8,128)(2,1)} %fusion.31), channel_id=1, source_target_pairs={{0,16},{8,24},{16,0},{24,8},{1,17},{9,25},{17,1},{25,9},{2,18},{10... | collective-permute-start | bytes 2359304 | tf_op jit(solution)/shard_map/ppermute | solution.py:534
  115.0 35.9 %collective-permute-start.2 = (bf16[256,1536]{1,0:T(8,128)(2,1)}, bf16[256,1536]{1,0:T(8,128)(2,1)}, u32[]{:S(2)}, u32[]{:S(2)}) collective-permute-start(bf16[256,1536]{1,0:T(8,128)(2,1)} %collective-permute-done), channel_id=1, source_target_pairs={{0,2},{2,4},{4,6},{6,7},{7,5},{5,3},{3,1},{1,0},{8,10},{10,12},{12... | collective-permute-start | bytes 2359304 | tf_op jit(solution)/shard_map/ppermute | solution.py:487
  117.0 38.5 %collective-permute-start.3 = (bf16[256,1536]{1,0:T(8,128)(2,1)}, bf16[256,1536]{1,0:T(8,128)(2,1)}, u32[]{:S(2)}, u32[]{:S(2)}) collective-permute-start(bf16[256,1536]{1,0:T(8,128)(2,1)} %collective-permute-done.1), channel_id=1, source_target_pairs={{2,0},{4,2},{6,4},{7,6},{5,7},{3,5},{1,3},{0,1},{10,8},{12,10},{14... | collective-permute-start | bytes 2359304 | tf_op jit(solution)/shard_map/ppermute | solution.py:490
  124.3 17.8 %collective-permute-start.14 = (bf16[192,2,256]{2,0,1:T(8,128)(2,1)}, bf16[192,2,256]{2,0,1:T(8,128)(2,1)}, u32[]{:S(2)}, u32[]{:S(2)}) collective-permute-start(bf16[192,2,256]{2,0,1:T(8,128)(2,1)} %get-tuple-element.131), channel_id=1, source_target_pairs={{0,2},{2,4},{4,6},{6,7},{7,5},{5,3},{3,1},{1,0},{8,10},{10,12},{12... | collective-permute-start | bytes 589832 | tf_op jit(solution)/shard_map/ppermute | solution.py:487
  142.1 17.9 %collective-permute-start.9 = (bf16[8,48,576]{2,1,0:T(8,128)(2,1)}, bf16[8,48,576]{2,1,0:T(8,128)(2,1)S(1)}, u32[]{:S(2)}, u32[]{:S(2)}) collective-permute-start(bf16[8,48,576]{2,1,0:T(8,128)(2,1)} %all-to-all-done.1), channel_id=1, source_target_pairs={{0,8},{8,0},{16,24},{24,16},{1,9},{9,1},{17,25},{25,17},{2,10},{10... | collective-permute-start | bytes 1327112 | tf_op jit(solution)/shard_map/ppermute | solution.py:534
  150.9 22.3 %collective-permute-start.4 = (bf16[256,1536]{1,0:T(8,128)(2,1)}, bf16[256,1536]{1,0:T(8,128)(2,1)}, u32[]{:S(2)}, u32[]{:S(2)}) collective-permute-start(bf16[256,1536]{1,0:T(8,128)(2,1)} %collective-permute-done.2), channel_id=1, source_target_pairs={{0,2},{2,4},{4,6},{6,7},{7,5},{5,3},{3,1},{1,0},{8,10},{10,12},{12... | collective-permute-start | bytes 2359304 | tf_op jit(solution)/shard_map/ppermute | solution.py:487
  155.5 21.3 %collective-permute-start.5 = (bf16[256,1536]{1,0:T(8,128)(2,1)}, bf16[256,1536]{1,0:T(8,128)(2,1)}, u32[]{:S(2)}, u32[]{:S(2)}) collective-permute-start(bf16[256,1536]{1,0:T(8,128)(2,1)} %collective-permute-done.3), channel_id=1, source_target_pairs={{2,0},{4,2},{6,4},{7,6},{5,7},{3,5},{1,3},{0,1},{10,8},{12,10},{14... | collective-permute-start | bytes 2359304 | tf_op jit(solution)/shard_map/ppermute | solution.py:490
  159.7 182.8 %collective-permute-start.53 = (bf16[256,1536]{1,0:T(8,128)(2,1)}, bf16[256,1536]{1,0:T(8,128)(2,1)}, u32[]{:S(2)}, u32[]{:S(2)}) collective-permute-start(bf16[256,1536]{1,0:T(8,128)(2,1)} %fusion.31), channel_id=1, source_target_pairs={{0,8},{8,0},{16,24},{24,16},{1,9},{9,1},{17,25},{25,17},{2,10},{10... | collective-permute-start | bytes 2359304 | tf_op jit(solution)/shard_map/ppermute | solution.py:534
  160.0 184.1 %collective-permute-start.54 = (bf16[256,1536]{1,0:T(8,128)(2,1)}, bf16[256,1536]{1,0:T(8,128)(2,1)}, u32[]{:S(2)}, u32[]{:S(2)}) collective-permute-start(bf16[256,1536]{1,0:T(8,128)(2,1)} %collective-permute-done.52), channel_id=1, source_target_pairs={{0,8},{8,0},{16,24},{24,16},{1,9},{9,1},{17,25},{25,17},{2,10},{10... | collective-permute-start | bytes 2359304 | tf_op jit(solution)/shard_map/ppermute | solution.py:534
  189.3 47.0 %collective-permute-start.19 = (bf16[192,384]{1,0:T(8,128)(2,1)}, bf16[192,384]{1,0:T(8,128)(2,1)}, u32[]{:S(2)}, u32[]{:S(2)}) collective-permute-start(bf16[192,384]{1,0:T(8,128)(2,1)} %constant_dynamic-slice_fusion.40), channel_id=1, source_target_pairs={{0,2},{2,4},{4,6},{6,7},{7,5},{5,3},{3,1},{1,0},{8,10},{10,12},{12... | collective-permute-start | bytes 442376 | tf_op jit(solution)/shard_map/ppermute | solution.py:487
  189.8 47.7 %collective-permute-start.20 = (bf16[192,384]{1,0:T(8,128)(2,1)}, bf16[192,384]{1,0:T(8,128)(2,1)}, u32[]{:S(2)}, u32[]{:S(2)}) collective-permute-start(bf16[192,384]{1,0:T(8,128)(2,1)} %constant_dynamic-slice_fusion.40), channel_id=1, source_target_pairs={{2,0},{4,2},{6,4},{7,6},{5,7},{3,5},{1,3},{0,1},{10,8},{12,10},{14... | collective-permute-start | bytes 442376 | tf_op jit(solution)/shard_map/ppermute | solution.py:490
  227.6 163.2 %all-to-all-start.3 = ((bf16[8,192,256]{2,1,0:T(8,128)(2,1)}), bf16[8,192,256]{2,1,0:T(8,128)(2,1)}, u32[]{:S(2)}, u32[]{:S(2)}) async-start(bf16[8,192,256]{2,1,0:T(8,128)(2,1)} %get-tuple-element.30), calls=%async_computation.3 | async-start | bytes 1572864 | tf_op jit(solution)/shard_map/all_to_all | solution.py:565
  231.8 34.2 %collective-permute-start.41 = (bf16[128,1536]{1,0:T(8,128)(2,1)S(1)}, bf16[128,1536]{1,0:T(8,128)(2,1)S(1)}, u32[]{:S(2)}, u32[]{:S(2)}) collective-permute-start(bf16[128,1536]{1,0:T(8,128)(2,1)S(1)} %constant_dynamic-slice_fusion.39), channel_id=1, source_target_pairs={{0,2},{2,4},{4,6},{6,7},{7,5},{5,3},{3,1},{1,0},{8,10},{10,12},{12... | collective-permute-start | bytes 1179656 | tf_op jit(solution)/shard_map/ppermute | solution.py:487
  236.3 31.0 %collective-permute-start.42 = (bf16[128,1536]{1,0:T(8,128)(2,1)S(1)}, bf16[128,1536]{1,0:T(8,128)(2,1)S(1)}, u32[]{:S(2)}, u32[]{:S(2)}) collective-permute-start(bf16[128,1536]{1,0:T(8,128)(2,1)S(1)} %constant_dynamic-slice_fusion.39), channel_id=1, source_target_pairs={{2,0},{4,2},{6,4},{7,6},{5,7},{3,5},{1,3},{0,1},{10,8},{12,10},{14... | collective-permute-start | bytes 1179656 | tf_op jit(solution)/shard_map/ppermute | solution.py:490
  263.6 37.7 %collective-permute-start.33 = (bf16[192,2048]{1,0:T(8,128)(2,1)S(1)}, bf16[192,2048]{1,0:T(8,128)(2,1)S(1)}, u32[]{:S(2)}, u32[]{:S(2)}) collective-permute-start(bf16[192,2048]{1,0:T(8,128)(2,1)S(1)} %copy-done.67), channel_id=1, source_target_pairs={{0,2},{2,4},{4,6},{6,7},{7,5},{5,3},{3,1},{1,0},{8,10},{10,12},{12... | collective-permute-start | bytes 2359304 | tf_op jit(solution)/shard_map/ppermute | solution.py:487
  266.0 36.1 %collective-permute-start.34 = (bf16[192,2048]{1,0:T(8,128)(2,1)S(1)}, bf16[192,2048]{1,0:T(8,128)(2,1)S(1)}, u32[]{:S(2)}, u32[]{:S(2)}) collective-permute-start(bf16[192,2048]{1,0:T(8,128)(2,1)S(1)} %copy-done.67), channel_id=1, source_target_pairs={{2,0},{4,2},{6,4},{7,6},{5,7},{3,5},{1,3},{0,1},{10,8},{12,10},{14... | collective-permute-start | bytes 2359304 | tf_op jit(solution)/shard_map/ppermute | solution.py:490
  302.2 41.9 %collective-permute-start.27 = (bf16[1536,384]{1,0:T(8,128)(2,1)S(1)}, bf16[1536,384]{1,0:T(8,128)(2,1)S(1)}, u32[]{:S(2)}, u32[]{:S(2)}) collective-permute-start(bf16[1536,384]{1,0:T(8,128)(2,1)S(1)} %bitcast.550), channel_id=1, source_target_pairs={{0,16},{8,24},{16,0},{24,8},{1,17},{9,25},{17,1},{25,9},{2,18},{10... | collective-permute-start | bytes 3538952 | tf_op jit(solution)/shard_map/ppermute | solution.py:534
  307.8 72.4 %collective-permute-start.28 = (bf16[1536,384]{1,0:T(8,128)(2,1)S(1)}, bf16[1536,384]{1,0:T(8,128)(2,1)S(1)}, u32[]{:S(2)}, u32[]{:S(2)}) collective-permute-start(bf16[1536,384]{1,0:T(8,128)(2,1)S(1)} %bitcast.551), channel_id=1, source_target_pairs={{0,8},{8,0},{16,24},{24,16},{1,9},{9,1},{17,25},{25,17},{2,10},{10... | collective-permute-start | bytes 3538952 | tf_op jit(solution)/shard_map/ppermute | solution.py:534
  342.5 17.8 %collective-permute-start.36 = (bf16[192,2048]{1,0:T(8,128)(2,1)S(1)}, bf16[192,2048]{1,0:T(8,128)(2,1)S(1)}, u32[]{:S(2)}, u32[]{:S(2)}) collective-permute-start(bf16[192,2048]{1,0:T(8,128)(2,1)S(1)} %collective-permute-done.34), channel_id=1, source_target_pairs={{2,0},{4,2},{6,4},{7,6},{5,7},{3,5},{1,3},{0,1},{10,8},{12,10},{14... | collective-permute-start | bytes 2359304 | tf_op jit(solution)/shard_map/ppermute | solution.py:490
  344.0 36.1 %collective-permute-start.29 = (bf16[1536,384]{1,0:T(8,128)(2,1)S(1)}, bf16[1536,384]{1,0:T(8,128)(2,1)S(1)}, u32[]{:S(2)}, u32[]{:S(2)}) collective-permute-start(bf16[1536,384]{1,0:T(8,128)(2,1)S(1)} %collective-permute-done.27), channel_id=1, source_target_pairs={{0,8},{8,0},{16,24},{24,16},{1,9},{9,1},{17,25},{25,17},{2,10},{10... | collective-permute-start | bytes 3538952 | tf_op jit(solution)/shard_map/ppermute | solution.py:534
  377.1 31.2 %collective-permute-start.39 = (bf16[96,2048]{1,0:T(8,128)(2,1)}, bf16[96,2048]{1,0:T(8,128)(2,1)}, u32[]{:S(2)}, u32[]{:S(2)}) collective-permute-start(bf16[96,2048]{1,0:T(8,128)(2,1)} %slice.353), channel_id=1, source_target_pairs={{0,2},{2,4},{4,6},{6,7},{7,5},{5,3},{3,1},{1,0},{8,10},{10,12},{12... | collective-permute-start | bytes 1179656 | tf_op jit(solution)/shard_map/ppermute | solution.py:487
  378.2 31.4 %collective-permute-start.40 = (bf16[96,2048]{1,0:T(8,128)(2,1)}, bf16[96,2048]{1,0:T(8,128)(2,1)}, u32[]{:S(2)}, u32[]{:S(2)}) collective-permute-start(bf16[96,2048]{1,0:T(8,128)(2,1)} %slice.354), channel_id=1, source_target_pairs={{2,0},{4,2},{6,4},{7,6},{5,7},{3,5},{1,3},{0,1},{10,8},{12,10},{14... | collective-permute-start | bytes 1179656 | tf_op jit(solution)/shard_map/ppermute | solution.py:490
  437.0 71.1 %collective-permute-start.56 = (bf16[256,1536]{1,0:T(8,128)(2,1)}, bf16[256,1536]{1,0:T(8,128)(2,1)}, u32[]{:S(2)}, u32[]{:S(2)}) collective-permute-start(bf16[256,1536]{1,0:T(8,128)(2,1)} %get-tuple-element.97), channel_id=1, source_target_pairs={{0,8},{8,0},{16,24},{24,16},{1,9},{9,1},{17,25},{25,17},{2,10},{10... | collective-permute-start | bytes 2359304 | tf_op jit(solution)/shard_map/ppermute | solution.py:534
  437.2 115.8 %collective-permute-start.55 = (bf16[256,1536]{1,0:T(8,128)(2,1)S(1)}, bf16[256,1536]{1,0:T(8,128)(2,1)}, u32[]{:S(2)}, u32[]{:S(2)}) collective-permute-start(bf16[256,1536]{1,0:T(8,128)(2,1)S(1)} %get-tuple-element.96), channel_id=1, source_target_pairs={{0,8},{8,0},{16,24},{24,16},{1,9},{9,1},{17,25},{25,17},{2,10},{10... | collective-permute-start | bytes 2359304 | tf_op jit(solution)/shard_map/ppermute | solution.py:534
  445.6 64.5 %collective-permute-start.50 = (bf16[256,1536]{1,0:T(8,128)(2,1)S(1)}, bf16[256,1536]{1,0:T(8,128)(2,1)S(1)}, u32[]{:S(2)}, u32[]{:S(2)}) collective-permute-start(bf16[256,1536]{1,0:T(8,128)(2,1)S(1)} %get-tuple-element.99), channel_id=1, source_target_pairs={{0,8},{8,0},{16,24},{24,16},{1,9},{9,1},{17,25},{25,17},{2,10},{10... | collective-permute-start | bytes 2359304 | tf_op jit(solution)/shard_map/ppermute | solution.py:534
  492.4 18.0 %collective-permute-start.105 = (bf16[192,1024]{1,0:T(8,128)(2,1)S(1)}, bf16[192,1024]{1,0:T(8,128)(2,1)S(1)}, u32[]{:S(2)}, u32[]{:S(2)}) collective-permute-start(bf16[192,1024]{1,0:T(8,128)(2,1)S(1)} %pad_maximum_fusion.16), channel_id=1, source_target_pairs={{2,0},{4,2},{6,4},{7,6},{5,7},{3,5},{1,3},{0,1},{10,8},{12,10},{14... | collective-permute-start | bytes 1179656 | tf_op jit(solution)/shard_map/ppermute | solution.py:490
  510.4 18.6 %collective-permute-start.127 = (bf16[128,1536]{1,0:T(8,128)(2,1)S(1)}, bf16[128,1536]{1,0:T(8,128)(2,1)S(1)}, u32[]{:S(2)}, u32[]{:S(2)}) collective-permute-start(bf16[128,1536]{1,0:T(8,128)(2,1)S(1)} %pad_maximum_fusion.20), channel_id=1, source_target_pairs={{2,0},{4,2},{6,4},{7,6},{5,7},{3,5},{1,3},{0,1},{10,8},{12,10},{14... | collective-permute-start | bytes 1179656 | tf_op jit(solution)/shard_map/ppermute | solution.py:490
  521.9 36.1 %collective-permute-start.49 = (bf16[256,1536]{1,0:T(8,128)(2,1)S(1)}, bf16[256,1536]{1,0:T(8,128)(2,1)S(1)}, u32[]{:S(2)}, u32[]{:S(2)}) collective-permute-start(bf16[256,1536]{1,0:T(8,128)(2,1)S(1)} %get-tuple-element.98), channel_id=1, source_target_pairs={{0,8},{8,0},{16,24},{24,16},{1,9},{9,1},{17,25},{25,17},{2,10},{10... | collective-permute-start | bytes 2359304 | tf_op jit(solution)/shard_map/ppermute | solution.py:534
  526.9 27.8 %collective-permute-start.57 = (bf16[256,1536]{1,0:T(8,128)(2,1)S(1)}, bf16[256,1536]{1,0:T(8,128)(2,1)S(1)}, u32[]{:S(2)}, u32[]{:S(2)}) collective-permute-start(bf16[256,1536]{1,0:T(8,128)(2,1)S(1)} %fusion.32), channel_id=1, source_target_pairs={{0,16},{8,24},{16,0},{24,8},{1,17},{9,25},{17,1},{25,9},{2,18},{10... | collective-permute-start | bytes 2359304 | tf_op jit(solution)/shard_map/ppermute | solution.py:534
  552.1 26.0 %collective-permute-start.103 = (bf16[192,1024]{1,0:T(8,128)(2,1)}, bf16[192,1024]{1,0:T(8,128)(2,1)}, u32[]{:S(2)}, u32[]{:S(2)}) collective-permute-start(bf16[192,1024]{1,0:T(8,128)(2,1)} %get-tuple-element.82), channel_id=1, source_target_pairs={{0,2},{2,4},{4,6},{6,7},{7,5},{5,3},{3,1},{1,0},{8,10},{10,12},{12... | collective-permute-start | bytes 1179656 | tf_op jit(solution)/shard_map/ppermute | solution.py:487
  553.0 32.1 %collective-permute-start.114 = (bf16[192,1024]{1,0:T(8,128)(2,1)}, bf16[192,1024]{1,0:T(8,128)(2,1)}, u32[]{:S(2)}, u32[]{:S(2)}) collective-permute-start(bf16[192,1024]{1,0:T(8,128)(2,1)} %get-tuple-element.74), channel_id=1, source_target_pairs={{0,2},{2,4},{4,6},{6,7},{7,5},{5,3},{3,1},{1,0},{8,10},{10,12},{12... | collective-permute-start | bytes 1179656 | tf_op jit(solution)/shard_map/ppermute | solution.py:487
  554.7 33.2 %collective-permute-start.125 = (bf16[128,1536]{1,0:T(8,128)(2,1)}, bf16[128,1536]{1,0:T(8,128)(2,1)}, u32[]{:S(2)}, u32[]{:S(2)}) collective-permute-start(bf16[128,1536]{1,0:T(8,128)(2,1)} %get-tuple-element.66), channel_id=1, source_target_pairs={{0,2},{2,4},{4,6},{6,7},{7,5},{5,3},{3,1},{1,0},{8,10},{10,12},{12... | collective-permute-start | bytes 1179656 | tf_op jit(solution)/shard_map/ppermute | solution.py:487
  558.0 22.1 %collective-permute-start.107 = (bf16[192,1024]{1,0:T(8,128)(2,1)}, bf16[192,1024]{1,0:T(8,128)(2,1)}, u32[]{:S(2)}, u32[]{:S(2)}) collective-permute-start(bf16[192,1024]{1,0:T(8,128)(2,1)} %add_convert_fusion.15), channel_id=1, source_target_pairs={{2,0},{4,2},{6,4},{7,6},{5,7},{3,5},{1,3},{0,1},{10,8},{12,10},{14... | collective-permute-start | bytes 1179656 | tf_op jit(solution)/shard_map/ppermute | solution.py:490
  560.0 25.1 %collective-permute-start.118 = (bf16[192,1024]{1,0:T(8,128)(2,1)}, bf16[192,1024]{1,0:T(8,128)(2,1)}, u32[]{:S(2)}, u32[]{:S(2)}) collective-permute-start(bf16[192,1024]{1,0:T(8,128)(2,1)} %add_convert_fusion.10), channel_id=1, source_target_pairs={{2,0},{4,2},{6,4},{7,6},{5,7},{3,5},{1,3},{0,1},{10,8},{12,10},{14... | collective-permute-start | bytes 1179656 | tf_op jit(solution)/shard_map/ppermute | solution.py:490
  571.2 68.0 %all-to-all-start.4 = ((bf16[8,192,256]{2,1,0:T(8,128)(2,1)}), bf16[8,192,256]{2,1,0:T(8,128)(2,1)S(1)}, u32[]{:S(2)}, u32[]{:S(2)}) async-start(bf16[8,192,256]{2,1,0:T(8,128)(2,1)} %bitcast.571), calls=%async_computation.4 | async-start | bytes 1572864 | tf_op jit(solution)/shard_map/all_to_all | solution.py:565
  599.5 35.7 %collective-permute-start.81 = (bf16[1536,384]{1,0:T(8,128)(2,1)}, bf16[1536,384]{1,0:T(8,128)(2,1)}, u32[]{:S(2)}, u32[]{:S(2)}) collective-permute-start(bf16[1536,384]{1,0:T(8,128)(2,1)} %get-tuple-element.61), channel_id=1, source_target_pairs={{0,8},{8,0},{16,24},{24,16},{1,9},{9,1},{17,25},{25,17},{2,10},{10... | collective-permute-start | bytes 3538952 | tf_op jit(solution)/shard_map/ppermute | solution.py:534
  600.0 197.8 %collective-permute-start.80 = (bf16[1536,384]{1,0:T(8,128)(2,1)}, bf16[1536,384]{1,0:T(8,128)(2,1)}, u32[]{:S(2)}, u32[]{:S(2)}) collective-permute-start(bf16[1536,384]{1,0:T(8,128)(2,1)} %get-tuple-element.60), channel_id=1, source_target_pairs={{0,8},{8,0},{16,24},{24,16},{1,9},{9,1},{17,25},{25,17},{2,10},{10... | collective-permute-start | bytes 3538952 | tf_op jit(solution)/shard_map/ppermute | solution.py:534
  638.2 159.7 %collective-permute-start.82 = (bf16[1536,384]{1,0:T(8,128)(2,1)}, bf16[1536,384]{1,0:T(8,128)(2,1)}, u32[]{:S(2)}, u32[]{:S(2)}) collective-permute-start(bf16[1536,384]{1,0:T(8,128)(2,1)} %add_convert_fusion.1), channel_id=1, source_target_pairs={{0,16},{8,24},{16,0},{24,8},{1,17},{9,25},{17,1},{25,9},{2,18},{10... | collective-permute-start | bytes 3538952 | tf_op jit(solution)/shard_map/ppermute | solution.py:534
  693.8 35.3 %collective-permute-start.66 = (bf16[192,2,256]{2,0,1:T(8,128)(2,1)}, bf16[192,2,256]{2,0,1:T(8,128)(2,1)}, u32[]{:S(2)}, u32[]{:S(2)}) collective-permute-start(bf16[192,2,256]{2,0,1:T(8,128)(2,1)} %bitcast.136), channel_id=1, source_target_pairs={{0,2},{2,4},{4,6},{6,7},{7,5},{5,3},{3,1},{1,0},{8,10},{10,12},{12... | collective-permute-start | bytes 589832 | tf_op jit(solution)/shard_map/ppermute | solution.py:487
  694.2 38.6 %collective-permute-start.67 = (bf16[192,2,256]{2,0,1:T(8,128)(2,1)}, bf16[192,2,256]{2,0,1:T(8,128)(2,1)}, u32[]{:S(2)}, u32[]{:S(2)}) collective-permute-start(bf16[192,2,256]{2,0,1:T(8,128)(2,1)} %bitcast.136), channel_id=1, source_target_pairs={{2,0},{4,2},{6,4},{7,6},{5,7},{3,5},{1,3},{0,1},{10,8},{12,10},{14... | collective-permute-start | bytes 589832 | tf_op jit(solution)/shard_map/ppermute | solution.py:490
  697.6 36.8 %collective-permute-start.62 = (bf16[128,1536]{1,0:T(8,128)(2,1)}, bf16[128,1536]{1,0:T(8,128)(2,1)}, u32[]{:S(2)}, u32[]{:S(2)}) collective-permute-start(bf16[128,1536]{1,0:T(8,128)(2,1)} %convolution_convert_fusion.9), channel_id=1, source_target_pairs={{2,0},{4,2},{6,4},{7,6},{5,7},{3,5},{1,3},{0,1},{10,8},{12,10},{14... | collective-permute-start | bytes 1179656 | tf_op jit(solution)/shard_map/ppermute | solution.py:490
  699.8 20.1 %all-to-all-start.10 = ((f32[8,1,3]{2,1,0:T(1,128)}), f32[8,1,3]{2,1,0:T(1,128)S(1)}, u32[]{:S(2)}, u32[]{:S(2)}) async-start(f32[8,1,3]{2,1,0:T(1,128)} %broadcast_in_dim.270), calls=%async_computation.10 | async-start | bytes 8192 | tf_op jit(solution)/shard_map/all_to_all | solution.py:559
  732.8 23.1 %collective-permute-start.75 = (bf16[8,48,576]{2,1,0:T(8,128)(2,1)}, bf16[8,48,576]{2,1,0:T(8,128)(2,1)S(1)}, u32[]{:S(2)}, u32[]{:S(2)}) collective-permute-start(bf16[8,48,576]{2,1,0:T(8,128)(2,1)} %get-tuple-element.113), channel_id=1, source_target_pairs={{0,8},{8,0},{16,24},{24,16},{1,9},{9,1},{17,25},{25,17},{2,10},{10... | collective-permute-start | bytes 1327112 | tf_op jit(solution)/shard_map/ppermute | solution.py:534
  734.4 78.4 %collective-permute-start.74 = (bf16[8,48,576]{2,1,0:T(8,128)(2,1)}, bf16[8,48,576]{2,1,0:T(8,128)(2,1)}, u32[]{:S(2)}, u32[]{:S(2)}) collective-permute-start(bf16[8,48,576]{2,1,0:T(8,128)(2,1)} %get-tuple-element.112), channel_id=1, source_target_pairs={{0,8},{8,0},{16,24},{24,16},{1,9},{9,1},{17,25},{25,17},{2,10},{10... | collective-permute-start | bytes 1327112 | tf_op jit(solution)/shard_map/ppermute | solution.py:534
  752.6 80.2 %collective-permute-start.63 = (bf16[256,1536]{1,0:T(8,128)(2,1)}, bf16[256,1536]{1,0:T(8,128)(2,1)}, u32[]{:S(2)}, u32[]{:S(2)}) collective-permute-start(bf16[256,1536]{1,0:T(8,128)(2,1)} %pad_maximum_fusion.11), channel_id=1, source_target_pairs={{2,0},{4,2},{6,4},{7,6},{5,7},{3,5},{1,3},{0,1},{10,8},{12,10},{14... | collective-permute-start | bytes 2359304 | tf_op jit(solution)/shard_map/ppermute | solution.py:490
  782.9 59.8 %collective-permute-start.59 = (bf16[256,1536]{1,0:T(8,128)(2,1)}, bf16[256,1536]{1,0:T(8,128)(2,1)}, u32[]{:S(2)}, u32[]{:S(2)}) collective-permute-start(bf16[256,1536]{1,0:T(8,128)(2,1)} %pad_maximum_fusion.10), channel_id=1, source_target_pairs={{0,2},{2,4},{4,6},{6,7},{7,5},{5,3},{3,1},{1,0},{8,10},{10,12},{12... | collective-permute-start | bytes 2359304 | tf_op jit(solution)/shard_map/ppermute | solution.py:487
  789.3 33.1 %all-to-all-start.5 = ((bf16[8,2,16,512]{3,2,1,0:T(8,128)(2,1)}), bf16[8,2,16,512]{3,2,1,0:T(8,128)(2,1)S(1)}, u32[]{:S(2)}, u32[]{:S(2)}) async-start(bf16[8,2,16,512]{3,2,1,0:T(8,128)(2,1)} %bitcast.495), calls=%async_computation.5 | async-start | bytes 524288 | tf_op jit(solution)/shard_map/all_to_all | solution.py:565
  812.8 35.5 %collective-permute-start.95 = (bf16[128,3072]{0,1:T(8,128)(2,1)}, bf16[128,3072]{0,1:T(8,128)(2,1)}, u32[]{:S(2)}, u32[]{:S(2)}) collective-permute-start(bf16[128,3072]{0,1:T(8,128)(2,1)} %get-tuple-element.95), channel_id=1, source_target_pairs={{0,8},{8,0},{16,24},{24,16},{1,9},{9,1},{17,25},{25,17},{2,10},{10... | collective-permute-start | bytes 2359304 | tf_op jit(solution)/shard_map/ppermute | solution.py:534
  819.1 50.7 %collective-permute-start.94 = (bf16[128,3072]{0,1:T(8,128)(2,1)}, bf16[128,3072]{0,1:T(8,128)(2,1)}, u32[]{:S(2)}, u32[]{:S(2)}) collective-permute-start(bf16[128,3072]{0,1:T(8,128)(2,1)} %get-tuple-element.94), channel_id=1, source_target_pairs={{0,8},{8,0},{16,24},{24,16},{1,9},{9,1},{17,25},{25,17},{2,10},{10... | collective-permute-start | bytes 2359304 | tf_op jit(solution)/shard_map/ppermute | solution.py:534
  822.4 29.1 %all-to-all-start.9 = ((bf16[8,48,576]{2,1,0:T(8,128)(2,1)}), bf16[8,48,576]{2,1,0:T(8,128)(2,1)}, u32[]{:S(2)}, u32[]{:S(2)}) async-start(bf16[8,48,576]{2,1,0:T(8,128)(2,1)} %fusion.44), calls=%async_computation.9 | async-start | bytes 983040 | tf_op jit(solution)/shard_map/all_to_all | solution.py:565
  837.3 21.4 %collective-permute-start.64 = (bf16[256,1536]{1,0:T(8,128)(2,1)}, bf16[256,1536]{1,0:T(8,128)(2,1)}, u32[]{:S(2)}, u32[]{:S(2)}) collective-permute-start(bf16[256,1536]{1,0:T(8,128)(2,1)} %fusion.40), channel_id=1, source_target_pairs={{2,0},{4,2},{6,4},{7,6},{5,7},{3,5},{1,3},{0,1},{10,8},{12,10},{14... | collective-permute-start | bytes 2359304 | tf_op jit(solution)/shard_map/ppermute | solution.py:490
  844.9 20.9 %collective-permute-start.60 = (bf16[256,1536]{1,0:T(8,128)(2,1)}, bf16[256,1536]{1,0:T(8,128)(2,1)}, u32[]{:S(2)}, u32[]{:S(2)}) collective-permute-start(bf16[256,1536]{1,0:T(8,128)(2,1)} %fusion.38), channel_id=1, source_target_pairs={{0,2},{2,4},{4,6},{6,7},{7,5},{5,3},{3,1},{1,0},{8,10},{10,12},{12... | collective-permute-start | bytes 2359304 | tf_op jit(solution)/shard_map/ppermute | solution.py:487
  850.8 30.1 %collective-permute-start.96 = (bf16[128,3072]{0,1:T(8,128)(2,1)S(1)}, bf16[128,3072]{0,1:T(8,128)(2,1)}, u32[]{:S(2)}, u32[]{:S(2)}) collective-permute-start(bf16[128,3072]{0,1:T(8,128)(2,1)S(1)} %add_convert_fusion.3), channel_id=1, source_target_pairs={{0,16},{8,24},{16,0},{24,8},{1,17},{9,25},{17,1},{25,9},{2,18},{10... | collective-permute-start | bytes 2359304 | tf_op jit(solution)/shard_map/ppermute | solution.py:534
  851.5 29.3 %collective-permute-start.77 = (bf16[8,48,576]{2,1,0:T(8,128)(2,1)}, bf16[8,48,576]{2,1,0:T(8,128)(2,1)S(1)}, u32[]{:S(2)}, u32[]{:S(2)}) collective-permute-start(bf16[8,48,576]{2,1,0:T(8,128)(2,1)} %all-to-all-done.9), channel_id=1, source_target_pairs={{0,16},{8,24},{16,0},{24,8},{1,17},{9,25},{17,1},{25,9},{2,18},{10... | collective-permute-start | bytes 1327112 | tf_op jit(solution)/shard_map/ppermute | solution.py:534
  858.6 25.5 %collective-permute-start.78 = (bf16[8,48,576]{2,1,0:T(8,128)(2,1)}, bf16[8,48,576]{2,1,0:T(8,128)(2,1)S(1)}, u32[]{:S(2)}, u32[]{:S(2)}) collective-permute-start(bf16[8,48,576]{2,1,0:T(8,128)(2,1)} %all-to-all-done.9), channel_id=1, source_target_pairs={{0,8},{8,0},{16,24},{24,16},{1,9},{9,1},{17,25},{25,17},{2,10},{10... | collective-permute-start | bytes 1327112 | tf_op jit(solution)/shard_map/ppermute | solution.py:534
  865.8 58.7 %collective-permute-start.65 = (bf16[256,1536]{1,0:T(8,128)(2,1)}, bf16[256,1536]{1,0:T(8,128)(2,1)}, u32[]{:S(2)}, u32[]{:S(2)}) collective-permute-start(bf16[256,1536]{1,0:T(8,128)(2,1)} %fusion.39), channel_id=1, source_target_pairs={{2,0},{4,2},{6,4},{7,6},{5,7},{3,5},{1,3},{0,1},{10,8},{12,10},{14... | collective-permute-start | bytes 2359304 | tf_op jit(solution)/shard_map/ppermute | solution.py:490
  869.8 54.7 %collective-permute-start.61 = (bf16[256,1536]{1,0:T(8,128)(2,1)}, bf16[256,1536]{1,0:T(8,128)(2,1)}, u32[]{:S(2)}, u32[]{:S(2)}) collective-permute-start(bf16[256,1536]{1,0:T(8,128)(2,1)} %fusion.37), channel_id=1, source_target_pairs={{0,2},{2,4},{4,6},{6,7},{7,5},{5,3},{3,1},{1,0},{8,10},{10,12},{12... | collective-permute-start | bytes 2359304 | tf_op jit(solution)/shard_map/ppermute | solution.py:487
  883.4 64.0 %collective-permute-start.97 = (bf16[128,3072]{0,1:T(8,128)(2,1)}, bf16[128,3072]{0,1:T(8,128)(2,1)}, u32[]{:S(2)}, u32[]{:S(2)}) collective-permute-start(bf16[128,3072]{0,1:T(8,128)(2,1)} %add_convert_fusion.2), channel_id=1, source_target_pairs={{0,16},{8,24},{16,0},{24,8},{1,17},{9,25},{17,1},{25,9},{2,18},{10... | collective-permute-start | bytes 2359304 | tf_op jit(solution)/shard_map/ppermute | solution.py:534
  884.1 79.4 %collective-permute-start.98 = (bf16[128,3072]{0,1:T(8,128)(2,1)}, bf16[128,3072]{0,1:T(8,128)(2,1)}, u32[]{:S(2)}, u32[]{:S(2)}) collective-permute-start(bf16[128,3072]{0,1:T(8,128)(2,1)} %add_convert_fusion.2), channel_id=1, source_target_pairs={{0,8},{8,0},{16,24},{24,16},{1,9},{9,1},{17,25},{25,17},{2,10},{10... | collective-permute-start | bytes 2359304 | tf_op jit(solution)/shard_map/ppermute | solution.py:534
  (182 other events, 2322.8 us)

commit v2 on v1

--- a/solution.py
+++ b/solution.py
@@ -458,6 +458,7 @@
 
 MIN_CLIP = 1024
 N_DP = 4
+OFFSETS = (0, 2, 1, 3)
 VMEM_BYTES = 48 * 1024 * 1024
 NT = (((1,), (1,)), ((), ()))
 TN = (((0,), (0,)), ((), ()))
@@ -469,65 +470,68 @@
     return lax.dot_general(left, right, dims, preferred_element_type=F32)
 
 
+def ordered(tree):
+    arrays, shape = jax.tree.flatten(tree)
+    spec = pl.BlockSpec(memory_space=pl.ANY)
+    out = pl.pallas_call(
+        lambda *refs: None,
+        in_specs=[spec] * len(arrays),
+        out_specs=[spec] * len(arrays),
+        out_shape=[jax.ShapeDtypeStruct(a.shape, a.dtype) for a in arrays],
+        input_output_aliases={i: i for i in range(len(arrays))},
+        cost_estimate=pl.CostEstimate(flops=0, bytes_accessed=0, transcendentals=0),
+    )(*arrays)
+    return jax.tree.unflatten(shape, out)
+
+
 class Ring:
     def __init__(self, size):
         self.size = size
+        self.far = size // 2
         self.order = list(range(0, size, 2)) + list(range(size - 1, 0, -2))
         self.up = [(self.order[i], self.order[(i + 1) % size]) for i in range(size)]
         self.down = [(b, a) for a, b in self.up]
-        place = [0] * size
+        shifts = [0]
+        for step in range(1, self.far):
+            shifts += [-step, step]
+        shifts += [self.far]
+        self.spots = {shift: i for i, shift in enumerate(shifts)}
+        rows = [None] * size
         for spot, device in enumerate(self.order):
-            place[device] = spot
-        self.spot = jnp.array(place, jnp.int32)[lax.axis_index("sp")]
-
-    def device(self, shift):
-        return jnp.array(self.order, jnp.int32)[(self.spot + shift + self.size) % self.size]
-
-    def send_up(self, value):
-        return lax.ppermute(value, "sp", self.up)
-
-    def send_down(self, value):
-        return lax.ppermute(value, "sp", self.down)
-
-    def gather(self, own):
-        half = own.shape[0] // 2
-        blocks = [(self.device(0), 0, own)]
-        above = below = own
-        for step in range(1, self.size // 2):
-            above, below = self.send_up(above), self.send_down(below)
-            blocks += [(self.device(-step), 0, above), (self.device(step), 0, below)]
-        step = self.size // 2
-        blocks += [
-            (self.device(step), 0, self.send_up(above[:half])),
-            (self.device(step), half, self.send_down(below[half:])),
-        ]
-        return blocks
-
-    def gather_whole(self, own):
-        whole = jnp.zeros((self.size,) + own.shape, own.dtype)
-        for device, start, block in self.gather(own):
-            whole = lax.dynamic_update_slice(
-                whole, block[None], (device, start) + (0,) * (own.ndim - 1)
-            )
-        return whole
-
-    def scatter(self, part):
-        far = self.size // 2
-        first = part(self.device(far))
-        half = first.shape[0] // 2
-        above = self.send_up(first[:half].astype(BF16))
-        below = self.send_down(first[half:].astype(BF16))
-        for step in range(far - 1, 0, -1):
-            upper, lower = part(self.device(step)), part(self.device(-step))
-            if step == far - 1:
-                upper = jnp.concatenate([upper[:half] + above.astype(F32), upper[half:].astype(F32)])
-                lower = jnp.concatenate([lower[:half].astype(F32), lower[half:] + below.astype(F32)])
-            else:
-                upper = upper + above.astype(F32)
-                lower = lower + below.astype(F32)
-            above = self.send_up(upper.astype(BF16))
-            below = self.send_down(lower.astype(BF16))
-        return part(self.device(0)) + above.astype(F32) + below.astype(F32)
+            devices = [self.order[(spot + shift) % size] for shift in shifts]
+            rows[device] = [devices + [m ^ offset for offset in OFFSETS] for m in range(N_DP)]
+        table = jnp.array(rows, jnp.int32).reshape(size * N_DP, -1)
+        index = lax.axis_index("sp") * N_DP + lax.axis_index("dp")
+        self.table = lax.dynamic_index_in_dim(table, index, 0, False)
+
+    def send_up(self, values):
+        return [lax.ppermute(v, "sp", self.up) for v in values]
+
+    def send_down(self, values):
+        return [lax.ppermute(v, "sp", self.down) for v in values]
+
+
+class Gather:
+    def __init__(self, ring, own):
+        self.ring, self.own = ring, own
+        self.step, self.live = 0, (own, own)
+        self.blocks = [(0, own)]
+
+    def send(self):
+        ring = self.ring
+        self.step += 1
+        above, below = self.live
+        if self.step == ring.far:
+            above = [v[: v.shape[0] // 2] for v in above]
+            below = [v[v.shape[0] // 2 :] for v in below]
+        self.live = ring.send_up(above), ring.send_down(below)
+
+    def keep(self):
+        above, below = self.live
+        if self.step == self.ring.far:
+            self.halves = above, below
+        else:
+            self.blocks += [(-self.step, above), (self.step, below)]
 
 
 def across(value, bit):
@@ -539,19 +543,10 @@
     return [value, far, across(value, 1), across(far, 1)]
 
 
-def sum_packs(parts):
+def sum_packs_near(parts):
     own = parts[0].astype(F32) + across(parts[2].astype(BF16), 1).astype(F32)
     far = parts[1].astype(F32) + across(parts[3].astype(BF16), 1).astype(F32)
-    return own + across(far.astype(BF16), 2).astype(F32)
-
-
-def in_order(blocks):
-    member = lax.axis_index("dp")
-    stacked = jnp.stack(blocks)
-    place = jnp.array([0, 2, 1, 3], jnp.int32)
-    return jnp.stack(
-        [lax.dynamic_index_in_dim(stacked, place[member ^ i], 0, False) for i in range(N_DP)]
-    )
+    return own, far.astype(BF16)
 
 
 def gather_small(value, axis_name):
@@ -565,6 +560,797 @@
     return lax.all_to_all(value, "sp", 0, 0, tiled=True)
 
 
+def aligned(index, by):
+    return index if isinstance(index, int) else pl.multiple_of(index, by)
+
+
+def place(ring, write, blocks, shapes):
+    first = ring.size
+    listed = isinstance(blocks, list)
+    arrays = blocks if listed else [blocks]
+
+    def kernel(index_ref, *refs):
+        for i in range(N_DP):
+            if listed:
+                write(refs[i], index_ref[first + i], refs[N_DP:])
+            else:
+                write(refs[0].at[i], i, refs[1:])
+
+    vmem = pl.BlockSpec(memory_space=pltpu.VMEM)
+    return pl.pallas_call(
+        kernel,
+        in_specs=[pl.BlockSpec(memory_space=pltpu.SMEM)] + [vmem] * len(arrays),
+        out_specs=[vmem] * len(shapes),
+        out_shape=shapes,
+        compiler_params=pltpu.CompilerParams(vmem_limit_bytes=VMEM_BYTES),
+        cost_estimate=pl.CostEstimate(
+            flops=0,
+            bytes_accessed=sum(s.size * s.dtype.itemsize for s in [*arrays, *shapes]),
+            transcendentals=0,
+        ),
+    )(ring.table, *arrays)
+
+
+def place_units(block_ref, index, out_refs):
+    columns = block_ref.shape[1] - FOLD
+    groups = columns // (2 * 128)
+    for i, out_ref in enumerate(out_refs[:2]):
+        for group in range(groups):
+            start = unit_column(i, group)
+            spot = pl.ds(aligned((group * N_DP + index) * 128, 128), 128)
+            out_ref[:, spot] = block_ref[:, start : start + 128].astype(out_ref.dtype)
+    for row, column, there_row, there_column, height, wide in folded():
+        spot = pl.ds(aligned(index * 128 + row, 64), height)
+        out_refs[2][spot, column : column + wide] = block_ref[
+            there_row : there_row + height,
+            columns + there_column : columns + there_column + wide,
+        ].astype(out_refs[2].dtype)
+
+
+def place_heads(block_ref, index, out_refs):
+    groups, rows, width = block_ref.shape
+    width = width // len(out_refs)
+    spot = pl.ds(aligned(index * rows, rows), rows)
+    for i, out_ref in enumerate(out_refs):
+        for group in range(0, groups, 2):
+            pair = [
+                block_ref[group + k, :, i * width : (i + 1) * width].astype(F32) for k in range(2)
+            ]
+            columns = slice(group * width, (group + 2) * width)
+            out_ref[spot, columns] = jnp.concatenate(pair, axis=1).astype(out_ref.dtype)
+
+
+def join_projections(ring, blocks):
+    size, part, columns = blocks[0].shape
+    width = size * part * N_DP
+
+    def kernel(index_ref, *refs):
+        out_ref, turned_ref = refs[N_DP:]
+        for i in range(N_DP):
+            for device in range(size):
+                start = (device * N_DP + index_ref[size + i]) * part
+                out_ref[pl.ds(aligned(start, part), part), :] = refs[i][device]
+        turned_ref[...] = jnp.transpose(out_ref[...])
+
+    vmem = pl.BlockSpec(memory_space=pltpu.VMEM)
+    return pl.pallas_call(
+        kernel,
+        in_specs=[pl.BlockSpec(memory_space=pltpu.SMEM)] + [vmem] * N_DP,
+        out_specs=[vmem] * 2,
+        out_shape=[
+            jax.ShapeDtypeStruct((width, columns), BF16),
+            jax.ShapeDtypeStruct((columns, width), BF16),
+        ],
+        compiler_params=pltpu.CompilerParams(vmem_limit_bytes=VMEM_BYTES),
+        cost_estimate=pl.CostEstimate(
+            flops=0, bytes_accessed=6 * width * columns, transcendentals=0
+        ),
+    )(ring.table, *blocks)
+
+
+def caption_terms(w_key, w_value, captions):
+    features, width = w_key.shape
+    tokens = captions.shape[0]
+    size = lax.axis_size("sp")
+    columns = width // size
+
+    def kernel(key_ref, value_ref, cap_ref, out_ref):
+        for i, ref in enumerate((key_ref, value_ref)):
+            total = jnp.transpose(dot(cap_ref[...], ref[...])).astype(BF16)
+            for device in range(size):
+                out_ref[device, :, i * tokens : (i + 1) * tokens] = total[
+                    device * columns : (device + 1) * columns
+                ]
+
+    vmem = pl.BlockSpec(memory_space=pltpu.VMEM)
+    return pl.pallas_call(
+        kernel,
+        in_specs=[vmem] * 3,
+        out_specs=vmem,
+        out_shape=jax.ShapeDtypeStruct((size, columns, 2 * tokens), BF16),
+        compiler_params=pltpu.CompilerParams(vmem_limit_bytes=VMEM_BYTES),
+        cost_estimate=pl.CostEstimate(
+            flops=4 * tokens * features * width,
+            bytes_accessed=4 * (features + tokens) * width,
+            transcendentals=0,
+        ),
+    )(w_key, w_value, captions)
+
+
+def text_grads(ring, captions, grads):
+    width, columns = grads[0].shape
+    tokens = columns // 2
+    features = captions.shape[1]
+    size = ring.size
+
+    def kernel(index_ref, cap_ref, *refs):
+        caps = [
+            jnp.transpose(cap_ref[pl.ds(aligned(index_ref[size + i] * tokens, tokens), tokens), :])
+            for i in range(N_DP)
+        ]
+        for which, out_ref in enumerate(refs[N_DP:]):
+            total = None
+            for i in range(N_DP):
+                grad = refs[i][:, which * tokens : (which + 1) * tokens]
+                term = dot(caps[i], jnp.transpose(grad))
+                total = term if total is None else total + term
+            out_ref[...] = total
+
+    vmem = pl.BlockSpec(memory_space=pltpu.VMEM)
+    return pl.pallas_call(
+        kernel,
+        in_specs=[pl.BlockSpec(memory_space=pltpu.SMEM)] + [vmem] * (1 + N_DP),
+        out_specs=[vmem] * 2,
+        out_shape=[jax.ShapeDtypeStruct((features, width), F32)] * 2,
+        compiler_params=pltpu.CompilerParams(vmem_limit_bytes=VMEM_BYTES),
+        cost_estimate=pl.CostEstimate(
+            flops=4 * N_DP * tokens * features * width,
+            bytes_accessed=8 * features * width + 4 * N_DP * tokens * width,
+            transcendentals=0,
+        ),
+    )(ring.table, captions, *grads)
+
+
+def out_terms(mixed, grad):
+    width, rows = mixed.shape
+    columns = width // N_DP
+
+    def kernel(mixed_ref, grad_ref, out_ref):
+        out_ref[0] = dot(mixed_ref[...], grad_ref[...]).astype(BF16)
+
+    return pl.pallas_call(
+        kernel,
+        grid=(N_DP,),
+        in_specs=[
+            pl.BlockSpec((width, rows), lambda i: (0, 0)),
+            pl.BlockSpec((rows, columns), lambda i: (0, i)),
+        ],
+        out_specs=pl.BlockSpec((1, width, columns), lambda i: (i, 0, 0)),
+        out_shape=jax.ShapeDtypeStruct((N_DP, width, columns), BF16),
+        compiler_params=pltpu.CompilerParams(vmem_limit_bytes=VMEM_BYTES),
+        cost_estimate=pl.CostEstimate(
+            flops=2 * width * width * rows, bytes_accessed=2 * width * width, transcendentals=0
+        ),
+    )(mixed, grad)
+
+
+def finish_tokens(terms, received, middle_grad, tokens, scale):
+    rows, width = tokens.shape
+    half = rows // CLIPS
+    last = terms.shape[0] // rows - 1
+
+    def kernel(terms_ref, above_ref, below_ref, middle_ref, x_ref, scale_ref, out_ref, sums_ref):
+        for clip in range(CLIPS):
+            span = slice(clip * half, (clip + 1) * half)
+            grad = (
+                terms_ref[span].astype(F32) + above_ref[span].astype(F32) + below_ref[span].astype(F32)
+            )
+            x = x_ref[span].astype(F32)
+            inverse = lax.rsqrt(jnp.mean(x * x, axis=-1, keepdims=True) + EPSILON)
+            normed = x * inverse
+            scaled = grad * (1.0 + scale_ref[clip : clip + 1, :])
+            mean = jnp.mean(scaled * normed, axis=-1, keepdims=True)
+            out_ref[span] = middle_ref[span] + inverse * (scaled - normed * mean)
+            sums_ref[clip : clip + 1, :width] = jnp.sum(grad, axis=0, keepdims=True)
+            sums_ref[clip : clip + 1, width:] = jnp.sum(grad * normed, axis=0, keepdims=True)
+
+    fixed = pl.BlockSpec((rows, width), lambda i: (0, 0))
+    return pl.pallas_call(
+        kernel,
+        grid=(1,),
+        in_specs=[pl.BlockSpec((rows, width), lambda i: (last, 0))]
+        + [fixed] * 4
+        + [pl.BlockSpec((CLIPS, width), lambda i: (0, 0))],
+        out_specs=[fixed, pl.BlockSpec((CLIPS, 2 * width), lambda i: (0, 0))],
+        out_shape=[
+            jax.ShapeDtypeStruct((rows, width), F32),
+            jax.ShapeDtypeStruct((CLIPS, 2 * width), F32),
+        ],
+        compiler_params=pltpu.CompilerParams(vmem_limit_bytes=VMEM_BYTES),
+        cost_estimate=pl.CostEstimate(
+            flops=0, bytes_accessed=16 * rows * width, transcendentals=0
+        ),
+    )(terms, *received, middle_grad, tokens, scale)
+
+
+def place_columns(block_ref, index, out_refs):
+    width = block_ref.shape[1]
+    out_refs[0][:, pl.ds(aligned(index * width, 128), width)] = block_ref[...].astype(
+        out_refs[0].dtype
+    )
+
+
+UNITS = 512
+
+
+HELD = 32
+
+
+def pack_tokens(tokens, w_out):
+    rows, width = tokens.shape
+    half = rows // 2
+    columns = width // N_DP
+    k_rows = w_out.shape[0]
+    part = k_rows // N_DP
+    member = jnp.reshape(lax.axis_index("dp"), (1,)).astype(jnp.int32)
+
+    def kernel(member_ref, tokens_ref, w_ref, out_ref):
+        spot = pl.ds(aligned(member_ref[0] * columns, 128), columns)
+        for clip in range(CLIPS):
+            start = clip * (half + HELD)
+            out_ref[start : start + half] = tokens_ref[clip * half : (clip + 1) * half]
+            count = min(part - clip * HELD, HELD)
+            for group in range(N_DP):
+                top = group * part + clip * HELD
+                out_ref[
+                    start + half : start + half + count, group * columns : (group + 1) * columns
+                ] = w_ref[top : top + count, spot]
+            if count < HELD:
+                out_ref[start + half + count : start + half + HELD] = jnp.zeros(
+                    (HELD - count, width), BF16
+                )
+
+    vmem = pl.BlockSpec(memory_space=pltpu.VMEM)
+    return pl.pallas_call(
+        kernel,
+        in_specs=[pl.BlockSpec(memory_space=pltpu.SMEM), vmem, vmem],
+        out_specs=vmem,
+        out_shape=jax.ShapeDtypeStruct((rows + CLIPS * HELD, width), BF16),
+        compiler_params=pltpu.CompilerParams(vmem_limit_bytes=VMEM_BYTES),
+        cost_estimate=pl.CostEstimate(
+            flops=0, bytes_accessed=6 * rows * width, transcendentals=0
+        ),
+    )(member, tokens, w_out)
+
+
+def unpack_w_out(ring, flow, half):
+    width = flow.own[0].shape[1]
+    columns = width // N_DP
+    k_rows = width // ring.size
+    part = k_rows // N_DP
+    block = (half + HELD) // HELD
+    groups = [[arrays[0]] for _, arrays in flow.blocks]
+    groups += [[flow.halves[0][0], flow.halves[1][0]]]
+    spots = [ring.spots[shift] for shift, _ in flow.blocks] + [ring.spots[ring.far]]
+    operands, specs = [], []
+    for group in groups:
+        for clip in range(CLIPS):
+            operands.append(group[clip] if len(group) > 1 else group[0])
+            index = block - 1 if len(group) > 1 else (clip + 1) * block - 1
+            specs.append(pl.BlockSpec((HELD, width), lambda i, index=index: (index, 0)))
+
+    def kernel(index_ref, *refs):
+        for i, spot in enumerate(spots):
+            for clip in range(CLIPS):
+                count = min(part - clip * HELD, HELD)
+                for group in range(N_DP):
+                    top = index_ref[spot] * k_rows + group * part + clip * HELD
+                    refs[-1][pl.ds(aligned(top, 16), count), :] = refs[CLIPS * i + clip][
+                        :count, group * columns : (group + 1) * columns
+                    ]
+
+    return pl.pallas_call(
+        kernel,
+        grid=(1,),
+        in_specs=[pl.BlockSpec(memory_space=pltpu.SMEM)] + specs,
+        out_specs=pl.BlockSpec((width, columns), lambda i: (0, 0)),
+        out_shape=jax.ShapeDtypeStruct((width, columns), BF16),
+        compiler_params=pltpu.CompilerParams(vmem_limit_bytes=VMEM_BYTES),
+        cost_estimate=pl.CostEstimate(
+            flops=0, bytes_accessed=4 * width * columns, transcendentals=0
+        ),
+    )(ring.table, *operands)
+
+
+def unit_pieces(w_gate, w_up, w_down, after):
+    rows, columns = w_gate.shape
+    groups = columns // (N_DP * 128)
+    member = jnp.reshape(lax.axis_index("dp"), (1,)).astype(jnp.int32)
+    first = 2 * groups * 128
+    width = first + FOLD
+
+    def kernel(member_ref, gate_ref, up_ref, down_ref, after_ref, out_ref):
+        for i, ref in enumerate((gate_ref, up_ref)):
+            for group in range(groups):
+                spot = aligned((group * N_DP + member_ref[0]) * 128, 128)
+                start = unit_column(i, group)
+                out_ref[:, start : start + 128] = ref[:, pl.ds(spot, 128)]
+        spot = aligned(member_ref[0] * 128, 128)
+        for row, column, there_row, there_column, height, wide in folded():
+            out_ref[there_row : there_row + height, first + there_column : first + there_column + wide] = (
+                down_ref[pl.ds(aligned(spot + row, 32), height), column : column + wide]
+            )
+
+    vmem = pl.BlockSpec(memory_space=pltpu.VMEM)
+    return pl.pallas_call(
+        kernel,
+        in_specs=[pl.BlockSpec(memory_space=pltpu.SMEM), vmem, vmem, vmem, pl.BlockSpec(memory_space=pl.ANY)],
+        out_specs=vmem,
+        out_shape=jax.ShapeDtypeStruct((rows, width), w_gate.dtype),
+        compiler_params=pltpu.CompilerParams(vmem_limit_bytes=VMEM_BYTES),
+        cost_estimate=pl.CostEstimate(
+            flops=0, bytes_accessed=8 * rows * columns, transcendentals=0
+        ),
+    )(member, w_gate, w_up, w_down, after)
+
+
+FOLD = 1024
+
+
+def folded(low=0, high=192):
+    spots = []
+    if low < 128:
+        end = min(high, 128)
+        spots.append((low, 0, 0, 0, end - low, FOLD))
+    if high > 128:
+        start = max(low, 128) - 128
+        count = high - 128 - start
+        for side in range(2):
+            spots.append(
+                (64 * side + start, FOLD, 128 + start - low, 512 * side, count, 512)
+            )
+    return spots
+
+
+def unit_column(which, group):
+    per_tile = UNITS // 128
+    tile, rest = divmod(group, per_tile)
+    return tile * 2 * UNITS + which * UNITS + rest * 128
+
+
+def pack_first(w_query, w_key, w_value, captions, modulation):
+    k_rows, width = w_query.shape
+    size = width // k_rows
+    part = k_rows // N_DP
+    tokens, features = captions.shape
+    columns = 3 * k_rows
+    clips, own_mod = modulation.shape
+    pieces = own_mod // columns
+    mod_rows = 2 * clips * pieces
+    member = jnp.reshape(lax.axis_index("dp"), (1,)).astype(jnp.int32)
+    rows = part + tokens + 16
+
+    def kernel(member_ref, q_ref, k_ref, v_ref, cap_ref, mod_ref, out_ref):
+        spot = pl.ds(aligned(member_ref[0] * part, part), part)
+        mod = jnp.concatenate(
+            [mod_ref[:, i * columns : (i + 1) * columns] for i in range(pieces)], axis=0
+        )
+        high = mod.astype(BF16).astype(F32)
+        fill = jnp.zeros((16 - mod_rows, columns), F32)
+        mod = jnp.concatenate([high, mod - high, fill], axis=0).astype(BF16)
+        each = features // size
+        fill = jnp.zeros((tokens, columns - each), BF16)
+        for device in range(size):
+            own = slice(device * k_rows, (device + 1) * k_rows)
+            row = [ref[spot, own].astype(F32) for ref in (q_ref, k_ref, v_ref)]
+            out_ref[device, :part] = jnp.concatenate(row, axis=1).astype(BF16)
+            cap = cap_ref[:, device * each : (device + 1) * each]
+            out_ref[device, part : part + tokens] = jnp.concatenate([cap, fill], axis=1)
+            out_ref[device, part + tokens :] = mod
+
+    vmem = pl.BlockSpec(memory_space=pltpu.VMEM)
+    return pl.pallas_call(
+        kernel,
+        in_specs=[pl.BlockSpec(memory_space=pltpu.SMEM)] + [vmem] * 5,
+        out_specs=vmem,
+        out_shape=jax.ShapeDtypeStruct((size, rows, columns), BF16),
+        compiler_params=pltpu.CompilerParams(vmem_limit_bytes=VMEM_BYTES),
+        cost_estimate=pl.CostEstimate(
+            flops=0, bytes_accessed=8 * size * rows * columns, transcendentals=0
+        ),
+    )(member, w_query, w_key, w_value, captions, modulation)
+
+
+def unpack_first(packed, part, tokens, features, clips, own_mod):
+    size, _, columns = packed.shape
+    pieces = own_mod // columns
+    each = tokens // clips
+
+    def kernel(in_ref, quarter_ref, cap_ref, mod_ref):
+        for device in range(size):
+            quarter_ref[device] = in_ref[device, :part]
+            for clip in range(clips):
+                start = part + clip * each
+                cap_ref[clip, device * each : (device + 1) * each] = in_ref[
+                    device, start : start + each, :features
+                ]
+            mod = in_ref[device, part + tokens :].astype(F32)
+            count = clips * pieces
+            mod = mod[:count] + mod[count : 2 * count]
+            mod = [mod[i * clips : (i + 1) * clips] for i in range(pieces)]
+            mod_ref[:, device * own_mod : (device + 1) * own_mod] = jnp.concatenate(mod, axis=1)
+
+    vmem = pl.BlockSpec(memory_space=pltpu.VMEM)
+    return pl.pallas_call(
+        kernel,
+        in_specs=[vmem],
+        out_specs=[vmem] * 3,
+        out_shape=[
+            jax.ShapeDtypeStruct((size, part, columns), BF16),
+            jax.ShapeDtypeStruct((clips, size * each, features), BF16),
+            jax.ShapeDtypeStruct((clips, size * own_mod), F32),
+        ],
+        compiler_params=pltpu.CompilerParams(vmem_limit_bytes=VMEM_BYTES),
+        cost_estimate=pl.CostEstimate(
+            flops=0, bytes_accessed=4 * packed.size, transcendentals=0
+        ),
+    )(packed)
+
+
+def feed_kernel(ids_ref, *refs, size, places):
+    count = len(places)
+    x_refs, grad_ref = refs[:N_DP], refs[N_DP]
+    piece_refs = refs[N_DP + 1 : N_DP + 1 + count]
+    hidden_ref, grads_ref, near_ref, far_ref = refs[N_DP + 1 + count : N_DP + 5 + count]
+    down_out, x_out = refs[N_DP + 5 + count : N_DP + 7 + count]
+    x_all, grad_all, w_all, down_all, total, sems, out_sems = refs[N_DP + 7 + count :]
+    rows = x_refs[0].shape[0]
+    columns = w_all.shape[1]
+    tile = pl.program_id(0)
+    last = pl.num_programs(0) - 1
+
+    def spot(i):
+        return pl.ds(aligned(ids_ref[size + i] * rows, rows), rows)
+
+    def copies(first, end=None):
+        pairs = []
+        for i in range(N_DP):
+            pairs.append((x_refs[i], x_all.at[spot(i)]))
+        for i, (place_, start, height) in enumerate(places):
+            top = aligned(ids_ref[place_] * 192 + start, 32)
+            pairs.append((piece_refs[i].at[:, pl.ds(0, columns)], w_all.at[pl.ds(top, height)]))
+        pairs.append((grad_ref, grad_all))
+        for i, (place_, start, height) in enumerate(places):
+            for row, column, there_row, there_column, high, wide in folded(start, start + height):
+                top = aligned(ids_ref[place_] * 128 + row, 32)
+                pairs.append(
+                    (
+                        piece_refs[i].at[
+                            pl.ds(there_row, high), pl.ds(columns + there_column, wide)
+                        ],
+                        down_all.at[pl.ds(top, high), pl.ds(column, wide)],
+                    )
+                )
+        numbered = list(enumerate(pairs))[first:end]
+        return [pltpu.make_async_copy(a, b, sems.at[i]) for i, (a, b) in numbered]
+
+    def keep(i):
+        source, there = ((x_all, x_out), (down_all, down_out))[i]
+        return pltpu.make_async_copy(source, there, out_sems.at[i])
+
+    early = N_DP + count
+
+    @pl.when(tile == 0)
+    def _():
+        for copy in copies(0):
+            copy.start()
+        for copy in copies(0, early):
+            copy.wait()
+        keep(0).start()
+
+    weight = w_all[:, pl.ds(aligned(tile * 2 * UNITS, 2 * UNITS), 2 * UNITS)]
+    both = dot(x_all[...], weight)
+    gate, up = both[:, :UNITS], both[:, UNITS:]
+
+    @pl.when(tile == 0)
+    def _():
+        for copy in copies(early):
+            copy.wait()
+        keep(1).start()
+
+    down = down_all[pl.ds(aligned(tile * UNITS, UNITS), UNITS), :]
+    hidden_grad = dot(grad_all[...], down, NT)
+    sigmoid = jax.nn.sigmoid(gate)
+    silu = gate * sigmoid
+    hidden_ref[...] = (silu * up).astype(BF16)
+    gate_grad = hidden_grad * up * sigmoid * (1.0 + gate * (1.0 - sigmoid))
+    grads = jnp.concatenate([gate_grad.astype(BF16), (hidden_grad * silu).astype(BF16)], axis=1)
+    grads_ref[...] = grads
+    term = dot(grads, weight, NT)
+
+    @pl.when(tile == 0)
+    def _():
+        total[...] = term
+
+    @pl.when(tile > 0)
+    def _():
+        total[...] += term
+
+    @pl.when(tile == last)
+    def _():
+        for i, out_ref in enumerate((near_ref, far_ref)):
+            out_ref[:rows] = total[spot(i), :].astype(BF16)
+            out_ref[rows:] = total[spot(2 + i), :].astype(BF16)
+        keep(0).wait()
+        keep(1).wait()
+
+
+def feed(ring, xs, grads, pieces):
+    rows, width = xs[0].shape
+    units = (pieces[0][2].shape[1] - FOLD) // 2
+    places = tuple((ring.spots[shift], start, piece.shape[0]) for shift, start, piece in pieces)
+    copies = N_DP + 1 + len(pieces)
+    copies += sum(len(folded(start, start + height)) for _, start, height in places)
+    anywhere = pl.BlockSpec(memory_space=pl.ANY)
+    return pl.pallas_call(
+        functools.partial(feed_kernel, size=ring.size, places=places),
+        grid_spec=pltpu.PrefetchScalarGridSpec(
+            num_scalar_prefetch=1,
+            grid=(units // UNITS,),
+            in_specs=[anywhere] * (N_DP + 1 + len(pieces)),
+            out_specs=[
+                pl.BlockSpec((N_DP * rows, UNITS), lambda t, ids: (0, t)),
+                pl.BlockSpec((N_DP * rows, 2 * UNITS), lambda t, ids: (0, t)),
+                pl.BlockSpec((2 * rows, width), lambda t, ids: (0, 0)),
+                pl.BlockSpec((2 * rows, width), lambda t, ids: (0, 0)),
+                anywhere,
+                anywhere,
+            ],
+            scratch_shapes=[
+                pltpu.VMEM((N_DP * rows, width), BF16),
+                pltpu.VMEM((N_DP * rows, width), BF16),
+                pltpu.VMEM((width, 2 * units), BF16),
+                pltpu.VMEM((units, width), BF16),
+                pltpu.VMEM((N_DP * rows, width), F32),
+                pltpu.SemaphoreType.DMA((copies,)),
+                pltpu.SemaphoreType.DMA((2,)),
+            ],
+        ),
+        out_shape=[
+            jax.ShapeDtypeStruct((N_DP * rows, units), BF16),
+            jax.ShapeDtypeStruct((N_DP * rows, 2 * units), BF16),
+            jax.ShapeDtypeStruct((2 * rows, width), BF16),
+            jax.ShapeDtypeStruct((2 * rows, width), BF16),
+            jax.ShapeDtypeStruct((units, width), BF16),
+            jax.ShapeDtypeStruct((N_DP * rows, width), BF16),
+        ],
+        compiler_params=pltpu.CompilerParams(vmem_limit_bytes=VMEM_BYTES),
+        cost_estimate=pl.CostEstimate(
+            flops=10 * N_DP * rows * width * units,
+            bytes_accessed=24 * N_DP * rows * width,
+            transcendentals=N_DP * rows * units,
+        ),
+    )(ring.table, *xs, grads, *[piece for _, _, piece in pieces])
+
+
+def add_units(table, spots, d_weight, d_down, received, shape):
+    units, width = d_down.shape
+    columns = d_weight.shape[1]
+    rows = width // lax.axis_size("sp")
+    half = rows // 2
+    sides = 1 if shape == "home" else 2
+    heights = [rows] * 2 if shape == "whole" else [half] * 2
+
+    def kernel(ids_ref, *refs):
+        own, arrived = refs[: 2 * sides], refs[2 * sides : 2 * sides + len(received)]
+        out, whole = refs[2 * sides + len(received) : -1], refs[-1]
+        for side in range(sides):
+            whole[:, :columns] = own[2 * side][...].astype(F32)
+            for row, column, there_row, there_column, height, wide in folded(0, rows):
+                whole[
+                    there_row : there_row + height,
+                    columns + there_column : columns + there_column + wide,
+                ] = own[2 * side + 1][row : row + height, column : column + wide].astype(F32)
+            if shape == "home":
+                value = whole[...] + arrived[0][...].astype(F32) + arrived[1][...].astype(F32)
+                out[0][...] = value.astype(BF16)
+            elif shape == "halves":
+                out[side][...] = whole[side * half : (side + 1) * half].astype(BF16)
+            else:
+                count = arrived[side].shape[0]
+                start = side * half if count < rows else 0
+                span = slice(start, start + count)
+                whole[span] += arrived[side][...].astype(F32)
+                out[side][...] = whole[...].astype(BF16)
+
+    own_specs = []
+    for side in range(sides):
+        own_specs += [
+            pl.BlockSpec((rows, columns), lambda i, ids, side=side: (ids[spots[side]], 0)),
+            pl.BlockSpec((128, width), lambda i, ids, side=side: (ids[spots[side]], 0)),
+        ]
+    whole_spec = lambda height: pl.BlockSpec((height, columns + FOLD), lambda i, ids: (0, 0))
+    outs = [rows] if shape == "home" else heights
+    return pl.pallas_call(
+        kernel,
+        grid_spec=pltpu.PrefetchScalarGridSpec(
+            num_scalar_prefetch=1,
+            grid=(1,),
+            in_specs=own_specs + [whole_spec(a.shape[0]) for a in received],
+            out_specs=[whole_spec(height) for height in outs],
+            scratch_shapes=[pltpu.VMEM((rows, columns + FOLD), F32)],
+        ),
+        out_shape=[jax.ShapeDtypeStruct((height, columns + FOLD), BF16) for height in outs],
+        compiler_params=pltpu.CompilerParams(vmem_limit_bytes=VMEM_BYTES),
+        cost_estimate=pl.CostEstimate(
+            flops=0, bytes_accessed=12 * rows * (columns + FOLD), transcendentals=0
+        ),
+    )(table, *([d_weight, d_down] * sides), *received)
+
+
+def feed_back_kernel(
+    x_ref, grad_ref, hidden_ref, grads_ref, down_ref, d_w_ref, d_down_ref, out_ref, x_turned, total
+):
+    tile = pl.program_id(0)
+
+    @pl.when(tile == 0)
+    def _():
+        x_turned[...] = jnp.transpose(x_ref[...])
+
+    d_w_ref[...] = dot(x_turned[...], grads_ref[...]).astype(BF16)
+    d_down_ref[...] = dot(hidden_ref[...], grad_ref[...], TN).astype(BF16)
+    term = dot(hidden_ref[...], down_ref[...])
+
+    @pl.when(tile == 0)
+    def _():
+        total[...] = term
+
+    @pl.when(tile > 0)
+    def _():
+        total[...] += term
+
+    @pl.when(tile == pl.num_programs(0) - 1)
+    def _():
+        out_ref[...] = total[...].astype(BF16)
+
+
+def feed_back(xs, grads, hidden, unit_grads, down):
+    rows, width = xs.shape
+    units = down.shape[0]
+    fixed = pl.BlockSpec((rows, width), lambda t: (0, 0))
+    return pl.pallas_call(
+        feed_back_kernel,
+        grid=(units // UNITS,),
+        in_specs=[
+            fixed,
+            fixed,
+            pl.BlockSpec((rows, UNITS), lambda t: (0, t)),
+            pl.BlockSpec((rows, 2 * UNITS), lambda t: (0, t)),
+            pl.BlockSpec((UNITS, width), lambda t: (t, 0)),
+        ],
+        out_specs=[
+            pl.BlockSpec((width, 2 * UNITS), lambda t: (0, t)),
+            pl.BlockSpec((UNITS, width), lambda t: (t, 0)),
+            fixed,
+        ],
+        out_shape=[
+            jax.ShapeDtypeStruct((width, 2 * units), BF16),
+            jax.ShapeDtypeStruct((units, width), BF16),
+            jax.ShapeDtypeStruct((rows, width), BF16),
+        ],
+        scratch_shapes=[pltpu.VMEM((width, rows), BF16), pltpu.VMEM((rows, width), F32)],
+        compiler_params=pltpu.CompilerParams(vmem_limit_bytes=VMEM_BYTES),
+        cost_estimate=pl.CostEstimate(
+            flops=8 * rows * width * units, bytes_accessed=24 * rows * width, transcendentals=0
+        ),
+    )(xs, grads, hidden, unit_grads, down)
+
+
+def token_terms(table, first, count, grads, weight, apart):
+    clips, columns, length = grads.shape
+    width = weight.shape[1]
+    half = length // lax.axis_size("sp")
+
+    def kernel(ids_ref, grads_ref, w_ref, *out_refs):
+        for clip in range(clips):
+            value = dot(jnp.transpose(grads_ref[clip]), w_ref[...]).astype(BF16)
+            if apart:
+                out_refs[clip][...] = value
+            else:
+                out_refs[0][clip * half : (clip + 1) * half] = value
+
+    outs, rows = (clips, half) if apart else (1, clips * half)
+    return pl.pallas_call(
+        kernel,
+        grid_spec=pltpu.PrefetchScalarGridSpec(
+            num_scalar_prefetch=1,
+            grid=(count,),
+            in_specs=[
+                pl.BlockSpec((clips, columns, half), lambda i, ids: (0, 0, ids[first - i])),
+                pl.BlockSpec((columns, width), lambda i, ids: (0, 0)),
+            ],
+            out_specs=[pl.BlockSpec((rows, width), lambda i, ids: (i, 0))] * outs,
+        ),
+        out_shape=[jax.ShapeDtypeStruct((count * rows, width), BF16)] * outs,
+        compiler_params=pltpu.CompilerParams(vmem_limit_bytes=VMEM_BYTES),
+        cost_estimate=pl.CostEstimate(
+            flops=2 * clips * count * half * columns * width,
+            bytes_accessed=2 * clips * count * half * (columns + width) + 2 * width * columns,
+            transcendentals=0,
+        ),
+    )(table, grads, weight)
+
+
+def add_received(index, terms, received):
+    width = terms.shape[1]
+    rows = terms.shape[0] // (2 * (lax.axis_size("sp") // 2 - 1) + 1)
+    half = rows // 2
+
+    def kernel(*refs):
+        for side in range(2):
+            own, arrived, out = refs[side], refs[2 + side], refs[4 + side]
+            value = own[...].astype(F32)
+            if arrived.shape[0] == rows:
+                out[...] = (value + arrived[...].astype(F32)).astype(BF16)
+            else:
+                span = slice(side * half, (side + 1) * half)
+                rest = slice((1 - side) * half, (2 - side) * half)
+                out[span] = (value[span] + arrived[...].astype(F32)).astype(BF16)
+                out[rest] = own[rest]
+
+    def spec(height, block=0):
+        return pl.BlockSpec((height, width), lambda i: (block, 0))
+
+    return pl.pallas_call(
+        kernel,
+        grid=(1,),
+        in_specs=[spec(rows, index[0]), spec(rows, index[1])]
+        + [spec(a.shape[0]) for a in received],
+        out_specs=[spec(rows)] * 2,
+        out_shape=[jax.ShapeDtypeStruct((rows, width), BF16)] * 2,
+        compiler_params=pltpu.CompilerParams(vmem_limit_bytes=VMEM_BYTES),
+        cost_estimate=pl.CostEstimate(
+            flops=0, bytes_accessed=12 * rows * width, transcendentals=0
+        ),
+    )(terms, terms, *received)
+
+
+def head_weight_terms(block_in, grads):
+    clips, length, width = block_in.shape
+    columns = grads.shape[1]
+    size = lax.axis_size("sp")
+    k_rows = width // size
+    part = k_rows // N_DP
+    tile = 2 * k_rows
+
+    def kernel(in_ref, grads_ref, out_ref):
+        total = dot(grads_ref[0], in_ref[0])
+        for clip in range(1, clips):
+            total = total + dot(grads_ref[clip], in_ref[clip])
+        turned = jnp.transpose(total).astype(BF16)
+        for member in range(N_DP):
+            for shard in range(2):
+                start = shard * k_rows + member * part
+                out_ref[member, shard] = turned[start : start + part]
+
+    return pl.pallas_call(
+        kernel,
+        grid=(width // tile,),
+        in_specs=[
+            pl.BlockSpec((clips, length, tile), lambda t: (0, 0, t)),
+            pl.BlockSpec((clips, columns, length), lambda t: (0, 0, 0)),
+        ],
+        out_specs=pl.BlockSpec((N_DP, 2, part, columns), lambda t: (0, t, 0, 0)),
+        out_shape=jax.ShapeDtypeStruct((N_DP, size, part, columns), BF16),
+        compiler_params=pltpu.CompilerParams(vmem_limit_bytes=VMEM_BYTES),
+        cost_estimate=pl.CostEstimate(
+            flops=2 * clips * length * width * columns,
+            bytes_accessed=2 * clips * length * (width + columns) + 2 * width * columns,
+            transcendentals=0,
+        ),
+    )(block_in, grads)
+
+
 def turn(values, cos, sin):
     half = HD // 2
     a, b = values[:half], values[half:]
@@ -581,16 +1367,21 @@
     return lax.rsqrt(jnp.mean(values * values, axis=0, keepdims=True) + EPSILON)
 
 
-def project_kernel(x_ref, shift_ref, scale_ref, w_ref, cos_ref, sin_ref, in_ref, out_ref, raw_ref):
-    heads = w_ref.shape[0] // (3 * HD)
-    half = x_ref.shape[1] // 2
-    for clip in range(CLIPS):
-        x = x_ref[0, clip * half : (clip + 1) * half, :].astype(F32)
+def project_kernel(place_ref, *refs, sizes):
+    count = sum(sizes)
+    blocks = refs[:count]
+    shift_ref, scale_ref, w_ref, cos_ref, sin_ref = refs[count : count + 5]
+    in_ref, out_ref, raw_ref = refs[-3:]
+    half = in_ref.shape[1]
+    heads = w_ref.shape[1] // (3 * HD)
+
+    def run(x, clip):
+        x = x.astype(F32)
         inverse = lax.rsqrt(jnp.mean(x * x, axis=-1, keepdims=True) + EPSILON)
         block = x * inverse * (1.0 + scale_ref[clip : clip + 1, :]) + shift_ref[clip : clip + 1, :]
         block = block.astype(BF16)
         in_ref[clip] = block
-        raw = dot(w_ref[...], block, NT)
+        raw = jnp.transpose(dot(block, w_ref[...]))
         raw_ref[clip] = raw[: 2 * heads * HD]
         cos, sin = cos_ref[clip], sin_ref[clip]
         for head in range(2 * heads):
@@ -599,40 +1390,63 @@
             out_ref[clip, head * HD : (head + 1) * HD, :] = rotated.astype(BF16)
         out_ref[clip, 2 * heads * HD :, :] = raw[2 * heads * HD :].astype(BF16)
 
-
-def project(tokens, shift, scale, weight, cos, sin):
-    devices, rows, width = tokens.shape
-    half = rows // 2
-    columns = weight.shape[0]
-    length = devices * half
+    first = 0
+    for step, size in enumerate(sizes):
+        group = blocks[first : first + size]
+        first += size
+
+        @pl.when(pl.program_id(0) == step)
+        def _(group=group):
+            for clip in range(CLIPS):
+                if len(group) == 1:
+                    start = clip * (half + HELD)
+                    run(group[0][start : start + half, :], clip)
+                else:
+                    run(group[clip][:half], clip)
+
+
+def project(table, first, groups, shift, scale, weight, cos, sin, before):
+    sizes = tuple(len(g) for g in groups)
+    blocks = [b for g in groups for b in g]
+    width, columns = weight.shape
+    length = cos.shape[2]
+    half = groups[0][0].shape[0] * len(groups[0]) // CLIPS - HELD
+    fixed = lambda a: pl.BlockSpec(a.shape, lambda i, ids: (0,) * a.ndim)
+    out_shape = [
+        jax.ShapeDtypeStruct((CLIPS, length, width), BF16),
+        jax.ShapeDtypeStruct((CLIPS, columns, length), BF16),
+        jax.ShapeDtypeStruct((CLIPS, 2 * columns // 3, length), F32),
+    ]
+    in_specs = [fixed(a) for a in (*blocks, shift, scale, weight)]
+    in_specs += [pl.BlockSpec((CLIPS, HD // 2, half), lambda i, ids: (0, 0, ids[first + i]))] * 2
+    operands = [*blocks, shift, scale, weight, cos, sin]
+    aliases = {}
+    if before is not None:
+        aliases = {1 + len(operands) + i: i for i in range(3)}
+        in_specs += [pl.BlockSpec(memory_space=pl.ANY)] * 3
+        operands += before
+    rows = CLIPS * half * len(groups)
     return pl.pallas_call(
-        project_kernel,
-        grid=(devices,),
-        in_specs=[
-            pl.BlockSpec((1, rows, width), lambda i: (i, 0, 0)),
-            pl.BlockSpec((CLIPS, width), lambda i: (0, 0)),
-            pl.BlockSpec((CLIPS, width), lambda i: (0, 0)),
-            pl.BlockSpec((columns, width), lambda i: (0, 0)),
-            pl.BlockSpec((CLIPS, HD // 2, half), lambda i: (0, 0, i)),
-            pl.BlockSpec((CLIPS, HD // 2, half), lambda i: (0, 0, i)),
-        ],
-        out_specs=[
-            pl.BlockSpec((CLIPS, half, width), lambda i: (0, i, 0)),
-            pl.BlockSpec((CLIPS, columns, half), lambda i: (0, 0, i)),
-            pl.BlockSpec((CLIPS, 2 * columns // 3, half), lambda i: (0, 0, i)),
-        ],
-        out_shape=[
-            jax.ShapeDtypeStruct((CLIPS, length, width), BF16),
-            jax.ShapeDtypeStruct((CLIPS, columns, length), BF16),
-            jax.ShapeDtypeStruct((CLIPS, 2 * columns // 3, length), F32),
-        ],
+        functools.partial(project_kernel, sizes=sizes),
+        grid_spec=pltpu.PrefetchScalarGridSpec(
+            num_scalar_prefetch=1,
+            grid=(len(groups),),
+            in_specs=in_specs,
+            out_specs=[
+                pl.BlockSpec((CLIPS, half, width), lambda i, ids: (0, ids[first + i], 0)),
+                pl.BlockSpec((CLIPS, columns, half), lambda i, ids: (0, 0, ids[first + i])),
+                pl.BlockSpec((CLIPS, 2 * columns // 3, half), lambda i, ids: (0, 0, ids[first + i])),
+            ],
+        ),
+        out_shape=out_shape,
+        input_output_aliases=aliases,
         compiler_params=pltpu.CompilerParams(vmem_limit_bytes=VMEM_BYTES),
         cost_estimate=pl.CostEstimate(
-            flops=2 * CLIPS * length * width * columns,
-            bytes_accessed=4 * CLIPS * length * width + 8 * CLIPS * length * columns,
+            flops=2 * rows * width * columns,
+            bytes_accessed=4 * rows * width + 8 * rows * columns + 2 * width * columns,
             transcendentals=0,
         ),
-    )(tokens, shift, scale, weight, cos, sin)
+    )(table, *operands)
 
 
 def cross_probabilities(cap_key, query):
@@ -647,10 +1461,10 @@
     length = q_ref.shape[2]
     half = mixed_ref.shape[2]
     gate = gate_ref[pl.program_id(1)]
-    keys = k_ref[0]
+    keys = jnp.transpose(k_ref[0])
     for start in range(0, length, block):
         query = q_ref[0, :, start : start + block]
-        grown = jnp.exp(dot(keys, query, TN) * HD**-0.5)
+        grown = jnp.exp(dot(keys, query) * HD**-0.5)
         total = jnp.sum(grown, axis=0, keepdims=True)
         self_out = dot(v_ref[0], grown.astype(BF16)) / total
         probs = cross_probabilities(ck_ref[...], query)
@@ -670,7 +1484,7 @@
     cap_spec = pl.BlockSpec((HD, CAP), lambda c, h: (h, c))
     own_spec = pl.BlockSpec((1, HD, length), lambda c, h: (c, h, 0))
     return pl.pallas_call(
-        functools.partial(attend_kernel, block=2 * half),
+        functools.partial(attend_kernel, block=length),
         grid=(clips, heads),
         in_specs=[
             pl.BlockSpec(memory_space=pltpu.SMEM),
@@ -729,6 +1543,7 @@
     score_scale = HD**-0.5
     gate = gate_ref[pl.program_id(1)]
     keys, values = k_ref[0], v_ref[0]
+    keys_turned, values_turned = jnp.transpose(keys), jnp.transpose(values)
     cap_key, cap_value = ck_ref[...], cv_ref[...]
     cap_key_grad = jnp.zeros((HD, CAP), F32)
     cap_value_grad = jnp.zeros((HD, CAP), F32)
@@ -743,10 +1558,10 @@
         gate_grad_ref[0, 0, :, span] = jnp.sum(
             wide * cross_ref[0, :, span], axis=0, keepdims=True
         )
-        probs = jnp.exp(dot(keys, query, TN) * score_scale - log_ref[0, 0, :, span])
-        score_grad = (probs * (dot(values, grad, TN) - delta)).astype(BF16)
-        value_part = dot(grad, probs.astype(BF16), NT)
-        key_part = dot(query, score_grad, NT)
+        probs = jnp.exp(dot(keys_turned, query) * score_scale - log_ref[0, 0, :, span])
+        score_grad = (probs * (dot(values_turned, grad) - delta)).astype(BF16)
+        value_part = jnp.transpose(dot(probs.astype(BF16), jnp.transpose(grad)))
+        key_part = jnp.transpose(dot(score_grad, jnp.transpose(query)))
         if start == 0:
             value_acc[...] = value_part
             key_acc[...] = key_part
@@ -794,7 +1609,7 @@
     table_spec = pl.BlockSpec((1, HD // 2, length), lambda c, h: (c, 0, 0))
     row_spec = pl.BlockSpec((1, 1, 1, length), lambda c, h: (c, h, 0, 0))
     return pl.pallas_call(
-        functools.partial(attend_back_kernel, block=2 * half),
+        functools.partial(attend_back_kernel, block=length // 2),
         grid=(clips, heads),
         in_specs=[
             pl.BlockSpec(memory_space=pltpu.SMEM),
@@ -887,232 +1702,248 @@
 
     inputs = tokens[0].astype(F32)
     out_grad = cotangent[0].astype(F32)
-
+    hidden_units = ff // N_DP
+
+    def by_row(values):
+        return jnp.repeat(values, half, axis=0)
+
+    far = size // 2
+    out_cols_part = D // N_DP
+    table = ring.table
+    tanh_gate = jnp.tanh(gate_cross)
+    own_gate = lax.dynamic_slice(tanh_gate, (shard * heads,), (heads,))
+
+    token_flow = Gather(ring, [pack_tokens(tokens[0], w_out)])
+    token_flow.send()
     cond_row = conditioning[0]
     cond_act = jax.nn.silu(cond_row).astype(BF16)
     mod_part = dot(cond_act, w_ada) + b_ada[None, :]
-    modulation = jnp.transpose(gather_small(mod_part, "sp"), (1, 0, 2)).reshape(CLIPS, -1)
+    flat_caption = captions[0].reshape(-1, size * text_rows)
+    packed = exchange(pack_first(w_query, w_key, w_value, flat_caption, mod_part))
+    token_flow.live, packed = ordered((token_flow.live, packed))
+    token_flow.keep()
+
+    token_flow.send()
+    quarter, caption_cols, modulation = unpack_first(
+        packed, k_part, flat_caption.shape[0], text_rows, CLIPS, mod_part.shape[1]
+    )
+    caption_cols = caption_cols.reshape(-1, text_rows)
+    quarter_far = across(quarter, 2)
+    cap_terms = caption_terms(w_text_key, w_text_value, caption_cols)
+    caption_all = lax.all_gather(caption_cols, "dp", axis=0, tiled=True)
+    token_flow.live, quarter, quarter_far, modulation, cap_terms = ordered(
+        (token_flow.live, quarter, quarter_far, modulation, cap_terms)
+    )
+    token_flow.keep()
+
+    token_flow.send()
+    quarters = [quarter, quarter_far, across(quarter, 1), across(quarter_far, 1)]
+    w_qkv, w_turned = join_projections(ring, quarters)
+    cap_terms = exchange(cap_terms)
     shift_one, scale_one, gate_one, shift_two, scale_two, gate_two = jnp.split(modulation, 6, axis=1)
-
-    def by_row(values):
-        return jnp.repeat(values, half, axis=0)
-
-    start = member * k_part
-    quarter = jnp.stack(
-        [
-            lax.dynamic_slice(w, (start, 0), (k_part, D)).reshape(k_part, size, own_cols)
-            for w in (w_query, w_key, w_value)
-        ],
-        axis=2,
-    )
-    quarter = jnp.transpose(quarter, (1, 0, 2, 3)).reshape(size, k_part, 3 * own_cols)
-    w_qkv = in_order(gather_packs(exchange(quarter)))
-    w_qkv = jnp.transpose(w_qkv, (3, 1, 0, 2)).reshape(3 * own_cols, D)
-
-    cap_part = captions[0].reshape(-1, size, text_rows)
-    caption_cols = exchange(jnp.transpose(cap_part, (1, 0, 2)))
-    caption_cols = (
-        caption_cols.reshape(size, CLIPS, -1, text_rows).transpose(1, 0, 2, 3).reshape(-1, text_rows)
-    )
-    cap_terms = jnp.stack(
-        [
-            dot(w, caption_cols, (((0,), (1,)), ((), ()))).astype(BF16)
-            for w in (w_text_key, w_text_value)
-        ]
-    )
-
-    token_blocks = ring.gather_whole(tokens[0])
-
-    cap_heads = ring.scatter(
-        lambda device: jnp.transpose(
-            lax.dynamic_slice(
-                cap_terms, (0, device * own_cols, 0), (2, own_cols, CLIPS * CAP)
-            ),
-            (1, 0, 2),
-        )
-    ).astype(BF16)
-    cap_key, cap_value = cap_heads[:, 0], cap_heads[:, 1]
-
+    branch_grad = (by_row(gate_two) * out_grad).astype(BF16)
+    branch_grads = lax.all_gather(branch_grad, "dp", axis=0, tiled=True)
     lane = jnp.arange(size * half, dtype=jnp.int32)
     mirrored = (size - 1 - lane // half) * half + lane % half
     freq = 10000.0 ** (-(jnp.arange(HD // 2, dtype=F32) * 2.0 / HD))
     angle = jnp.stack([lane, mirrored]).astype(F32)[:, None, :] * freq[None, :, None]
     cos, sin = jnp.cos(angle), jnp.sin(angle)
-
-    block_in, qkv, raw = project(token_blocks, shift_one, scale_one, w_qkv, cos, sin)
-
-    out_piece = lax.dynamic_slice(w_out, (0, member * (D // N_DP)), (k_rows, D // N_DP))
-    gate_piece = jnp.concatenate(
-        [
-            lax.dynamic_slice(w, (0, i * ff_rows + member * ff_part), (k_rows, ff_part))
-            for w in (w_gate, w_up)
-            for i in range(size)
-        ],
-        axis=1,
-    )
-    down_piece = lax.dynamic_slice(w_down, (member * ff_part, 0), (ff_part, D))
-    token_blocks, out_piece, gate_piece, down_piece = lax.optimization_barrier(
-        (token_blocks, out_piece, gate_piece, down_piece)
-    )
-    out_cols = ring.gather_whole(out_piece).reshape(D, D // N_DP)
-    out_full = jnp.transpose(in_order(gather_packs(out_cols)), (1, 0, 2)).reshape(D, D)
-    gate_up = ring.gather_whole(gate_piece).reshape(D, 2 * ff // N_DP)
-    down = ring.gather_whole(down_piece).reshape(ff // N_DP, D)
-
-    tanh_gate = jnp.tanh(gate_cross)
-    own_gate = lax.dynamic_slice(tanh_gate, (shard * heads,), (heads,))
+    token_flow.live, w_qkv = ordered((token_flow.live, w_qkv))
+    token_flow.keep()
+
+    def project_some(first, groups, before):
+        return project(table, first, groups, shift_one, scale_one, w_qkv, cos, sin, before)
+
+    token_flow.send()
+    blocks = [b for _, b in token_flow.blocks]
+    projected = project_some(0, blocks[:5], None)
+    token_flow.live, projected, cap_terms = ordered((token_flow.live, projected, cap_terms))
+    token_flow.keep()
+
+    weight_flow = Gather(ring, [unit_pieces(w_gate, w_up, w_down, token_flow.halves[0][0])])
+    weight_flow.send()
+    out_cols = unpack_w_out(ring, token_flow, half)
+    out_full = lax.all_gather(out_cols, "dp", axis=1, tiled=True)
+    halves = token_flow.halves
+    block_in, qkv, raw = project_some(
+        5, [*blocks[5:], [halves[0][0], halves[1][0]]], projected
+    )
+    cap_heads = jnp.sum(cap_terms.astype(F32), axis=0).astype(BF16)
+    cap_key, cap_value = cap_heads[:, : CLIPS * CAP], cap_heads[:, CLIPS * CAP :]
+    weight_flow.live, block_in, qkv, raw, cap_key, cap_value = ordered(
+        (weight_flow.live, block_in, qkv, raw, cap_key, cap_value)
+    )
+    weight_flow.keep()
+
+    weight_flow.send()
     mixed_blocks, self_out, cross_out, log_total = attend(own_gate, qkv, cap_key, cap_value, half)
-    mixed = exchange(mixed_blocks).reshape(D, rows)
-    attn_out = dot(mixed, out_full, TN)
-
+    weight_flow.live, mixed_blocks = ordered((weight_flow.live, mixed_blocks))
+    weight_flow.keep()
+
+    mixed = exchange(mixed_blocks)
     inverse_one = inverse_rms(inputs)
     normed_one = inputs * inverse_one
+    mixed, out_full = ordered((mixed, out_full))
+
+    weight_flow.send()
+    mixed = mixed.reshape(D, rows)
+    attn_out = dot(mixed, out_full, TN)
     middle = inputs + by_row(gate_one) * attn_out
     inverse_two = inverse_rms(middle)
     normed_two = middle * inverse_two
     ffn_in = (normed_two * (1.0 + by_row(scale_two)) + by_row(shift_two)).astype(BF16)
-    branch_grad = (by_row(gate_two) * out_grad).astype(BF16)
-    branch_grads = jnp.concatenate(gather_packs(branch_grad))
-    ffn_ins = jnp.concatenate(gather_packs(ffn_in))
-    hidden_units = ff // N_DP
-    gate_proj = dot(ffn_ins, gate_up[:, :hidden_units])
-    up_proj = dot(ffn_ins, gate_up[:, hidden_units:])
-    sigmoid_gate = jax.nn.sigmoid(gate_proj)
-    silu_gate = gate_proj * sigmoid_gate
-    hidden = (silu_gate * up_proj).astype(BF16)
-    hidden_grad = dot(branch_grads, down, NT)
-    gate_grad = (
-        hidden_grad * up_proj * sigmoid_gate * (1.0 + gate_proj * (1.0 - sigmoid_gate))
-    ).astype(BF16)
-    up_grad = (hidden_grad * silu_gate).astype(BF16)
-    ffn_terms = dot(gate_grad, gate_up[:, :hidden_units], NT) + dot(
-        up_grad, gate_up[:, hidden_units:], NT
-    )
-    ffn_in_grad = sum_packs([ffn_terms[i * rows : (i + 1) * rows] for i in range(N_DP)])
-    branch_terms = dot(hidden, down)
-    branch = sum_packs([branch_terms[i * rows : (i + 1) * rows] for i in range(N_DP)])
-    result = (middle + by_row(gate_two) * branch).astype(BF16)
-    grad_down = dot(hidden, branch_grads, TN).astype(BF16)
-    grad_gate = dot(ffn_ins, gate_grad, TN).astype(BF16)
-    grad_up = dot(ffn_ins, up_grad, TN).astype(BF16)
-
+    ffn_far = across(ffn_in, 2)
+    weight_flow.live, ffn_in, ffn_far, branch_grads = ordered(
+        (weight_flow.live, ffn_in, ffn_far, branch_grads)
+    )
+    weight_flow.keep()
+
+    weight_flow.send()
+    weight_flow.keep()
+    pieces = [(shift, 0, arrays[0]) for shift, arrays in weight_flow.blocks]
+    pieces += [(far, 0, weight_flow.halves[0][0])]
+    pieces += [(far, k_rows // 2, weight_flow.halves[1][0])]
+    hidden, unit_grads, ffn_own, ffn_next, down, ffn_ins = feed(
+        ring, [ffn_in, ffn_far, across(ffn_in, 1), across(ffn_far, 1)], branch_grads, pieces
+    )
+    near = across(jnp.concatenate([ffn_own[rows:], ffn_next[rows:]]), 1)
+    ffn_far = (ffn_next[:rows].astype(F32) + near[rows:].astype(F32)).astype(BF16)
+    ffn_own = ffn_own[:rows].astype(F32) + near[:rows].astype(F32)
+    ffn_own, ffn_far, hidden, unit_grads = ordered((ffn_own, ffn_far, hidden, unit_grads))
+
+    ffn_far = across(ffn_far, 2)
+    d_units, d_down_units, branch_terms = feed_back(
+        ffn_ins, branch_grads, hidden, unit_grads, down
+    )
+    ffn_far, d_units, d_down_units, branch_terms = ordered(
+        (ffn_far, d_units, d_down_units, branch_terms)
+    )
+
+    def add_unit_step(step, received):
+        shift = far - step
+        spots = (ring.spots[shift], ring.spots[-shift if step else shift])
+        kind = "halves" if step == 0 else "whole"
+        return add_units(table, spots, d_units, d_down_units, received, kind)
+
+    def send(values):
+        return ring.send_up(values[:1]) + ring.send_down(values[1:])
+
+    unit_back = send(add_unit_step(0, []))
+    branch = lax.psum_scatter(branch_terms, "dp", scatter_dimension=0, tiled=True)
+    ffn_in_grad = ffn_own + ffn_far.astype(F32)
     middle_grad = out_grad + norm_back(
         ffn_in_grad * (1.0 + by_row(scale_two)), normed_two, inverse_two
     )
     attn_grad = (by_row(gate_one) * middle_grad).astype(BF16)
     mixed_grad = dot(out_full, attn_grad, NT).astype(BF16).reshape(size, own_cols, rows)
-    grad_out = dot(mixed, attn_grad).astype(BF16)
+    unit_back, mixed_grad, mixed, attn_grad = ordered((unit_back, mixed_grad, mixed, attn_grad))
+
     head_grad = exchange(mixed_grad)
-
+    unit_back = add_unit_step(1, unit_back)
+    grad_out = out_terms(mixed, attn_grad)
+    unit_back, head_grad, grad_out = ordered((unit_back, head_grad, grad_out))
+
+    unit_back = send(unit_back)
+    out_sum = lax.psum_scatter(grad_out, "dp", scatter_dimension=0, tiled=True)
     grads, cap_grads, gate_rows = attend_back(
         own_gate, qkv, cap_key, cap_value, head_grad, self_out, cross_out, log_total, raw, cos, sin
     )
+    unit_back, grads, cap_grads = ordered((unit_back, grads, cap_grads))
     grads = grads.reshape(CLIPS, 3 * own_cols, size * half)
 
-    def token_grad(device):
-        columns = lax.dynamic_slice(
-            grads, (0, 0, device * half), (CLIPS, 3 * own_cols, half)
-        )
-        return jnp.concatenate([dot(columns[c], w_qkv, TN) for c in range(CLIPS)])
-
-    block_in_grad = ring.scatter(token_grad)
-    grad_qkv = (
-        dot(block_in[0], grads[0], (((0,), (1,)), ((), ())))
-        + dot(block_in[1], grads[1], (((0,), (1,)), ((), ())))
-    ).astype(BF16)
-
-    inputs_grad = middle_grad + norm_back(
-        block_in_grad * (1.0 + by_row(scale_one)), normed_one, inverse_one
-    )
-
-    mod_terms = jnp.concatenate(
-        [
-            clip_sums(block_in_grad),
-            clip_sums(block_in_grad * normed_one),
-            clip_sums(middle_grad * attn_out),
-            clip_sums(ffn_in_grad),
-            clip_sums(ffn_in_grad * normed_two),
-            clip_sums(out_grad * branch),
-        ],
-        axis=1,
-    )
+    token_back = send(token_terms(table, ring.spots[far], 1, grads, w_turned, True))
+    unit_back = send(add_unit_step(2, unit_back))
+    last = ring.spots[far - 1]
+    (terms,) = token_terms(table, last, last + 1, grads, w_turned, False)
+    token_back, terms, grads, cap_grads = ordered((token_back, terms, grads, cap_grads))
+
+    def add_token_step(step, received):
+        return add_received((2 * step, 2 * step + 1), terms, received)
+
+    token_back = send(add_token_step(0, token_back))
+    cap_all = jnp.transpose(cap_grads, (1, 0, 2)).reshape(own_cols, 2 * CLIPS * CAP)
+    cap_all = gather_small(cap_all, "sp").reshape(D, 2 * CLIPS * CAP)
+    qkv_sum = head_weight_terms(block_in, grads)
+    token_back, unit_back, qkv_sum = ordered((token_back, unit_back, qkv_sum))
+
+    token_back = send(add_token_step(1, token_back))
+    unit_back = send(add_unit_step(3, unit_back))
+    qkv_sum = lax.psum_scatter(qkv_sum, "dp", scatter_dimension=0, tiled=True)[0]
+    token_back, unit_back, cap_all, branch, out_sum = ordered(
+        (token_back, unit_back, cap_all, branch, out_sum)
+    )
+
+    token_back = send(add_token_step(2, token_back))
+    cap_far = across(cap_all, 2)
+    spot = ring.spots[0]
+    (unit_home,) = add_units(table, (spot,), d_units, d_down_units, unit_back, "home")
+    unit_far = across(unit_home, 2)
+    qkv_home = exchange(qkv_sum)
+    result = (middle + by_row(gate_two) * branch.astype(F32)).astype(BF16)
+    sums = [
+        clip_sums(middle_grad * attn_out),
+        clip_sums(ffn_in_grad),
+        clip_sums(ffn_in_grad * normed_two),
+        clip_sums(out_grad * branch.astype(F32)),
+    ]
+    token_back, sums, cap_all, cap_far, unit_home, unit_far, qkv_home, out_sum = ordered(
+        (token_back, sums, cap_all, cap_far, unit_home, unit_far, qkv_home, out_sum)
+    )
+
+    inputs_grad, own_sums = finish_tokens(terms, token_back, middle_grad, tokens[0], scale_one)
+
+    mod_terms = jnp.concatenate([own_sums, *sums], axis=1)
     mod_terms = jnp.transpose(mod_terms.reshape(CLIPS, size, -1), (1, 0, 2))
-    mod_low = jnp.sum(exchange(mod_terms), axis=0).astype(BF16)
+    gate_own = jnp.sum(gate_rows, axis=(2, 3))
+    gate_own = jnp.broadcast_to(gate_own[None], (size, CLIPS, heads))
+    mod_terms = jnp.concatenate([mod_terms, gate_own], axis=2)
+    mod_terms, cap_all, cap_far, unit_home, unit_far, qkv_home, out_sum = ordered(
+        (mod_terms, cap_all, cap_far, unit_home, unit_far, qkv_home, out_sum)
+    )
+
+    arrived = exchange(mod_terms)
+    out_home = exchange(out_sum.reshape(size, k_rows, out_cols_part))
+    unit_blocks = [unit_home, unit_far, across(unit_home, 1), across(unit_far, 1)]
+    cap_blocks = [cap_all, cap_far, across(cap_all, 1), across(cap_far, 1)]
+    qkv_far = across(qkv_home, 2)
+    shape = lambda *dims: jax.ShapeDtypeStruct(dims, F32)
+    d_gate_w, d_up_w, d_down = place(
+        ring, place_units, unit_blocks, [shape(k_rows, ff), shape(k_rows, ff), shape(ff_rows, D)]
+    )
+    d_text_key, d_text_value = text_grads(ring, caption_all, cap_blocks)
+    arrived, out_home, qkv_home, qkv_far = ordered((arrived, out_home, qkv_home, qkv_far))
+
+    own_mod = w_ada.shape[1]
+    mod_low = jnp.sum(arrived[:, :, :own_mod], axis=0).astype(BF16)
+    gate_all = jnp.transpose(arrived[:, :, own_mod:], (1, 0, 2)).reshape(CLIPS, HEADS)
     cond_part = dot(mod_low, w_ada, NT)
     cond_sum = jnp.sum(gather_small(cond_part, "sp"), axis=0)
     sigmoid_cond = jax.nn.sigmoid(cond_row)
     cond_grad = cond_sum * sigmoid_cond * (1.0 + cond_row * (1.0 - sigmoid_cond))
-    both = jnp.concatenate([cond_act, mod_low], axis=1)
+    both = jnp.concatenate([cond_act.astype(F32), mod_low.astype(F32), gate_all], axis=1)
     both_all = gather_small(both, "dp").reshape(N_DP * CLIPS, -1)
-    cond_all, mod_all = both_all[:, : cond_act.shape[1]], both_all[:, cond_act.shape[1] :]
+    cond_size = cond_act.shape[1]
+    cond_all = both_all[:, :cond_size].astype(BF16)
+    mod_all = both_all[:, cond_size : cond_size + own_mod].astype(BF16)
     d_ada = dot(cond_all, mod_all, TN)
     d_bias = jnp.sum(mod_all.astype(F32), axis=0)
-    gate_own = jnp.sum(gate_rows, axis=(0, 2, 3))
-    gate_all = jnp.sum(
-        gather_small(gather_small(gate_own, "sp").reshape(-1), "dp"), axis=0
-    )
-    d_gate_cross = gate_all * (1.0 - tanh_gate * tanh_gate)
-
-    cap_all = ring.gather_whole(jnp.transpose(cap_grads, (1, 0, 2)))
-    cap_all = cap_all.reshape(D, 2, CLIPS * CAP)
-    caption_grad = dot(w_text_key, cap_all[:, 0]) + dot(w_text_value, cap_all[:, 1])
-    caption_grad = caption_grad.astype(BF16).reshape(text_rows, CLIPS, size, -1)
-    caption_grad = exchange(jnp.transpose(caption_grad, (2, 1, 3, 0)))
+    d_gate_cross = jnp.sum(both_all[:, cond_size + own_mod :], axis=0) * (
+        1.0 - tanh_gate * tanh_gate
+    )
+
+    caption_grad = dot(cap_all[:, : CLIPS * CAP], w_text_key, (((0,), (1,)), ((), ()))) + dot(
+        cap_all[:, CLIPS * CAP :], w_text_value, (((0,), (1,)), ((), ()))
+    )
+    caption_grad = caption_grad.astype(BF16).reshape(CLIPS, size, -1, text_rows)
+    caption_grad = exchange(jnp.transpose(caption_grad, (1, 0, 2, 3)))
     caption_grad = (
         jnp.transpose(caption_grad, (1, 2, 0, 3)).reshape(CLIPS, -1, size * text_rows).astype(F32)
     )
-    text_terms = [
-        dot(caption_cols, cap_all[:, i], (((0,), (1,)), ((), ()))).astype(BF16) for i in range(2)
-    ]
-    text_rows_part = text_rows // N_DP
-    text_terms = jnp.concatenate(text_terms, axis=1)
-
-    def rows_for(offset):
-        return lax.dynamic_slice(
-            text_terms, ((member ^ offset) * text_rows_part, 0), (text_rows_part, 2 * D)
-        )
-
-    text_home = sum_packs([rows_for(offset) for offset in (0, 2, 1, 3)]).astype(BF16)
-    text_home = in_order(gather_packs(text_home)).reshape(text_rows, 2 * D).astype(F32)
-    d_text_key, d_text_value = text_home[:, :D], text_home[:, D:]
-
-    down_home = ring.scatter(
-        lambda device: lax.dynamic_slice(grad_down, (device * ff_part, 0), (ff_part, D))
-    ).astype(BF16)
-    d_down = in_order(gather_packs(down_home)).reshape(ff_rows, D).astype(F32)
-
-    def gate_home(terms):
-        home = ring.scatter(
-            lambda device: lax.dynamic_slice(
-                terms, (device * k_rows, 0), (k_rows, hidden_units)
-            )
-        ).astype(BF16)
-        whole = in_order(gather_packs(home.reshape(k_rows, size, ff_part)))
-        return jnp.transpose(whole, (1, 2, 0, 3)).reshape(k_rows, ff).astype(F32)
-
-    d_gate_w = gate_home(grad_gate)
-    d_up_w = gate_home(grad_up)
-
-    out_cols_part = D // N_DP
-
-    def cols_for(offset):
-        return lax.dynamic_slice(grad_out, (0, (member ^ offset) * out_cols_part), (D, out_cols_part))
-
-    out_sum = sum_packs([cols_for(offset) for offset in (0, 2, 1, 3)])
-    out_home = ring.scatter(
-        lambda device: lax.dynamic_slice(out_sum, (device * k_rows, 0), (k_rows, out_cols_part))
-    ).astype(BF16)
-    d_out = jnp.transpose(in_order(gather_packs(out_home)), (1, 0, 2)).reshape(k_rows, D).astype(F32)
-
-    grad_qkv = grad_qkv.reshape(size, N_DP, k_part, 3 * own_cols)
-
-    def quarter_for(offset):
-        return lax.dynamic_index_in_dim(grad_qkv, member ^ offset, 1, False)
-
-    qkv_sum = sum_packs([quarter_for(offset) for offset in (0, 2, 1, 3)]).astype(BF16)
-    qkv_home = in_order(gather_packs(exchange(qkv_sum)))
-    qkv_home = qkv_home.reshape(N_DP, size, k_part, 3, own_cols)
-    qkv_home = jnp.transpose(qkv_home, (3, 0, 2, 1, 4)).reshape(3, k_rows, D).astype(F32)
+
+    out_home = jnp.sum(out_home.astype(F32), axis=0).astype(BF16)
+    (d_out,) = place(ring, place_columns, gather_packs(out_home), [shape(k_rows, D)])
+    qkv_blocks = [qkv_home, qkv_far, across(qkv_home, 1), across(qkv_far, 1)]
+    d_query, d_key, d_value = place(ring, place_heads, qkv_blocks, [shape(k_rows, D)] * 3)
     return (
         result[None],
         inputs_grad[None],
@@ -1120,9 +1951,9 @@
         cond_grad[None],
         d_ada,
         d_bias,
-        qkv_home[0],
-        qkv_home[1],
-        qkv_home[2],
+        d_query,
+        d_key,
+        d_value,
         d_out,
         d_gate_cross,
         d_text_key,

time: 996 us -> 759 us (0.76)
  Pallas kernels: 59.1 us -> 176 us
  local copies, waits for them, and re-layouts: 193 us -> 94.6 us
  matrix products: 115 us -> 16.8 us
  starting transfers between devices: 191 us -> 122 us
  other arithmetic: 93.5 us -> 31.1 us
  between operations: 42.4 us -> 15.5 us
  blocking collectives: 0 us -> 12.4 us
    pallas_call x3 -> x49, Pallas kernels: 59.1 us -> 176 us  [the longest x1 26.1 us: feed(): pl.pallas_call(functools.partial(feed_kernel, size=ring.size, places=plac...]
    dot_general x39 -> x7, matrix products: 115 us -> 16.8 us  [dot(): return lax.dot_general(left, right, dims, preferred_element_type=F32)]
    ppermute x88 -> x32, starting transfers between devices: 116 us -> 56.9 us  [the longest x16 39.7 us: send_up(): return [lax.ppermute(v, 'sp', self.up) for v in values]]
    unnamed x225 -> x252, local copies, waits for them, and re-layouts: 34.5 us -> 76.8 us
    all_to_all x7, waiting for transfers between devices: 2 us -> 44.3 us  [exchange(): return lax.all_to_all(value, 'sp', 0, 0, tiled=True)]
    convert_element_type x8 -> x0, local copies, waits for them, and re-layouts: 39.4 us -> none  [the longest x4 19.7 us: gate_home(): return jnp.transpose(whole, (1, 2, 0, 3)).reshape(k_rows, ff).astype(F32)]
    ppermute x88 -> x32, waiting for transfers between devices: 236 us -> 196 us  [the longest x16 174 us: send_up(): return [lax.ppermute(v, 'sp', self.up) for v in values]]
    convert_element_type x34 -> x4, other arithmetic: 44.1 us -> 5.83 us  [the longest x1 2.73 us: split_heads(): result = (middle + by_row(gate_two) * branch.astype(F32)).astype(BF16)]
  transfers between devices with their start and end apart: 145 -> 68, of which waited for: 61 -> 31; matrix products, arithmetic and copies ran while one was open for 35% -> 8% of each run, Pallas kernels for 6% -> 19%
where the time goes in v2:
time: 759 us; the launch traced here: 748 us
  waiting for transfers between devices  278 us (37%)
  Pallas kernels  176 us (23%)
  starting transfers between devices  122 us (16%)
  local copies, waits for them, and re-layouts  94.6 us (12%)
  other arithmetic  31.1 us (4%)
  matrix products  16.8 us (2%)
  between operations  15.5 us (2%)
  blocking collectives  12.4 us (2%)
    ppermute x16, waiting for transfers between devices, send_up(): return [lax.ppermute(v, 'sp', self.up) for v in values]  174 us
    unnamed x252, local copies, waits for them, and re-layouts  76.8 us
    all_to_all x7, waiting for transfers between devices, exchange(): return lax.all_to_all(value, 'sp', 0, 0, tiled=True)  44.3 us
    all_to_all x7, starting transfers between devices, exchange(): return lax.all_to_all(value, 'sp', 0, 0, tiled=True)  40.3 us
    ppermute x16, starting transfers between devices, send_up(): return [lax.ppermute(v, 'sp', self.up) for v in values]  39.7 us
    pallas_call x1, Pallas kernels, feed(): pl.pallas_call(functools.partial(feed_kernel, size=ring.size, places=plac...  26.1 us
    ppermute x20, waiting for transfers between devices, across(): return lax.ppermute(value, 'dp', [(i, i ^ bit) for i in range(N_DP)])  25.4 us
    pallas_call x1, Pallas kernels, attend_back(): pl.pallas_call(functools.partial(attend_back_kernel, block=length // 2),...  23.9 us
  transfers between devices with their start and end apart: 68, of which 31 were waited for; matrix products, arithmetic and copies ran while one was open for 8% of the time, Pallas kernels for 19%

profile of v2, /device:TPU:0, one launch (start us, length us, event | category | flops | bytes accessed | tf_op | source)
XLA Modules:
  0.0 747.7 jit_solution(13796821410861984408)
XLA Ops:
  11.2 7.3 all-to-all-start
  23.9 31.7 %collective-permute-done.refs_0_ = bf16[320,1536]{1,0:T(8,128)(2,1)S(1)} collective-permute-done((bf16[320,1536]{1,0:T(8,128)(2,1)S(1)}, bf16[320,1536]{1,0:T(8,128)(2,1)S(1)}, u32[]{:S(2)}, u32[]{:S(2)}) %collective-permute-start) | collective-permute-done | bytes 983072 | tf_op jit(solution)/shard_map/ppermute | solution.py:508
  58.8 6.8 collective-permute-start.2
  76.5 4.4 collective-permute-done.4.refs_3_
  80.9 4.9 collective-permute-done.2.refs_0_
  85.8 2.8 collective-permute-done.3.refs_1_
  88.7 4.3 all-to-all-start.1
  102.7 35.9 %collective-permute-done.5.refs_0_ = bf16[320,1536]{1,0:T(8,128)(2,1)S(1)} collective-permute-done((bf16[320,1536]{1,0:T(8,128)(2,1)}, bf16[320,1536]{1,0:T(8,128)(2,1)S(1)}, u32[]{:S(2)}, u32[]{:S(2)}) %collective-permute-start.5) | collective-permute-done | bytes 983072 | tf_op jit(solution)/shard_map/ppermute | solution.py:508
  145.4 8.2 %collective-permute-start.9 = (bf16[160,1536]{1,0:T(8,128)(2,1)S(1)}, bf16[160,1536]{1,0:T(8,128)(2,1)}, u32[]{:S(2)}, u32[]{:S(2)}) collective-permute-start(bf16[160,1536]{1,0:T(8,128)(2,1)S(1)} %slice.59), channel_id=1, source_target_pairs={{0,2},{2,4},{4,6},{6,7},{7,5},{5,3},{3,1},{1,0},{8,10},{10,12},{12... | collective-permute-start | bytes 1474568 | tf_op jit(solution)/shard_map/ppermute | solution.py:508
  157.4 9.5 %shard_map.296 = (bf16[2,1024,1536]{2,1,0:T(8,128)(2,1)}, bf16[2,576,1024]{2,1,0:T(8,128)(2,1)}, f32[2,384,1024]{2,1,0:T(8,128)}) custom-call(s32[12]{0:T(128)S(1)} %dynamic-slice_bitcast_fusion.index_ref.place_ref.ids_ref, bf16[320,1536]{1,0:T(8,128)(2,1)S(1)} %copy-done.16, bf16[320,1536]{1,0:T(8,128)(2,1)S(1)} %copy-done.23, ...), custom_call_target="tpu_custom_call" | custom-call | flops 2264924160 | bytes 15532032 | tf_op jit(solution)/shard_map/pallas_call | solution.py:1429
  174.7 2.7 shard_map.298.refs_5_
  180.7 2.6 reduce_sum.125
  186.7 6.5 shard_map.299
  193.9 10.4 %collective-permute-done.11.refs_0_ = bf16[192,3072]{1,0:T(8,128)(2,1)} collective-permute-done((bf16[192,3072]{1,0:T(8,128)(2,1)}, bf16[192,3072]{1,0:T(8,128)(2,1)}, u32[]{:S(2)}, u32[]{:S(2)}) %collective-permute-start.11) | collective-permute-done | bytes 1179680 | tf_op jit(solution)/shard_map/ppermute | solution.py:508
  211.4 10.5 %shard_map.301 = (bf16[8,192,256]{2,1,0:T(8,128)(2,1)S(1)}, f32[2,192,1024]{2,1,0:T(8,128)S(1)}, f32[2,192,1024]{2,1,0:T(8,128)S(1)}, f32[2,3,1,1024]{3,2,1,0:T(1,128)S(1)}) custom-call(f32[3]{0:T(128)S(1)} %dynamic_slice.8.gate_ref, bf16[2,576,1024]{2,1,0:T(8,128)(2,1)} %get-tuple-element.195.q_ref.k_ref.v_ref, ...), custom_call_target="tpu_custom_call" | custom-call | flops 6442450944 | bytes 7864320 | tf_op jit(solution)/shard_map/pallas_call | solution.py:1486
  225.8 5.5 collective-permute-done.13.refs_0_
  233.4 3.7 all-to-all-start.2
  239.3 18.4 %all-to-all-done.2.refs_0_ = bf16[8,192,256]{2,1,0:T(8,128)(2,1)S(1)} async-done(((bf16[8,192,256]{2,1,0:T(8,128)(2,1)}), bf16[8,192,256]{2,1,0:T(8,128)(2,1)S(1)}, u32[]{:S(2)}, u32[]{:S(2)}) %all-to-all-start.2) | async-done | bytes 786464 | tf_op jit(solution)/shard_map/all_to_all | solution.py:560
  258.6 5.4 multiply_reduce_fusion.1
  267.0 5.8 collective-permute-done.15.refs_0_
  274.9 2.7 collective-permute-done.17.refs_3_
  279.2 3.2 collective-permute-start.20
  284.0 11.3 %collective-permute-done.20.refs_12_ = bf16[96,3072]{1,0:T(8,128)(2,1)S(1)} collective-permute-done((bf16[96,3072]{1,0:T(8,128)(2,1)S(1)}, bf16[96,3072]{1,0:T(8,128)(2,1)S(1)}, u32[]{:S(2)}, u32[]{:S(2)}) %collective-permute-start.20) | collective-permute-done | bytes 589856 | tf_op jit(solution)/shard_map/ppermute | solution.py:508
  295.3 3.8 collective-permute-done.21.refs_13_
  299.0 26.1 %shard_map.306 = (bf16[1024,1024]{1,0:T(8,128)(2,1)}, bf16[1024,2048]{1,0:T(8,128)(2,1)}, bf16[512,1536]{1,0:T(8,128)(2,1)}, bf16[512,1536]{1,0:T(8,128)(2,1)}, ...) custom-call(s32[12]{0:T(128)S(1)} %dynamic-slice_bitcast_fusion.index_ref.place_ref.ids_ref, ...), custom_call_target="tpu_custom_call" | custom-call | flops 16106127360 | bytes 37748736 | tf_op jit(solution)/shard_map/pallas_call | solution.py:1095
  327.1 3.4 collective-permute-done.22
  335.4 22.4 %shard_map.308 = (bf16[1536,2048]{1,0:T(8,128)(2,1)}, bf16[1024,1536]{1,0:T(8,128)(2,1)S(1)}, bf16[1024,1536]{1,0:T(8,128)(2,1)}) custom-call(bf16[1024,1536]{1,0:T(8,128)(2,1)} %get-tuple-element.214.x_ref, bf16[1024,1536]{1,0:T(8,128)(2,1)} %get-tuple-element.206.refs_4_.grad_ref, bf16[1024,1024]{1,0:T(8,128)(2,1)S(1)} %copy-done.52, ...), custom_call_target="tpu_custom_call" | custom-call | flops 12884901888 | bytes 37748736 | tf_op jit(solution)/shard_map/pallas_call | solution.py:1221
  362.2 2.8 shard_map.310
  367.5 3.5 fusion.25
  373.5 6.2 collective-permute-done.24.refs_0_
  381.4 3.8 all-to-all-start.3
  391.8 3.8 shard_map.313.refs_3_
  395.7 8.6 %all-to-all-done.3.refs_2_ = bf16[8,192,256]{2,1,0:T(8,128)(2,1)S(1)} async-done(((bf16[8,192,256]{2,1,0:T(8,128)(2,1)}), bf16[8,192,256]{2,1,0:T(8,128)(2,1)S(1)}, u32[]{:S(2)}, u32[]{:S(2)}) %all-to-all-start.3) | async-done | bytes 786464 | tf_op jit(solution)/shard_map/all_to_all | solution.py:560
  416.6 23.9 %shard_map.315 = (bf16[2,3,192,1024]{3,2,1,0:T(8,128)(2,1)}, bf16[2,192,256]{2,1,0:T(8,128)(2,1)S(1)}, f32[2,3,1,1024]{3,2,1,0:T(1,128)S(1)}) custom-call(f32[3]{0:T(128)S(1)} %copy-done.87, bf16[2,576,1024]{2,1,0:T(8,128)(2,1)} %get-tuple-element.195.q_ref.k_ref.v_ref, bf16[2,576,1024]{2,1,0:T(8,128)(2,1)} %get-tuple-element.195.q_ref.k_ref.v_ref, ...), custom_call_target="tpu_custom_call" | custom-call | flops 16106127360 | bytes 12582912 | tf_op jit(solution)/shard_map/pallas_call | solution.py:1611
  449.5 4.6 shard_map.321
  456.1 7.8 %shard_map.318.refs_2_ = bf16[1792,1536]{1,0:T(8,128)(2,1)} custom-call(s32[12]{0:T(128)S(1)} %dynamic-slice_bitcast_fusion.index_ref.place_ref.ids_ref, bf16[2,576,1024]{2,1,0:T(8,128)(2,1)S(1)} %bitcast.108, bf16[576,1536]{1,0:T(8,128)(2,1)S(1)} %copy-done.57), custom_call_target="tpu_custom_call" | custom-call | flops 3170893824 | bytes 9338880 | tf_op jit(solution)/shard_map/pallas_call | solution.py:1263
  463.9 2.9 shard_map.320
  470.1 4.3 all-to-all-start.4
  476.2 7.5 shard_map.322.refs_4_
  484.9 17.3 %collective-permute-done.30.refs_0_ = bf16[256,1536]{1,0:T(8,128)(2,1)} collective-permute-done((bf16[256,1536]{1,0:T(8,128)(2,1)}, bf16[256,1536]{1,0:T(8,128)(2,1)}, u32[]{:S(2)}, u32[]{:S(2)}) %collective-permute-start.30) | collective-permute-done | bytes 786464 | tf_op jit(solution)/shard_map/ppermute | solution.py:508
  502.2 3.8 collective-permute-done.31.refs_1_
  507.3 3.1 shard_map.325
  510.4 3.1 collective-permute-start.37
  518.1 45.5 %collective-permute-done.34.refs_0_ = bf16[256,1536]{1,0:T(8,128)(2,1)S(1)} collective-permute-done((bf16[256,1536]{1,0:T(8,128)(2,1)S(1)}, bf16[256,1536]{1,0:T(8,128)(2,1)S(1)}, u32[]{:S(2)}, u32[]{:S(2)}) %collective-permute-start.34) | collective-permute-done | bytes 786464 | tf_op jit(solution)/shard_map/ppermute | solution.py:508
  570.2 2.6 shard_map.328.refs_8_
  573.7 2.7 shard_map.327
  576.4 10.0 %collective-permute-start.38 = (bf16[256,1536]{1,0:T(8,128)(2,1)}, bf16[256,1536]{1,0:T(8,128)(2,1)}, u32[]{:S(2)}, u32[]{:S(2)}) collective-permute-start(bf16[256,1536]{1,0:T(8,128)(2,1)} %get-tuple-element.273), channel_id=1, source_target_pairs={{0,2},{2,4},{4,6},{6,7},{7,5},{5,3},{3,1},{1,0},{8,10},{10,12},{12... | collective-permute-start | bytes 2359304 | tf_op jit(solution)/shard_map/ppermute | solution.py:508
  586.4 4.6 all-to-all-start.5
  591.0 3.2 bitcast_reduce_fusion.1
  598.6 15.2 %all-to-all-done.5.refs_10_ = bf16[8,48,576]{2,1,0:T(8,128)(2,1)} async-done(((bf16[8,48,576]{2,1,0:T(8,128)(2,1)}), bf16[8,48,576]{2,1,0:T(8,128)(2,1)}, u32[]{:S(2)}, u32[]{:S(2)}) %all-to-all-start.5) | async-done | bytes 442400 | tf_op jit(solution)/shard_map/all_to_all | solution.py:560
  613.8 13.8 %collective-permute-done.41.refs_9_ = bf16[192,3072]{1,0:T(8,128)(2,1)} collective-permute-done((bf16[192,3072]{1,0:T(8,128)(2,1)S(1)}, bf16[192,3072]{1,0:T(8,128)(2,1)}, u32[]{:S(2)}, u32[]{:S(2)}) %collective-permute-start.41) | collective-permute-done | bytes 1179680 | tf_op jit(solution)/shard_map/ppermute | solution.py:538
  630.1 4.0 shard_map.330
  635.0 12.3 %all-to-all-start.7 = ((f32[8,2,1155]{2,1,0:T(2,128)}), f32[8,2,1155]{2,1,0:T(2,128)S(1)}, u32[]{:S(2)}, u32[]{:S(2)}) async-start(f32[8,2,1155]{2,1,0:T(2,128)} %get-tuple-element.296), calls=%async_computation.10 | async-start | bytes 163840 | tf_op jit(solution)/shard_map/all_to_all | solution.py:560
  654.9 12.4 %all_to_all.55 = bf16[8,2,16,512]{3,2,1,0:T(8,128)(2,1)} all-to-all(bf16[8,2,16,512]{3,2,1,0:T(8,128)(2,1)} %bitcast.121), channel_id=1, replica_groups=mesh['dp'=4,'sp'=8] {'sp'}, dimensions={0} | all-to-all | bytes 524288 | tf_op jit(solution)/shard_map/all_to_all | solution.py:560
  667.3 4.3 all-to-all-start.8
  674.6 2.7 fusion.3
  681.6 6.9 shard_map.336
  688.5 8.6 %all-gather.8.cloned.1.call-done.cap_ref = bf16[1024,512]{1,0:T(8,128)(2,1)} async-done(((bf16[256,512]{1,0:T(8,128)(2,1)}), bf16[1024,512]{1,0:T(8,128)(2,1)}) %all-gather.8.cloned.1.call-update) | async-done | bytes 1048592 | tf_op jit(solution)/shard_map/all_gather | solution.py:1733
  698.3 8.0 %shard_map.335 = (f32[512,1536]{1,0:T(8,128)}, f32[512,1536]{1,0:T(8,128)}) custom-call(s32[12]{0:T(128)S(1)} %dynamic-slice_bitcast_fusion.index_ref.place_ref.ids_ref, bf16[1024,512]{1,0:T(8,128)(2,1)S(1)} %copy-done.85, bf16[1536,512]{1,0:T(8,128)(2,1)} %get-tuple-element.295.refs_0_, bf16[1536,512]{1,0:T(8,128)(2,1)} %get-tuple-element.306.refs_1_, ...), custom_call_target="tpu_custom_call" | custom-call | flops 3221225472 | bytes 12582912 | tf_op jit(solution)/shard_map/pallas_call | solution.py:700
  710.6 3.9 all-to-all-start.10
  715.8 3.0 all-to-all-done.10
  719.4 5.7 all-to-all-start.9
  728.3 3.0 fusion.11
  737.1 3.3 shard_map.333
  (445 shorter events, 189.3 us)
Async XLA Ops:
  11.2 46.7 %all-to-all-start = ((bf16[8,96,576]{2,1,0:T(8,128)(2,1)}), bf16[8,96,576]{2,1,0:T(8,128)(2,1)S(1)}, u32[]{:S(2)}, u32[]{:S(2)}) async-start(bf16[8,96,576]{2,1,0:T(8,128)(2,1)} %copy-done.38), calls=%async_computation | async-start | bytes 1966080 | tf_op jit(solution)/shard_map/all_to_all | solution.py:560
  20.8 34.8 %collective-permute-start = (bf16[320,1536]{1,0:T(8,128)(2,1)S(1)}, bf16[320,1536]{1,0:T(8,128)(2,1)S(1)}, u32[]{:S(2)}, u32[]{:S(2)}) collective-permute-start(bf16[320,1536]{1,0:T(8,128)(2,1)S(1)} %shard_map.288.refs_0_.refs_1_), channel_id=1, source_target_pairs={{0,2},{2,4},{4,6},{6,7},{7,5},{5,3},{3,1},{1,0},{8,10},{10,12},{12... | collective-permute-start | bytes 2949128 | tf_op jit(solution)/shard_map/ppermute | solution.py:508
  22.9 35.0 %collective-permute-start.1 = (bf16[320,1536]{1,0:T(8,128)(2,1)S(1)}, bf16[320,1536]{1,0:T(8,128)(2,1)}, u32[]{:S(2)}, u32[]{:S(2)}) collective-permute-start(bf16[320,1536]{1,0:T(8,128)(2,1)S(1)} %shard_map.288.refs_0_.refs_1_), channel_id=1, source_target_pairs={{2,0},{4,2},{6,4},{7,6},{5,7},{3,5},{1,3},{0,1},{10,8},{12,10},{14... | collective-permute-start | bytes 2949128 | tf_op jit(solution)/shard_map/ppermute | solution.py:511
  58.8 27.0 %collective-permute-start.2 = (bf16[320,1536]{1,0:T(8,128)(2,1)}, bf16[320,1536]{1,0:T(8,128)(2,1)S(1)}, u32[]{:S(2)}, u32[]{:S(2)}) collective-permute-start(bf16[320,1536]{1,0:T(8,128)(2,1)} %get-tuple-element.165.refs_1_.refs_2_.refs_3_), channel_id=1, source_target_pairs={{0,2},{2,4},{4,6},{6,7},{7,5},{5,3},{3,1},{1,0},{8,10},{10,12},{12... | collective-permute-start | bytes 2949128 | tf_op jit(solution)/shard_map/ppermute | solution.py:508
  65.6 23.0 %collective-permute-start.3 = (bf16[320,1536]{1,0:T(8,128)(2,1)}, bf16[320,1536]{1,0:T(8,128)(2,1)}, u32[]{:S(2)}, u32[]{:S(2)}) collective-permute-start(bf16[320,1536]{1,0:T(8,128)(2,1)} %get-tuple-element.166.refs_2_.refs_4_.refs_5_), channel_id=1, source_target_pairs={{2,0},{4,2},{6,4},{7,6},{5,7},{3,5},{1,3},{0,1},{10,8},{12,10},{14... | collective-permute-start | bytes 2949128 | tf_op jit(solution)/shard_map/ppermute | solution.py:511
  69.0 11.9 %collective-permute-start.4 = (bf16[8,48,576]{2,1,0:T(8,128)(2,1)}, bf16[8,48,576]{2,1,0:T(8,128)(2,1)}, u32[]{:S(2)}, u32[]{:S(2)}) collective-permute-start(bf16[8,48,576]{2,1,0:T(8,128)(2,1)} %get-tuple-element.168.refs_2_), channel_id=1, source_target_pairs={{0,16},{8,24},{16,0},{24,8},{1,17},{9,25},{17,1},{25,9},{2,18},{10... | collective-permute-start | bytes 1327112 | tf_op jit(solution)/shard_map/ppermute | solution.py:538
  88.7 78.3 %all-to-all-start.1 = ((bf16[8,192,512]{2,1,0:T(8,128)(2,1)}), bf16[8,192,512]{2,1,0:T(8,128)(2,1)}, u32[]{:S(2)}, u32[]{:S(2)}) async-start(bf16[8,192,512]{2,1,0:T(8,128)(2,1)} %get-tuple-element.183), calls=%async_computation.1 | async-start | bytes 3145728 | tf_op jit(solution)/shard_map/all_to_all | solution.py:560
  93.0 164.7 %all-gather.4.cloned.1.call-start = ((), (), s32[]{:S(2)}) async-start(), calls=%async_computation.14 | async-start | bytes 5898240 | tf_op jit(solution)/shard_map/all_gather | solution.py:1766
  93.0 45.6 %collective-permute-start.5 = (bf16[320,1536]{1,0:T(8,128)(2,1)}, bf16[320,1536]{1,0:T(8,128)(2,1)S(1)}, u32[]{:S(2)}, u32[]{:S(2)}) collective-permute-start(bf16[320,1536]{1,0:T(8,128)(2,1)} %get-tuple-element.172.refs_3_.refs_6_.refs_7_), channel_id=1, source_target_pairs={{0,2},{2,4},{4,6},{6,7},{7,5},{5,3},{3,1},{1,0},{8,10},{10,12},{12... | collective-permute-start | bytes 2949128 | tf_op jit(solution)/shard_map/ppermute | solution.py:508
  94.9 46.0 %collective-permute-start.6 = (bf16[320,1536]{1,0:T(8,128)(2,1)}, bf16[320,1536]{1,0:T(8,128)(2,1)}, u32[]{:S(2)}, u32[]{:S(2)}) collective-permute-start(bf16[320,1536]{1,0:T(8,128)(2,1)} %get-tuple-element.173.refs_4_.refs_8_.refs_9_), channel_id=1, source_target_pairs={{2,0},{4,2},{6,4},{7,6},{5,7},{3,5},{1,3},{0,1},{10,8},{12,10},{14... | collective-permute-start | bytes 2949128 | tf_op jit(solution)/shard_map/ppermute | solution.py:511
  142.2 24.7 %collective-permute-start.10 = (bf16[160,1536]{1,0:T(8,128)(2,1)S(1)}, bf16[160,1536]{1,0:T(8,128)(2,1)}, u32[]{:S(2)}, u32[]{:S(2)}) collective-permute-start(bf16[160,1536]{1,0:T(8,128)(2,1)S(1)} %slice.60), channel_id=1, source_target_pairs={{2,0},{4,2},{6,4},{7,6},{5,7},{3,5},{1,3},{0,1},{10,8},{12,10},{14... | collective-permute-start | bytes 1474568 | tf_op jit(solution)/shard_map/ppermute | solution.py:511
  145.4 21.5 %collective-permute-start.9 = (bf16[160,1536]{1,0:T(8,128)(2,1)S(1)}, bf16[160,1536]{1,0:T(8,128)(2,1)}, u32[]{:S(2)}, u32[]{:S(2)}) collective-permute-start(bf16[160,1536]{1,0:T(8,128)(2,1)S(1)} %slice.59), channel_id=1, source_target_pairs={{0,2},{2,4},{4,6},{6,7},{7,5},{5,3},{3,1},{1,0},{8,10},{10,12},{12... | collective-permute-start | bytes 1474568 | tf_op jit(solution)/shard_map/ppermute | solution.py:508
  171.8 95.2 %all-gather.6.cloned.1.call-start = ((), (), s32[]{:S(2)}) async-start(), calls=%async_computation.15 | async-start | bytes 3932160 | tf_op jit(solution)/shard_map/all_gather | solution.py:1745
  177.4 27.0 %collective-permute-start.11 = (bf16[192,3072]{1,0:T(8,128)(2,1)}, bf16[192,3072]{1,0:T(8,128)(2,1)}, u32[]{:S(2)}, u32[]{:S(2)}) collective-permute-start(bf16[192,3072]{1,0:T(8,128)(2,1)} %shard_map.298.refs_5_), channel_id=1, source_target_pairs={{0,2},{2,4},{4,6},{6,7},{7,5},{5,3},{3,1},{1,0},{8,10},{10,12},{12... | collective-permute-start | bytes 3538952 | tf_op jit(solution)/shard_map/ppermute | solution.py:508
  179.4 26.2 %collective-permute-start.12 = (bf16[192,3072]{1,0:T(8,128)(2,1)}, bf16[192,3072]{1,0:T(8,128)(2,1)}, u32[]{:S(2)}, u32[]{:S(2)}) collective-permute-start(bf16[192,3072]{1,0:T(8,128)(2,1)} %shard_map.298.refs_5_), channel_id=1, source_target_pairs={{2,0},{4,2},{6,4},{7,6},{5,7},{3,5},{1,3},{0,1},{10,8},{12,10},{14... | collective-permute-start | bytes 3538952 | tf_op jit(solution)/shard_map/ppermute | solution.py:511
  205.7 25.5 %collective-permute-start.13 = (bf16[192,3072]{1,0:T(8,128)(2,1)}, bf16[192,3072]{1,0:T(8,128)(2,1)S(1)}, u32[]{:S(2)}, u32[]{:S(2)}) collective-permute-start(bf16[192,3072]{1,0:T(8,128)(2,1)} %get-tuple-element.193.refs_6_), channel_id=1, source_target_pairs={{0,2},{2,4},{4,6},{6,7},{7,5},{5,3},{3,1},{1,0},{8,10},{10,12},{12... | collective-permute-start | bytes 3538952 | tf_op jit(solution)/shard_map/ppermute | solution.py:508
  207.4 26.0 %collective-permute-start.14 = (bf16[192,3072]{1,0:T(8,128)(2,1)}, bf16[192,3072]{1,0:T(8,128)(2,1)}, u32[]{:S(2)}, u32[]{:S(2)}) collective-permute-start(bf16[192,3072]{1,0:T(8,128)(2,1)} %get-tuple-element.194.refs_7_), channel_id=1, source_target_pairs={{2,0},{4,2},{6,4},{7,6},{5,7},{3,5},{1,3},{0,1},{10,8},{12,10},{14... | collective-permute-start | bytes 3538952 | tf_op jit(solution)/shard_map/ppermute | solution.py:511
  233.4 24.3 %all-to-all-start.2 = ((bf16[8,192,256]{2,1,0:T(8,128)(2,1)}), bf16[8,192,256]{2,1,0:T(8,128)(2,1)S(1)}, u32[]{:S(2)}, u32[]{:S(2)}) async-start(bf16[8,192,256]{2,1,0:T(8,128)(2,1)} %get-tuple-element.199), calls=%async_computation.2 | async-start | bytes 1572864 | tf_op jit(solution)/shard_map/all_to_all | solution.py:560
  237.2 329.6 %reduce-scatter.4.cloned.1.call-start = ((), (), s32[]{:S(2)}) async-start(), calls=%async_computation.16 | async-start | bytes 3932160 | tf_op jit(solution)/shard_map/reduce_scatter | solution.py:1832
  237.2 35.6 %collective-permute-start.15 = (bf16[192,3072]{1,0:T(8,128)(2,1)}, bf16[192,3072]{1,0:T(8,128)(2,1)}, u32[]{:S(2)}, u32[]{:S(2)}) collective-permute-start(bf16[192,3072]{1,0:T(8,128)(2,1)} %get-tuple-element.202.refs_8_), channel_id=1, source_target_pairs={{0,2},{2,4},{4,6},{6,7},{7,5},{5,3},{3,1},{1,0},{8,10},{10,12},{12... | collective-permute-start | bytes 3538952 | tf_op jit(solution)/shard_map/ppermute | solution.py:508
  239.2 35.7 %collective-permute-start.16 = (bf16[192,3072]{1,0:T(8,128)(2,1)}, bf16[192,3072]{1,0:T(8,128)(2,1)}, u32[]{:S(2)}, u32[]{:S(2)}) collective-permute-start(bf16[192,3072]{1,0:T(8,128)(2,1)} %get-tuple-element.203.refs_9_), channel_id=1, source_target_pairs={{2,0},{4,2},{6,4},{7,6},{5,7},{3,5},{1,3},{0,1},{10,8},{12,10},{14... | collective-permute-start | bytes 3538952 | tf_op jit(solution)/shard_map/ppermute | solution.py:511
  265.5 12.2 %collective-permute-start.17 = (bf16[256,1536]{1,0:T(8,128)(2,1)S(1)}, bf16[256,1536]{1,0:T(8,128)(2,1)}, u32[]{:S(2)}, u32[]{:S(2)}) collective-permute-start(bf16[256,1536]{1,0:T(8,128)(2,1)S(1)} %fusion.5.refs_2_), channel_id=1, source_target_pairs={{0,16},{8,24},{16,0},{24,8},{1,17},{9,25},{17,1},{25,9},{2,18},{10... | collective-permute-start | bytes 2359304 | tf_op jit(solution)/shard_map/ppermute | solution.py:538
  277.6 21.4 %collective-permute-start.18 = (bf16[256,1536]{1,0:T(8,128)(2,1)}, bf16[256,1536]{1,0:T(8,128)(2,1)S(1)}, u32[]{:S(2)}, u32[]{:S(2)}) collective-permute-start(bf16[256,1536]{1,0:T(8,128)(2,1)} %get-tuple-element.204.refs_0_), channel_id=1, source_target_pairs={{0,8},{8,0},{16,24},{24,16},{1,9},{9,1},{17,25},{25,17},{2,10},{10... | collective-permute-start | bytes 2359304 | tf_op jit(solution)/shard_map/ppermute | solution.py:538
  277.6 21.4 %collective-permute-start.19 = (bf16[256,1536]{1,0:T(8,128)(2,1)}, bf16[256,1536]{1,0:T(8,128)(2,1)S(1)}, u32[]{:S(2)}, u32[]{:S(2)}) collective-permute-start(bf16[256,1536]{1,0:T(8,128)(2,1)} %get-tuple-element.205.refs_1_), channel_id=1, source_target_pairs={{0,8},{8,0},{16,24},{24,16},{1,9},{9,1},{17,25},{25,17},{2,10},{10... | collective-permute-start | bytes 2359304 | tf_op jit(solution)/shard_map/ppermute | solution.py:538
  279.2 16.0 %collective-permute-start.20 = (bf16[96,3072]{1,0:T(8,128)(2,1)S(1)}, bf16[96,3072]{1,0:T(8,128)(2,1)S(1)}, u32[]{:S(2)}, u32[]{:S(2)}) collective-permute-start(bf16[96,3072]{1,0:T(8,128)(2,1)S(1)} %slice.63), channel_id=1, source_target_pairs={{0,2},{2,4},{4,6},{6,7},{7,5},{5,3},{3,1},{1,0},{8,10},{10,12},{12... | collective-permute-start | bytes 1769480 | tf_op jit(solution)/shard_map/ppermute | solution.py:508
  283.5 15.5 %collective-permute-start.21 = (bf16[96,3072]{1,0:T(8,128)(2,1)S(1)}, bf16[96,3072]{1,0:T(8,128)(2,1)S(1)}, u32[]{:S(2)}, u32[]{:S(2)}) collective-permute-start(bf16[96,3072]{1,0:T(8,128)(2,1)S(1)} %slice.64), channel_id=1, source_target_pairs={{2,0},{4,2},{6,4},{7,6},{5,7},{3,5},{1,3},{0,1},{10,8},{12,10},{14... | collective-permute-start | bytes 1769480 | tf_op jit(solution)/shard_map/ppermute | solution.py:511
  332.3 27.2 %collective-permute-start.23 = (bf16[256,1536]{1,0:T(8,128)(2,1)}, bf16[256,1536]{1,0:T(8,128)(2,1)S(1)}, u32[]{:S(2)}, u32[]{:S(2)}) collective-permute-start(bf16[256,1536]{1,0:T(8,128)(2,1)} %get-tuple-element.213), channel_id=1, source_target_pairs={{0,16},{8,24},{16,0},{24,8},{1,17},{9,25},{17,1},{25,9},{2,18},{10... | collective-permute-start | bytes 2359304 | tf_op jit(solution)/shard_map/ppermute | solution.py:538
  365.0 14.8 %collective-permute-start.24 = (bf16[96,3072]{1,0:T(8,128)(2,1)S(1)}, bf16[96,3072]{1,0:T(8,128)(2,1)S(1)}, u32[]{:S(2)}, u32[]{:S(2)}) collective-permute-start(bf16[96,3072]{1,0:T(8,128)(2,1)S(1)} %get-tuple-element.223), channel_id=1, source_target_pairs={{0,2},{2,4},{4,6},{6,7},{7,5},{5,3},{3,1},{1,0},{8,10},{10,12},{12... | collective-permute-start | bytes 1769480 | tf_op jit(solution)/shard_map/ppermute | solution.py:508
  365.1 15.5 %collective-permute-start.25 = (bf16[96,3072]{1,0:T(8,128)(2,1)S(1)}, bf16[96,3072]{1,0:T(8,128)(2,1)S(1)}, u32[]{:S(2)}, u32[]{:S(2)}) collective-permute-start(bf16[96,3072]{1,0:T(8,128)(2,1)S(1)} %get-tuple-element.224), channel_id=1, source_target_pairs={{2,0},{4,2},{6,4},{7,6},{5,7},{3,5},{1,3},{0,1},{10,8},{12,10},{14... | collective-permute-start | bytes 1769480 | tf_op jit(solution)/shard_map/ppermute | solution.py:511
  381.4 22.8 %all-to-all-start.3 = ((bf16[8,192,256]{2,1,0:T(8,128)(2,1)}), bf16[8,192,256]{2,1,0:T(8,128)(2,1)S(1)}, u32[]{:S(2)}, u32[]{:S(2)}) async-start(bf16[8,192,256]{2,1,0:T(8,128)(2,1)} %get-tuple-element.231), calls=%async_computation.3 | async-start | bytes 1572864 | tf_op jit(solution)/shard_map/all_to_all | solution.py:560
  385.2 181.6 %reduce-scatter.6.cloned.1.call-start = ((), (), s32[]{:S(2)}) async-start(), calls=%async_computation.17 | async-start | bytes 5898240 | tf_op jit(solution)/shard_map/reduce_scatter | solution.py:1847
  405.1 36.6 %collective-permute-start.26 = (bf16[192,3072]{1,0:T(8,128)(2,1)}, bf16[192,3072]{1,0:T(8,128)(2,1)S(1)}, u32[]{:S(2)}, u32[]{:S(2)}) collective-permute-start(bf16[192,3072]{1,0:T(8,128)(2,1)} %get-tuple-element.234), channel_id=1, source_target_pairs={{0,2},{2,4},{4,6},{6,7},{7,5},{5,3},{3,1},{1,0},{8,10},{10,12},{12... | collective-permute-start | bytes 3538952 | tf_op jit(solution)/shard_map/ppermute | solution.py:508
  405.5 36.3 %collective-permute-start.27 = (bf16[192,3072]{1,0:T(8,128)(2,1)}, bf16[192,3072]{1,0:T(8,128)(2,1)}, u32[]{:S(2)}, u32[]{:S(2)}) collective-permute-start(bf16[192,3072]{1,0:T(8,128)(2,1)} %get-tuple-element.235), channel_id=1, source_target_pairs={{2,0},{4,2},{6,4},{7,6},{5,7},{3,5},{1,3},{0,1},{10,8},{12,10},{14... | collective-permute-start | bytes 3538952 | tf_op jit(solution)/shard_map/ppermute | solution.py:511
  447.4 16.5 %collective-permute-start.28 = (bf16[128,1536]{1,0:T(8,128)(2,1)S(1)}, bf16[128,1536]{1,0:T(8,128)(2,1)}, u32[]{:S(2)}, u32[]{:S(2)}) collective-permute-start(bf16[128,1536]{1,0:T(8,128)(2,1)S(1)} %get-tuple-element.245), channel_id=1, source_target_pairs={{0,2},{2,4},{4,6},{6,7},{7,5},{5,3},{3,1},{1,0},{8,10},{10,12},{12... | collective-permute-start | bytes 1179656 | tf_op jit(solution)/shard_map/ppermute | solution.py:508
  447.9 16.0 %collective-permute-start.29 = (bf16[128,1536]{1,0:T(8,128)(2,1)S(1)}, bf16[128,1536]{1,0:T(8,128)(2,1)}, u32[]{:S(2)}, u32[]{:S(2)}) collective-permute-start(bf16[128,1536]{1,0:T(8,128)(2,1)S(1)} %get-tuple-element.246), channel_id=1, source_target_pairs={{2,0},{4,2},{6,4},{7,6},{5,7},{3,5},{1,3},{0,1},{10,8},{12,10},{14... | collective-permute-start | bytes 1179656 | tf_op jit(solution)/shard_map/ppermute | solution.py:511
  454.1 30.8 %collective-permute-start.32 = (bf16[192,3072]{1,0:T(8,128)(2,1)}, bf16[192,3072]{1,0:T(8,128)(2,1)S(1)}, u32[]{:S(2)}, u32[]{:S(2)}) collective-permute-start(bf16[192,3072]{1,0:T(8,128)(2,1)} %get-tuple-element.255), channel_id=1, source_target_pairs={{0,2},{2,4},{4,6},{6,7},{7,5},{5,3},{3,1},{1,0},{8,10},{10,12},{12... | collective-permute-start | bytes 3538952 | tf_op jit(solution)/shard_map/ppermute | solution.py:508
  454.4 30.5 %collective-permute-start.33 = (bf16[192,3072]{1,0:T(8,128)(2,1)}, bf16[192,3072]{1,0:T(8,128)(2,1)}, u32[]{:S(2)}, u32[]{:S(2)}) collective-permute-start(bf16[192,3072]{1,0:T(8,128)(2,1)} %get-tuple-element.256), channel_id=1, source_target_pairs={{2,0},{4,2},{6,4},{7,6},{5,7},{3,5},{1,3},{0,1},{10,8},{12,10},{14... | collective-permute-start | bytes 3538952 | tf_op jit(solution)/shard_map/ppermute | solution.py:511
  466.8 35.4 %collective-permute-start.30 = (bf16[256,1536]{1,0:T(8,128)(2,1)}, bf16[256,1536]{1,0:T(8,128)(2,1)}, u32[]{:S(2)}, u32[]{:S(2)}) collective-permute-start(bf16[256,1536]{1,0:T(8,128)(2,1)} %get-tuple-element.251), channel_id=1, source_target_pairs={{0,2},{2,4},{4,6},{6,7},{7,5},{5,3},{3,1},{1,0},{8,10},{10,12},{12... | collective-permute-start | bytes 2359304 | tf_op jit(solution)/shard_map/ppermute | solution.py:508
  467.2 38.8 %collective-permute-start.31 = (bf16[256,1536]{1,0:T(8,128)(2,1)}, bf16[256,1536]{1,0:T(8,128)(2,1)}, u32[]{:S(2)}, u32[]{:S(2)}) collective-permute-start(bf16[256,1536]{1,0:T(8,128)(2,1)} %get-tuple-element.252), channel_id=1, source_target_pairs={{2,0},{4,2},{6,4},{7,6},{5,7},{3,5},{1,3},{0,1},{10,8},{12,10},{14... | collective-permute-start | bytes 2359304 | tf_op jit(solution)/shard_map/ppermute | solution.py:511
  470.1 96.6 %all-to-all-start.4 = ((bf16[8,192,512]{2,1,0:T(8,128)(2,1)}), bf16[8,192,512]{2,1,0:T(8,128)(2,1)}, u32[]{:S(2)}, u32[]{:S(2)}) async-start(bf16[8,192,512]{2,1,0:T(8,128)(2,1)} %broadcast_in_dim.27), calls=%async_computation.4 | async-start | bytes 3145728 | tf_op jit(solution)/shard_map/all_to_all | solution.py:554
  474.4 112.0 %reduce-scatter.8.cloned.1.call-start = ((), (), s32[]{:S(2)}) async-start(), calls=%async_computation.18 | async-start | bytes 2457600 | tf_op jit(solution)/shard_map/reduce_scatter | solution.py:1871
  510.3 55.5 %collective-permute-start.36 = (bf16[192,3072]{1,0:T(8,128)(2,1)S(1)}, bf16[192,3072]{1,0:T(8,128)(2,1)S(1)}, u32[]{:S(2)}, u32[]{:S(2)}) collective-permute-start(bf16[192,3072]{1,0:T(8,128)(2,1)S(1)} %get-tuple-element.265), channel_id=1, source_target_pairs={{0,2},{2,4},{4,6},{6,7},{7,5},{5,3},{3,1},{1,0},{8,10},{10,12},{12... | collective-permute-start | bytes 3538952 | tf_op jit(solution)/shard_map/ppermute | solution.py:508
  510.4 56.3 %collective-permute-start.37 = (bf16[192,3072]{1,0:T(8,128)(2,1)S(1)}, bf16[192,3072]{1,0:T(8,128)(2,1)}, u32[]{:S(2)}, u32[]{:S(2)}) collective-permute-start(bf16[192,3072]{1,0:T(8,128)(2,1)S(1)} %get-tuple-element.266), channel_id=1, source_target_pairs={{2,0},{4,2},{6,4},{7,6},{5,7},{3,5},{1,3},{0,1},{10,8},{12,10},{14... | collective-permute-start | bytes 3538952 | tf_op jit(solution)/shard_map/ppermute | solution.py:511
  515.9 47.7 %collective-permute-start.34 = (bf16[256,1536]{1,0:T(8,128)(2,1)S(1)}, bf16[256,1536]{1,0:T(8,128)(2,1)S(1)}, u32[]{:S(2)}, u32[]{:S(2)}) collective-permute-start(bf16[256,1536]{1,0:T(8,128)(2,1)S(1)} %get-tuple-element.261), channel_id=1, source_target_pairs={{0,2},{2,4},{4,6},{6,7},{7,5},{5,3},{3,1},{1,0},{8,10},{10,12},{12... | collective-permute-start | bytes 2359304 | tf_op jit(solution)/shard_map/ppermute | solution.py:508
  516.0 49.9 %collective-permute-start.35 = (bf16[256,1536]{1,0:T(8,128)(2,1)S(1)}, bf16[256,1536]{1,0:T(8,128)(2,1)S(1)}, u32[]{:S(2)}, u32[]{:S(2)}) collective-permute-start(bf16[256,1536]{1,0:T(8,128)(2,1)S(1)} %get-tuple-element.262), channel_id=1, source_target_pairs={{2,0},{4,2},{6,4},{7,6},{5,7},{3,5},{1,3},{0,1},{10,8},{12,10},{14... | collective-permute-start | bytes 2359304 | tf_op jit(solution)/shard_map/ppermute | solution.py:511
  567.7 59.8 %collective-permute-start.40 = (bf16[1536,512]{1,0:T(8,128)(2,1)}, bf16[1536,512]{1,0:T(8,128)(2,1)}, u32[]{:S(2)}, u32[]{:S(2)}) collective-permute-start(bf16[1536,512]{1,0:T(8,128)(2,1)} %get-tuple-element.275.refs_6_), channel_id=1, source_target_pairs={{0,16},{8,24},{16,0},{24,8},{1,17},{9,25},{17,1},{25,9},{2,18},{10... | collective-permute-start | bytes 4718600 | tf_op jit(solution)/shard_map/ppermute | solution.py:538
  572.8 54.7 %collective-permute-start.41 = (bf16[192,3072]{1,0:T(8,128)(2,1)S(1)}, bf16[192,3072]{1,0:T(8,128)(2,1)}, u32[]{:S(2)}, u32[]{:S(2)}) collective-permute-start(bf16[192,3072]{1,0:T(8,128)(2,1)S(1)} %shard_map.328.refs_8_), channel_id=1, source_target_pairs={{0,16},{8,24},{16,0},{24,8},{1,17},{9,25},{17,1},{25,9},{2,18},{10... | collective-permute-start | bytes 3538952 | tf_op jit(solution)/shard_map/ppermute | solution.py:538
  576.4 37.3 %collective-permute-start.38 = (bf16[256,1536]{1,0:T(8,128)(2,1)}, bf16[256,1536]{1,0:T(8,128)(2,1)}, u32[]{:S(2)}, u32[]{:S(2)}) collective-permute-start(bf16[256,1536]{1,0:T(8,128)(2,1)} %get-tuple-element.273), channel_id=1, source_target_pairs={{0,2},{2,4},{4,6},{6,7},{7,5},{5,3},{3,1},{1,0},{8,10},{10,12},{12... | collective-permute-start | bytes 2359304 | tf_op jit(solution)/shard_map/ppermute | solution.py:508
  586.4 27.4 %collective-permute-start.39 = (bf16[256,1536]{1,0:T(8,128)(2,1)}, bf16[256,1536]{1,0:T(8,128)(2,1)}, u32[]{:S(2)}, u32[]{:S(2)}) collective-permute-start(bf16[256,1536]{1,0:T(8,128)(2,1)} %get-tuple-element.274), channel_id=1, source_target_pairs={{2,0},{4,2},{6,4},{7,6},{5,7},{3,5},{1,3},{0,1},{10,8},{12,10},{14... | collective-permute-start | bytes 2359304 | tf_op jit(solution)/shard_map/ppermute | solution.py:511
  586.4 27.4 %all-to-all-start.5 = ((bf16[8,48,576]{2,1,0:T(8,128)(2,1)}), bf16[8,48,576]{2,1,0:T(8,128)(2,1)}, u32[]{:S(2)}, u32[]{:S(2)}) async-start(bf16[8,48,576]{2,1,0:T(8,128)(2,1)} %bitcast.124), calls=%async_computation.8 | async-start | bytes 983040 | tf_op jit(solution)/shard_map/all_to_all | solution.py:560
  635.0 19.3 %all-to-all-start.7 = ((f32[8,2,1155]{2,1,0:T(2,128)}), f32[8,2,1155]{2,1,0:T(2,128)S(1)}, u32[]{:S(2)}, u32[]{:S(2)}) async-start(f32[8,2,1155]{2,1,0:T(2,128)} %get-tuple-element.296), calls=%async_computation.10 | async-start | bytes 163840 | tf_op jit(solution)/shard_map/all_to_all | solution.py:560
  667.3 39.0 %all-to-all-start.8 = ((bf16[8,192,384]{2,1,0:T(8,128)(2,1)}), bf16[8,192,384]{2,1,0:T(8,128)(2,1)}, u32[]{:S(2)}, u32[]{:S(2)}) async-start(bf16[8,192,384]{2,1,0:T(8,128)(2,1)} %bitcast.117), calls=%async_computation.11 | async-start | bytes 2359296 | tf_op jit(solution)/shard_map/all_to_all | solution.py:560
  671.6 25.5 %all-gather.8.cloned.1.call-start = ((), (), s32[]{:S(2)}) async-start(), calls=%async_computation.19 | async-start | bytes 1310720 | tf_op jit(solution)/shard_map/all_gather | solution.py:1733
  672.1 24.9 %collective-permute-start.48 = (bf16[1536,512]{1,0:T(8,128)(2,1)}, bf16[1536,512]{1,0:T(8,128)(2,1)}, u32[]{:S(2)}, u32[]{:S(2)}) collective-permute-start(bf16[1536,512]{1,0:T(8,128)(2,1)} %get-tuple-element.295.refs_0_), channel_id=1, source_target_pairs={{0,8},{8,0},{16,24},{24,16},{1,9},{9,1},{17,25},{25,17},{2,10},{10... | collective-permute-start | bytes 4718600 | tf_op jit(solution)/shard_map/ppermute | solution.py:538
  672.2 24.8 %collective-permute-start.49 = (bf16[1536,512]{1,0:T(8,128)(2,1)}, bf16[1536,512]{1,0:T(8,128)(2,1)}, u32[]{:S(2)}, u32[]{:S(2)}) collective-permute-start(bf16[1536,512]{1,0:T(8,128)(2,1)} %get-tuple-element.306.refs_1_), channel_id=1, source_target_pairs={{0,8},{8,0},{16,24},{24,16},{1,9},{9,1},{17,25},{25,17},{2,10},{10... | collective-permute-start | bytes 4718600 | tf_op jit(solution)/shard_map/ppermute | solution.py:538
  672.7 8.8 %collective-permute-start.50 = (bf16[192,3072]{1,0:T(8,128)(2,1)S(1)}, bf16[192,3072]{1,0:T(8,128)(2,1)}, u32[]{:S(2)}, u32[]{:S(2)}) collective-permute-start(bf16[192,3072]{1,0:T(8,128)(2,1)S(1)} %copy-done.11), channel_id=1, source_target_pairs={{0,8},{8,0},{16,24},{24,16},{1,9},{9,1},{17,25},{25,17},{2,10},{10... | collective-permute-start | bytes 3538952 | tf_op jit(solution)/shard_map/ppermute | solution.py:538
  672.8 8.8 %collective-permute-start.51 = (bf16[192,3072]{1,0:T(8,128)(2,1)}, bf16[192,3072]{1,0:T(8,128)(2,1)}, u32[]{:S(2)}, u32[]{:S(2)}) collective-permute-start(bf16[192,3072]{1,0:T(8,128)(2,1)} %get-tuple-element.310.refs_1_), channel_id=1, source_target_pairs={{0,8},{8,0},{16,24},{24,16},{1,9},{9,1},{17,25},{25,17},{2,10},{10... | collective-permute-start | bytes 3538952 | tf_op jit(solution)/shard_map/ppermute | solution.py:538
  677.3 29.0 %collective-permute-start.42 = (bf16[8,48,576]{2,1,0:T(8,128)(2,1)}, bf16[8,48,576]{2,1,0:T(8,128)(2,1)}, u32[]{:S(2)}, u32[]{:S(2)}) collective-permute-start(bf16[8,48,576]{2,1,0:T(8,128)(2,1)} %get-tuple-element.298.refs_2_), channel_id=1, source_target_pairs={{0,16},{8,24},{16,0},{24,8},{1,17},{9,25},{17,1},{25,9},{2,18},{10... | collective-permute-start | bytes 1327112 | tf_op jit(solution)/shard_map/ppermute | solution.py:538
  707.7 25.6 %collective-permute-start.45 = (bf16[192,384]{1,0:T(8,128)(2,1)S(1)}, bf16[192,384]{1,0:T(8,128)(2,1)}, u32[]{:S(2)}, u32[]{:S(2)}) collective-permute-start(bf16[192,384]{1,0:T(8,128)(2,1)S(1)} %reduce_sum.137.refs_0_), channel_id=1, source_target_pairs={{0,16},{8,24},{16,0},{24,8},{1,17},{9,25},{17,1},{25,9},{2,18},{10... | collective-permute-start | bytes 442376 | tf_op jit(solution)/shard_map/ppermute | solution.py:538
  708.2 25.8 %collective-permute-start.46 = (bf16[192,384]{1,0:T(8,128)(2,1)S(1)}, bf16[192,384]{1,0:T(8,128)(2,1)}, u32[]{:S(2)}, u32[]{:S(2)}) collective-permute-start(bf16[192,384]{1,0:T(8,128)(2,1)S(1)} %reduce_sum.137.refs_0_), channel_id=1, source_target_pairs={{0,8},{8,0},{16,24},{24,16},{1,9},{9,1},{17,25},{25,17},{2,10},{10... | collective-permute-start | bytes 442376 | tf_op jit(solution)/shard_map/ppermute | solution.py:538
  710.6 8.1 %all-to-all-start.10 = ((f32[4,2,2200]{2,1,0:T(2,128)}), f32[4,2,2200]{2,1,0:T(2,128)}, u32[]{:S(2)}, u32[]{:S(2)}) async-start(f32[4,2,2200]{2,1,0:T(2,128)} %broadcast_in_dim.63), calls=%async_computation.13 | async-start | bytes 147456 | tf_op jit(solution)/shard_map/all_to_all | solution.py:554
  715.2 21.9 %collective-permute-start.43 = (bf16[8,48,576]{2,1,0:T(8,128)(2,1)}, bf16[8,48,576]{2,1,0:T(8,128)(2,1)S(1)}, u32[]{:S(2)}, u32[]{:S(2)}) collective-permute-start(bf16[8,48,576]{2,1,0:T(8,128)(2,1)} %get-tuple-element.300.refs_0_), channel_id=1, source_target_pairs={{0,8},{8,0},{16,24},{24,16},{1,9},{9,1},{17,25},{25,17},{2,10},{10... | collective-permute-start | bytes 1327112 | tf_op jit(solution)/shard_map/ppermute | solution.py:538
  715.7 21.3 %collective-permute-start.44 = (bf16[8,48,576]{2,1,0:T(8,128)(2,1)}, bf16[8,48,576]{2,1,0:T(8,128)(2,1)S(1)}, u32[]{:S(2)}, u32[]{:S(2)}) collective-permute-start(bf16[8,48,576]{2,1,0:T(8,128)(2,1)} %get-tuple-element.301.refs_1_), channel_id=1, source_target_pairs={{0,8},{8,0},{16,24},{24,16},{1,9},{9,1},{17,25},{25,17},{2,10},{10... | collective-permute-start | bytes 1327112 | tf_op jit(solution)/shard_map/ppermute | solution.py:538
  719.4 13.1 %all-to-all-start.9 = ((f32[8,2,1024]{2,1,0:T(2,128)}), f32[8,2,1024]{2,1,0:T(2,128)}, u32[]{:S(2)}, u32[]{:S(2)}) async-start(f32[8,2,1024]{2,1,0:T(2,128)} %broadcast_in_dim.62), calls=%async_computation.12 | async-start | bytes 131072 | tf_op jit(solution)/shard_map/all_to_all | solution.py:554
  (128 other events, 545.7 us)
Sparse Core Ops, SparseCore 0:
  171.9 37.2 all-gather.3
  211.4 28.5 all-gather.5
  360.5 35.9 reduce-scatter.3
  405.3 46.1 reduce-scatter.5
  506.1 32.0 reduce-scatter.7
  673.7 23.2 all-gather.7

commit v3 on v2

--- a/solution.py
+++ b/solution.py
@@ -918,7 +918,7 @@
     return tile * 2 * UNITS + which * UNITS + rest * 128
 
 
-def pack_first(w_query, w_key, w_value, captions, modulation):
+def pack_first(w_query, w_key, w_value, captions, modulation, after):
     k_rows, width = w_query.shape
     size = width // k_rows
     part = k_rows // N_DP
@@ -930,7 +930,7 @@
     member = jnp.reshape(lax.axis_index("dp"), (1,)).astype(jnp.int32)
     rows = part + tokens + 16
 
-    def kernel(member_ref, q_ref, k_ref, v_ref, cap_ref, mod_ref, out_ref):
+    def kernel(member_ref, q_ref, k_ref, v_ref, cap_ref, mod_ref, after_ref, out_ref):
         spot = pl.ds(aligned(member_ref[0] * part, part), part)
         mod = jnp.concatenate(
             [mod_ref[:, i * columns : (i + 1) * columns] for i in range(pieces)], axis=0
@@ -951,14 +951,14 @@
     vmem = pl.BlockSpec(memory_space=pltpu.VMEM)
     return pl.pallas_call(
         kernel,
-        in_specs=[pl.BlockSpec(memory_space=pltpu.SMEM)] + [vmem] * 5,
+        in_specs=[pl.BlockSpec(memory_space=pltpu.SMEM)] + [vmem] * 5 + [pl.BlockSpec(memory_space=pl.ANY)],
         out_specs=vmem,
         out_shape=jax.ShapeDtypeStruct((size, rows, columns), BF16),
         compiler_params=pltpu.CompilerParams(vmem_limit_bytes=VMEM_BYTES),
         cost_estimate=pl.CostEstimate(
             flops=0, bytes_accessed=8 * size * rows * columns, transcendentals=0
         ),
-    )(member, w_query, w_key, w_value, captions, modulation)
+    )(member, w_query, w_key, w_value, captions, modulation, after)
 
 
 def unpack_first(packed, part, tokens, features, clips, own_mod):
@@ -1133,117 +1133,77 @@
     )(ring.table, *xs, grads, *[piece for _, _, piece in pieces])
 
 
-def add_units(table, spots, d_weight, d_down, received, shape):
-    units, width = d_down.shape
-    columns = d_weight.shape[1]
-    rows = width // lax.axis_size("sp")
-    half = rows // 2
-    sides = 1 if shape == "home" else 2
-    heights = [rows] * 2 if shape == "whole" else [half] * 2
-
-    def kernel(ids_ref, *refs):
-        own, arrived = refs[: 2 * sides], refs[2 * sides : 2 * sides + len(received)]
-        out, whole = refs[2 * sides + len(received) : -1], refs[-1]
-        for side in range(sides):
-            whole[:, :columns] = own[2 * side][...].astype(F32)
-            for row, column, there_row, there_column, height, wide in folded(0, rows):
-                whole[
-                    there_row : there_row + height,
-                    columns + there_column : columns + there_column + wide,
-                ] = own[2 * side + 1][row : row + height, column : column + wide].astype(F32)
-            if shape == "home":
-                value = whole[...] + arrived[0][...].astype(F32) + arrived[1][...].astype(F32)
-                out[0][...] = value.astype(BF16)
-            elif shape == "halves":
-                out[side][...] = whole[side * half : (side + 1) * half].astype(BF16)
-            else:
-                count = arrived[side].shape[0]
-                start = side * half if count < rows else 0
-                span = slice(start, start + count)
-                whole[span] += arrived[side][...].astype(F32)
-                out[side][...] = whole[...].astype(BF16)
-
-    own_specs = []
-    for side in range(sides):
-        own_specs += [
-            pl.BlockSpec((rows, columns), lambda i, ids, side=side: (ids[spots[side]], 0)),
-            pl.BlockSpec((128, width), lambda i, ids, side=side: (ids[spots[side]], 0)),
-        ]
-    whole_spec = lambda height: pl.BlockSpec((height, columns + FOLD), lambda i, ids: (0, 0))
-    outs = [rows] if shape == "home" else heights
+def add_home(terms, received):
+    rows, width = received[0].shape
+    last = terms.shape[0] // rows - 1
+
+    def kernel(own_ref, above_ref, below_ref, out_ref):
+        total = own_ref[...].astype(F32) + above_ref[...].astype(F32) + below_ref[...].astype(F32)
+        out_ref[...] = total.astype(BF16)
+
+    fixed = pl.BlockSpec((rows, width), lambda i: (0, 0))
+    return pl.pallas_call(
+        kernel,
+        grid=(1,),
+        in_specs=[pl.BlockSpec((rows, width), lambda i: (last, 0)), fixed, fixed],
+        out_specs=fixed,
+        out_shape=jax.ShapeDtypeStruct((rows, width), BF16),
+        compiler_params=pltpu.CompilerParams(vmem_limit_bytes=VMEM_BYTES),
+        cost_estimate=pl.CostEstimate(
+            flops=0, bytes_accessed=8 * rows * width, transcendentals=0
+        ),
+    )(terms, *received)
+
+
+def unit_terms(table, first, count, xs, hidden, unit_grads, grads, apart):
+    rows, width = xs.shape
+    columns = unit_grads.shape[1]
+    k_rows = width // lax.axis_size("sp")
+    half = k_rows // 2
+
+    def kernel(ids_ref, x_ref, hidden_ref, units_ref, grads_ref, *refs):
+        out_refs, turned, whole = refs[:-2], refs[-2], refs[-1]
+        device = ids_ref[first - pl.program_id(0)]
+        turned[...] = jnp.transpose(x_ref[...])
+        spot = pl.ds(aligned(lax.rem(device, 2) * k_rows, k_rows), k_rows)
+        down = dot(hidden_ref[...], grads_ref[...], TN).astype(BF16)
+        target = whole if apart else out_refs[0]
+        target[:, :columns] = dot(turned[spot, :], units_ref[...]).astype(BF16)
+        for row, column, there_row, there_column, height, wide in folded(0, k_rows):
+            target[
+                there_row : there_row + height,
+                columns + there_column : columns + there_column + wide,
+            ] = down[row : row + height, column : column + wide]
+        if apart:
+            out_refs[0][...] = whole[:half]
+            out_refs[1][...] = whole[half:]
+
+    outs, height = (2, half) if apart else (1, k_rows)
     return pl.pallas_call(
         kernel,
         grid_spec=pltpu.PrefetchScalarGridSpec(
             num_scalar_prefetch=1,
-            grid=(1,),
-            in_specs=own_specs + [whole_spec(a.shape[0]) for a in received],
-            out_specs=[whole_spec(height) for height in outs],
-            scratch_shapes=[pltpu.VMEM((rows, columns + FOLD), F32)],
-        ),
-        out_shape=[jax.ShapeDtypeStruct((height, columns + FOLD), BF16) for height in outs],
+            grid=(count,),
+            in_specs=[
+                pl.BlockSpec((rows, 2 * k_rows), lambda i, ids: (0, ids[first - i] // 2)),
+                pl.BlockSpec((rows, 128), lambda i, ids: (0, ids[first - i])),
+                pl.BlockSpec((rows, columns), lambda i, ids: (0, 0)),
+                pl.BlockSpec((rows, width), lambda i, ids: (0, 0)),
+            ],
+            out_specs=[pl.BlockSpec((height, columns + FOLD), lambda i, ids: (i, 0))] * outs,
+            scratch_shapes=[
+                pltpu.VMEM((2 * k_rows, rows), BF16),
+                pltpu.VMEM((k_rows, columns + FOLD), BF16),
+            ],
+        ),
+        out_shape=[jax.ShapeDtypeStruct((count * height, columns + FOLD), BF16)] * outs,
         compiler_params=pltpu.CompilerParams(vmem_limit_bytes=VMEM_BYTES),
         cost_estimate=pl.CostEstimate(
-            flops=0, bytes_accessed=12 * rows * (columns + FOLD), transcendentals=0
-        ),
-    )(table, *([d_weight, d_down] * sides), *received)
-
-
-def feed_back_kernel(
-    x_ref, grad_ref, hidden_ref, grads_ref, down_ref, d_w_ref, d_down_ref, out_ref, x_turned, total
-):
-    tile = pl.program_id(0)
-
-    @pl.when(tile == 0)
-    def _():
-        x_turned[...] = jnp.transpose(x_ref[...])
-
-    d_w_ref[...] = dot(x_turned[...], grads_ref[...]).astype(BF16)
-    d_down_ref[...] = dot(hidden_ref[...], grad_ref[...], TN).astype(BF16)
-    term = dot(hidden_ref[...], down_ref[...])
-
-    @pl.when(tile == 0)
-    def _():
-        total[...] = term
-
-    @pl.when(tile > 0)
-    def _():
-        total[...] += term
-
-    @pl.when(tile == pl.num_programs(0) - 1)
-    def _():
-        out_ref[...] = total[...].astype(BF16)
-
-
-def feed_back(xs, grads, hidden, unit_grads, down):
-    rows, width = xs.shape
-    units = down.shape[0]
-    fixed = pl.BlockSpec((rows, width), lambda t: (0, 0))
-    return pl.pallas_call(
-        feed_back_kernel,
-        grid=(units // UNITS,),
-        in_specs=[
-            fixed,
-            fixed,
-            pl.BlockSpec((rows, UNITS), lambda t: (0, t)),
-            pl.BlockSpec((rows, 2 * UNITS), lambda t: (0, t)),
-            pl.BlockSpec((UNITS, width), lambda t: (t, 0)),
-        ],
-        out_specs=[
-            pl.BlockSpec((width, 2 * UNITS), lambda t: (0, t)),
-            pl.BlockSpec((UNITS, width), lambda t: (t, 0)),
-            fixed,
-        ],
-        out_shape=[
-            jax.ShapeDtypeStruct((width, 2 * units), BF16),
-            jax.ShapeDtypeStruct((units, width), BF16),
-            jax.ShapeDtypeStruct((rows, width), BF16),
-        ],
-        scratch_shapes=[pltpu.VMEM((width, rows), BF16), pltpu.VMEM((rows, width), F32)],
-        compiler_params=pltpu.CompilerParams(vmem_limit_bytes=VMEM_BYTES),
-        cost_estimate=pl.CostEstimate(
-            flops=8 * rows * width * units, bytes_accessed=24 * rows * width, transcendentals=0
-        ),
-    )(xs, grads, hidden, unit_grads, down)
+            flops=2 * count * rows * (k_rows * columns + 128 * width),
+            bytes_accessed=4 * rows * columns + 2 * count * k_rows * (columns + FOLD),
+            transcendentals=0,
+        ),
+    )(table, xs, hidden, unit_grads, grads)
 
 
 def token_terms(table, first, count, grads, weight, apart):
@@ -1315,40 +1275,43 @@
     )(terms, terms, *received)
 
 
-def head_weight_terms(block_in, grads):
+def head_weight_terms(ring, block_in, grads):
     clips, length, width = block_in.shape
     columns = grads.shape[1]
-    size = lax.axis_size("sp")
+    size = ring.size
     k_rows = width // size
     part = k_rows // N_DP
     tile = 2 * k_rows
 
-    def kernel(in_ref, grads_ref, out_ref):
+    def kernel(index_ref, in_ref, grads_ref, *refs):
+        out_refs, turned = refs[:N_DP], refs[N_DP]
         total = dot(grads_ref[0], in_ref[0])
         for clip in range(1, clips):
             total = total + dot(grads_ref[clip], in_ref[clip])
-        turned = jnp.transpose(total).astype(BF16)
-        for member in range(N_DP):
+        turned[...] = jnp.transpose(total)
+        for i, out_ref in enumerate(out_refs):
             for shard in range(2):
-                start = shard * k_rows + member * part
-                out_ref[member, shard] = turned[start : start + part]
+                start = shard * k_rows + index_ref[size + i] * part
+                out_ref[shard] = turned[pl.ds(aligned(start, part), part), :].astype(BF16)
 
     return pl.pallas_call(
         kernel,
         grid=(width // tile,),
         in_specs=[
+            pl.BlockSpec(memory_space=pltpu.SMEM),
             pl.BlockSpec((clips, length, tile), lambda t: (0, 0, t)),
             pl.BlockSpec((clips, columns, length), lambda t: (0, 0, 0)),
         ],
-        out_specs=pl.BlockSpec((N_DP, 2, part, columns), lambda t: (0, t, 0, 0)),
-        out_shape=jax.ShapeDtypeStruct((N_DP, size, part, columns), BF16),
+        out_specs=[pl.BlockSpec((2, part, columns), lambda t: (t, 0, 0))] * N_DP,
+        out_shape=[jax.ShapeDtypeStruct((size, part, columns), BF16)] * N_DP,
+        scratch_shapes=[pltpu.VMEM((tile, columns), F32)],
         compiler_params=pltpu.CompilerParams(vmem_limit_bytes=VMEM_BYTES),
         cost_estimate=pl.CostEstimate(
             flops=2 * clips * length * width * columns,
             bytes_accessed=2 * clips * length * (width + columns) + 2 * width * columns,
             transcendentals=0,
         ),
-    )(block_in, grads)
+    )(ring.table, block_in, grads)
 
 
 def turn(values, cos, sin):
@@ -1713,13 +1676,14 @@
     tanh_gate = jnp.tanh(gate_cross)
     own_gate = lax.dynamic_slice(tanh_gate, (shard * heads,), (heads,))
 
-    token_flow = Gather(ring, [pack_tokens(tokens[0], w_out)])
+    token_rows = pack_tokens(tokens[0], w_out)
+    token_flow = Gather(ring, [token_rows])
     token_flow.send()
     cond_row = conditioning[0]
     cond_act = jax.nn.silu(cond_row).astype(BF16)
     mod_part = dot(cond_act, w_ada) + b_ada[None, :]
     flat_caption = captions[0].reshape(-1, size * text_rows)
-    packed = exchange(pack_first(w_query, w_key, w_value, flat_caption, mod_part))
+    packed = exchange(pack_first(w_query, w_key, w_value, flat_caption, mod_part, token_rows))
     token_flow.live, packed = ordered((token_flow.live, packed))
     token_flow.keep()
 
@@ -1739,7 +1703,7 @@
     token_flow.send()
     quarters = [quarter, quarter_far, across(quarter, 1), across(quarter_far, 1)]
     w_qkv, w_turned = join_projections(ring, quarters)
-    cap_terms = exchange(cap_terms)
+    cap_terms = lax.psum_scatter(cap_terms, "sp", scatter_dimension=0, tiled=True)
     shift_one, scale_one, gate_one, shift_two, scale_two, gate_two = jnp.split(modulation, 6, axis=1)
     branch_grad = (by_row(gate_two) * out_grad).astype(BF16)
     branch_grads = lax.all_gather(branch_grad, "dp", axis=0, tiled=True)
@@ -1748,19 +1712,26 @@
     freq = 10000.0 ** (-(jnp.arange(HD // 2, dtype=F32) * 2.0 / HD))
     angle = jnp.stack([lane, mirrored]).astype(F32)[:, None, :] * freq[None, :, None]
     cos, sin = jnp.cos(angle), jnp.sin(angle)
-    token_flow.live, w_qkv = ordered((token_flow.live, w_qkv))
+    unit_piece = unit_pieces(w_gate, w_up, w_down, quarter)
+    token_flow.live, w_qkv, unit_piece, caption_all = ordered(
+        (token_flow.live, w_qkv, unit_piece, caption_all)
+    )
     token_flow.keep()
 
     def project_some(first, groups, before):
         return project(table, first, groups, shift_one, scale_one, w_qkv, cos, sin, before)
 
     token_flow.send()
+    weight_flow = Gather(ring, [unit_piece])
+    weight_flow.send()
     blocks = [b for _, b in token_flow.blocks]
     projected = project_some(0, blocks[:5], None)
-    token_flow.live, projected, cap_terms = ordered((token_flow.live, projected, cap_terms))
+    token_flow.live, weight_flow.live, projected, cap_terms = ordered(
+        (token_flow.live, weight_flow.live, projected, cap_terms)
+    )
     token_flow.keep()
-
-    weight_flow = Gather(ring, [unit_pieces(w_gate, w_up, w_down, token_flow.halves[0][0])])
+    weight_flow.keep()
+
     weight_flow.send()
     out_cols = unpack_w_out(ring, token_flow, half)
     out_full = lax.all_gather(out_cols, "dp", axis=1, tiled=True)
@@ -1770,14 +1741,10 @@
     )
     cap_heads = jnp.sum(cap_terms.astype(F32), axis=0).astype(BF16)
     cap_key, cap_value = cap_heads[:, : CLIPS * CAP], cap_heads[:, CLIPS * CAP :]
-    weight_flow.live, block_in, qkv, raw, cap_key, cap_value = ordered(
-        (weight_flow.live, block_in, qkv, raw, cap_key, cap_value)
-    )
-    weight_flow.keep()
-
-    weight_flow.send()
     mixed_blocks, self_out, cross_out, log_total = attend(own_gate, qkv, cap_key, cap_value, half)
-    weight_flow.live, mixed_blocks = ordered((weight_flow.live, mixed_blocks))
+    weight_flow.live, mixed_blocks, branch_grads = ordered(
+        (weight_flow.live, mixed_blocks, branch_grads)
+    )
     weight_flow.keep()
 
     mixed = exchange(mixed_blocks)
@@ -1793,9 +1760,7 @@
     normed_two = middle * inverse_two
     ffn_in = (normed_two * (1.0 + by_row(scale_two)) + by_row(shift_two)).astype(BF16)
     ffn_far = across(ffn_in, 2)
-    weight_flow.live, ffn_in, ffn_far, branch_grads = ordered(
-        (weight_flow.live, ffn_in, ffn_far, branch_grads)
-    )
+    weight_flow.live, ffn_in, ffn_far = ordered((weight_flow.live, ffn_in, ffn_far))
     weight_flow.keep()
 
     weight_flow.send()
@@ -1812,82 +1777,100 @@
     ffn_own, ffn_far, hidden, unit_grads = ordered((ffn_own, ffn_far, hidden, unit_grads))
 
     ffn_far = across(ffn_far, 2)
-    d_units, d_down_units, branch_terms = feed_back(
-        ffn_ins, branch_grads, hidden, unit_grads, down
-    )
-    ffn_far, d_units, d_down_units, branch_terms = ordered(
-        (ffn_far, d_units, d_down_units, branch_terms)
-    )
-
-    def add_unit_step(step, received):
-        shift = far - step
-        spots = (ring.spots[shift], ring.spots[-shift if step else shift])
-        kind = "halves" if step == 0 else "whole"
-        return add_units(table, spots, d_units, d_down_units, received, kind)
+    last = ring.spots[far - 1]
+    unit_args = (ffn_ins, hidden, unit_grads, branch_grads)
+    unit_back = unit_terms(table, ring.spots[far], 1, *unit_args, True)
 
     def send(values):
         return ring.send_up(values[:1]) + ring.send_down(values[1:])
 
-    unit_back = send(add_unit_step(0, []))
-    branch = lax.psum_scatter(branch_terms, "dp", scatter_dimension=0, tiled=True)
+    unit_back = send(unit_back)
+    (d_units,) = unit_terms(table, last, last + 1, *unit_args, False)
+
+    def add_step(step, terms, received):
+        return add_received((2 * step, 2 * step + 1), terms, received)
+
+    ffn_far, d_units, unit_back, hidden = ordered(
+        (ffn_far, d_units, add_step(0, d_units, unit_back), hidden)
+    )
+
+    unit_back = send(unit_back)
     ffn_in_grad = ffn_own + ffn_far.astype(F32)
     middle_grad = out_grad + norm_back(
         ffn_in_grad * (1.0 + by_row(scale_two)), normed_two, inverse_two
     )
     attn_grad = (by_row(gate_one) * middle_grad).astype(BF16)
     mixed_grad = dot(out_full, attn_grad, NT).astype(BF16).reshape(size, own_cols, rows)
-    unit_back, mixed_grad, mixed, attn_grad = ordered((unit_back, mixed_grad, mixed, attn_grad))
+    mixed_grad, mixed, attn_grad, hidden = ordered((mixed_grad, mixed, attn_grad, hidden))
 
     head_grad = exchange(mixed_grad)
-    unit_back = add_unit_step(1, unit_back)
+    branch_terms = dot(hidden, down).astype(BF16)
     grad_out = out_terms(mixed, attn_grad)
-    unit_back, head_grad, grad_out = ordered((unit_back, head_grad, grad_out))
-
-    unit_back = send(unit_back)
-    out_sum = lax.psum_scatter(grad_out, "dp", scatter_dimension=0, tiled=True)
-    grads, cap_grads, gate_rows = attend_back(
-        own_gate, qkv, cap_key, cap_value, head_grad, self_out, cross_out, log_total, raw, cos, sin
-    )
-    unit_back, grads, cap_grads = ordered((unit_back, grads, cap_grads))
-    grads = grads.reshape(CLIPS, 3 * own_cols, size * half)
-
-    token_back = send(token_terms(table, ring.spots[far], 1, grads, w_turned, True))
-    unit_back = send(add_unit_step(2, unit_back))
-    last = ring.spots[far - 1]
-    (terms,) = token_terms(table, last, last + 1, grads, w_turned, False)
-    token_back, terms, grads, cap_grads = ordered((token_back, terms, grads, cap_grads))
-
-    def add_token_step(step, received):
-        return add_received((2 * step, 2 * step + 1), terms, received)
-
-    token_back = send(add_token_step(0, token_back))
-    cap_all = jnp.transpose(cap_grads, (1, 0, 2)).reshape(own_cols, 2 * CLIPS * CAP)
-    cap_all = gather_small(cap_all, "sp").reshape(D, 2 * CLIPS * CAP)
-    qkv_sum = head_weight_terms(block_in, grads)
-    token_back, unit_back, qkv_sum = ordered((token_back, unit_back, qkv_sum))
-
-    token_back = send(add_token_step(1, token_back))
-    unit_back = send(add_unit_step(3, unit_back))
-    qkv_sum = lax.psum_scatter(qkv_sum, "dp", scatter_dimension=0, tiled=True)[0]
-    token_back, unit_back, cap_all, branch, out_sum = ordered(
-        (token_back, unit_back, cap_all, branch, out_sum)
-    )
-
-    token_back = send(add_token_step(2, token_back))
-    cap_far = across(cap_all, 2)
-    spot = ring.spots[0]
-    (unit_home,) = add_units(table, (spot,), d_units, d_down_units, unit_back, "home")
-    unit_far = across(unit_home, 2)
-    qkv_home = exchange(qkv_sum)
-    result = (middle + by_row(gate_two) * branch.astype(F32)).astype(BF16)
     sums = [
         clip_sums(middle_grad * attn_out),
         clip_sums(ffn_in_grad),
         clip_sums(ffn_in_grad * normed_two),
-        clip_sums(out_grad * branch.astype(F32)),
     ]
-    token_back, sums, cap_all, cap_far, unit_home, unit_far, qkv_home, out_sum = ordered(
-        (token_back, sums, cap_all, cap_far, unit_home, unit_far, qkv_home, out_sum)
+    head_grad, grad_out, branch_terms, sums = ordered((head_grad, grad_out, branch_terms, sums))
+
+    out_sum = lax.psum_scatter(grad_out, "dp", scatter_dimension=0, tiled=True)
+    out_home = lax.psum_scatter(out_sum[0], "sp", scatter_dimension=0, tiled=True)
+    grads, cap_grads, gate_rows = attend_back(
+        own_gate, qkv, cap_key, cap_value, head_grad, self_out, cross_out, log_total, raw, cos, sin
+    )
+    grads = grads.reshape(CLIPS, 3 * own_cols, size * half)
+    token_back = token_terms(table, ring.spots[far], 1, grads, w_turned, True)
+    unit_back, grads, cap_grads, token_back, branch_terms = ordered(
+        (unit_back, grads, cap_grads, token_back, branch_terms)
+    )
+
+    token_back = send(token_back)
+    branch = lax.psum_scatter(branch_terms, "dp", scatter_dimension=0, tiled=True)
+    unit_back = send(add_step(1, d_units, unit_back))
+    (terms,) = token_terms(table, last, last + 1, grads, w_turned, False)
+    qkv_terms = head_weight_terms(ring, block_in, grads)
+    cap_all = jnp.transpose(cap_grads, (1, 0, 2)).reshape(own_cols, 2 * CLIPS * CAP)
+    cap_all = gather_small(cap_all, "sp").reshape(D, 2 * CLIPS * CAP)
+    token_back, unit_back, qkv_terms, cap_all = ordered(
+        (add_step(0, terms, token_back), add_step(2, d_units, unit_back), qkv_terms, cap_all)
+    )
+
+    token_back = send(token_back)
+    unit_back = send(unit_back)
+    qkv_own, qkv_far = sum_packs_near(qkv_terms)
+    qkv_far = across(qkv_far, 2)
+    cap_far = across(cap_all, 2)
+    token_back, unit_back, qkv_own, qkv_far, cap_all, cap_far = ordered(
+        (add_step(1, terms, token_back), unit_back, qkv_own, qkv_far, cap_all, cap_far)
+    )
+
+    token_back = send(token_back)
+    unit_home = add_home(d_units, unit_back)
+    unit_far = across(unit_home, 2)
+    qkv_home = exchange((qkv_own + qkv_far.astype(F32)).astype(BF16))
+    cap_blocks = [cap_all, cap_far, across(cap_all, 1), across(cap_far, 1)]
+    token_back, unit_home, unit_far, qkv_home, cap_blocks, branch = ordered(
+        (add_step(2, terms, token_back), unit_home, unit_far, qkv_home, cap_blocks, branch)
+    )
+    cap_all = cap_blocks[0]
+
+    token_back = send(token_back)
+    qkv_far = across(qkv_home, 2)
+    caption_grad = dot(cap_all[:, : CLIPS * CAP], w_text_key, (((0,), (1,)), ((), ()))) + dot(
+        cap_all[:, CLIPS * CAP :], w_text_value, (((0,), (1,)), ((), ()))
+    )
+    caption_grad = caption_grad.astype(BF16).reshape(CLIPS, size, -1, text_rows)
+    caption_grad = jnp.transpose(caption_grad, (1, 0, 2, 3))
+    d_text_key, d_text_value = text_grads(ring, caption_all, cap_blocks)
+    shape = lambda *dims: jax.ShapeDtypeStruct(dims, F32)
+    unit_blocks = [unit_home, unit_far, across(unit_home, 1), across(unit_far, 1)]
+    d_gate_w, d_up_w, d_down = place(
+        ring, place_units, unit_blocks, [shape(k_rows, ff), shape(k_rows, ff), shape(ff_rows, D)]
+    )
+    result = (middle + by_row(gate_two) * branch.astype(F32)).astype(BF16)
+    sums = [*sums, clip_sums(out_grad * branch.astype(F32))]
+    token_back, sums, qkv_home, qkv_far, out_home, result, d_down, caption_grad = ordered(
+        (token_back, sums, qkv_home, qkv_far, out_home, result, d_down, caption_grad)
     )
 
     inputs_grad, own_sums = finish_tokens(terms, token_back, middle_grad, tokens[0], scale_one)
@@ -1897,21 +1880,11 @@
     gate_own = jnp.sum(gate_rows, axis=(2, 3))
     gate_own = jnp.broadcast_to(gate_own[None], (size, CLIPS, heads))
     mod_terms = jnp.concatenate([mod_terms, gate_own], axis=2)
-    mod_terms, cap_all, cap_far, unit_home, unit_far, qkv_home, out_sum = ordered(
-        (mod_terms, cap_all, cap_far, unit_home, unit_far, qkv_home, out_sum)
-    )
-
-    arrived = exchange(mod_terms)
-    out_home = exchange(out_sum.reshape(size, k_rows, out_cols_part))
-    unit_blocks = [unit_home, unit_far, across(unit_home, 1), across(unit_far, 1)]
-    cap_blocks = [cap_all, cap_far, across(cap_all, 1), across(cap_far, 1)]
-    qkv_far = across(qkv_home, 2)
-    shape = lambda *dims: jax.ShapeDtypeStruct(dims, F32)
-    d_gate_w, d_up_w, d_down = place(
-        ring, place_units, unit_blocks, [shape(k_rows, ff), shape(k_rows, ff), shape(ff_rows, D)]
-    )
-    d_text_key, d_text_value = text_grads(ring, caption_all, cap_blocks)
-    arrived, out_home, qkv_home, qkv_far = ordered((arrived, out_home, qkv_home, qkv_far))
+    mod_terms, qkv_home, qkv_far, out_home = ordered((mod_terms, qkv_home, qkv_far, out_home))
+
+    arrived, caption_grad = ordered((exchange(mod_terms), caption_grad))
+    qkv_blocks = [qkv_home, qkv_far, across(qkv_home, 1), across(qkv_far, 1)]
+    out_blocks = gather_packs(out_home)
 
     own_mod = w_ada.shape[1]
     mod_low = jnp.sum(arrived[:, :, :own_mod], axis=0).astype(BF16)
@@ -1931,18 +1904,12 @@
         1.0 - tanh_gate * tanh_gate
     )
 
-    caption_grad = dot(cap_all[:, : CLIPS * CAP], w_text_key, (((0,), (1,)), ((), ()))) + dot(
-        cap_all[:, CLIPS * CAP :], w_text_value, (((0,), (1,)), ((), ()))
-    )
-    caption_grad = caption_grad.astype(BF16).reshape(CLIPS, size, -1, text_rows)
-    caption_grad = exchange(jnp.transpose(caption_grad, (1, 0, 2, 3)))
+    caption_grad = exchange(caption_grad)
     caption_grad = (
         jnp.transpose(caption_grad, (1, 2, 0, 3)).reshape(CLIPS, -1, size * text_rows).astype(F32)
     )
 
-    out_home = jnp.sum(out_home.astype(F32), axis=0).astype(BF16)
-    (d_out,) = place(ring, place_columns, gather_packs(out_home), [shape(k_rows, D)])
-    qkv_blocks = [qkv_home, qkv_far, across(qkv_home, 1), across(qkv_far, 1)]
+    (d_out,) = place(ring, place_columns, out_blocks, [shape(k_rows, D)])
     d_query, d_key, d_value = place(ring, place_heads, qkv_blocks, [shape(k_rows, D)] * 3)
     return (
         result[None],

time: 759 us -> 706 us (0.930)
  starting transfers between devices: 122 us -> 106 us
  local copies, waits for them, and re-layouts: 94.6 us -> 79.3 us
  blocking collectives: 12.4 us -> 0 us
    ppermute x16, waiting for transfers between devices: 22 us -> 69.8 us  [send_down(): return [lax.ppermute(v, 'sp', self.down) for v in values]]
    ppermute x16, waiting for transfers between devices: 174 us -> 148 us  [send_up(): return [lax.ppermute(v, 'sp', self.up) for v in values]]
    pallas_call x7 -> x4, Pallas kernels: 45.3 us -> 32.7 us  [the longest x2 21.6 us: unit_terms(): pl.pallas_call(kernel, grid_spec=pltpu.PrefetchScalarGridSpec(num_scalar_...]
    all_to_all x1 -> x0, blocking collectives: 12.4 us -> none  [exchange(): return lax.all_to_all(value, 'sp', 0, 0, tiled=True)]
    all_to_all x7 -> x6, waiting for transfers between devices: 44.3 us -> 32 us  [exchange(): return lax.all_to_all(value, 'sp', 0, 0, tiled=True)]
    all_to_all x7 -> x6, starting transfers between devices: 40.3 us -> 29.2 us  [exchange(): return lax.all_to_all(value, 'sp', 0, 0, tiled=True)]
    unnamed x252 -> x262, local copies, waits for them, and re-layouts: 76.8 us -> 65.9 us
    ppermute x20 -> x23, waiting for transfers between devices: 25.4 us -> 16.3 us  [across(): return lax.ppermute(value, 'dp', [(i, i ^ bit) for i in range(N_DP)])]
  transfers between devices with their start and end apart: 68 -> 71, of which waited for: 31 -> 29; matrix products, arithmetic and copies ran while one was open for 8% -> 7% of each run, Pallas kernels for 19% -> 19%
where the time goes in v3:
time: 706 us; the launch traced here: 695 us
  waiting for transfers between devices  272 us (39%)
  Pallas kernels  170 us (24%)
  starting transfers between devices  106 us (15%)
  local copies, waits for them, and re-layouts  79.3 us (11%)
  other arithmetic  29 us (4%)
  matrix products  20.8 us (3%)
  between operations  17.1 us (2%)
    ppermute x16, waiting for transfers between devices, send_up(): return [lax.ppermute(v, 'sp', self.up) for v in values]  148 us
    ppermute x16, waiting for transfers between devices, send_down(): return [lax.ppermute(v, 'sp', self.down) for v in values]  69.8 us
    unnamed x262, local copies, waits for them, and re-layouts  65.9 us
    ppermute x16, starting transfers between devices, send_up(): return [lax.ppermute(v, 'sp', self.up) for v in values]  35.7 us
    all_to_all x6, waiting for transfers between devices, exchange(): return lax.all_to_all(value, 'sp', 0, 0, tiled=True)  32 us
    all_to_all x6, starting transfers between devices, exchange(): return lax.all_to_all(value, 'sp', 0, 0, tiled=True)  29.2 us
    pallas_call x1, Pallas kernels, feed(): pl.pallas_call(functools.partial(feed_kernel, size=ring.size, places=plac...  26 us
    pallas_call x1, Pallas kernels, attend_back(): pl.pallas_call(functools.partial(attend_back_kernel, block=length // 2),...  23.8 us
  transfers between devices with their start and end apart: 71, of which 29 were waited for; matrix products, arithmetic and copies ran while one was open for 7% of the time, Pallas kernels for 19%

profile of v3, /device:TPU:0, one launch (start us, length us, event | category | flops | bytes accessed | tf_op | source)
XLA Modules:
  0.0 694.6 jit_solution(13296407898769519119)
XLA Ops:
  14.1 7.3 %all-to-all-start = ((bf16[8,96,576]{2,1,0:T(8,128)(2,1)}), bf16[8,96,576]{2,1,0:T(8,128)(2,1)}, u32[]{:S(2)}, u32[]{:S(2)}) async-start(bf16[8,96,576]{2,1,0:T(8,128)(2,1)} %copy-done.37), calls=%async_computation | async-start | bytes 1966080 | tf_op jit(solution)/shard_map/all_to_all | solution.py:560
  23.5 34.9 %collective-permute-done.refs_0_ = bf16[320,1536]{1,0:T(8,128)(2,1)S(1)} collective-permute-done((bf16[320,1536]{1,0:T(8,128)(2,1)S(1)}, bf16[320,1536]{1,0:T(8,128)(2,1)S(1)}, u32[]{:S(2)}, u32[]{:S(2)}) %collective-permute-start) | collective-permute-done | bytes 983072 | tf_op jit(solution)/shard_map/ppermute | solution.py:508
  64.2 6.9 collective-permute-start.2
  78.5 9.9 %collective-permute-done.4.refs_3_ = bf16[8,48,576]{2,1,0:T(8,128)(2,1)S(1)} collective-permute-done((bf16[8,48,576]{2,1,0:T(8,128)(2,1)}, bf16[8,48,576]{2,1,0:T(8,128)(2,1)S(1)}, u32[]{:S(2)}, u32[]{:S(2)}) %collective-permute-start.4) | collective-permute-done | bytes 442400 | tf_op jit(solution)/shard_map/ppermute | solution.py:538
  88.4 2.8 collective-permute-done.2.refs_0_
  91.3 2.8 collective-permute-done.3.refs_1_
  110.9 20.2 %collective-permute-done.5.refs_0_ = bf16[320,1536]{1,0:T(8,128)(2,1)S(1)} collective-permute-done((bf16[320,1536]{1,0:T(8,128)(2,1)}, bf16[320,1536]{1,0:T(8,128)(2,1)S(1)}, u32[]{:S(2)}, u32[]{:S(2)}) %collective-permute-start.5) | collective-permute-done | bytes 983072 | tf_op jit(solution)/shard_map/ppermute | solution.py:508
  131.1 2.2 collective-permute-done.6.refs_1_
  142.1 9.5 %shard_map.297 = (bf16[2,1024,1536]{2,1,0:T(8,128)(2,1)}, bf16[2,576,1024]{2,1,0:T(8,128)(2,1)}, f32[2,384,1024]{2,1,0:T(8,128)}) custom-call(s32[12]{0:T(128)S(1)} %dynamic-slice_bitcast_fusion.index_ref.place_ref.ids_ref, bf16[320,1536]{1,0:T(8,128)(2,1)S(1)} %copy-done.8, bf16[320,1536]{1,0:T(8,128)(2,1)S(1)} %copy-done.20, ...), custom_call_target="tpu_custom_call" | custom-call | flops 2264924160 | bytes 15532032 | tf_op jit(solution)/shard_map/pallas_call | solution.py:1392
  151.7 26.1 %collective-permute-done.10.refs_1_ = bf16[160,1536]{1,0:T(8,128)(2,1)} collective-permute-done((bf16[160,1536]{1,0:T(8,128)(2,1)S(1)}, bf16[160,1536]{1,0:T(8,128)(2,1)}, u32[]{:S(2)}, u32[]{:S(2)}) %collective-permute-start.10) | collective-permute-done | bytes 491552 | tf_op jit(solution)/shard_map/ppermute | solution.py:511
  180.2 2.4 shard_map.302
  188.5 6.7 shard_map.299
  195.2 10.6 %shard_map.300 = (bf16[8,192,256]{2,1,0:T(8,128)(2,1)S(1)}, f32[2,192,1024]{2,1,0:T(8,128)S(1)}, f32[2,192,1024]{2,1,0:T(8,128)S(1)}, f32[2,3,1,1024]{3,2,1,0:T(1,128)S(1)}) custom-call(f32[3]{0:T(128)S(1)} %dynamic_slice.8.gate_ref, bf16[2,576,1024]{2,1,0:T(8,128)(2,1)} %get-tuple-element.200.q_ref.k_ref.v_ref, ...), custom_call_target="tpu_custom_call" | custom-call | flops 6442450944 | bytes 7864320 | tf_op jit(solution)/shard_map/pallas_call | solution.py:1449
  209.7 3.8 all-to-all-start.1
  215.5 18.0 %all-to-all-done.1.refs_0_ = bf16[8,192,256]{2,1,0:T(8,128)(2,1)S(1)} async-done(((bf16[8,192,256]{2,1,0:T(8,128)(2,1)}), bf16[8,192,256]{2,1,0:T(8,128)(2,1)S(1)}, u32[]{:S(2)}, u32[]{:S(2)}) %all-to-all-start.1) | async-done | bytes 786464 | tf_op jit(solution)/shard_map/all_to_all | solution.py:560
  234.4 5.4 multiply_reduce_fusion.1
  242.8 5.6 collective-permute-done.15.refs_0_
  250.4 2.9 collective-permute-done.17.refs_3_
  255.1 2.9 collective-permute-start.20
  259.6 11.3 %collective-permute-done.20.refs_12_ = bf16[96,3072]{1,0:T(8,128)(2,1)S(1)} collective-permute-done((bf16[96,3072]{1,0:T(8,128)(2,1)S(1)}, bf16[96,3072]{1,0:T(8,128)(2,1)S(1)}, u32[]{:S(2)}, u32[]{:S(2)}) %collective-permute-start.20) | collective-permute-done | bytes 589856 | tf_op jit(solution)/shard_map/ppermute | solution.py:508
  270.8 3.8 collective-permute-done.21.refs_13_
  274.6 26.0 %shard_map.305 = (bf16[1024,1024]{1,0:T(8,128)(2,1)}, bf16[1024,2048]{1,0:T(8,128)(2,1)}, bf16[512,1536]{1,0:T(8,128)(2,1)}, bf16[512,1536]{1,0:T(8,128)(2,1)}, ...) custom-call(s32[12]{0:T(128)S(1)} %dynamic-slice_bitcast_fusion.index_ref.place_ref.ids_ref, ...), custom_call_target="tpu_custom_call" | custom-call | flops 16106127360 | bytes 37748736 | tf_op jit(solution)/shard_map/pallas_call | solution.py:1095
  302.5 3.4 collective-permute-done.22
  309.3 5.6 shard_map.308
  318.6 15.9 %shard_map.307.refs_0_.refs_1_ = bf16[1344,3072]{1,0:T(8,128)(2,1)} custom-call(s32[12]{0:T(128)S(1)} %dynamic-slice_bitcast_fusion.index_ref.place_ref.ids_ref, bf16[1024,1536]{1,0:T(8,128)(2,1)S(1)} %copy-done.39, bf16[1024,1024]{1,0:T(8,128)(2,1)S(1)} %copy-done.1, bf16[1024,2048]{1,0:T(8,128)(2,1)} %get-tuple-element.220.units_ref, ...), custom_call_target="tpu_custom_call" | custom-call | flops 8455716864 | bytes 16646144 | tf_op jit(solution)/shard_map/pallas_call | solution.py:1182
  339.4 2.7 multiply_reduce_fusion
  342.5 3.9 fusion.25
  346.5 2.4 convolution_convert_fusion.1
  348.9 4.2 all-to-all-start.2
  353.2 3.2 bitcast_reduce_fusion.1
  356.4 3.8 shard_map.312.refs_1_
  361.1 4.8 convolution_convert_fusion.refs_2_
  365.8 7.3 %all-to-all-done.2.refs_0_ = bf16[8,192,256]{2,1,0:T(8,128)(2,1)} async-done(((bf16[8,192,256]{2,1,0:T(8,128)(2,1)}), bf16[8,192,256]{2,1,0:T(8,128)(2,1)}, u32[]{:S(2)}, u32[]{:S(2)}) %all-to-all-start.2) | async-done | bytes 786464 | tf_op jit(solution)/shard_map/all_to_all | solution.py:560
  383.2 23.8 %shard_map.314 = (bf16[2,3,192,1024]{3,2,1,0:T(8,128)(2,1)}, bf16[2,192,256]{2,1,0:T(8,128)(2,1)S(1)}, f32[2,3,1,1024]{3,2,1,0:T(1,128)S(1)}) custom-call(f32[3]{0:T(128)S(1)} %dynamic_slice.8.gate_ref, bf16[2,576,1024]{2,1,0:T(8,128)(2,1)} %get-tuple-element.200.q_ref.k_ref.v_ref, bf16[2,576,1024]{2,1,0:T(8,128)(2,1)} %get-tuple-element.200.q_ref.k_ref.v_ref, ...), custom_call_target="tpu_custom_call" | custom-call | flops 16106127360 | bytes 12582912 | tf_op jit(solution)/shard_map/pallas_call | solution.py:1574
  415.5 4.4 all-to-all-start.3
  420.0 2.7 shard_map.319
  427.0 7.7 %shard_map.317.refs_0_.refs_1_.terms_ref = bf16[1792,1536]{1,0:T(8,128)(2,1)} custom-call(s32[12]{0:T(128)S(1)} %dynamic-slice_bitcast_fusion.index_ref.place_ref.ids_ref, bf16[2,576,1024]{2,1,0:T(8,128)(2,1)S(1)} %copy-done.15, bf16[576,1536]{1,0:T(8,128)(2,1)S(1)} %copy-done.49), custom_call_target="tpu_custom_call" | custom-call | flops 3170893824 | bytes 9338880 | tf_op jit(solution)/shard_map/pallas_call | solution.py:1223
  434.8 8.0 %shard_map.321 = (bf16[8,48,576]{2,1,0:T(8,128)(2,1)S(1)}, bf16[8,48,576]{2,1,0:T(8,128)(2,1)S(1)}, bf16[8,48,576]{2,1,0:T(8,128)(2,1)S(1)}, bf16[8,48,576]{2,1,0:T(8,128)(2,1)S(1)}) custom-call(s32[12]{0:T(128)S(1)} %dynamic-slice_bitcast_fusion.index_ref.place_ref.ids_ref, bf16[2,1024,1536]{2,1,0:T(8,128)(2,1)} %get-tuple-element.258.in_ref, ...), custom_call_target="tpu_custom_call" | custom-call | flops 3623878656 | bytes 10420224 | tf_op jit(solution)/shard_map/pallas_call | solution.py:1297
  442.9 35.3 %collective-permute-done.28.refs_2_ = bf16[128,1536]{1,0:T(8,128)(2,1)S(1)} collective-permute-done((bf16[128,1536]{1,0:T(8,128)(2,1)S(1)}, bf16[128,1536]{1,0:T(8,128)(2,1)S(1)}, u32[]{:S(2)}, u32[]{:S(2)}) %collective-permute-start.28) | collective-permute-done | bytes 393248 | tf_op jit(solution)/shard_map/ppermute | solution.py:508
  478.1 2.2 collective-permute-done.29.refs_3_
  488.4 10.1 %collective-permute-start.32 = (bf16[256,1536]{1,0:T(8,128)(2,1)}, bf16[256,1536]{1,0:T(8,128)(2,1)S(1)}, u32[]{:S(2)}, u32[]{:S(2)}) collective-permute-start(bf16[256,1536]{1,0:T(8,128)(2,1)} %get-tuple-element.264), channel_id=1, source_target_pairs={{0,2},{2,4},{4,6},{6,7},{7,5},{5,3},{3,1},{1,0},{8,10},{10,12},{12... | collective-permute-start | bytes 2359304 | tf_op jit(solution)/shard_map/ppermute | solution.py:508
  502.5 14.2 %collective-permute-done.32.refs_2_ = bf16[256,1536]{1,0:T(8,128)(2,1)S(1)} collective-permute-done((bf16[256,1536]{1,0:T(8,128)(2,1)}, bf16[256,1536]{1,0:T(8,128)(2,1)S(1)}, u32[]{:S(2)}, u32[]{:S(2)}) %collective-permute-start.32) | collective-permute-done | bytes 786464 | tf_op jit(solution)/shard_map/ppermute | solution.py:508
  519.5 24.1 %collective-permute-done.33.refs_3_ = bf16[256,1536]{1,0:T(8,128)(2,1)S(1)} collective-permute-done((bf16[256,1536]{1,0:T(8,128)(2,1)}, bf16[256,1536]{1,0:T(8,128)(2,1)S(1)}, u32[]{:S(2)}, u32[]{:S(2)}) %collective-permute-start.33) | collective-permute-done | bytes 786464 | tf_op jit(solution)/shard_map/ppermute | solution.py:511
  543.5 2.7 shard_map.323
  549.8 3.1 shard_map.326.refs_2_
  558.6 4.6 all-to-all-start.4
  563.2 18.6 %collective-permute-done.40.refs_2_ = bf16[256,1536]{1,0:T(8,128)(2,1)} collective-permute-done((bf16[256,1536]{1,0:T(8,128)(2,1)}, bf16[256,1536]{1,0:T(8,128)(2,1)}, u32[]{:S(2)}, u32[]{:S(2)}) %collective-permute-start.40) | collective-permute-done | bytes 786464 | tf_op jit(solution)/shard_map/ppermute | solution.py:508
  581.9 2.7 collective-permute-done.41.refs_3_
  584.5 2.2 shard_map.325
  588.5 6.5 all-to-all-done.4.refs_4_
  600.5 2.3 fusion.8
  607.4 6.7 shard_map.328
  614.1 5.2 collective-permute-done.45.refs_0_
  619.3 2.5 collective-permute-done.46.refs_1_
  621.9 2.3 reduce-scatter.11.cloned.1.call-done.refs_8_
  626.7 4.0 shard_map.330
  631.5 4.2 all-to-all-start.5
  637.0 8.0 %shard_map.335 = (f32[512,1536]{1,0:T(8,128)}, f32[512,1536]{1,0:T(8,128)}) custom-call(s32[12]{0:T(128)S(1)} %dynamic-slice_bitcast_fusion.index_ref.place_ref.ids_ref, bf16[1024,512]{1,0:T(8,128)(2,1)S(1)} %copy-done.66, bf16[1536,512]{1,0:T(8,128)(2,1)} %get-tuple-element.297.refs_0_, bf16[1536,512]{1,0:T(8,128)(2,1)} %get-tuple-element.322.refs_1_, ...), custom_call_target="tpu_custom_call" | custom-call | flops 3221225472 | bytes 12582912 | tf_op jit(solution)/shard_map/pallas_call | solution.py:700
  649.3 3.9 all-to-all-start.8
  654.5 3.0 all-to-all-done.8
  658.1 6.0 all-to-all-start.7
  666.5 3.0 fusion.11
  671.1 5.1 all-to-all-start.6
  681.0 3.3 shard_map.333
  (462 shorter events, 166.1 us)
Async XLA Ops:
  14.1 46.7 %all-to-all-start = ((bf16[8,96,576]{2,1,0:T(8,128)(2,1)}), bf16[8,96,576]{2,1,0:T(8,128)(2,1)}, u32[]{:S(2)}, u32[]{:S(2)}) async-start(bf16[8,96,576]{2,1,0:T(8,128)(2,1)} %copy-done.37), calls=%async_computation | async-start | bytes 1966080 | tf_op jit(solution)/shard_map/all_to_all | solution.py:560
  21.3 89.6 %all-gather.4.cloned.1.call-start = ((), (), s32[]{:S(2)}) async-start(), calls=%async_computation.13 | async-start | bytes 1310720 | tf_op jit(solution)/shard_map/all_gather | solution.py:1697
  21.4 37.0 %collective-permute-start = (bf16[320,1536]{1,0:T(8,128)(2,1)S(1)}, bf16[320,1536]{1,0:T(8,128)(2,1)S(1)}, u32[]{:S(2)}, u32[]{:S(2)}) collective-permute-start(bf16[320,1536]{1,0:T(8,128)(2,1)S(1)} %shard_map.288.after_ref.refs_0_.refs_1_), channel_id=1, source_target_pairs={{0,2},{2,4},{4,6},{6,7},{7,5},{5,3},{3,1},{1,0},{8,10},{10,12},{12... | collective-permute-start | bytes 2949128 | tf_op jit(solution)/shard_map/ppermute | solution.py:508
  23.4 37.3 %collective-permute-start.1 = (bf16[320,1536]{1,0:T(8,128)(2,1)S(1)}, bf16[320,1536]{1,0:T(8,128)(2,1)}, u32[]{:S(2)}, u32[]{:S(2)}) collective-permute-start(bf16[320,1536]{1,0:T(8,128)(2,1)S(1)} %shard_map.288.after_ref.refs_0_.refs_1_), channel_id=1, source_target_pairs={{2,0},{4,2},{6,4},{7,6},{5,7},{3,5},{1,3},{0,1},{10,8},{12,10},{14... | collective-permute-start | bytes 2949128 | tf_op jit(solution)/shard_map/ppermute | solution.py:511
  64.1 113.6 %reduce-scatter.5.cloned.1.call-start = ((), (), s32[]{:S(2)}) async-start(), calls=%async_computation.14 | async-start | bytes 1769472 | tf_op jit(solution)/shard_map/reduce_scatter | solution.py:1706
  64.2 27.1 %collective-permute-start.2 = (bf16[320,1536]{1,0:T(8,128)(2,1)}, bf16[320,1536]{1,0:T(8,128)(2,1)S(1)}, u32[]{:S(2)}, u32[]{:S(2)}) collective-permute-start(bf16[320,1536]{1,0:T(8,128)(2,1)} %get-tuple-element.173.refs_1_.refs_2_.refs_3_), channel_id=1, source_target_pairs={{0,2},{2,4},{4,6},{6,7},{7,5},{5,3},{3,1},{1,0},{8,10},{10,12},{12... | collective-permute-start | bytes 2949128 | tf_op jit(solution)/shard_map/ppermute | solution.py:508
  71.0 23.0 %collective-permute-start.3 = (bf16[320,1536]{1,0:T(8,128)(2,1)}, bf16[320,1536]{1,0:T(8,128)(2,1)}, u32[]{:S(2)}, u32[]{:S(2)}) collective-permute-start(bf16[320,1536]{1,0:T(8,128)(2,1)} %get-tuple-element.174.refs_2_.refs_4_.refs_5_), channel_id=1, source_target_pairs={{2,0},{4,2},{6,4},{7,6},{5,7},{3,5},{1,3},{0,1},{10,8},{12,10},{14... | collective-permute-start | bytes 2949128 | tf_op jit(solution)/shard_map/ppermute | solution.py:511
  71.0 17.4 %collective-permute-start.4 = (bf16[8,48,576]{2,1,0:T(8,128)(2,1)}, bf16[8,48,576]{2,1,0:T(8,128)(2,1)S(1)}, u32[]{:S(2)}, u32[]{:S(2)}) collective-permute-start(bf16[8,48,576]{2,1,0:T(8,128)(2,1)} %copy-done.34), channel_id=1, source_target_pairs={{0,16},{8,24},{16,0},{24,8},{1,17},{9,25},{17,1},{25,9},{2,18},{10... | collective-permute-start | bytes 1327112 | tf_op jit(solution)/shard_map/ppermute | solution.py:538
  94.1 115.6 %all-gather.6.cloned.1.call-start = ((), (), s32[]{:S(2)}) async-start(), calls=%async_computation.15 | async-start | bytes 3932160 | tf_op jit(solution)/shard_map/all_gather | solution.py:1709
  96.3 137.2 %all-gather.8.cloned.1.call-start = ((), (), s32[]{:S(2)}) async-start(), calls=%async_computation.16 | async-start | bytes 5898240 | tf_op jit(solution)/shard_map/all_gather | solution.py:1737
  96.3 34.8 %collective-permute-start.5 = (bf16[320,1536]{1,0:T(8,128)(2,1)}, bf16[320,1536]{1,0:T(8,128)(2,1)S(1)}, u32[]{:S(2)}, u32[]{:S(2)}) collective-permute-start(bf16[320,1536]{1,0:T(8,128)(2,1)} %get-tuple-element.179.refs_3_.refs_6_.refs_7_), channel_id=1, source_target_pairs={{0,2},{2,4},{4,6},{6,7},{7,5},{5,3},{3,1},{1,0},{8,10},{10,12},{12... | collective-permute-start | bytes 2949128 | tf_op jit(solution)/shard_map/ppermute | solution.py:508
  98.1 35.2 %collective-permute-start.6 = (bf16[320,1536]{1,0:T(8,128)(2,1)}, bf16[320,1536]{1,0:T(8,128)(2,1)}, u32[]{:S(2)}, u32[]{:S(2)}) collective-permute-start(bf16[320,1536]{1,0:T(8,128)(2,1)} %get-tuple-element.180.refs_4_.refs_8_.refs_9_), channel_id=1, source_target_pairs={{2,0},{4,2},{6,4},{7,6},{5,7},{3,5},{1,3},{0,1},{10,8},{12,10},{14... | collective-permute-start | bytes 2949128 | tf_op jit(solution)/shard_map/ppermute | solution.py:511
  133.3 44.4 %collective-permute-start.11 = (bf16[192,3072]{1,0:T(8,128)(2,1)}, bf16[192,3072]{1,0:T(8,128)(2,1)}, u32[]{:S(2)}, u32[]{:S(2)}) collective-permute-start(bf16[192,3072]{1,0:T(8,128)(2,1)} %get-tuple-element.186.refs_5_), channel_id=1, source_target_pairs={{0,2},{2,4},{4,6},{6,7},{7,5},{5,3},{3,1},{1,0},{8,10},{10,12},{12... | collective-permute-start | bytes 3538952 | tf_op jit(solution)/shard_map/ppermute | solution.py:508
  134.9 42.8 %collective-permute-start.12 = (bf16[192,3072]{1,0:T(8,128)(2,1)}, bf16[192,3072]{1,0:T(8,128)(2,1)}, u32[]{:S(2)}, u32[]{:S(2)}) collective-permute-start(bf16[192,3072]{1,0:T(8,128)(2,1)} %get-tuple-element.186.refs_5_), channel_id=1, source_target_pairs={{2,0},{4,2},{6,4},{7,6},{5,7},{3,5},{1,3},{0,1},{10,8},{12,10},{14... | collective-permute-start | bytes 3538952 | tf_op jit(solution)/shard_map/ppermute | solution.py:511
  136.5 41.2 %collective-permute-start.10 = (bf16[160,1536]{1,0:T(8,128)(2,1)S(1)}, bf16[160,1536]{1,0:T(8,128)(2,1)}, u32[]{:S(2)}, u32[]{:S(2)}) collective-permute-start(bf16[160,1536]{1,0:T(8,128)(2,1)S(1)} %slice.60), channel_id=1, source_target_pairs={{2,0},{4,2},{6,4},{7,6},{5,7},{3,5},{1,3},{0,1},{10,8},{12,10},{14... | collective-permute-start | bytes 1474568 | tf_op jit(solution)/shard_map/ppermute | solution.py:511
  137.9 39.8 %collective-permute-start.9 = (bf16[160,1536]{1,0:T(8,128)(2,1)S(1)}, bf16[160,1536]{1,0:T(8,128)(2,1)}, u32[]{:S(2)}, u32[]{:S(2)}) collective-permute-start(bf16[160,1536]{1,0:T(8,128)(2,1)S(1)} %slice.59), channel_id=1, source_target_pairs={{0,2},{2,4},{4,6},{6,7},{7,5},{5,3},{3,1},{1,0},{8,10},{10,12},{12... | collective-permute-start | bytes 1474568 | tf_op jit(solution)/shard_map/ppermute | solution.py:508
  182.7 27.0 %collective-permute-start.13 = (bf16[192,3072]{1,0:T(8,128)(2,1)}, bf16[192,3072]{1,0:T(8,128)(2,1)}, u32[]{:S(2)}, u32[]{:S(2)}) collective-permute-start(bf16[192,3072]{1,0:T(8,128)(2,1)} %get-tuple-element.193.refs_6_), channel_id=1, source_target_pairs={{0,2},{2,4},{4,6},{6,7},{7,5},{5,3},{3,1},{1,0},{8,10},{10,12},{12... | collective-permute-start | bytes 3538952 | tf_op jit(solution)/shard_map/ppermute | solution.py:508
  184.2 25.5 %collective-permute-start.14 = (bf16[192,3072]{1,0:T(8,128)(2,1)}, bf16[192,3072]{1,0:T(8,128)(2,1)}, u32[]{:S(2)}, u32[]{:S(2)}) collective-permute-start(bf16[192,3072]{1,0:T(8,128)(2,1)} %get-tuple-element.194.refs_7_), channel_id=1, source_target_pairs={{2,0},{4,2},{6,4},{7,6},{5,7},{3,5},{1,3},{0,1},{10,8},{12,10},{14... | collective-permute-start | bytes 3538952 | tf_op jit(solution)/shard_map/ppermute | solution.py:511
  209.7 23.8 %all-to-all-start.1 = ((bf16[8,192,256]{2,1,0:T(8,128)(2,1)}), bf16[8,192,256]{2,1,0:T(8,128)(2,1)S(1)}, u32[]{:S(2)}, u32[]{:S(2)}) async-start(bf16[8,192,256]{2,1,0:T(8,128)(2,1)} %get-tuple-element.205), calls=%async_computation.2 | async-start | bytes 1572864 | tf_op jit(solution)/shard_map/all_to_all | solution.py:560
  213.5 34.9 %collective-permute-start.15 = (bf16[192,3072]{1,0:T(8,128)(2,1)}, bf16[192,3072]{1,0:T(8,128)(2,1)}, u32[]{:S(2)}, u32[]{:S(2)}) collective-permute-start(bf16[192,3072]{1,0:T(8,128)(2,1)} %get-tuple-element.203.refs_8_), channel_id=1, source_target_pairs={{0,2},{2,4},{4,6},{6,7},{7,5},{5,3},{3,1},{1,0},{8,10},{10,12},{12... | collective-permute-start | bytes 3538952 | tf_op jit(solution)/shard_map/ppermute | solution.py:508
  215.5 34.9 %collective-permute-start.16 = (bf16[192,3072]{1,0:T(8,128)(2,1)}, bf16[192,3072]{1,0:T(8,128)(2,1)}, u32[]{:S(2)}, u32[]{:S(2)}) collective-permute-start(bf16[192,3072]{1,0:T(8,128)(2,1)} %get-tuple-element.204.refs_9_), channel_id=1, source_target_pairs={{2,0},{4,2},{6,4},{7,6},{5,7},{3,5},{1,3},{0,1},{10,8},{12,10},{14... | collective-permute-start | bytes 3538952 | tf_op jit(solution)/shard_map/ppermute | solution.py:511
  241.2 12.2 %collective-permute-start.17 = (bf16[256,1536]{1,0:T(8,128)(2,1)S(1)}, bf16[256,1536]{1,0:T(8,128)(2,1)}, u32[]{:S(2)}, u32[]{:S(2)}) collective-permute-start(bf16[256,1536]{1,0:T(8,128)(2,1)S(1)} %fusion.5.refs_2_), channel_id=1, source_target_pairs={{0,16},{8,24},{16,0},{24,8},{1,17},{9,25},{17,1},{25,9},{2,18},{10... | collective-permute-start | bytes 2359304 | tf_op jit(solution)/shard_map/ppermute | solution.py:538
  253.4 21.2 %collective-permute-start.18 = (bf16[256,1536]{1,0:T(8,128)(2,1)}, bf16[256,1536]{1,0:T(8,128)(2,1)S(1)}, u32[]{:S(2)}, u32[]{:S(2)}) collective-permute-start(bf16[256,1536]{1,0:T(8,128)(2,1)} %get-tuple-element.208.refs_0_), channel_id=1, source_target_pairs={{0,8},{8,0},{16,24},{24,16},{1,9},{9,1},{17,25},{25,17},{2,10},{10... | collective-permute-start | bytes 2359304 | tf_op jit(solution)/shard_map/ppermute | solution.py:538
  253.5 21.1 %collective-permute-start.19 = (bf16[256,1536]{1,0:T(8,128)(2,1)}, bf16[256,1536]{1,0:T(8,128)(2,1)S(1)}, u32[]{:S(2)}, u32[]{:S(2)}) collective-permute-start(bf16[256,1536]{1,0:T(8,128)(2,1)} %get-tuple-element.209.refs_1_), channel_id=1, source_target_pairs={{0,8},{8,0},{16,24},{24,16},{1,9},{9,1},{17,25},{25,17},{2,10},{10... | collective-permute-start | bytes 2359304 | tf_op jit(solution)/shard_map/ppermute | solution.py:538
  255.1 15.7 %collective-permute-start.20 = (bf16[96,3072]{1,0:T(8,128)(2,1)S(1)}, bf16[96,3072]{1,0:T(8,128)(2,1)S(1)}, u32[]{:S(2)}, u32[]{:S(2)}) collective-permute-start(bf16[96,3072]{1,0:T(8,128)(2,1)S(1)} %slice.63), channel_id=1, source_target_pairs={{0,2},{2,4},{4,6},{6,7},{7,5},{5,3},{3,1},{1,0},{8,10},{10,12},{12... | collective-permute-start | bytes 1769480 | tf_op jit(solution)/shard_map/ppermute | solution.py:508
  259.1 15.5 %collective-permute-start.21 = (bf16[96,3072]{1,0:T(8,128)(2,1)S(1)}, bf16[96,3072]{1,0:T(8,128)(2,1)S(1)}, u32[]{:S(2)}, u32[]{:S(2)}) collective-permute-start(bf16[96,3072]{1,0:T(8,128)(2,1)S(1)} %slice.64), channel_id=1, source_target_pairs={{2,0},{4,2},{6,4},{7,6},{5,7},{3,5},{1,3},{0,1},{10,8},{12,10},{14... | collective-permute-start | bytes 1769480 | tf_op jit(solution)/shard_map/ppermute | solution.py:511
  314.9 19.6 %collective-permute-start.24 = (bf16[96,3072]{1,0:T(8,128)(2,1)S(1)}, bf16[96,3072]{1,0:T(8,128)(2,1)S(1)}, u32[]{:S(2)}, u32[]{:S(2)}) collective-permute-start(bf16[96,3072]{1,0:T(8,128)(2,1)S(1)} %get-tuple-element.221), channel_id=1, source_target_pairs={{0,2},{2,4},{4,6},{6,7},{7,5},{5,3},{3,1},{1,0},{8,10},{10,12},{12... | collective-permute-start | bytes 1769480 | tf_op jit(solution)/shard_map/ppermute | solution.py:508
  315.3 19.3 %collective-permute-start.25 = (bf16[96,3072]{1,0:T(8,128)(2,1)S(1)}, bf16[96,3072]{1,0:T(8,128)(2,1)S(1)}, u32[]{:S(2)}, u32[]{:S(2)}) collective-permute-start(bf16[96,3072]{1,0:T(8,128)(2,1)S(1)} %get-tuple-element.222), channel_id=1, source_target_pairs={{2,0},{4,2},{6,4},{7,6},{5,7},{3,5},{1,3},{0,1},{10,8},{12,10},{14... | collective-permute-start | bytes 1769480 | tf_op jit(solution)/shard_map/ppermute | solution.py:511
  317.2 21.4 %collective-permute-start.23 = (bf16[256,1536]{1,0:T(8,128)(2,1)S(1)}, bf16[256,1536]{1,0:T(8,128)(2,1)S(1)}, u32[]{:S(2)}, u32[]{:S(2)}) collective-permute-start(bf16[256,1536]{1,0:T(8,128)(2,1)S(1)} %copy-done.109), channel_id=1, source_target_pairs={{0,16},{8,24},{16,0},{24,8},{1,17},{9,25},{17,1},{25,9},{2,18},{10... | collective-permute-start | bytes 2359304 | tf_op jit(solution)/shard_map/ppermute | solution.py:538
  348.9 24.2 %all-to-all-start.2 = ((bf16[8,192,256]{2,1,0:T(8,128)(2,1)}), bf16[8,192,256]{2,1,0:T(8,128)(2,1)}, u32[]{:S(2)}, u32[]{:S(2)}) async-start(bf16[8,192,256]{2,1,0:T(8,128)(2,1)} %get-tuple-element.230), calls=%async_computation.3 | async-start | bytes 1572864 | tf_op jit(solution)/shard_map/all_to_all | solution.py:560
  353.1 201.5 %reduce-scatter.9.cloned.1.call-start = ((), (), s32[]{:S(2)}) async-start(), calls=%async_computation.18 | async-start | bytes 5898240 | tf_op jit(solution)/shard_map/reduce_scatter | solution.py:1816
  373.1 222.0 %reduce-scatter.7.cloned.1.call-start = ((), (), s32[]{:S(2)}) async-start(), calls=%async_computation.17 | async-start | bytes 3932160 | tf_op jit(solution)/shard_map/reduce_scatter | solution.py:1828
  373.2 39.1 %collective-permute-start.26 = (bf16[192,3072]{1,0:T(8,128)(2,1)}, bf16[192,3072]{1,0:T(8,128)(2,1)S(1)}, u32[]{:S(2)}, u32[]{:S(2)}) collective-permute-start(bf16[192,3072]{1,0:T(8,128)(2,1)} %get-tuple-element.225), channel_id=1, source_target_pairs={{0,2},{2,4},{4,6},{6,7},{7,5},{5,3},{3,1},{1,0},{8,10},{10,12},{12... | collective-permute-start | bytes 3538952 | tf_op jit(solution)/shard_map/ppermute | solution.py:508
  373.5 38.8 %collective-permute-start.27 = (bf16[192,3072]{1,0:T(8,128)(2,1)}, bf16[192,3072]{1,0:T(8,128)(2,1)}, u32[]{:S(2)}, u32[]{:S(2)}) collective-permute-start(bf16[192,3072]{1,0:T(8,128)(2,1)} %get-tuple-element.226), channel_id=1, source_target_pairs={{2,0},{4,2},{6,4},{7,6},{5,7},{3,5},{1,3},{0,1},{10,8},{12,10},{14... | collective-permute-start | bytes 3538952 | tf_op jit(solution)/shard_map/ppermute | solution.py:511
  415.5 72.4 %all-to-all-start.3 = ((bf16[8,192,512]{2,1,0:T(8,128)(2,1)}), bf16[8,192,512]{2,1,0:T(8,128)(2,1)}, u32[]{:S(2)}, u32[]{:S(2)}) async-start(bf16[8,192,512]{2,1,0:T(8,128)(2,1)} %broadcast_in_dim.27), calls=%async_computation.4 | async-start | bytes 3145728 | tf_op jit(solution)/shard_map/all_to_all | solution.py:554
  419.9 204.2 %reduce-scatter.11.cloned.1.call-start = ((), (), s32[]{:S(2)}) async-start(), calls=%async_computation.19 | async-start | bytes 1327104 | tf_op jit(solution)/shard_map/reduce_scatter | solution.py:1817
  422.7 61.0 %collective-permute-start.30 = (bf16[192,3072]{1,0:T(8,128)(2,1)S(1)}, bf16[192,3072]{1,0:T(8,128)(2,1)S(1)}, u32[]{:S(2)}, u32[]{:S(2)}) collective-permute-start(bf16[192,3072]{1,0:T(8,128)(2,1)S(1)} %get-tuple-element.254), channel_id=1, source_target_pairs={{0,2},{2,4},{4,6},{6,7},{7,5},{5,3},{3,1},{1,0},{8,10},{10,12},{12... | collective-permute-start | bytes 3538952 | tf_op jit(solution)/shard_map/ppermute | solution.py:508
  424.8 58.9 %collective-permute-start.31 = (bf16[192,3072]{1,0:T(8,128)(2,1)S(1)}, bf16[192,3072]{1,0:T(8,128)(2,1)S(1)}, u32[]{:S(2)}, u32[]{:S(2)}) collective-permute-start(bf16[192,3072]{1,0:T(8,128)(2,1)S(1)} %get-tuple-element.255), channel_id=1, source_target_pairs={{2,0},{4,2},{6,4},{7,6},{5,7},{3,5},{1,3},{0,1},{10,8},{12,10},{14... | collective-permute-start | bytes 3538952 | tf_op jit(solution)/shard_map/ppermute | solution.py:511
  425.0 53.1 %collective-permute-start.28 = (bf16[128,1536]{1,0:T(8,128)(2,1)S(1)}, bf16[128,1536]{1,0:T(8,128)(2,1)S(1)}, u32[]{:S(2)}, u32[]{:S(2)}) collective-permute-start(bf16[128,1536]{1,0:T(8,128)(2,1)S(1)} %copy-done.80), channel_id=1, source_target_pairs={{0,2},{2,4},{4,6},{6,7},{7,5},{5,3},{3,1},{1,0},{8,10},{10,12},{12... | collective-permute-start | bytes 1179656 | tf_op jit(solution)/shard_map/ppermute | solution.py:508
  426.9 53.5 %collective-permute-start.29 = (bf16[128,1536]{1,0:T(8,128)(2,1)S(1)}, bf16[128,1536]{1,0:T(8,128)(2,1)S(1)}, u32[]{:S(2)}, u32[]{:S(2)}) collective-permute-start(bf16[128,1536]{1,0:T(8,128)(2,1)S(1)} %copy-done.82), channel_id=1, source_target_pairs={{2,0},{4,2},{6,4},{7,6},{5,7},{3,5},{1,3},{0,1},{10,8},{12,10},{14... | collective-permute-start | bytes 1179656 | tf_op jit(solution)/shard_map/ppermute | solution.py:511
  487.9 59.1 %collective-permute-start.39 = (bf16[1536,512]{1,0:T(8,128)(2,1)}, bf16[1536,512]{1,0:T(8,128)(2,1)}, u32[]{:S(2)}, u32[]{:S(2)}) collective-permute-start(bf16[1536,512]{1,0:T(8,128)(2,1)} %get-tuple-element.274.refs_6_), channel_id=1, source_target_pairs={{0,16},{8,24},{16,0},{24,8},{1,17},{9,25},{17,1},{25,9},{2,18},{10... | collective-permute-start | bytes 4718600 | tf_op jit(solution)/shard_map/ppermute | solution.py:538
  488.2 12.4 %collective-permute-start.36 = (bf16[8,48,576]{2,1,0:T(8,128)(2,1)}, bf16[8,48,576]{2,1,0:T(8,128)(2,1)S(1)}, u32[]{:S(2)}, u32[]{:S(2)}) collective-permute-start(bf16[8,48,576]{2,1,0:T(8,128)(2,1)} %get-tuple-element.271), channel_id=1, source_target_pairs={{0,8},{8,0},{16,24},{24,16},{1,9},{9,1},{17,25},{25,17},{2,10},{10... | collective-permute-start | bytes 1327112 | tf_op jit(solution)/shard_map/ppermute | solution.py:538
  488.4 28.3 %collective-permute-start.32 = (bf16[256,1536]{1,0:T(8,128)(2,1)}, bf16[256,1536]{1,0:T(8,128)(2,1)S(1)}, u32[]{:S(2)}, u32[]{:S(2)}) collective-permute-start(bf16[256,1536]{1,0:T(8,128)(2,1)} %get-tuple-element.264), channel_id=1, source_target_pairs={{0,2},{2,4},{4,6},{6,7},{7,5},{5,3},{3,1},{1,0},{8,10},{10,12},{12... | collective-permute-start | bytes 2359304 | tf_op jit(solution)/shard_map/ppermute | solution.py:508
  498.5 47.7 %collective-permute-start.34 = (bf16[192,3072]{1,0:T(8,128)(2,1)}, bf16[192,3072]{1,0:T(8,128)(2,1)S(1)}, u32[]{:S(2)}, u32[]{:S(2)}) collective-permute-start(bf16[192,3072]{1,0:T(8,128)(2,1)} %get-tuple-element.268), channel_id=1, source_target_pairs={{0,2},{2,4},{4,6},{6,7},{7,5},{5,3},{3,1},{1,0},{8,10},{10,12},{12... | collective-permute-start | bytes 3538952 | tf_op jit(solution)/shard_map/ppermute | solution.py:508
  498.6 48.4 %collective-permute-start.35 = (bf16[192,3072]{1,0:T(8,128)(2,1)}, bf16[192,3072]{1,0:T(8,128)(2,1)}, u32[]{:S(2)}, u32[]{:S(2)}) collective-permute-start(bf16[192,3072]{1,0:T(8,128)(2,1)} %get-tuple-element.269), channel_id=1, source_target_pairs={{2,0},{4,2},{6,4},{7,6},{5,7},{3,5},{1,3},{0,1},{10,8},{12,10},{14... | collective-permute-start | bytes 3538952 | tf_op jit(solution)/shard_map/ppermute | solution.py:511
  500.5 43.0 %collective-permute-start.33 = (bf16[256,1536]{1,0:T(8,128)(2,1)}, bf16[256,1536]{1,0:T(8,128)(2,1)S(1)}, u32[]{:S(2)}, u32[]{:S(2)}) collective-permute-start(bf16[256,1536]{1,0:T(8,128)(2,1)} %get-tuple-element.265), channel_id=1, source_target_pairs={{2,0},{4,2},{6,4},{7,6},{5,7},{3,5},{1,3},{0,1},{10,8},{12,10},{14... | collective-permute-start | bytes 2359304 | tf_op jit(solution)/shard_map/ppermute | solution.py:511
  516.7 29.5 %collective-permute-start.38 = (bf16[8,48,576]{2,1,0:T(8,128)(2,1)S(1)}, bf16[8,48,576]{2,1,0:T(8,128)(2,1)S(1)}, u32[]{:S(2)}, u32[]{:S(2)}) collective-permute-start(bf16[8,48,576]{2,1,0:T(8,128)(2,1)S(1)} %add_convert_fusion.2), channel_id=1, source_target_pairs={{0,16},{8,24},{16,0},{24,8},{1,17},{9,25},{17,1},{25,9},{2,18},{10... | collective-permute-start | bytes 1327112 | tf_op jit(solution)/shard_map/ppermute | solution.py:538
  548.0 47.0 %collective-permute-start.43 = (bf16[1536,512]{1,0:T(8,128)(2,1)}, bf16[1536,512]{1,0:T(8,128)(2,1)}, u32[]{:S(2)}, u32[]{:S(2)}) collective-permute-start(bf16[1536,512]{1,0:T(8,128)(2,1)} %get-tuple-element.283.refs_5_), channel_id=1, source_target_pairs={{0,8},{8,0},{16,24},{24,16},{1,9},{9,1},{17,25},{25,17},{2,10},{10... | collective-permute-start | bytes 4718600 | tf_op jit(solution)/shard_map/ppermute | solution.py:538
  548.0 47.1 %collective-permute-start.44 = (bf16[1536,512]{1,0:T(8,128)(2,1)}, bf16[1536,512]{1,0:T(8,128)(2,1)}, u32[]{:S(2)}, u32[]{:S(2)}) collective-permute-start(bf16[1536,512]{1,0:T(8,128)(2,1)} %get-tuple-element.284.refs_6_), channel_id=1, source_target_pairs={{0,8},{8,0},{16,24},{24,16},{1,9},{9,1},{17,25},{25,17},{2,10},{10... | collective-permute-start | bytes 4718600 | tf_op jit(solution)/shard_map/ppermute | solution.py:538
  552.9 42.2 %collective-permute-start.42 = (bf16[192,3072]{1,0:T(8,128)(2,1)}, bf16[192,3072]{1,0:T(8,128)(2,1)}, u32[]{:S(2)}, u32[]{:S(2)}) collective-permute-start(bf16[192,3072]{1,0:T(8,128)(2,1)} %shard_map.326.refs_2_), channel_id=1, source_target_pairs={{0,16},{8,24},{16,0},{24,8},{1,17},{9,25},{17,1},{25,9},{2,18},{10... | collective-permute-start | bytes 3538952 | tf_op jit(solution)/shard_map/ppermute | solution.py:538
  554.6 27.3 %collective-permute-start.40 = (bf16[256,1536]{1,0:T(8,128)(2,1)}, bf16[256,1536]{1,0:T(8,128)(2,1)}, u32[]{:S(2)}, u32[]{:S(2)}) collective-permute-start(bf16[256,1536]{1,0:T(8,128)(2,1)} %get-tuple-element.275), channel_id=1, source_target_pairs={{0,2},{2,4},{4,6},{6,7},{7,5},{5,3},{3,1},{1,0},{8,10},{10,12},{12... | collective-permute-start | bytes 2359304 | tf_op jit(solution)/shard_map/ppermute | solution.py:508
  555.0 29.5 %collective-permute-start.41 = (bf16[256,1536]{1,0:T(8,128)(2,1)}, bf16[256,1536]{1,0:T(8,128)(2,1)}, u32[]{:S(2)}, u32[]{:S(2)}) collective-permute-start(bf16[256,1536]{1,0:T(8,128)(2,1)} %get-tuple-element.276), channel_id=1, source_target_pairs={{2,0},{4,2},{6,4},{7,6},{5,7},{3,5},{1,3},{0,1},{10,8},{12,10},{14... | collective-permute-start | bytes 2359304 | tf_op jit(solution)/shard_map/ppermute | solution.py:511
  558.6 36.5 %all-to-all-start.4 = ((bf16[8,48,576]{2,1,0:T(8,128)(2,1)}), bf16[8,48,576]{2,1,0:T(8,128)(2,1)S(1)}, u32[]{:S(2)}, u32[]{:S(2)}) async-start(bf16[8,48,576]{2,1,0:T(8,128)(2,1)} %add_convert_fusion.1), calls=%async_computation.5 | async-start | bytes 983040 | tf_op jit(solution)/shard_map/all_to_all | solution.py:560
  595.8 11.6 %collective-permute-start.48 = (bf16[192,3072]{1,0:T(8,128)(2,1)}, bf16[192,3072]{1,0:T(8,128)(2,1)S(1)}, u32[]{:S(2)}, u32[]{:S(2)}) collective-permute-start(bf16[192,3072]{1,0:T(8,128)(2,1)} %get-tuple-element.294.refs_0_), channel_id=1, source_target_pairs={{0,8},{8,0},{16,24},{24,16},{1,9},{9,1},{17,25},{25,17},{2,10},{10... | collective-permute-start | bytes 3538952 | tf_op jit(solution)/shard_map/ppermute | solution.py:538
  598.0 21.3 %collective-permute-start.45 = (bf16[256,1536]{1,0:T(8,128)(2,1)}, bf16[256,1536]{1,0:T(8,128)(2,1)}, u32[]{:S(2)}, u32[]{:S(2)}) collective-permute-start(bf16[256,1536]{1,0:T(8,128)(2,1)} %get-tuple-element.286), channel_id=1, source_target_pairs={{0,2},{2,4},{4,6},{6,7},{7,5},{5,3},{3,1},{1,0},{8,10},{10,12},{12... | collective-permute-start | bytes 2359304 | tf_op jit(solution)/shard_map/ppermute | solution.py:508
  598.1 23.8 %collective-permute-start.46 = (bf16[256,1536]{1,0:T(8,128)(2,1)}, bf16[256,1536]{1,0:T(8,128)(2,1)}, u32[]{:S(2)}, u32[]{:S(2)}) collective-permute-start(bf16[256,1536]{1,0:T(8,128)(2,1)} %get-tuple-element.287), channel_id=1, source_target_pairs={{2,0},{4,2},{6,4},{7,6},{5,7},{3,5},{1,3},{0,1},{10,8},{12,10},{14... | collective-permute-start | bytes 2359304 | tf_op jit(solution)/shard_map/ppermute | solution.py:511
  600.1 14.0 %collective-permute-start.47 = (bf16[8,48,576]{2,1,0:T(8,128)(2,1)}, bf16[8,48,576]{2,1,0:T(8,128)(2,1)}, u32[]{:S(2)}, u32[]{:S(2)}) collective-permute-start(bf16[8,48,576]{2,1,0:T(8,128)(2,1)} %get-tuple-element.292.refs_6_), channel_id=1, source_target_pairs={{0,16},{8,24},{16,0},{24,8},{1,17},{9,25},{17,1},{25,9},{2,18},{10... | collective-permute-start | bytes 1327112 | tf_op jit(solution)/shard_map/ppermute | solution.py:538
  631.5 15.4 %all-to-all-start.5 = ((f32[8,2,1155]{2,1,0:T(2,128)}), f32[8,2,1155]{2,1,0:T(2,128)}, u32[]{:S(2)}, u32[]{:S(2)}) async-start(f32[8,2,1155]{2,1,0:T(2,128)} %get-tuple-element.311), calls=%async_computation.9 | async-start | bytes 163840 | tf_op jit(solution)/shard_map/all_to_all | solution.py:560
  646.4 32.5 %collective-permute-start.53 = (bf16[192,384]{1,0:T(8,128)(2,1)S(1)}, bf16[192,384]{1,0:T(8,128)(2,1)}, u32[]{:S(2)}, u32[]{:S(2)}) collective-permute-start(bf16[192,384]{1,0:T(8,128)(2,1)S(1)} %copy-done.55), channel_id=1, source_target_pairs={{0,8},{8,0},{16,24},{24,16},{1,9},{9,1},{17,25},{25,17},{2,10},{10... | collective-permute-start | bytes 442376 | tf_op jit(solution)/shard_map/ppermute | solution.py:538
  646.4 34.6 %collective-permute-start.50 = (bf16[8,48,576]{2,1,0:T(8,128)(2,1)S(1)}, bf16[8,48,576]{2,1,0:T(8,128)(2,1)S(1)}, u32[]{:S(2)}, u32[]{:S(2)}) collective-permute-start(bf16[8,48,576]{2,1,0:T(8,128)(2,1)S(1)} %copy-done.13), channel_id=1, source_target_pairs={{0,8},{8,0},{16,24},{24,16},{1,9},{9,1},{17,25},{25,17},{2,10},{10... | collective-permute-start | bytes 1327112 | tf_op jit(solution)/shard_map/ppermute | solution.py:538
  646.9 34.1 %collective-permute-start.51 = (bf16[8,48,576]{2,1,0:T(8,128)(2,1)}, bf16[8,48,576]{2,1,0:T(8,128)(2,1)}, u32[]{:S(2)}, u32[]{:S(2)}) collective-permute-start(bf16[8,48,576]{2,1,0:T(8,128)(2,1)} %get-tuple-element.316.refs_1_), channel_id=1, source_target_pairs={{0,8},{8,0},{16,24},{24,16},{1,9},{9,1},{17,25},{25,17},{2,10},{10... | collective-permute-start | bytes 1327112 | tf_op jit(solution)/shard_map/ppermute | solution.py:538
  653.9 25.0 %collective-permute-start.54 = (bf16[192,384]{1,0:T(8,128)(2,1)}, bf16[192,384]{1,0:T(8,128)(2,1)}, u32[]{:S(2)}, u32[]{:S(2)}) collective-permute-start(bf16[192,384]{1,0:T(8,128)(2,1)} %collective-permute-done.52.refs_1_), channel_id=1, source_target_pairs={{0,8},{8,0},{16,24},{24,16},{1,9},{9,1},{17,25},{25,17},{2,10},{10... | collective-permute-start | bytes 442376 | tf_op jit(solution)/shard_map/ppermute | solution.py:538
  658.1 13.0 %all-to-all-start.7 = ((f32[8,2,1024]{2,1,0:T(2,128)}), f32[8,2,1024]{2,1,0:T(2,128)}, u32[]{:S(2)}, u32[]{:S(2)}) async-start(f32[8,2,1024]{2,1,0:T(2,128)} %broadcast_in_dim.62), calls=%async_computation.11 | async-start | bytes 131072 | tf_op jit(solution)/shard_map/all_to_all | solution.py:554
  671.1 13.5 %all-to-all-start.6 = ((bf16[8,2,16,512]{3,2,1,0:T(8,128)(2,1)}), bf16[8,2,16,512]{3,2,1,0:T(8,128)(2,1)}, u32[]{:S(2)}, u32[]{:S(2)}) async-start(bf16[8,2,16,512]{3,2,1,0:T(8,128)(2,1)} %get-tuple-element.313), calls=%async_computation.10 | async-start | bytes 524288 | tf_op jit(solution)/shard_map/all_to_all | solution.py:560
  (136 other events, 762.4 us)
Sparse Core Ops, SparseCore 0:
  64.3 25.2 all-gather.3
  97.2 28.1 all-gather.5
  182.8 36.6 all-gather.7
  373.2 45.7 reduce-scatter.8
  422.0 38.0 reduce-scatter.6
  554.7 69.3 reduce-scatter.10
Sparse Core Ops, SparseCore 1:
  94.2 72.8 reduce-scatter.4

commit v4 on v3

--- a/solution.py
+++ b/solution.py
@@ -459,7 +459,7 @@
 MIN_CLIP = 1024
 N_DP = 4
 OFFSETS = (0, 2, 1, 3)
-VMEM_BYTES = 48 * 1024 * 1024
+VMEM_BYTES = 62 * 1024 * 1024
 NT = (((1,), (1,)), ((), ()))
 TN = (((0,), (0,)), ((), ()))
 F32 = jnp.float32
@@ -479,6 +479,7 @@
         out_specs=[spec] * len(arrays),
         out_shape=[jax.ShapeDtypeStruct(a.shape, a.dtype) for a in arrays],
         input_output_aliases={i: i for i in range(len(arrays))},
+        compiler_params=pltpu.CompilerParams(vmem_limit_bytes=VMEM_BYTES),
         cost_estimate=pl.CostEstimate(flops=0, bytes_accessed=0, transcendentals=0),
     )(*arrays)
     return jax.tree.unflatten(shape, out)
@@ -1760,7 +1761,7 @@
     normed_two = middle * inverse_two
     ffn_in = (normed_two * (1.0 + by_row(scale_two)) + by_row(shift_two)).astype(BF16)
     ffn_far = across(ffn_in, 2)
-    weight_flow.live, ffn_in, ffn_far = ordered((weight_flow.live, ffn_in, ffn_far))
+    weight_flow.live, ffn_in = ordered((weight_flow.live, ffn_in))
     weight_flow.keep()
 
     weight_flow.send()
@@ -1840,8 +1841,22 @@
     qkv_own, qkv_far = sum_packs_near(qkv_terms)
     qkv_far = across(qkv_far, 2)
     cap_far = across(cap_all, 2)
-    token_back, unit_back, qkv_own, qkv_far, cap_all, cap_far = ordered(
-        (add_step(1, terms, token_back), unit_back, qkv_own, qkv_far, cap_all, cap_far)
+    caption_grad = dot(cap_all[:, : CLIPS * CAP], w_text_key, (((0,), (1,)), ((), ()))) + dot(
+        cap_all[:, CLIPS * CAP :], w_text_value, (((0,), (1,)), ((), ()))
+    )
+    caption_grad = caption_grad.astype(BF16).reshape(CLIPS, size, -1, text_rows)
+    caption_grad = jnp.transpose(caption_grad, (1, 0, 2, 3))
+    caption_grad = exchange(caption_grad)
+    token_back, unit_back, qkv_own, qkv_far, cap_all, cap_far, caption_grad = ordered(
+        (
+            add_step(1, terms, token_back),
+            unit_back,
+            qkv_own,
+            qkv_far,
+            cap_all,
+            cap_far,
+            caption_grad,
+        )
     )
 
     token_back = send(token_back)
@@ -1849,18 +1864,13 @@
     unit_far = across(unit_home, 2)
     qkv_home = exchange((qkv_own + qkv_far.astype(F32)).astype(BF16))
     cap_blocks = [cap_all, cap_far, across(cap_all, 1), across(cap_far, 1)]
-    token_back, unit_home, unit_far, qkv_home, cap_blocks, branch = ordered(
-        (add_step(2, terms, token_back), unit_home, unit_far, qkv_home, cap_blocks, branch)
+    token_back, unit_home, unit_far, cap_blocks, branch, out_home = ordered(
+        (add_step(2, terms, token_back), unit_home, unit_far, cap_blocks, branch, out_home)
     )
     cap_all = cap_blocks[0]
 
     token_back = send(token_back)
     qkv_far = across(qkv_home, 2)
-    caption_grad = dot(cap_all[:, : CLIPS * CAP], w_text_key, (((0,), (1,)), ((), ()))) + dot(
-        cap_all[:, CLIPS * CAP :], w_text_value, (((0,), (1,)), ((), ()))
-    )
-    caption_grad = caption_grad.astype(BF16).reshape(CLIPS, size, -1, text_rows)
-    caption_grad = jnp.transpose(caption_grad, (1, 0, 2, 3))
     d_text_key, d_text_value = text_grads(ring, caption_all, cap_blocks)
     shape = lambda *dims: jax.ShapeDtypeStruct(dims, F32)
     unit_blocks = [unit_home, unit_far, across(unit_home, 1), across(unit_far, 1)]
@@ -1869,8 +1879,8 @@
     )
     result = (middle + by_row(gate_two) * branch.astype(F32)).astype(BF16)
     sums = [*sums, clip_sums(out_grad * branch.astype(F32))]
-    token_back, sums, qkv_home, qkv_far, out_home, result, d_down, caption_grad = ordered(
-        (token_back, sums, qkv_home, qkv_far, out_home, result, d_down, caption_grad)
+    token_back, sums, qkv_home, qkv_far, out_home, result, d_down = ordered(
+        (token_back, sums, qkv_home, qkv_far, out_home, result, d_down)
     )
 
     inputs_grad, own_sums = finish_tokens(terms, token_back, middle_grad, tokens[0], scale_one)
@@ -1882,7 +1892,7 @@
     mod_terms = jnp.concatenate([mod_terms, gate_own], axis=2)
     mod_terms, qkv_home, qkv_far, out_home = ordered((mod_terms, qkv_home, qkv_far, out_home))
 
-    arrived, caption_grad = ordered((exchange(mod_terms), caption_grad))
+    arrived = exchange(mod_terms)
     qkv_blocks = [qkv_home, qkv_far, across(qkv_home, 1), across(qkv_far, 1)]
     out_blocks = gather_packs(out_home)
 
@@ -1894,7 +1904,7 @@
     sigmoid_cond = jax.nn.sigmoid(cond_row)
     cond_grad = cond_sum * sigmoid_cond * (1.0 + cond_row * (1.0 - sigmoid_cond))
     both = jnp.concatenate([cond_act.astype(F32), mod_low.astype(F32), gate_all], axis=1)
-    both_all = gather_small(both, "dp").reshape(N_DP * CLIPS, -1)
+    both_all = jnp.concatenate(gather_packs(both))
     cond_size = cond_act.shape[1]
     cond_all = both_all[:, :cond_size].astype(BF16)
     mod_all = both_all[:, cond_size : cond_size + own_mod].astype(BF16)
@@ -1904,7 +1914,6 @@
         1.0 - tanh_gate * tanh_gate
     )
 
-    caption_grad = exchange(caption_grad)
     caption_grad = (
         jnp.transpose(caption_grad, (1, 2, 0, 3)).reshape(CLIPS, -1, size * text_rows).astype(F32)
     )

time: 706 us -> 669 us (0.948)
  local copies, waits for them, and re-layouts: 79.3 us -> 24.9 us
  Pallas kernels: 170 us -> 205 us
  waiting for transfers between devices: 272 us -> 259 us
  matrix products: 20.8 us -> 28.9 us
  starting transfers between devices: 106 us -> 98.6 us
    unnamed x262 -> x102, local copies, waits for them, and re-layouts: 65.9 us -> 12.7 us
    ppermute x16, waiting for transfers between devices: 148 us -> 132 us  [send_up(): return [lax.ppermute(v, 'sp', self.up) for v in values]]
    dot_general x8, matrix products: 20.8 us -> 28.9 us  [dot(): return lax.dot_general(left, right, dims, preferred_element_type=F32)]
    pallas_call x6, Pallas kernels: 13.2 us -> 20.7 us  [add_received(): pl.pallas_call(kernel, grid=(1,), in_specs=[spec(rows, index[0]), spec(ro...]
    all_to_all x3 -> x2, starting transfers between devices: 14.3 us -> 7.66 us  [gather_small(): lax.all_to_all(jnp.broadcast_to(value[None], (size,) + value.shape), axis...]
    ppermute x23 -> x26, waiting for transfers between devices: 16.3 us -> 20.9 us  [across(): return lax.ppermute(value, 'dp', [(i, i ^ bit) for i in range(N_DP)])]
  transfers between devices with their start and end apart: 71 -> 73, of which waited for: 29 -> 32; matrix products, arithmetic and copies ran while one was open for 7% -> 8% of each run, Pallas kernels for 19% -> 24%
where the time goes in v4:
time: 669 us; the launch traced here: 659 us
  waiting for transfers between devices  259 us (39%)
  Pallas kernels  205 us (31%)
  starting transfers between devices  98.6 us (15%)
  matrix products  28.9 us (4%)
  other arithmetic  26.5 us (4%)
  local copies, waits for them, and re-layouts  24.9 us (4%)
  between operations  16.7 us (2%)
    ppermute x16, waiting for transfers between devices, send_up(): return [lax.ppermute(v, 'sp', self.up) for v in values]  132 us
    ppermute x16, waiting for transfers between devices, send_down(): return [lax.ppermute(v, 'sp', self.down) for v in values]  74.5 us
    ppermute x16, starting transfers between devices, send_up(): return [lax.ppermute(v, 'sp', self.up) for v in values]  36.1 us
    all_to_all x6, waiting for transfers between devices, exchange(): return lax.all_to_all(value, 'sp', 0, 0, tiled=True)  29.4 us
    dot_general x8, matrix products, dot(): return lax.dot_general(left, right, dims, preferred_element_type=F32)  28.9 us
    all_to_all x6, starting transfers between devices, exchange(): return lax.all_to_all(value, 'sp', 0, 0, tiled=True)  27.5 us
    pallas_call x1, Pallas kernels, feed(): pl.pallas_call(functools.partial(feed_kernel, size=ring.size, places=plac...  27 us
    pallas_call x1, Pallas kernels, attend_back(): pl.pallas_call(functools.partial(attend_back_kernel, block=length // 2),...  24.4 us
  transfers between devices with their start and end apart: 73, of which 32 were waited for; matrix products, arithmetic and copies ran while one was open for 8% of the time, Pallas kernels for 24%

profile of v4, /device:TPU:0, one launch (start us, length us, event | category | flops | bytes accessed | tf_op | source)
XLA Modules:
  0.0 659.1 jit_solution(2596066822473176379)
XLA Ops:
  10.4 2.7 convolution_add_fusion.mod_ref
  13.0 2.6 shard_map.289
  15.7 7.4 %all-to-all-start = ((bf16[8,96,576]{2,1,0:T(8,128)(2,1)}), bf16[8,96,576]{2,1,0:T(8,128)(2,1)S(1)}, u32[]{:S(2)}, u32[]{:S(2)}) async-start(bf16[8,96,576]{2,1,0:T(8,128)(2,1)} %shard_map.289), calls=%async_computation | async-start | bytes 1966080 | tf_op jit(solution)/shard_map/all_to_all | solution.py:561
  25.2 34.9 %collective-permute-done.refs_0_ = bf16[320,1536]{1,0:T(8,128)(2,1)S(1)} collective-permute-done((bf16[320,1536]{1,0:T(8,128)(2,1)S(1)}, bf16[320,1536]{1,0:T(8,128)(2,1)S(1)}, u32[]{:S(2)}, u32[]{:S(2)}) %collective-permute-start) | collective-permute-done | bytes 983072 | tf_op jit(solution)/shard_map/ppermute | solution.py:509
  65.6 6.9 %collective-permute-start.2 = (bf16[320,1536]{1,0:T(8,128)(2,1)}, bf16[320,1536]{1,0:T(8,128)(2,1)}, u32[]{:S(2)}, u32[]{:S(2)}) collective-permute-start(bf16[320,1536]{1,0:T(8,128)(2,1)} %get-tuple-element.170.refs_1_.refs_2_.refs_3_), channel_id=1, source_target_pairs={{0,2},{2,4},{4,6},{6,7},{7,5},{5,3},{3,1},{1,0},{8,10},{10,12},{12... | collective-permute-start | bytes 2949128 | tf_op jit(solution)/shard_map/ppermute | solution.py:509
  74.0 4.1 shard_map.292.refs_5_
  78.1 11.9 %collective-permute-done.4.refs_3_ = bf16[8,48,576]{2,1,0:T(8,128)(2,1)} collective-permute-done((bf16[8,48,576]{2,1,0:T(8,128)(2,1)}, bf16[8,48,576]{2,1,0:T(8,128)(2,1)}, u32[]{:S(2)}, u32[]{:S(2)}) %collective-permute-start.4) | collective-permute-done | bytes 442400 | tf_op jit(solution)/shard_map/ppermute | solution.py:539
  90.0 2.7 collective-permute-done.2.refs_0_
  92.7 2.8 collective-permute-done.3.refs_1_
  101.9 3.7 shard_map.295.refs_3_
  105.6 3.9 shard_map.294
  109.5 23.3 %collective-permute-done.5.refs_0_ = bf16[320,1536]{1,0:T(8,128)(2,1)S(1)} collective-permute-done((bf16[320,1536]{1,0:T(8,128)(2,1)}, bf16[320,1536]{1,0:T(8,128)(2,1)S(1)}, u32[]{:S(2)}, u32[]{:S(2)}) %collective-permute-start.5) | collective-permute-done | bytes 983072 | tf_op jit(solution)/shard_map/ppermute | solution.py:509
  144.1 10.6 %shard_map.297 = (bf16[2,1024,1536]{2,1,0:T(8,128)(2,1)}, bf16[2,576,1024]{2,1,0:T(8,128)(2,1)}, f32[2,384,1024]{2,1,0:T(8,128)}) custom-call(s32[12]{0:T(128)} %dynamic-slice_bitcast_fusion.index_ref.place_ref.ids_ref, bf16[320,1536]{1,0:T(8,128)(2,1)} %shard_map.288.after_ref.refs_0_.refs_1_, bf16[320,1536]{1,0:T(8,128)(2,1)} %get-tuple-element.170.refs_1_.refs_2_.refs_3_, ...), custom_call_target="tpu_custom_call" | custom-call | flops 2264924160 | bytes 15532032 | tf_op jit(solution)/shard_map/pallas_call | solution.py:1393
  154.7 24.6 %collective-permute-done.10.refs_1_ = bf16[160,1536]{1,0:T(8,128)(2,1)S(1)} collective-permute-done((bf16[160,1536]{1,0:T(8,128)(2,1)S(1)}, bf16[160,1536]{1,0:T(8,128)(2,1)S(1)}, u32[]{:S(2)}, u32[]{:S(2)}) %collective-permute-start.10) | collective-permute-done | bytes 491552 | tf_op jit(solution)/shard_map/ppermute | solution.py:512
  180.2 2.6 shard_map.302
  185.7 8.3 %shard_map.299 = (bf16[2,1024,1536]{2,1,0:T(8,128)(2,1)}, bf16[2,576,1024]{2,1,0:T(8,128)(2,1)}, f32[2,384,1024]{2,1,0:T(8,128)}) custom-call(s32[12]{0:T(128)} %dynamic-slice_bitcast_fusion.index_ref.place_ref.ids_ref, bf16[320,1536]{1,0:T(8,128)(2,1)} %get-tuple-element.181.refs_0_.refs_10_.refs_11_, ...), custom_call_target="tpu_custom_call", output_to_operand_aliasing={{0}: (10, {}), {1}: (11, {}), {2}: (12, {})} | custom-call | flops 1358954496 | bytes 10027008 | tf_op jit(solution)/shard_map/pallas_call | solution.py:1393
  194.7 11.3 %shard_map.300 = (bf16[8,192,256]{2,1,0:T(8,128)(2,1)}, f32[2,192,1024]{2,1,0:T(8,128)}, f32[2,192,1024]{2,1,0:T(8,128)}, f32[2,3,1,1024]{3,2,1,0:T(1,128)}) custom-call(f32[3]{0:T(128)} %dynamic_slice.8.gate_ref, bf16[2,576,1024]{2,1,0:T(8,128)(2,1)} %get-tuple-element.197.q_ref.k_ref.v_ref, bf16[2,576,1024]{2,1,0:T(8,128)(2,1)} %get-tuple-element.197.q_ref.k_ref.v_ref, ...), custom_call_target="tpu_custom_call" | custom-call | flops 6442450944 | bytes 7864320 | tf_op jit(solution)/shard_map/pallas_call | solution.py:1450
  208.8 3.5 all-to-all-start.1
  214.4 17.4 %all-to-all-done.1.refs_0_ = bf16[8,192,256]{2,1,0:T(8,128)(2,1)S(1)} async-done(((bf16[8,192,256]{2,1,0:T(8,128)(2,1)}), bf16[8,192,256]{2,1,0:T(8,128)(2,1)S(1)}, u32[]{:S(2)}, u32[]{:S(2)}) %all-to-all-start.1) | async-done | bytes 786464 | tf_op jit(solution)/shard_map/all_to_all | solution.py:561
  232.7 5.4 multiply_reduce_fusion.1
  240.8 5.9 collective-permute-done.15.refs_0_
  248.7 2.7 collective-permute-done.17.refs_1_
  253.0 3.2 collective-permute-start.20
  257.8 11.2 %collective-permute-done.20.refs_12_ = bf16[96,3072]{1,0:T(8,128)(2,1)S(1)} collective-permute-done((bf16[96,3072]{1,0:T(8,128)(2,1)S(1)}, bf16[96,3072]{1,0:T(8,128)(2,1)S(1)}, u32[]{:S(2)}, u32[]{:S(2)}) %collective-permute-start.20) | collective-permute-done | bytes 589856 | tf_op jit(solution)/shard_map/ppermute | solution.py:509
  269.0 3.8 collective-permute-done.21.refs_13_
  273.6 27.0 %shard_map.305 = (bf16[1024,1024]{1,0:T(8,128)(2,1)}, bf16[1024,2048]{1,0:T(8,128)(2,1)}, bf16[512,1536]{1,0:T(8,128)(2,1)}, bf16[512,1536]{1,0:T(8,128)(2,1)}, ...) custom-call(s32[12]{0:T(128)} %dynamic-slice_bitcast_fusion.index_ref.place_ref.ids_ref, ...), custom_call_target="tpu_custom_call" | custom-call | flops 16106127360 | bytes 37748736 | tf_op jit(solution)/shard_map/pallas_call | solution.py:1096
  302.5 3.4 collective-permute-done.22
  307.7 6.5 shard_map.308
  317.9 15.9 %shard_map.307.refs_0_.refs_1_ = bf16[1344,3072]{1,0:T(8,128)(2,1)} custom-call(s32[12]{0:T(128)} %dynamic-slice_bitcast_fusion.index_ref.place_ref.ids_ref, bf16[1024,1536]{1,0:T(8,128)(2,1)} %get-tuple-element.214.x_ref, bf16[1024,1024]{1,0:T(8,128)(2,1)} %get-tuple-element.215.hidden_ref.refs_4_, bf16[1024,2048]{1,0:T(8,128)(2,1)} %get-tuple-element.216.units_ref, ...), custom_call_target="tpu_custom_call" | custom-call | flops 8455716864 | bytes 16646144 | tf_op jit(solution)/shard_map/pallas_call | solution.py:1183
  333.8 3.5 shard_map.309
  339.5 3.8 fusion.26
  345.8 4.2 all-to-all-start.2
  350.1 2.6 bitcast_reduce_fusion.1
  352.7 5.4 shard_map.312.refs_1_
  360.2 7.6 %convolution_convert_fusion.refs_2_ = bf16[1024,1536]{1,0:T(8,128)(2,1)} fusion(bf16[1024,1024]{1,0:T(8,128)(2,1)} %get-tuple-element.229, bf16[1024,1536]{1,0:T(8,128)(2,1)} %get-tuple-element.230), kind=kOutput, calls=%fused_computation | convolution fusion | flops 3222798336 | bytes 8388608 | tf_op jit(solution)/shard_map/dot_general | solution.py:470
  372.2 24.4 %shard_map.314 = (bf16[2,3,192,1024]{3,2,1,0:T(8,128)(2,1)}, bf16[2,192,256]{2,1,0:T(8,128)(2,1)}, f32[2,3,1,1024]{3,2,1,0:T(1,128)}) custom-call(f32[3]{0:T(128)} %dynamic_slice.8.gate_ref, bf16[2,576,1024]{2,1,0:T(8,128)(2,1)} %get-tuple-element.197.q_ref.k_ref.v_ref, bf16[2,576,1024]{2,1,0:T(8,128)(2,1)} %get-tuple-element.197.q_ref.k_ref.v_ref, ...), custom_call_target="tpu_custom_call" | custom-call | flops 16106127360 | bytes 12582912 | tf_op jit(solution)/shard_map/pallas_call | solution.py:1575
  396.6 3.7 shard_map.315
  402.5 4.3 all-to-all-start.3
  407.1 4.0 shard_map.319
  415.2 10.2 %shard_map.317.refs_0_.refs_1_.terms_ref = bf16[1792,1536]{1,0:T(8,128)(2,1)} custom-call(s32[12]{0:T(128)} %dynamic-slice_bitcast_fusion.index_ref.place_ref.ids_ref, bf16[2,576,1024]{2,1,0:T(8,128)(2,1)} %get-tuple-element.242.grads_ref, bf16[576,1536]{1,0:T(8,128)(2,1)} %get-tuple-element.238.w_ref), custom_call_target="tpu_custom_call" | custom-call | flops 3170893824 | bytes 9338880 | tf_op jit(solution)/shard_map/pallas_call | solution.py:1224
  425.3 10.1 %shard_map.321 = (bf16[8,48,576]{2,1,0:T(8,128)(2,1)}, bf16[8,48,576]{2,1,0:T(8,128)(2,1)}, bf16[8,48,576]{2,1,0:T(8,128)(2,1)}, bf16[8,48,576]{2,1,0:T(8,128)(2,1)}) custom-call(s32[12]{0:T(128)} %dynamic-slice_bitcast_fusion.index_ref.place_ref.ids_ref, bf16[2,1024,1536]{2,1,0:T(8,128)(2,1)} %get-tuple-element.254.in_ref, ...), custom_call_target="tpu_custom_call" | custom-call | flops 3623878656 | bytes 10420224 | tf_op jit(solution)/shard_map/pallas_call | solution.py:1298
  435.4 29.2 %collective-permute-done.28.refs_2_ = bf16[128,1536]{1,0:T(8,128)(2,1)S(1)} collective-permute-done((bf16[128,1536]{1,0:T(8,128)(2,1)}, bf16[128,1536]{1,0:T(8,128)(2,1)S(1)}, u32[]{:S(2)}, u32[]{:S(2)}) %collective-permute-start.28) | collective-permute-done | bytes 393248 | tf_op jit(solution)/shard_map/ppermute | solution.py:509
  466.8 2.8 shard_map.318
  469.7 4.0 shard_map.320
  474.4 10.1 %collective-permute-start.32 = (bf16[256,1536]{1,0:T(8,128)(2,1)}, bf16[256,1536]{1,0:T(8,128)(2,1)}, u32[]{:S(2)}, u32[]{:S(2)}) collective-permute-start(bf16[256,1536]{1,0:T(8,128)(2,1)} %get-tuple-element.260), channel_id=1, source_target_pairs={{0,2},{2,4},{4,6},{6,7},{7,5},{5,3},{3,1},{1,0},{8,10},{10,12},{12... | collective-permute-start | bytes 2359304 | tf_op jit(solution)/shard_map/ppermute | solution.py:509
  486.6 3.1 fusion.9
  494.7 3.5 all-to-all-start.4
  499.1 7.6 %collective-permute-done.32.refs_2_ = bf16[256,1536]{1,0:T(8,128)(2,1)} collective-permute-done((bf16[256,1536]{1,0:T(8,128)(2,1)}, bf16[256,1536]{1,0:T(8,128)(2,1)}, u32[]{:S(2)}, u32[]{:S(2)}) %collective-permute-start.32) | collective-permute-done | bytes 786464 | tf_op jit(solution)/shard_map/ppermute | solution.py:509
  509.3 31.2 %collective-permute-done.33.refs_3_ = bf16[256,1536]{1,0:T(8,128)(2,1)} collective-permute-done((bf16[256,1536]{1,0:T(8,128)(2,1)}, bf16[256,1536]{1,0:T(8,128)(2,1)}, u32[]{:S(2)}, u32[]{:S(2)}) %collective-permute-start.33) | collective-permute-done | bytes 786464 | tf_op jit(solution)/shard_map/ppermute | solution.py:512
  540.5 3.2 shard_map.323
  546.8 3.4 shard_map.326.refs_2_
  555.2 5.1 all-to-all-start.5
  560.2 10.9 %collective-permute-done.40.refs_2_ = bf16[256,1536]{1,0:T(8,128)(2,1)} collective-permute-done((bf16[256,1536]{1,0:T(8,128)(2,1)}, bf16[256,1536]{1,0:T(8,128)(2,1)}, u32[]{:S(2)}, u32[]{:S(2)}) %collective-permute-start.40) | collective-permute-done | bytes 786464 | tf_op jit(solution)/shard_map/ppermute | solution.py:509
  572.8 3.2 shard_map.325
  576.0 2.4 collective-permute-done.42.refs_3_
  587.3 7.1 %shard_map.328 = (f32[192,4096]{1,0:T(8,128)}, f32[192,4096]{1,0:T(8,128)}, f32[512,1536]{1,0:T(8,128)}) custom-call(s32[12]{0:T(128)} %dynamic-slice_bitcast_fusion.index_ref.place_ref.ids_ref, bf16[192,3072]{1,0:T(8,128)(2,1)} %get-tuple-element.290.refs_0_, bf16[192,3072]{1,0:T(8,128)(2,1)} %get-tuple-element.291.refs_1_, ...), custom_call_target="tpu_custom_call" | custom-call | bytes 14155776 | tf_op jit(solution)/shard_map/pallas_call | solution.py:581
  594.9 4.1 collective-permute-done.45.refs_0_
  600.0 4.7 shard_map.330
  606.3 3.8 all-to-all-start.6
  611.3 5.7 all-to-all-done.6
  619.0 8.3 %shard_map.334 = (f32[512,1536]{1,0:T(8,128)}, f32[512,1536]{1,0:T(8,128)}) custom-call(s32[12]{0:T(128)} %dynamic-slice_bitcast_fusion.index_ref.place_ref.ids_ref, bf16[1024,512]{1,0:T(8,128)(2,1)} %get-tuple-element.314.cap_ref, bf16[1536,512]{1,0:T(8,128)(2,1)} %get-tuple-element.315.refs_0_, bf16[1536,512]{1,0:T(8,128)(2,1)} %get-tuple-element.316.refs_1_, ...), custom_call_target="tpu_custom_call" | custom-call | flops 3221225472 | bytes 12582912 | tf_op jit(solution)/shard_map/pallas_call | solution.py:701
  631.6 3.4 all-to-all-start.7
  635.7 3.0 fusion.11
  647.6 3.6 shard_map.332
  (304 shorter events, 125.1 us)
Async XLA Ops:
  15.7 46.8 %all-to-all-start = ((bf16[8,96,576]{2,1,0:T(8,128)(2,1)}), bf16[8,96,576]{2,1,0:T(8,128)(2,1)S(1)}, u32[]{:S(2)}, u32[]{:S(2)}) async-start(bf16[8,96,576]{2,1,0:T(8,128)(2,1)} %shard_map.289), calls=%async_computation | async-start | bytes 1966080 | tf_op jit(solution)/shard_map/all_to_all | solution.py:561
  23.1 86.4 %all-gather.4.cloned.1.call-start = ((), (), s32[]{:S(2)}) async-start(), calls=%async_computation.12 | async-start | bytes 1310720 | tf_op jit(solution)/shard_map/all_gather | solution.py:1698
  23.1 37.0 %collective-permute-start = (bf16[320,1536]{1,0:T(8,128)(2,1)S(1)}, bf16[320,1536]{1,0:T(8,128)(2,1)S(1)}, u32[]{:S(2)}, u32[]{:S(2)}) collective-permute-start(bf16[320,1536]{1,0:T(8,128)(2,1)S(1)} %copy-done.4), channel_id=1, source_target_pairs={{0,2},{2,4},{4,6},{6,7},{7,5},{5,3},{3,1},{1,0},{8,10},{10,12},{12... | collective-permute-start | bytes 2949128 | tf_op jit(solution)/shard_map/ppermute | solution.py:509
  25.2 37.3 %collective-permute-start.1 = (bf16[320,1536]{1,0:T(8,128)(2,1)S(1)}, bf16[320,1536]{1,0:T(8,128)(2,1)}, u32[]{:S(2)}, u32[]{:S(2)}) collective-permute-start(bf16[320,1536]{1,0:T(8,128)(2,1)S(1)} %copy-done.4), channel_id=1, source_target_pairs={{2,0},{4,2},{6,4},{7,6},{5,7},{3,5},{1,3},{0,1},{10,8},{12,10},{14... | collective-permute-start | bytes 2949128 | tf_op jit(solution)/shard_map/ppermute | solution.py:512
  65.6 113.7 %reduce-scatter.5.cloned.1.call-start = ((), (), s32[]{:S(2)}) async-start(), calls=%async_computation.13 | async-start | bytes 1769472 | tf_op jit(solution)/shard_map/reduce_scatter | solution.py:1707
  65.6 27.1 %collective-permute-start.2 = (bf16[320,1536]{1,0:T(8,128)(2,1)}, bf16[320,1536]{1,0:T(8,128)(2,1)}, u32[]{:S(2)}, u32[]{:S(2)}) collective-permute-start(bf16[320,1536]{1,0:T(8,128)(2,1)} %get-tuple-element.170.refs_1_.refs_2_.refs_3_), channel_id=1, source_target_pairs={{0,2},{2,4},{4,6},{6,7},{7,5},{5,3},{3,1},{1,0},{8,10},{10,12},{12... | collective-permute-start | bytes 2949128 | tf_op jit(solution)/shard_map/ppermute | solution.py:509
  72.5 23.0 %collective-permute-start.3 = (bf16[320,1536]{1,0:T(8,128)(2,1)}, bf16[320,1536]{1,0:T(8,128)(2,1)}, u32[]{:S(2)}, u32[]{:S(2)}) collective-permute-start(bf16[320,1536]{1,0:T(8,128)(2,1)} %get-tuple-element.171.refs_2_.refs_4_.refs_5_), channel_id=1, source_target_pairs={{2,0},{4,2},{6,4},{7,6},{5,7},{3,5},{1,3},{0,1},{10,8},{12,10},{14... | collective-permute-start | bytes 2949128 | tf_op jit(solution)/shard_map/ppermute | solution.py:512
  72.5 17.5 %collective-permute-start.4 = (bf16[8,48,576]{2,1,0:T(8,128)(2,1)}, bf16[8,48,576]{2,1,0:T(8,128)(2,1)}, u32[]{:S(2)}, u32[]{:S(2)}) collective-permute-start(bf16[8,48,576]{2,1,0:T(8,128)(2,1)} %get-tuple-element.173.refs_2_), channel_id=1, source_target_pairs={{0,16},{8,24},{16,0},{24,8},{1,17},{9,25},{17,1},{25,9},{2,18},{10... | collective-permute-start | bytes 1327112 | tf_op jit(solution)/shard_map/ppermute | solution.py:539
  95.5 113.2 %all-gather.6.cloned.1.call-start = ((), (), s32[]{:S(2)}) async-start(), calls=%async_computation.14 | async-start | bytes 3932160 | tf_op jit(solution)/shard_map/all_gather | solution.py:1710
  98.0 133.8 %all-gather.8.cloned.1.call-start = ((), (), s32[]{:S(2)}) async-start(), calls=%async_computation.15 | async-start | bytes 5898240 | tf_op jit(solution)/shard_map/all_gather | solution.py:1738
  98.1 34.8 %collective-permute-start.5 = (bf16[320,1536]{1,0:T(8,128)(2,1)}, bf16[320,1536]{1,0:T(8,128)(2,1)S(1)}, u32[]{:S(2)}, u32[]{:S(2)}) collective-permute-start(bf16[320,1536]{1,0:T(8,128)(2,1)} %get-tuple-element.176.refs_3_.refs_6_.refs_7_), channel_id=1, source_target_pairs={{0,2},{2,4},{4,6},{6,7},{7,5},{5,3},{3,1},{1,0},{8,10},{10,12},{12... | collective-permute-start | bytes 2949128 | tf_op jit(solution)/shard_map/ppermute | solution.py:509
  99.9 35.1 %collective-permute-start.6 = (bf16[320,1536]{1,0:T(8,128)(2,1)}, bf16[320,1536]{1,0:T(8,128)(2,1)S(1)}, u32[]{:S(2)}, u32[]{:S(2)}) collective-permute-start(bf16[320,1536]{1,0:T(8,128)(2,1)} %get-tuple-element.177.refs_4_.refs_8_.refs_9_), channel_id=1, source_target_pairs={{2,0},{4,2},{6,4},{7,6},{5,7},{3,5},{1,3},{0,1},{10,8},{12,10},{14... | collective-permute-start | bytes 2949128 | tf_op jit(solution)/shard_map/ppermute | solution.py:512
  135.9 43.4 %collective-permute-start.11 = (bf16[192,3072]{1,0:T(8,128)(2,1)}, bf16[192,3072]{1,0:T(8,128)(2,1)}, u32[]{:S(2)}, u32[]{:S(2)}) collective-permute-start(bf16[192,3072]{1,0:T(8,128)(2,1)} %get-tuple-element.183.refs_5_), channel_id=1, source_target_pairs={{0,2},{2,4},{4,6},{6,7},{7,5},{5,3},{3,1},{1,0},{8,10},{10,12},{12... | collective-permute-start | bytes 3538952 | tf_op jit(solution)/shard_map/ppermute | solution.py:509
  136.6 42.7 %collective-permute-start.12 = (bf16[192,3072]{1,0:T(8,128)(2,1)}, bf16[192,3072]{1,0:T(8,128)(2,1)}, u32[]{:S(2)}, u32[]{:S(2)}) collective-permute-start(bf16[192,3072]{1,0:T(8,128)(2,1)} %get-tuple-element.183.refs_5_), channel_id=1, source_target_pairs={{2,0},{4,2},{6,4},{7,6},{5,7},{3,5},{1,3},{0,1},{10,8},{12,10},{14... | collective-permute-start | bytes 3538952 | tf_op jit(solution)/shard_map/ppermute | solution.py:512
  139.0 40.2 %collective-permute-start.10 = (bf16[160,1536]{1,0:T(8,128)(2,1)S(1)}, bf16[160,1536]{1,0:T(8,128)(2,1)S(1)}, u32[]{:S(2)}, u32[]{:S(2)}) collective-permute-start(bf16[160,1536]{1,0:T(8,128)(2,1)S(1)} %slice.60), channel_id=1, source_target_pairs={{2,0},{4,2},{6,4},{7,6},{5,7},{3,5},{1,3},{0,1},{10,8},{12,10},{14... | collective-permute-start | bytes 1474568 | tf_op jit(solution)/shard_map/ppermute | solution.py:512
  140.2 39.1 %collective-permute-start.9 = (bf16[160,1536]{1,0:T(8,128)(2,1)S(1)}, bf16[160,1536]{1,0:T(8,128)(2,1)S(1)}, u32[]{:S(2)}, u32[]{:S(2)}) collective-permute-start(bf16[160,1536]{1,0:T(8,128)(2,1)S(1)} %slice.59), channel_id=1, source_target_pairs={{0,2},{2,4},{4,6},{6,7},{7,5},{5,3},{3,1},{1,0},{8,10},{10,12},{12... | collective-permute-start | bytes 1474568 | tf_op jit(solution)/shard_map/ppermute | solution.py:509
  182.8 25.1 %collective-permute-start.13 = (bf16[192,3072]{1,0:T(8,128)(2,1)}, bf16[192,3072]{1,0:T(8,128)(2,1)}, u32[]{:S(2)}, u32[]{:S(2)}) collective-permute-start(bf16[192,3072]{1,0:T(8,128)(2,1)} %get-tuple-element.190.refs_6_), channel_id=1, source_target_pairs={{0,2},{2,4},{4,6},{6,7},{7,5},{5,3},{3,1},{1,0},{8,10},{10,12},{12... | collective-permute-start | bytes 3538952 | tf_op jit(solution)/shard_map/ppermute | solution.py:509
  183.8 25.0 %collective-permute-start.14 = (bf16[192,3072]{1,0:T(8,128)(2,1)}, bf16[192,3072]{1,0:T(8,128)(2,1)}, u32[]{:S(2)}, u32[]{:S(2)}) collective-permute-start(bf16[192,3072]{1,0:T(8,128)(2,1)} %get-tuple-element.191.refs_7_), channel_id=1, source_target_pairs={{2,0},{4,2},{6,4},{7,6},{5,7},{3,5},{1,3},{0,1},{10,8},{12,10},{14... | collective-permute-start | bytes 3538952 | tf_op jit(solution)/shard_map/ppermute | solution.py:512
  208.8 23.1 %all-to-all-start.1 = ((bf16[8,192,256]{2,1,0:T(8,128)(2,1)}), bf16[8,192,256]{2,1,0:T(8,128)(2,1)S(1)}, u32[]{:S(2)}, u32[]{:S(2)}) async-start(bf16[8,192,256]{2,1,0:T(8,128)(2,1)} %get-tuple-element.202), calls=%async_computation.2 | async-start | bytes 1572864 | tf_op jit(solution)/shard_map/all_to_all | solution.py:561
  212.3 34.4 %collective-permute-start.15 = (bf16[192,3072]{1,0:T(8,128)(2,1)}, bf16[192,3072]{1,0:T(8,128)(2,1)}, u32[]{:S(2)}, u32[]{:S(2)}) collective-permute-start(bf16[192,3072]{1,0:T(8,128)(2,1)} %get-tuple-element.200.refs_8_), channel_id=1, source_target_pairs={{0,2},{2,4},{4,6},{6,7},{7,5},{5,3},{3,1},{1,0},{8,10},{10,12},{12... | collective-permute-start | bytes 3538952 | tf_op jit(solution)/shard_map/ppermute | solution.py:509
  214.2 34.5 %collective-permute-start.16 = (bf16[192,3072]{1,0:T(8,128)(2,1)}, bf16[192,3072]{1,0:T(8,128)(2,1)}, u32[]{:S(2)}, u32[]{:S(2)}) collective-permute-start(bf16[192,3072]{1,0:T(8,128)(2,1)} %get-tuple-element.201.refs_9_), channel_id=1, source_target_pairs={{2,0},{4,2},{6,4},{7,6},{5,7},{3,5},{1,3},{0,1},{10,8},{12,10},{14... | collective-permute-start | bytes 3538952 | tf_op jit(solution)/shard_map/ppermute | solution.py:512
  239.3 12.1 %collective-permute-start.17 = (bf16[256,1536]{1,0:T(8,128)(2,1)S(1)}, bf16[256,1536]{1,0:T(8,128)(2,1)}, u32[]{:S(2)}, u32[]{:S(2)}) collective-permute-start(bf16[256,1536]{1,0:T(8,128)(2,1)S(1)} %fusion.5.refs_2_), channel_id=1, source_target_pairs={{0,16},{8,24},{16,0},{24,8},{1,17},{9,25},{17,1},{25,9},{2,18},{10... | collective-permute-start | bytes 2359304 | tf_op jit(solution)/shard_map/ppermute | solution.py:539
  251.4 21.4 %collective-permute-start.18 = (bf16[256,1536]{1,0:T(8,128)(2,1)}, bf16[256,1536]{1,0:T(8,128)(2,1)}, u32[]{:S(2)}, u32[]{:S(2)}) collective-permute-start(bf16[256,1536]{1,0:T(8,128)(2,1)} %get-tuple-element.205.refs_0_), channel_id=1, source_target_pairs={{0,8},{8,0},{16,24},{24,16},{1,9},{9,1},{17,25},{25,17},{2,10},{10... | collective-permute-start | bytes 2359304 | tf_op jit(solution)/shard_map/ppermute | solution.py:539
  251.4 22.2 %collective-permute-start.19 = (bf16[256,1536]{1,0:T(8,128)(2,1)}, bf16[256,1536]{1,0:T(8,128)(2,1)}, u32[]{:S(2)}, u32[]{:S(2)}) collective-permute-start(bf16[256,1536]{1,0:T(8,128)(2,1)} %collective-permute-done.17.refs_1_), channel_id=1, source_target_pairs={{0,8},{8,0},{16,24},{24,16},{1,9},{9,1},{17,25},{25,17},{2,10},{10... | collective-permute-start | bytes 2359304 | tf_op jit(solution)/shard_map/ppermute | solution.py:539
  253.0 16.0 %collective-permute-start.20 = (bf16[96,3072]{1,0:T(8,128)(2,1)S(1)}, bf16[96,3072]{1,0:T(8,128)(2,1)S(1)}, u32[]{:S(2)}, u32[]{:S(2)}) collective-permute-start(bf16[96,3072]{1,0:T(8,128)(2,1)S(1)} %slice.63), channel_id=1, source_target_pairs={{0,2},{2,4},{4,6},{6,7},{7,5},{5,3},{3,1},{1,0},{8,10},{10,12},{12... | collective-permute-start | bytes 1769480 | tf_op jit(solution)/shard_map/ppermute | solution.py:509
  257.3 15.5 %collective-permute-start.21 = (bf16[96,3072]{1,0:T(8,128)(2,1)S(1)}, bf16[96,3072]{1,0:T(8,128)(2,1)S(1)}, u32[]{:S(2)}, u32[]{:S(2)}) collective-permute-start(bf16[96,3072]{1,0:T(8,128)(2,1)S(1)} %slice.64), channel_id=1, source_target_pairs={{2,0},{4,2},{6,4},{7,6},{5,7},{3,5},{1,3},{0,1},{10,8},{12,10},{14... | collective-permute-start | bytes 1769480 | tf_op jit(solution)/shard_map/ppermute | solution.py:512
  314.2 19.6 %collective-permute-start.24 = (bf16[96,3072]{1,0:T(8,128)(2,1)}, bf16[96,3072]{1,0:T(8,128)(2,1)}, u32[]{:S(2)}, u32[]{:S(2)}) collective-permute-start(bf16[96,3072]{1,0:T(8,128)(2,1)} %get-tuple-element.217), channel_id=1, source_target_pairs={{0,2},{2,4},{4,6},{6,7},{7,5},{5,3},{3,1},{1,0},{8,10},{10,12},{12... | collective-permute-start | bytes 1769480 | tf_op jit(solution)/shard_map/ppermute | solution.py:509
  314.5 19.3 %collective-permute-start.25 = (bf16[96,3072]{1,0:T(8,128)(2,1)}, bf16[96,3072]{1,0:T(8,128)(2,1)}, u32[]{:S(2)}, u32[]{:S(2)}) collective-permute-start(bf16[96,3072]{1,0:T(8,128)(2,1)} %get-tuple-element.218), channel_id=1, source_target_pairs={{2,0},{4,2},{6,4},{7,6},{5,7},{3,5},{1,3},{0,1},{10,8},{12,10},{14... | collective-permute-start | bytes 1769480 | tf_op jit(solution)/shard_map/ppermute | solution.py:512
  316.4 20.9 %collective-permute-start.23 = (bf16[256,1536]{1,0:T(8,128)(2,1)}, bf16[256,1536]{1,0:T(8,128)(2,1)}, u32[]{:S(2)}, u32[]{:S(2)}) collective-permute-start(bf16[256,1536]{1,0:T(8,128)(2,1)} %get-tuple-element.213), channel_id=1, source_target_pairs={{0,16},{8,24},{16,0},{24,8},{1,17},{9,25},{17,1},{25,9},{2,18},{10... | collective-permute-start | bytes 2359304 | tf_op jit(solution)/shard_map/ppermute | solution.py:539
  345.8 24.2 %all-to-all-start.2 = ((bf16[8,192,256]{2,1,0:T(8,128)(2,1)}), bf16[8,192,256]{2,1,0:T(8,128)(2,1)}, u32[]{:S(2)}, u32[]{:S(2)}) async-start(bf16[8,192,256]{2,1,0:T(8,128)(2,1)} %get-tuple-element.226), calls=%async_computation.3 | async-start | bytes 1572864 | tf_op jit(solution)/shard_map/all_to_all | solution.py:561
  350.1 139.6 %reduce-scatter.9.cloned.1.call-start = ((), (), s32[]{:S(2)}) async-start(), calls=%async_computation.17 | async-start | bytes 5898240 | tf_op jit(solution)/shard_map/reduce_scatter | solution.py:1817
  370.1 208.3 %reduce-scatter.7.cloned.1.call-start = ((), (), s32[]{:S(2)}) async-start(), calls=%async_computation.16 | async-start | bytes 3932160 | tf_op jit(solution)/shard_map/reduce_scatter | solution.py:1829
  370.1 30.2 %collective-permute-start.26 = (bf16[192,3072]{1,0:T(8,128)(2,1)}, bf16[192,3072]{1,0:T(8,128)(2,1)}, u32[]{:S(2)}, u32[]{:S(2)}) collective-permute-start(bf16[192,3072]{1,0:T(8,128)(2,1)} %get-tuple-element.221), channel_id=1, source_target_pairs={{0,2},{2,4},{4,6},{6,7},{7,5},{5,3},{3,1},{1,0},{8,10},{10,12},{12... | collective-permute-start | bytes 3538952 | tf_op jit(solution)/shard_map/ppermute | solution.py:509
  370.5 29.8 %collective-permute-start.27 = (bf16[192,3072]{1,0:T(8,128)(2,1)}, bf16[192,3072]{1,0:T(8,128)(2,1)}, u32[]{:S(2)}, u32[]{:S(2)}) collective-permute-start(bf16[192,3072]{1,0:T(8,128)(2,1)} %get-tuple-element.222), channel_id=1, source_target_pairs={{2,0},{4,2},{6,4},{7,6},{5,7},{3,5},{1,3},{0,1},{10,8},{12,10},{14... | collective-permute-start | bytes 3538952 | tf_op jit(solution)/shard_map/ppermute | solution.py:512
  402.5 71.1 %all-to-all-start.3 = ((bf16[8,192,512]{2,1,0:T(8,128)(2,1)}), bf16[8,192,512]{2,1,0:T(8,128)(2,1)}, u32[]{:S(2)}, u32[]{:S(2)}) async-start(bf16[8,192,512]{2,1,0:T(8,128)(2,1)} %broadcast_in_dim.25), calls=%async_computation.4 | async-start | bytes 3145728 | tf_op jit(solution)/shard_map/all_to_all | solution.py:555
  406.8 171.6 %reduce-scatter.11.cloned.1.call-start = ((), (), s32[]{:S(2)}) async-start(), calls=%async_computation.18 | async-start | bytes 1327104 | tf_op jit(solution)/shard_map/reduce_scatter | solution.py:1818
  411.1 58.5 %collective-permute-start.30 = (bf16[192,3072]{1,0:T(8,128)(2,1)}, bf16[192,3072]{1,0:T(8,128)(2,1)}, u32[]{:S(2)}, u32[]{:S(2)}) collective-permute-start(bf16[192,3072]{1,0:T(8,128)(2,1)} %get-tuple-element.250), channel_id=1, source_target_pairs={{0,2},{2,4},{4,6},{6,7},{7,5},{5,3},{3,1},{1,0},{8,10},{10,12},{12... | collective-permute-start | bytes 3538952 | tf_op jit(solution)/shard_map/ppermute | solution.py:509
  413.0 56.7 %collective-permute-start.31 = (bf16[192,3072]{1,0:T(8,128)(2,1)}, bf16[192,3072]{1,0:T(8,128)(2,1)}, u32[]{:S(2)}, u32[]{:S(2)}) collective-permute-start(bf16[192,3072]{1,0:T(8,128)(2,1)} %get-tuple-element.251), channel_id=1, source_target_pairs={{2,0},{4,2},{6,4},{7,6},{5,7},{3,5},{1,3},{0,1},{10,8},{12,10},{14... | collective-permute-start | bytes 3538952 | tf_op jit(solution)/shard_map/ppermute | solution.py:512
  413.1 51.5 %collective-permute-start.28 = (bf16[128,1536]{1,0:T(8,128)(2,1)}, bf16[128,1536]{1,0:T(8,128)(2,1)S(1)}, u32[]{:S(2)}, u32[]{:S(2)}) collective-permute-start(bf16[128,1536]{1,0:T(8,128)(2,1)} %get-tuple-element.243), channel_id=1, source_target_pairs={{0,2},{2,4},{4,6},{6,7},{7,5},{5,3},{3,1},{1,0},{8,10},{10,12},{12... | collective-permute-start | bytes 1179656 | tf_op jit(solution)/shard_map/ppermute | solution.py:509
  415.0 51.8 %collective-permute-start.29 = (bf16[128,1536]{1,0:T(8,128)(2,1)}, bf16[128,1536]{1,0:T(8,128)(2,1)}, u32[]{:S(2)}, u32[]{:S(2)}) collective-permute-start(bf16[128,1536]{1,0:T(8,128)(2,1)} %get-tuple-element.244), channel_id=1, source_target_pairs={{2,0},{4,2},{6,4},{7,6},{5,7},{3,5},{1,3},{0,1},{10,8},{12,10},{14... | collective-permute-start | bytes 1179656 | tf_op jit(solution)/shard_map/ppermute | solution.py:512
  473.7 11.6 %collective-permute-start.37 = (bf16[8,48,576]{2,1,0:T(8,128)(2,1)}, bf16[8,48,576]{2,1,0:T(8,128)(2,1)S(1)}, u32[]{:S(2)}, u32[]{:S(2)}) collective-permute-start(bf16[8,48,576]{2,1,0:T(8,128)(2,1)} %get-tuple-element.269), channel_id=1, source_target_pairs={{0,8},{8,0},{16,24},{24,16},{1,9},{9,1},{17,25},{25,17},{2,10},{10... | collective-permute-start | bytes 1327112 | tf_op jit(solution)/shard_map/ppermute | solution.py:539
  473.7 71.9 %collective-permute-start.39 = (bf16[1536,512]{1,0:T(8,128)(2,1)}, bf16[1536,512]{1,0:T(8,128)(2,1)}, u32[]{:S(2)}, u32[]{:S(2)}) collective-permute-start(bf16[1536,512]{1,0:T(8,128)(2,1)} %get-tuple-element.270.refs_6_), channel_id=1, source_target_pairs={{0,16},{8,24},{16,0},{24,8},{1,17},{9,25},{17,1},{25,9},{2,18},{10... | collective-permute-start | bytes 4718600 | tf_op jit(solution)/shard_map/ppermute | solution.py:539
  474.3 15.4 %collective-permute-start.36 = (bf16[8,48,576]{2,1,0:T(8,128)(2,1)}, bf16[8,48,576]{2,1,0:T(8,128)(2,1)S(1)}, u32[]{:S(2)}, u32[]{:S(2)}) collective-permute-start(bf16[8,48,576]{2,1,0:T(8,128)(2,1)} %get-tuple-element.267), channel_id=1, source_target_pairs={{0,8},{8,0},{16,24},{24,16},{1,9},{9,1},{17,25},{25,17},{2,10},{10... | collective-permute-start | bytes 1327112 | tf_op jit(solution)/shard_map/ppermute | solution.py:539
  474.4 32.3 %collective-permute-start.32 = (bf16[256,1536]{1,0:T(8,128)(2,1)}, bf16[256,1536]{1,0:T(8,128)(2,1)}, u32[]{:S(2)}, u32[]{:S(2)}) collective-permute-start(bf16[256,1536]{1,0:T(8,128)(2,1)} %get-tuple-element.260), channel_id=1, source_target_pairs={{0,2},{2,4},{4,6},{6,7},{7,5},{5,3},{3,1},{1,0},{8,10},{10,12},{12... | collective-permute-start | bytes 2359304 | tf_op jit(solution)/shard_map/ppermute | solution.py:509
  484.6 61.0 %collective-permute-start.34 = (bf16[192,3072]{1,0:T(8,128)(2,1)}, bf16[192,3072]{1,0:T(8,128)(2,1)}, u32[]{:S(2)}, u32[]{:S(2)}) collective-permute-start(bf16[192,3072]{1,0:T(8,128)(2,1)} %get-tuple-element.264), channel_id=1, source_target_pairs={{0,2},{2,4},{4,6},{6,7},{7,5},{5,3},{3,1},{1,0},{8,10},{10,12},{12... | collective-permute-start | bytes 3538952 | tf_op jit(solution)/shard_map/ppermute | solution.py:509
  485.2 60.3 %collective-permute-start.35 = (bf16[192,3072]{1,0:T(8,128)(2,1)}, bf16[192,3072]{1,0:T(8,128)(2,1)}, u32[]{:S(2)}, u32[]{:S(2)}) collective-permute-start(bf16[192,3072]{1,0:T(8,128)(2,1)} %get-tuple-element.265), channel_id=1, source_target_pairs={{2,0},{4,2},{6,4},{7,6},{5,7},{3,5},{1,3},{0,1},{10,8},{12,10},{14... | collective-permute-start | bytes 3538952 | tf_op jit(solution)/shard_map/ppermute | solution.py:512
  490.5 50.0 %collective-permute-start.33 = (bf16[256,1536]{1,0:T(8,128)(2,1)}, bf16[256,1536]{1,0:T(8,128)(2,1)}, u32[]{:S(2)}, u32[]{:S(2)}) collective-permute-start(bf16[256,1536]{1,0:T(8,128)(2,1)} %get-tuple-element.261), channel_id=1, source_target_pairs={{2,0},{4,2},{6,4},{7,6},{5,7},{3,5},{1,3},{0,1},{10,8},{12,10},{14... | collective-permute-start | bytes 2359304 | tf_op jit(solution)/shard_map/ppermute | solution.py:512
  494.7 50.8 %all-to-all-start.4 = ((bf16[8,2,16,512]{3,2,1,0:T(8,128)(2,1)}), bf16[8,2,16,512]{3,2,1,0:T(8,128)(2,1)S(1)}, u32[]{:S(2)}, u32[]{:S(2)}) async-start(bf16[8,2,16,512]{3,2,1,0:T(8,128)(2,1)} %bitcast.107), calls=%async_computation.5 | async-start | bytes 524288 | tf_op jit(solution)/shard_map/all_to_all | solution.py:561
  506.7 38.9 %collective-permute-start.38 = (bf16[8,48,576]{2,1,0:T(8,128)(2,1)}, bf16[8,48,576]{2,1,0:T(8,128)(2,1)}, u32[]{:S(2)}, u32[]{:S(2)}) collective-permute-start(bf16[8,48,576]{2,1,0:T(8,128)(2,1)} %add_convert_fusion.2), channel_id=1, source_target_pairs={{0,16},{8,24},{16,0},{24,8},{1,17},{9,25},{17,1},{25,9},{2,18},{10... | collective-permute-start | bytes 1327112 | tf_op jit(solution)/shard_map/ppermute | solution.py:539
  546.3 32.1 %collective-permute-start.43 = (bf16[1536,512]{1,0:T(8,128)(2,1)}, bf16[1536,512]{1,0:T(8,128)(2,1)}, u32[]{:S(2)}, u32[]{:S(2)}) collective-permute-start(bf16[1536,512]{1,0:T(8,128)(2,1)} %get-tuple-element.277.refs_4_), channel_id=1, source_target_pairs={{0,8},{8,0},{16,24},{24,16},{1,9},{9,1},{17,25},{25,17},{2,10},{10... | collective-permute-start | bytes 4718600 | tf_op jit(solution)/shard_map/ppermute | solution.py:539
  546.3 32.1 %collective-permute-start.44 = (bf16[1536,512]{1,0:T(8,128)(2,1)}, bf16[1536,512]{1,0:T(8,128)(2,1)}, u32[]{:S(2)}, u32[]{:S(2)}) collective-permute-start(bf16[1536,512]{1,0:T(8,128)(2,1)} %get-tuple-element.278.refs_5_), channel_id=1, source_target_pairs={{0,8},{8,0},{16,24},{24,16},{1,9},{9,1},{17,25},{25,17},{2,10},{10... | collective-permute-start | bytes 4718600 | tf_op jit(solution)/shard_map/ppermute | solution.py:539
  550.2 28.2 %collective-permute-start.42 = (bf16[192,3072]{1,0:T(8,128)(2,1)}, bf16[192,3072]{1,0:T(8,128)(2,1)}, u32[]{:S(2)}, u32[]{:S(2)}) collective-permute-start(bf16[192,3072]{1,0:T(8,128)(2,1)} %shard_map.326.refs_2_), channel_id=1, source_target_pairs={{0,16},{8,24},{16,0},{24,8},{1,17},{9,25},{17,1},{25,9},{2,18},{10... | collective-permute-start | bytes 3538952 | tf_op jit(solution)/shard_map/ppermute | solution.py:539
  551.0 20.2 %collective-permute-start.40 = (bf16[256,1536]{1,0:T(8,128)(2,1)}, bf16[256,1536]{1,0:T(8,128)(2,1)}, u32[]{:S(2)}, u32[]{:S(2)}) collective-permute-start(bf16[256,1536]{1,0:T(8,128)(2,1)} %get-tuple-element.271), channel_id=1, source_target_pairs={{0,2},{2,4},{4,6},{6,7},{7,5},{5,3},{3,1},{1,0},{8,10},{10,12},{12... | collective-permute-start | bytes 2359304 | tf_op jit(solution)/shard_map/ppermute | solution.py:509
  552.0 20.8 %collective-permute-start.41 = (bf16[256,1536]{1,0:T(8,128)(2,1)}, bf16[256,1536]{1,0:T(8,128)(2,1)}, u32[]{:S(2)}, u32[]{:S(2)}) collective-permute-start(bf16[256,1536]{1,0:T(8,128)(2,1)} %get-tuple-element.272), channel_id=1, source_target_pairs={{2,0},{4,2},{6,4},{7,6},{5,7},{3,5},{1,3},{0,1},{10,8},{12,10},{14... | collective-permute-start | bytes 2359304 | tf_op jit(solution)/shard_map/ppermute | solution.py:512
  555.2 28.0 %all-to-all-start.5 = ((bf16[8,48,576]{2,1,0:T(8,128)(2,1)}), bf16[8,48,576]{2,1,0:T(8,128)(2,1)}, u32[]{:S(2)}, u32[]{:S(2)}) async-start(bf16[8,48,576]{2,1,0:T(8,128)(2,1)} %add_convert_fusion.1), calls=%async_computation.9 | async-start | bytes 983040 | tf_op jit(solution)/shard_map/all_to_all | solution.py:561
  579.1 19.8 %collective-permute-start.45 = (bf16[256,1536]{1,0:T(8,128)(2,1)}, bf16[256,1536]{1,0:T(8,128)(2,1)}, u32[]{:S(2)}, u32[]{:S(2)}) collective-permute-start(bf16[256,1536]{1,0:T(8,128)(2,1)} %get-tuple-element.281), channel_id=1, source_target_pairs={{0,2},{2,4},{4,6},{6,7},{7,5},{5,3},{3,1},{1,0},{8,10},{10,12},{12... | collective-permute-start | bytes 2359304 | tf_op jit(solution)/shard_map/ppermute | solution.py:509
  579.4 20.5 %collective-permute-start.46 = (bf16[256,1536]{1,0:T(8,128)(2,1)}, bf16[256,1536]{1,0:T(8,128)(2,1)}, u32[]{:S(2)}, u32[]{:S(2)}) collective-permute-start(bf16[256,1536]{1,0:T(8,128)(2,1)} %get-tuple-element.282), channel_id=1, source_target_pairs={{2,0},{4,2},{6,4},{7,6},{5,7},{3,5},{1,3},{0,1},{10,8},{12,10},{14... | collective-permute-start | bytes 2359304 | tf_op jit(solution)/shard_map/ppermute | solution.py:512
  583.2 11.7 %collective-permute-start.47 = (bf16[8,48,576]{2,1,0:T(8,128)(2,1)}, bf16[8,48,576]{2,1,0:T(8,128)(2,1)}, u32[]{:S(2)}, u32[]{:S(2)}) collective-permute-start(bf16[8,48,576]{2,1,0:T(8,128)(2,1)} %all-to-all-done.5.refs_6_), channel_id=1, source_target_pairs={{0,16},{8,24},{16,0},{24,8},{1,17},{9,25},{17,1},{25,9},{2,18},{10... | collective-permute-start | bytes 1327112 | tf_op jit(solution)/shard_map/ppermute | solution.py:539
  606.3 10.7 %all-to-all-start.6 = ((f32[8,2,1155]{2,1,0:T(2,128)}), f32[8,2,1155]{2,1,0:T(2,128)S(1)}, u32[]{:S(2)}, u32[]{:S(2)}) async-start(f32[8,2,1155]{2,1,0:T(2,128)} %get-tuple-element.307), calls=%async_computation.10 | async-start | bytes 163840 | tf_op jit(solution)/shard_map/all_to_all | solution.py:561
  617.2 10.9 %collective-permute-start.50 = (f32[2,2200]{1,0:T(2,128)S(1)}, f32[2,2200]{1,0:T(2,128)S(1)}, u32[]{:S(2)}, u32[]{:S(2)}) collective-permute-start(f32[2,2200]{1,0:T(2,128)S(1)} %pad_maximum_fusion.3), channel_id=1, source_target_pairs={{0,16},{8,24},{16,0},{24,8},{1,17},{9,25},{17,1},{25,9},{2,18},{10... | collective-permute-start | bytes 52808 | tf_op jit(solution)/shard_map/ppermute | solution.py:539
  627.6 14.9 %collective-permute-start.56 = (bf16[192,384]{1,0:T(8,128)(2,1)S(1)}, bf16[192,384]{1,0:T(8,128)(2,1)S(1)}, u32[]{:S(2)}, u32[]{:S(2)}) collective-permute-start(bf16[192,384]{1,0:T(8,128)(2,1)S(1)} %copy-done.17), channel_id=1, source_target_pairs={{0,8},{8,0},{16,24},{24,16},{1,9},{9,1},{17,25},{25,17},{2,10},{10... | collective-permute-start | bytes 442376 | tf_op jit(solution)/shard_map/ppermute | solution.py:539
  627.6 18.5 %collective-permute-start.53 = (bf16[8,48,576]{2,1,0:T(8,128)(2,1)}, bf16[8,48,576]{2,1,0:T(8,128)(2,1)S(1)}, u32[]{:S(2)}, u32[]{:S(2)}) collective-permute-start(bf16[8,48,576]{2,1,0:T(8,128)(2,1)} %get-tuple-element.308.refs_0_), channel_id=1, source_target_pairs={{0,8},{8,0},{16,24},{24,16},{1,9},{9,1},{17,25},{25,17},{2,10},{10... | collective-permute-start | bytes 1327112 | tf_op jit(solution)/shard_map/ppermute | solution.py:539
  631.6 10.2 %all-to-all-start.7 = ((f32[8,2,1024]{2,1,0:T(2,128)}), f32[8,2,1024]{2,1,0:T(2,128)S(1)}, u32[]{:S(2)}, u32[]{:S(2)}) async-start(f32[8,2,1024]{2,1,0:T(2,128)} %broadcast_in_dim.56), calls=%async_computation.11 | async-start | bytes 131072 | tf_op jit(solution)/shard_map/all_to_all | solution.py:555
  635.0 11.0 %collective-permute-start.54 = (bf16[8,48,576]{2,1,0:T(8,128)(2,1)}, bf16[8,48,576]{2,1,0:T(8,128)(2,1)S(1)}, u32[]{:S(2)}, u32[]{:S(2)}) collective-permute-start(bf16[8,48,576]{2,1,0:T(8,128)(2,1)} %get-tuple-element.309.refs_1_), channel_id=1, source_target_pairs={{0,8},{8,0},{16,24},{24,16},{1,9},{9,1},{17,25},{25,17},{2,10},{10... | collective-permute-start | bytes 1327112 | tf_op jit(solution)/shard_map/ppermute | solution.py:539
  (58 other events, 232.2 us)
Sparse Core Ops, SparseCore 0:
  65.7 25.2 all-gather.3
  98.6 28.2 all-gather.5
  183.0 35.1 all-gather.7
  370.2 45.8 reduce-scatter.8
  419.1 37.9 reduce-scatter.6
  489.8 66.0 reduce-scatter.10
Sparse Core Ops, SparseCore 1:
  95.6 72.8 reduce-scatter.4
